TPU v7x, 32 devices: a whole 2x2x4 slice. The times are simulated.
32 devices in a mesh: seq: 8 (over z, x), kv: 4 (over y, core).
Axes of the slice: x: 2, y: 2, z: 4, core: 2. Of those that a mesh axis runs over, the one named last changes fastest.
Arguments:
- tokens: bfloat16 [8192, 2048], P('seq'), may hold values from -6 to 6
- attention_norm_gain: bfloat16 [2048], replicated, may hold values from 0.5 to 1.5
- query_weight: bfloat16 [2048, 2048], P(None, 'kv'), may hold values from -0.125 to 0.125
- key_weight: bfloat16 [2048, 512], P(None, 'kv'), may hold values from -0.125 to 0.125
- value_weight: bfloat16 [2048, 512], P(None, 'kv'), may hold values from -0.125 to 0.125
- query_down_adapter: bfloat16 [2048, 8], replicated, may hold values from -0.125 to 0.125
- query_up_adapter: bfloat16 [8, 32, 64], P(None, 'kv'), may hold values from -2 to 2
- key_down_adapter: bfloat16 [2048, 8], replicated, may hold values from -0.125 to 0.125
- key_up_adapter: bfloat16 [8, 8, 64], P(None, 'kv'), may hold values from -2 to 2
- value_down_adapter: bfloat16 [2048, 8], replicated, may hold values from -0.125 to 0.125
- value_up_adapter: bfloat16 [8, 8, 64], P(None, 'kv'), may hold values from -2 to 2
- query_feature_map: bfloat16 [32, 64, 64], P('kv'), may hold values from -0.75 to 0.75
- key_feature_map: bfloat16 [8, 64, 64], P('kv'), may hold values from -0.75 to 0.75
- output_weight: bfloat16 [2048, 2048], P('kv'), may hold values from -0.5 to 0.5
- output_down_adapter: bfloat16 [32, 64, 8], P('kv'), may hold values from -0.125 to 0.125
- output_up_adapter: bfloat16 [8, 2048], replicated, may hold values from -4 to 4
- feedforward_norm_gain: bfloat16 [2048], replicated, may hold values from 0.5 to 1.5
- gate_weight: bfloat16 [2048, 8192], P(None, 'kv'), may hold values from -0.125 to 0.125
- up_weight: bfloat16 [2048, 8192], P(None, 'kv'), may hold values from -0.125 to 0.125
- down_weight: bfloat16 [8192, 2048], P('kv'), may hold values from -0.0625 to 0.0625
- document_start_mask: int32 [8192], P('seq'), may hold values from 0 to 1, as said below
- output_cotangent: bfloat16 [8192, 2048], P('seq'), may hold values from -6 to 6
Outputs:
- output: bfloat16 [8192, 2048], P('seq')
- grad_tokens: float32 [8192, 2048], P('seq')
- grad_norm1: float32 [2048], P('seq')
- grad_wq: float32 [2048, 2048], P('seq', 'kv')
- grad_wk: float32 [2048, 512], P('seq', 'kv')
- grad_wv: float32 [2048, 512], P('seq', 'kv')
- grad_aq: float32 [2048, 8], P('seq')
- grad_bq: float32 [8, 32, 64], P(None, 'kv', 'seq')
- grad_ak: float32 [2048, 8], P('seq')
- grad_bk: float32 [8, 8, 64], P(None, 'kv', 'seq')
- grad_av: float32 [2048, 8], P('seq')
- grad_bv: float32 [8, 8, 64], P(None, 'kv', 'seq')
- grad_featq: float32 [32, 64, 64], P('kv', 'seq')
- grad_featk: float32 [8, 64, 64], P('kv', 'seq')
- grad_wo: float32 [2048, 2048], P('kv', 'seq')
- grad_ao: float32 [32, 64, 8], P('kv', 'seq')
- grad_bo: float32 [8, 2048], P(None, 'seq')
- grad_norm2: float32 [2048], P('seq')
- grad_gate: float32 [2048, 8192], P('seq', 'kv')
- grad_up: float32 [2048, 8192], P('seq', 'kv')
- grad_down: float32 [8192, 2048], P('kv', 'seq')
Inputs may be any that keep to these rules, and one draw needn't show every extreme that they name: `document_start_mask`: position 0 begins a document. One document begins in the first 512 positions and runs into the last 1024 positions of the stream; the other documents lie before or after it.
All inputs are finite; a program needn't handle non-finite values.
Results may differ from a plain program's by a relative error of at most 0.02.
Values may be sent and summed in bfloat16 or wider, within the bound.
No kernel may reach another device: no remote copies, remote signals or barrier semaphores. Data moves between devices by JAX's collectives and lax.ppermute only.
A program may use at most 384 MiB of HBM per device.

v0:
```python
import jax
import jax.numpy as jnp
from jax import lax
from jax.sharding import PartitionSpec as P

WIN = 64


EPSILON = 1e-05
MATRIX_EXACTNESS = lax.Precision.HIGHEST


def from_behind(x, axis, by):
    count = lax.axis_size(axis)
    pairs = [(i, i + by) for i in range(count) if 0 <= i + by < count]
    return lax.ppermute(x, axis, pairs)


def carried_in(part, axis, combine, identity):
    place = lax.axis_index(axis)
    gathered = jax.tree.map(lambda a: lax.all_gather(a, axis), part)
    state = jax.tree.map(lambda a, e: jnp.zeros_like(a) + jnp.asarray(e, a.dtype), part, identity)

    def one(step, state):
        return combine(
            state, jax.tree.map(lambda a: lax.dynamic_index_in_dim(a, step, 0, False), gathered)
        )

    return lax.fori_loop(0, place, one, state)


def carried_in_2(x, axis, join, neutral):
    count = lax.axis_size(axis)
    place = lax.axis_index(axis)
    ahead = count - 1 - place
    gathered = jax.tree.map(
        lambda a, kind: lax.all_gather(a.astype(kind), axis),
        x,
        (jnp.bfloat16, jnp.bfloat16, jnp.bfloat16),
    )
    state = jax.tree.map(lambda a, e: jnp.zeros_like(a) + jnp.asarray(e, a.dtype), x, neutral)

    def one(step, state):
        source = count - 1 - step
        return join(
            state,
            jax.tree.map(
                lambda a, own: lax.dynamic_index_in_dim(a, source, 0, False).astype(own.dtype),
                gathered,
                x,
            ),
        )

    return lax.fori_loop(0, ahead, one, state)


def chain_state(earlier, later):
    return (
        jnp.maximum(earlier[0], later[0]),
        later[1] + (1.0 - later[0]) * earlier[1],
        later[2] + (1.0 - later[0]) * earlier[2],
    )


def feature(inputs, table):
    logits = jnp.einsum("nhd,hde->nhe", inputs, table, preferred_element_type=jnp.float32)
    return (
        logits,
        jnp.concatenate([jax.nn.softmax(logits, -1), jax.nn.softmax(-logits, -1)], -1).astype(
            jnp.bfloat16
        ),
    )


def feature_back(logits, grad_phi):
    half = logits.shape[-1]
    plus = jax.nn.softmax(logits, -1)
    minus = jax.nn.softmax(-logits, -1)
    grad_plus = grad_phi[..., :half]
    grad_minus = grad_phi[..., half:]
    inner = plus * (grad_plus - jnp.sum(plus * grad_plus, -1, keepdims=True))
    outer = minus * (grad_minus - jnp.sum(minus * grad_minus, -1, keepdims=True))
    return (inner - outer).astype(jnp.bfloat16)


def local(
    tokens,
    attention_norm_gain,
    query_weight,
    key_weight,
    value_weight,
    query_down_adapter,
    query_up_adapter,
    key_down_adapter,
    key_up_adapter,
    value_down_adapter,
    value_up_adapter,
    query_feature_map,
    key_feature_map,
    output_weight,
    output_down_adapter,
    output_up_adapter,
    feedforward_norm_gain,
    gate_weight,
    up_weight,
    down_weight,
    document_start_mask,
    output_cotangent,
):
    rows_here = tokens.shape[0]
    adapter_rank_size = query_down_adapter.shape[1]
    head_dim = key_feature_map.shape[-1]
    kv_local = key_feature_map.shape[0]
    q_local = query_feature_map.shape[0]
    group_size = q_local // kv_local
    window = WIN
    scale = head_dim ** (-0.5)
    device = lax.axis_index("seq")
    offset = device * rows_here
    positions = offset + jnp.arange(rows_here, dtype=jnp.int32)
    starts_here = jnp.where(document_start_mask == 1, positions, jnp.int32(-1))
    opened = lax.cummax(starts_here, axis=0)
    last_reset = jnp.max(starts_here[: rows_here - window])
    resets = (last_reset >= offset - window).astype(jnp.float32)
    ext_pos = offset - window + jnp.arange(rows_here + window, dtype=jnp.int32)
    rows_index = jnp.arange(rows_here, dtype=jnp.int32)[:, None]
    cols_index = jnp.arange(rows_here + window, dtype=jnp.int32)[None, :]
    same_doc = ext_pos[None, :] >= opened[:, None]
    win_mask = ((cols_index > rows_index) & (cols_index <= rows_index + window) & same_doc).astype(
        jnp.float32
    )
    lin_mask = ((cols_index <= rows_index) & same_doc).astype(jnp.float32)
    carry_on = (opened < offset - window).astype(jnp.float32)
    key_keep = (
        (jnp.arange(rows_here + window, dtype=jnp.int32) < rows_here) & (ext_pos >= last_reset)
    ).astype(jnp.float32)
    stream = tokens.astype(jnp.float32)
    gain_one = attention_norm_gain.astype(jnp.float32)
    rms_one = lax.rsqrt(jnp.mean(stream * stream, -1, keepdims=True) + EPSILON)
    attention_normed_input = (stream * rms_one * gain_one).astype(jnp.bfloat16)
    query_up_rows = query_up_adapter.reshape(adapter_rank_size, -1)
    key_up_rows = key_up_adapter.reshape(adapter_rank_size, -1)
    value_up_rows = value_up_adapter.reshape(adapter_rank_size, -1)
    query_adapter_path = jnp.dot(
        attention_normed_input, query_down_adapter, preferred_element_type=jnp.float32
    )
    key_adapter_path = jnp.dot(
        attention_normed_input, key_down_adapter, preferred_element_type=jnp.float32
    )
    value_adapter_path = jnp.dot(
        attention_normed_input, value_down_adapter, preferred_element_type=jnp.float32
    )
    query_rows = (
        jnp.dot(attention_normed_input, query_weight, preferred_element_type=jnp.float32)
        + jnp.dot(query_adapter_path, query_up_rows.astype(jnp.float32), precision=MATRIX_EXACTNESS)
    ).astype(jnp.bfloat16)
    key = (
        jnp.dot(attention_normed_input, key_weight, preferred_element_type=jnp.float32)
        + jnp.dot(key_adapter_path, key_up_rows.astype(jnp.float32), precision=MATRIX_EXACTNESS)
    ).astype(jnp.bfloat16)
    value_rows = (
        jnp.dot(attention_normed_input, value_weight, preferred_element_type=jnp.float32)
        + jnp.dot(value_adapter_path, value_up_rows.astype(jnp.float32), precision=MATRIX_EXACTNESS)
    ).astype(jnp.bfloat16)
    key_width = key.shape[1]
    edge_rows = jnp.concatenate([key[rows_here - window :], value_rows[rows_here - window :]], 1)
    edge_prev = from_behind(edge_rows, "seq", 1)
    key_heads = jnp.concatenate([edge_prev[:, :key_width], key], 0).reshape(
        rows_here + window, kv_local, head_dim
    )
    value_heads = jnp.concatenate([edge_prev[:, key_width:], value_rows], 0).reshape(
        rows_here + window, kv_local, head_dim
    )
    query_heads = query_rows.reshape(rows_here, q_local, head_dim)
    q_logit, q_phi = feature(query_heads, query_feature_map)
    k_logit, k_phi = feature(key_heads, key_feature_map)
    query_grouped = query_heads.reshape(rows_here, kv_local, group_size, head_dim)
    qphi_grouped = q_phi.reshape(rows_here, kv_local, group_size, 2 * head_dim)
    weighted = k_phi * key_keep[:, None, None].astype(jnp.bfloat16)
    state_elem = jnp.einsum(
        "ekf,ekd->kfd", weighted, value_heads, preferred_element_type=jnp.float32
    )
    norm_elem = jnp.sum(weighted.astype(jnp.float32), 0)
    empty_state = (jnp.float32(0.0), jnp.zeros_like(state_elem), jnp.zeros_like(norm_elem))
    prior = carried_in((resets, state_elem, norm_elem), "seq", chain_state, empty_state)
    state_prev = prior[1]
    norm_prev = prior[2]
    scores = (
        jnp.einsum("ikgd,ekd->kgie", query_grouped, key_heads, preferred_element_type=jnp.float32)
        * scale
    )
    linear = jnp.einsum("ikgf,ekf->kgie", qphi_grouped, k_phi, preferred_element_type=jnp.float32)
    exp_window = jnp.exp(scores) * win_mask
    weight_matrix = exp_window + linear * lin_mask
    qphi_carry = qphi_grouped.astype(jnp.float32) * carry_on[:, None, None, None]
    carried = jnp.einsum("ikgf,kfd->kgid", qphi_carry, state_prev, precision=MATRIX_EXACTNESS)
    carried_norm = jnp.einsum("ikgf,kf->kgi", qphi_carry, norm_prev, precision=MATRIX_EXACTNESS)
    totals = jnp.sum(weight_matrix, -1) + carried_norm
    shares = (weight_matrix / totals[..., None]).astype(jnp.bfloat16)
    mixture = (
        jnp.einsum("kgie,ekd->kgid", shares, value_heads, preferred_element_type=jnp.float32)
        + carried / totals[..., None]
    )
    head_outputs = jnp.transpose(mixture, (2, 0, 1, 3)).reshape(rows_here, -1).astype(jnp.bfloat16)
    output_down_rows = output_down_adapter.reshape(-1, adapter_rank_size)
    output_adapter_path = jnp.dot(
        head_outputs, output_down_rows, preferred_element_type=jnp.float32
    )
    attn_part = jnp.dot(head_outputs, output_weight, preferred_element_type=jnp.float32) + jnp.dot(
        output_adapter_path, output_up_adapter.astype(jnp.float32), precision=MATRIX_EXACTNESS
    )
    gain_two = feedforward_norm_gain.astype(jnp.float32)
    grad_stream = output_cotangent.astype(jnp.float32)
    attention_result, low_o_all = lax.psum((attn_part, output_adapter_path), "kv")
    resid = stream + attention_result
    rms_two = lax.rsqrt(jnp.mean(resid * resid, -1, keepdims=True) + EPSILON)
    normed_two = (resid * rms_two * gain_two).astype(jnp.bfloat16)
    gate_pre = jnp.dot(normed_two, gate_weight, preferred_element_type=jnp.float32)
    up_pre = jnp.dot(normed_two, up_weight, preferred_element_type=jnp.float32)
    sigmoid_gate = jax.nn.sigmoid(gate_pre)
    silu_gate = gate_pre * sigmoid_gate
    hidden = (silu_gate * up_pre).astype(jnp.bfloat16)
    down_part = jnp.dot(hidden, down_weight, preferred_element_type=jnp.float32)
    g_hidden = jnp.dot(output_cotangent, down_weight.T, preferred_element_type=jnp.float32)
    grad_down = jnp.dot(hidden.T, output_cotangent, preferred_element_type=jnp.float32)
    g_gate = (g_hidden * up_pre * sigmoid_gate * (1.0 + gate_pre * (1.0 - sigmoid_gate))).astype(
        jnp.bfloat16
    )
    g_up = (g_hidden * silu_gate).astype(jnp.bfloat16)
    g_part_two = jnp.dot(g_gate, gate_weight.T, preferred_element_type=jnp.float32) + jnp.dot(
        g_up, up_weight.T, preferred_element_type=jnp.float32
    )
    ffn_out = lax.psum(down_part.astype(jnp.bfloat16), "kv").astype(jnp.float32)
    output = (resid + ffn_out).astype(jnp.bfloat16)
    g_normed_two = lax.psum(g_part_two, "kv")
    grad_norm2 = jnp.sum(g_normed_two * resid * rms_two, 0)
    scaled_two = g_normed_two * gain_two
    g_resid = (
        grad_stream
        + rms_two * scaled_two
        - resid * rms_two**3 * jnp.mean(resid * scaled_two, -1, keepdims=True)
    )
    attention_gradient = g_resid.astype(jnp.bfloat16)
    grad_wo = jnp.dot(head_outputs.T, attention_gradient, preferred_element_type=jnp.float32)
    output_adapter_gradient = jnp.dot(
        attention_gradient, output_up_adapter.T, preferred_element_type=jnp.float32
    )
    grad_bo = jnp.dot(
        low_o_all.T, attention_gradient.astype(jnp.float32), precision=MATRIX_EXACTNESS
    )
    grad_ao = jnp.dot(
        head_outputs.astype(jnp.float32).T, output_adapter_gradient, precision=MATRIX_EXACTNESS
    ).reshape(output_down_adapter.shape)
    g_heads = (
        jnp.dot(attention_gradient, output_weight.T, preferred_element_type=jnp.float32)
        + jnp.dot(
            output_adapter_gradient,
            output_down_rows.astype(jnp.float32).T,
            precision=MATRIX_EXACTNESS,
        )
    ).astype(jnp.bfloat16)
    g_mixture = g_heads.reshape(rows_here, kv_local, group_size, head_dim)
    g_mix_float = jnp.transpose(g_mixture.astype(jnp.float32), (1, 2, 0, 3))
    g_share = jnp.einsum(
        "ikgd,ekd->kgie", g_mixture, value_heads, preferred_element_type=jnp.float32
    )
    g_value = jnp.einsum("kgie,ikgd->ekd", shares, g_mixture, preferred_element_type=jnp.float32)
    g_total = -(jnp.sum(g_share * weight_matrix, -1) + jnp.sum(g_mix_float * carried, -1)) / (
        totals * totals
    )
    g_weight = g_share / totals[..., None] + g_total[..., None]
    g_carried = g_mix_float / totals[..., None]
    g_scores = (g_weight * exp_window).astype(jnp.bfloat16)
    g_linear = (g_weight * lin_mask).astype(jnp.bfloat16)
    g_query = (
        jnp.einsum("kgie,ekd->ikgd", g_scores, key_heads, preferred_element_type=jnp.float32)
        * scale
    )
    g_key = (
        jnp.einsum("kgie,ikgd->ekd", g_scores, query_grouped, preferred_element_type=jnp.float32)
        * scale
    )
    g_qphi = jnp.einsum("kgie,ekf->ikgf", g_linear, k_phi, preferred_element_type=jnp.float32)
    g_qphi = g_qphi + carry_on[:, None, None, None] * (
        jnp.einsum("kgid,kfd->ikgf", g_carried, state_prev, precision=MATRIX_EXACTNESS)
        + jnp.einsum("kgi,kf->ikgf", g_total, norm_prev, precision=MATRIX_EXACTNESS)
    )
    g_kphi = jnp.einsum(
        "kgie,ikgf->ekf", g_linear, qphi_grouped, preferred_element_type=jnp.float32
    )
    g_state = jnp.einsum("ikgf,kgid->kfd", qphi_carry, g_carried, precision=MATRIX_EXACTNESS)
    g_norm_state = jnp.einsum("ikgf,kgi->kf", qphi_carry, g_total, precision=MATRIX_EXACTNESS)
    later_grads = carried_in_2((resets, g_state, g_norm_state), "seq", chain_state, empty_state)
    keep_three = key_keep[:, None, None]
    g_kphi = g_kphi + keep_three * (
        jnp.einsum(
            "kfd,ekd->ekf",
            later_grads[1],
            value_heads.astype(jnp.float32),
            precision=MATRIX_EXACTNESS,
        )
        + later_grads[2][None]
    )
    g_value = g_value + keep_three * jnp.einsum(
        "ekf,kfd->ekd", k_phi.astype(jnp.float32), later_grads[1], precision=MATRIX_EXACTNESS
    )
    back_rows = jnp.concatenate(
        [
            g_key[:window].reshape(window, -1),
            g_value[:window].reshape(window, -1),
            g_kphi[:window].reshape(window, -1),
        ],
        1,
    )
    back_next = from_behind(back_rows.astype(jnp.bfloat16), "seq", -1).astype(back_rows.dtype)
    head_cols = kv_local * head_dim
    zero_rows = jnp.zeros((rows_here - window, head_cols), jnp.float32)
    tail_key = jnp.concatenate([zero_rows, back_next[:, :head_cols]], 0)
    tail_value = jnp.concatenate([zero_rows, back_next[:, head_cols : 2 * head_cols]], 0)
    tail_phi = jnp.concatenate(
        [
            jnp.zeros((rows_here - window, 2 * head_cols), jnp.float32),
            back_next[:, 2 * head_cols :],
        ],
        0,
    )
    g_kphi_own = g_kphi[window:] + tail_phi.reshape(rows_here, kv_local, 2 * head_dim)
    gq_logit = feature_back(q_logit, g_qphi.reshape(rows_here, q_local, 2 * head_dim))
    g_query_full = (
        g_query.reshape(rows_here, -1)
        + jnp.einsum(
            "nhe,hde->nhd", gq_logit, query_feature_map, preferred_element_type=jnp.float32
        ).reshape(rows_here, -1)
    ).astype(jnp.bfloat16)
    grad_featq = jnp.einsum(
        "nhd,nhe->hde", query_heads, gq_logit, preferred_element_type=jnp.float32
    )
    gk_logit = feature_back(k_logit[window:], g_kphi_own)
    g_key_full = (
        g_key[window:].reshape(rows_here, -1)
        + tail_key
        + jnp.einsum(
            "nhe,hde->nhd", gk_logit, key_feature_map, preferred_element_type=jnp.float32
        ).reshape(rows_here, -1)
    ).astype(jnp.bfloat16)
    grad_featk = jnp.einsum(
        "nhd,nhe->hde", key_heads[window:], gk_logit, preferred_element_type=jnp.float32
    )
    g_value_full = (g_value[window:].reshape(rows_here, -1) + tail_value).astype(jnp.bfloat16)
    grad_wq = jnp.dot(attention_normed_input.T, g_query_full, preferred_element_type=jnp.float32)
    grad_wk = jnp.dot(attention_normed_input.T, g_key_full, preferred_element_type=jnp.float32)
    grad_wv = jnp.dot(attention_normed_input.T, g_value_full, preferred_element_type=jnp.float32)
    grad_bq = jnp.dot(
        query_adapter_path.T, g_query_full.astype(jnp.float32), precision=MATRIX_EXACTNESS
    ).reshape(query_up_adapter.shape)
    grad_bk = jnp.dot(
        key_adapter_path.T, g_key_full.astype(jnp.float32), precision=MATRIX_EXACTNESS
    ).reshape(key_up_adapter.shape)
    grad_bv = jnp.dot(
        value_adapter_path.T, g_value_full.astype(jnp.float32), precision=MATRIX_EXACTNESS
    ).reshape(value_up_adapter.shape)
    g_low_part = jnp.concatenate(
        [
            jnp.dot(g_query_full, query_up_rows.T, preferred_element_type=jnp.float32),
            jnp.dot(g_key_full, key_up_rows.T, preferred_element_type=jnp.float32),
            jnp.dot(g_value_full, value_up_rows.T, preferred_element_type=jnp.float32),
        ],
        1,
    )
    g_part_one = (
        jnp.dot(g_query_full, query_weight.T, preferred_element_type=jnp.float32)
        + jnp.dot(g_key_full, key_weight.T, preferred_element_type=jnp.float32)
        + jnp.dot(g_value_full, value_weight.T, preferred_element_type=jnp.float32)
    )
    g_normed_one, adapter_gradients = (
        lax.psum(g_part_one.astype(jnp.bfloat16), "kv").astype(jnp.float32),
        lax.psum(g_low_part.astype(jnp.bfloat16), "kv").astype(jnp.float32),
    )
    query_adapter_gradient = adapter_gradients[:, :adapter_rank_size]
    key_adapter_gradient = adapter_gradients[:, adapter_rank_size : 2 * adapter_rank_size]
    value_adapter_gradient = adapter_gradients[:, 2 * adapter_rank_size :]
    g_normed_one = (
        g_normed_one
        + jnp.dot(
            query_adapter_gradient,
            query_down_adapter.astype(jnp.float32).T,
            precision=MATRIX_EXACTNESS,
        )
        + jnp.dot(
            key_adapter_gradient, key_down_adapter.astype(jnp.float32).T, precision=MATRIX_EXACTNESS
        )
        + jnp.dot(
            value_adapter_gradient,
            value_down_adapter.astype(jnp.float32).T,
            precision=MATRIX_EXACTNESS,
        )
    )
    normed_float = attention_normed_input.astype(jnp.float32)
    grad_aq = jnp.dot(normed_float.T, query_adapter_gradient, precision=MATRIX_EXACTNESS)
    grad_ak = jnp.dot(normed_float.T, key_adapter_gradient, precision=MATRIX_EXACTNESS)
    grad_av = jnp.dot(normed_float.T, value_adapter_gradient, precision=MATRIX_EXACTNESS)
    grad_norm1 = jnp.sum(g_normed_one * stream * rms_one, 0)
    scaled_one = g_normed_one * gain_one
    grad_tokens = (
        g_resid
        + rms_one * scaled_one
        - stream * rms_one**3 * jnp.mean(stream * scaled_one, -1, keepdims=True)
    )
    grad_gate_part = jnp.dot(normed_two.T, g_gate, preferred_element_type=jnp.float32)
    grad_up_part = jnp.dot(normed_two.T, g_up, preferred_element_type=jnp.float32)
    summed = (
        lax.psum_scatter(
            grad_norm1.astype(jnp.bfloat16), "seq", scatter_dimension=0, tiled=True
        ).astype(jnp.float32),
        lax.psum_scatter(
            grad_wq.astype(jnp.bfloat16), "seq", scatter_dimension=0, tiled=True
        ).astype(jnp.float32),
        lax.psum_scatter(
            grad_wk.astype(jnp.bfloat16), "seq", scatter_dimension=0, tiled=True
        ).astype(jnp.float32),
        lax.psum_scatter(
            grad_wv.astype(jnp.bfloat16), "seq", scatter_dimension=0, tiled=True
        ).astype(jnp.float32),
        lax.psum_scatter(
            grad_aq.astype(jnp.bfloat16), "seq", scatter_dimension=0, tiled=True
        ).astype(jnp.float32),
        lax.psum_scatter(
            grad_bq.astype(jnp.bfloat16), "seq", scatter_dimension=2, tiled=True
        ).astype(jnp.float32),
        lax.psum_scatter(
            grad_ak.astype(jnp.bfloat16), "seq", scatter_dimension=0, tiled=True
        ).astype(jnp.float32),
        lax.psum_scatter(
            grad_bk.astype(jnp.bfloat16), "seq", scatter_dimension=2, tiled=True
        ).astype(jnp.float32),
        lax.psum_scatter(
            grad_av.astype(jnp.bfloat16), "seq", scatter_dimension=0, tiled=True
        ).astype(jnp.float32),
        lax.psum_scatter(
            grad_bv.astype(jnp.bfloat16), "seq", scatter_dimension=2, tiled=True
        ).astype(jnp.float32),
        lax.psum_scatter(
            grad_featq.astype(jnp.bfloat16), "seq", scatter_dimension=1, tiled=True
        ).astype(jnp.float32),
        lax.psum_scatter(
            grad_featk.astype(jnp.bfloat16), "seq", scatter_dimension=1, tiled=True
        ).astype(jnp.float32),
        lax.psum_scatter(
            grad_wo.astype(jnp.bfloat16), "seq", scatter_dimension=1, tiled=True
        ).astype(jnp.float32),
        lax.psum_scatter(
            grad_ao.astype(jnp.bfloat16), "seq", scatter_dimension=1, tiled=True
        ).astype(jnp.float32),
        lax.psum_scatter(
            grad_bo.astype(jnp.bfloat16), "seq", scatter_dimension=1, tiled=True
        ).astype(jnp.float32),
        lax.psum_scatter(
            grad_norm2.astype(jnp.bfloat16), "seq", scatter_dimension=0, tiled=True
        ).astype(jnp.float32),
        lax.psum_scatter(
            grad_down.astype(jnp.bfloat16), "seq", scatter_dimension=1, tiled=True
        ).astype(jnp.float32),
        lax.psum_scatter(
            grad_gate_part.astype(jnp.bfloat16), "seq", scatter_dimension=0, tiled=True
        ).astype(jnp.float32),
        lax.psum_scatter(
            grad_up_part.astype(jnp.bfloat16), "seq", scatter_dimension=0, tiled=True
        ).astype(jnp.float32),
    )
    return (
        output,
        grad_tokens,
        summed[0],
        summed[1],
        summed[2],
        summed[3],
        summed[4],
        summed[5],
        summed[6],
        summed[7],
        summed[8],
        summed[9],
        summed[10],
        summed[11],
        summed[12],
        summed[13],
        summed[14],
        summed[15],
        summed[17],
        summed[18],
        summed[16],
    )


def solution(mesh):
    placed = (
        P("seq", None),
        P(),
        P(None, "kv"),
        P(None, "kv"),
        P(None, "kv"),
        P(),
        P(None, "kv", None),
        P(),
        P(None, "kv", None),
        P(),
        P(None, "kv", None),
        P("kv", None, None),
        P("kv", None, None),
        P("kv", None),
        P("kv", None, None),
        P(),
        P(),
        P(None, "kv"),
        P(None, "kv"),
        P("kv", None),
        P("seq"),
        P("seq", None),
    )
    return jax.shard_map(
        local,
        mesh=mesh,
        in_specs=placed,
        out_specs=(
            P("seq", None),
            P("seq", None),
            P("seq"),
            P("seq", "kv"),
            P("seq", "kv"),
            P("seq", "kv"),
            P("seq", None),
            P(None, "kv", "seq"),
            P("seq", None),
            P(None, "kv", "seq"),
            P("seq", None),
            P(None, "kv", "seq"),
            P("kv", "seq", None),
            P("kv", "seq", None),
            P("kv", "seq"),
            P("kv", "seq", None),
            P(None, "seq"),
            P("seq"),
            P("seq", "kv"),
            P("seq", "kv"),
            P("kv", "seq"),
        ),
        check_vma=False,
    )
```

profile of v0, /device:TPU:0, one launch (start us, length us, event | category | flops | bytes accessed | tf_op | source)
XLA Modules:
  0.0 2015.5 jit_solution(17785736598290144495)
XLA Ops:
  61.5 19.0 all-reduce.3
  91.1 16.4 all-gather.4
  108.9 33.3 %all-gather = f32[16,128,64]{1,2,0:T(8,128)} all-gather(f32[2,128,64]{1,2,0:T(8,128)S(1)} %fusion.104), channel_id=2, replica_groups=mesh['seq'=8,'kv'=4] {'seq'}, dimensions={0}, use_global_device_ids=true | all-gather | bytes 589824 | tf_op jit(solution)/shard_map/all_gather | solution.py:21
  152.6 15.8 bitcast_multiply_fusion.2
  168.3 28.5 %fusion.153 = (f32[2,4,1024]{2,1,0:T(4,128)S(1)}, f32[2,4,1024,1088]{2,3,1,0:T(8,128)}) fusion(f32[2,4,1024,1088]{2,3,1,0:T(8,128)} %bitcast_multiply_fusion.2, f32[1024,1088]{0,1:T(8,128)} %get-tuple-element.358, bf16[1024,2,4,128]{3,0,2,1:T(8,128)(2,1)} %pad_maximum_fusion, bf16[1088,2,64]{0,2,1:T(8,128)(2,1)} %copy-done.24, ...), kind=kOutput, calls=%fused_computation.266 | convolution fusion | flops 2309545984 | bytes 78446592 | tf_op jit(solution)/shard_map/ikgf,ekf->kgie/dot_general | solution.py:192
  203.1 14.0 divide_convert_fusion
  232.4 177.5 %all-reduce.18.cloned.1.call-done = f32[1024,2048]{1,0:T(8,128)} async-done(((f32[1024,2048]{1,0:T(8,128)}), f32[1024,2048]{1,0:T(8,128)}) %all-reduce.18.cloned.1.call-update) | async-done | bytes 8388624 | tf_op jit(solution)/shard_map/psum | solution.py:214
  419.0 14.8 fusion.167
  433.8 13.3 fusion.166
  447.1 21.8 %multiply_convert_fusion.2 = (bf16[1024,2048]{1,0:T(8,128)(2,1)}, bf16[1024,2048]{1,0:T(8,128)(2,1)}, bf16[1024,2048]{1,0:T(8,128)(2,1)}) fusion(f32[1024,2048]{1,0:T(8,128)} %fusion.166, f32[1024,2048]{1,0:T(8,128)} %fusion.167, bf16[1024,2048]{1,0:T(8,128)(2,1)} %param.47, bf16[2048,2048]{1,0:T(8,128)(2,1)} %param.45), kind=kOutput, calls=%fused_computation.50 | convolution fusion | flops 8621391872 | bytes 41943040 | tf_op jit(solution)/shard_map/dot_general | solution.py:224
  468.9 12.9 fusion.168
  481.8 13.5 convolution_add_fusion.1
  496.2 21.9 %all-reduce.4 = bf16[8]{0:T(256)(128)(2,1)} all-reduce(bf16[8]{0:T(256)(128)(2,1)S(1)} %dynamic-update-slice.1), channel_id=1, replica_groups=mesh['seq'=8,'kv'=4] {'seq'}, use_global_device_ids=true, to_apply=%add.4 | all-reduce | flops 8 | bytes 32
  518.7 12.9 psum.47
  534.1 114.9 %all-reduce.20.cloned.1.call-done = f32[1024,2048]{1,0:T(8,128)} async-done(((f32[1024,2048]{1,0:T(8,128)}), f32[1024,2048]{1,0:T(8,128)}) %all-reduce.20.cloned.1.call-update) | async-done | bytes 8388624 | tf_op jit(solution)/shard_map/psum | solution.py:235
  649.0 7.8 multiply_reduce_fusion
  658.4 6.8 fusion.145
  670.1 10.2 convolution_bitcast_fusion.1
  686.1 22.6 %fusion.15 = (f32[2,4,1024]{2,1,0:T(4,128)S(1)}, f32[2,1088,1024,4]{2,1,3,0:T(8,128)}) fusion(f32[2,4,1024,1088]{2,3,1,0:T(8,128)} %get-tuple-element.375, bf16[1088,2,64,1]{0,2,3,1:T(8,128)(2,1)S(1)} %bitcast.398, bf16[1024,2,4,64]{0,3,2,1:T(8,128)(2,1)S(1)} %bitcast.379), kind=kOutput, calls=%fused_computation.24 | convolution fusion | flops 1158668288 | bytes 72663040 | tf_op jit(solution)/shard_map/ikgd,ekd->kgie/dot_general | solution.py:264
  708.8 37.6 %multiply_convert_fusion.1 = (bf16[2,4,1024,1088]{2,3,1,0:T(8,128)(2,1)}, bf16[2,4,1024,1088]{2,3,1,0:T(8,128)(2,1)}) fusion(f32[2,4,1024,1088]{2,3,1,0:T(8,128)} %bitcast_multiply_fusion.2, f32[2,4,1024]{2,1,0:T(4,128)S(1)} %bitcast.414, f32[2,4,1024]{2,1,0:T(4,128)S(1)} %copy-done.57, f32[2,1088,1024,4]{2,1,3,0:T(8,128)} %get-tuple-element.377, ...), kind=kLoop, calls=%fused_computation.29 | loop fusion | flops 53477376 | bytes 111476736 | tf_op jit(solution)/shard_map/convert_element_type | solution.py:273
  746.3 10.1 convolution_bitcast_fusion
  756.4 8.0 fusion.98
  771.0 7.0 fusion.86
  778.0 7.6 fusion.74
  792.9 20.5 %all-gather.5 = bf16[8,2,128]{2,1,0:T(2,128)(2,1)S(1)} all-gather(bf16[1,2,128]{2,1,0:T(2,128)(2,1)S(1)} %convert_bitcast_fusion), channel_id=5, replica_groups=mesh['seq'=8,'kv'=4] {'seq'}, dimensions={0}, use_global_device_ids=true | all-gather | bytes 4608 | tf_op jit(solution)/shard_map/all_gather | solution.py:37
  813.4 31.0 %all-gather.2 = bf16[16,128,64]{1,2,0:T(8,128)(2,1)S(1)} all-gather(bf16[2,128,64]{1,2,0:T(8,128)(2,1)} %fusion.90), channel_id=4, replica_groups=mesh['seq'=8,'kv'=4] {'seq'}, dimensions={0}, use_global_device_ids=true | all-gather | bytes 294912 | tf_op jit(solution)/shard_map/all_gather | solution.py:37
  844.4 14.5 while.31
  863.2 10.5 fusion.43
  877.3 10.9 fusion.45
  900.7 11.0 psum.46
  944.5 14.0 convolution_convert_fusion.3
  965.7 14.1 convolution_convert_fusion
  979.9 14.0 convolution_convert_fusion.1
  994.4 14.1 convolution_convert_fusion.2
  1030.7 33.1 %reduce-scatter.28.cloned.1.call-done = bf16[256,8]{0,1:T(8,128)(2,1)} async-done(((bf16[2048,8]{0,1:T(8,128)(2,1)}), bf16[256,8]{0,1:T(8,128)(2,1)}) %reduce-scatter.28.cloned.1.call-update) | async-done | bytes 4112 | tf_op jit(solution)/shard_map/reduce_scatter | solution.py:430
  1065.1 55.0 %reduce-scatter.30.cloned.1.call-done = bf16[256,8]{0,1:T(8,128)(2,1)} async-done(((bf16[2048,8]{0,1:T(8,128)(2,1)}), bf16[256,8]{0,1:T(8,128)(2,1)}) %reduce-scatter.30.cloned.1.call-update) | async-done | bytes 4112 | tf_op jit(solution)/shard_map/reduce_scatter | solution.py:436
  1122.0 62.5 %reduce-scatter.24.cloned.1.call-done = bf16[256,128]{1,0:T(8,128)(2,1)} async-done(((bf16[2048,128]{1,0:T(8,128)(2,1)}), bf16[256,128]{1,0:T(8,128)(2,1)}) %reduce-scatter.24.cloned.1.call-update) | async-done | bytes 65552 | tf_op jit(solution)/shard_map/reduce_scatter | solution.py:421
  1186.0 63.2 %reduce-scatter.22.cloned.1.call-done = bf16[256,128]{1,0:T(8,128)(2,1)} async-done(((bf16[2048,128]{1,0:T(8,128)(2,1)}), bf16[256,128]{1,0:T(8,128)(2,1)}) %reduce-scatter.22.cloned.1.call-update) | async-done | bytes 65552 | tf_op jit(solution)/shard_map/reduce_scatter | solution.py:418
  1250.6 69.8 %reduce-scatter.32.cloned.1.call-done = bf16[512,256]{1,0:T(8,128)(2,1)} async-done(((bf16[512,2048]{1,0:T(8,128)(2,1)}), bf16[512,256]{1,0:T(8,128)(2,1)}) %reduce-scatter.32.cloned.1.call-update) | async-done | bytes 262160 | tf_op jit(solution)/shard_map/reduce_scatter | solution.py:448
  1322.2 69.2 %reduce-scatter.20.cloned.1.call-done = bf16[256,512]{1,0:T(8,128)(2,1)} async-done(((bf16[2048,512]{1,0:T(8,128)(2,1)}), bf16[256,512]{1,0:T(8,128)(2,1)}) %reduce-scatter.20.cloned.1.call-update) | async-done | bytes 262160 | tf_op jit(solution)/shard_map/reduce_scatter | solution.py:415
  1393.2 153.5 %all-reduce.22.cloned.1.call-done = (bf16[1024,2048]{1,0:T(8,128)(2,1)}, bf16[1024,2048]{1,0:T(8,128)(2,1)}) async-done(((bf16[1024,2048]{1,0:T(8,128)(2,1)}, bf16[1024,2048]{1,0:T(8,128)(2,1)}), (bf16[1024,2048]{1,0:T(8,128)(2,1)}, bf16[1024,2048]{1,0:T(8,128)(2,1)})) %all-reduce.22.cloned.1.call-update) | async-done | bytes 8388624 | tf_op jit(solution)/shard_map/psum | solution.py:233
  1546.7 13.7 fusion.24
  1560.4 44.7 %all-reduce.12 = (bf16[2048]{0:T(1024)(128)(2,1)S(1)}, bf16[8,8,64]{2,0,1:T(8,128)(2,1)S(1)}, bf16[8,2,64]{2,1,0:T(2,128)(2,1)S(1)}, bf16[8,2,64]{2,1,0:T(2,128)...) all-reduce(bf16[2048]{0:T(1024)(128)(2,1)S(1)} %get-tuple-element.3, ...), channel_id=6, replica_groups=mesh['seq'=8,'kv'=4] {'seq'}, use_global_device_ids=true, to_apply=%region_37.38.clone | all-reduce | flops 22528 | bytes 90112
  1609.7 8.6 add_convert_fusion.1
  1618.3 10.0 fusion.21
  1628.3 74.2 %reduce-scatter.40.cloned.1.call-done = bf16[2048,256]{1,0:T(8,128)(2,1)} async-done(((bf16[2048,2048]{1,0:T(8,128)(2,1)}), bf16[2048,256]{1,0:T(8,128)(2,1)}) %reduce-scatter.40.cloned.1.call-update) | async-done | bytes 1048592 | tf_op jit(solution)/shard_map/reduce_scatter | solution.py:460
  1705.2 149.3 %reduce-scatter.38.cloned.1.call-done = bf16[256,2048]{1,0:T(8,128)(2,1)} async-done(((bf16[2048,2048]{1,0:T(8,128)(2,1)}), bf16[256,2048]{1,0:T(8,128)(2,1)}) %reduce-scatter.38.cloned.1.call-update) | async-done | bytes 1048592 | tf_op jit(solution)/shard_map/reduce_scatter | solution.py:466
  1857.3 148.7 %reduce-scatter.36.cloned.1.call-done = bf16[256,2048]{1,0:T(8,128)(2,1)} async-done(((bf16[2048,2048]{1,0:T(8,128)(2,1)}), bf16[256,2048]{1,0:T(8,128)(2,1)}) %reduce-scatter.36.cloned.1.call-update) | async-done | bytes 1048592 | tf_op jit(solution)/shard_map/reduce_scatter | solution.py:463
  (428 shorter events, 249.6 us)
Async XLA Ops:
  7.2 216.3 %copy-start = (bf16[512,2048]{1,0:T(8,128)(2,1)S(1)}, bf16[512,2048]{1,0:T(8,128)(2,1)}, u32[]{:S(2)}) copy-start(bf16[512,2048]{1,0:T(8,128)(2,1)} %param.39) | copy-start | bytes 6291460
  7.2 402.7 %all-reduce.18.cloned.1.call-start = ((), (), s32[]{:S(2)}) async-start(), calls=%async_computation.12 | async-start | bytes 16777216 | tf_op jit(solution)/shard_map/psum | solution.py:214
  18.8 62.5 %copy-start.42 = (bf16[1024,128]{1,0:T(8,128)(2,1)}, bf16[1024,128]{1,0:T(8,128)(2,1)S(1)}, u32[]{:S(2)}) copy-start(bf16[1024,128]{1,0:T(8,128)(2,1)S(1)} %fusion.84) | copy-start | bytes 786436
  22.2 58.4 %collective-permute-start = (bf16[64,256]{1,0:T(8,128)(2,1)}, bf16[64,256]{1,0:T(8,128)(2,1)}, u32[]{:S(2)}, u32[]{:S(2)}) collective-permute-start(bf16[64,256]{1,0:T(8,128)(2,1)} %pad_maximum_fusion.6), channel_id=1, source_target_pairs={{0,4},{4,8},{8,12},{12,16},{16,20},{20,24},{24,28},{1,5},{5,9},{9,... | collective-permute-start | bytes 98312 | tf_op jit(solution)/shard_map/ppermute | solution.py:16
  37.4 115.1 %copy-start.12 = (bf16[1024,512]{0,1:T(8,128)(2,1)}, bf16[1024,512]{0,1:T(8,128)(2,1)S(1)}, u32[]{:S(2)}) copy-start(bf16[1024,512]{0,1:T(8,128)(2,1)S(1)} %add_convert_fusion.3) | copy-start | bytes 3145732
  44.7 152.2 %copy-start.79 = (f32[1024]{0:T(1024)}, f32[1024]{0:T(1024)S(1)}, u32[]{:S(2)}) copy-start(f32[1024]{0:T(1024)S(1)} %get-tuple-element.347) | copy-start | bytes 12292
  56.2 24.3 %copy-start.93 = (bf16[8,64,8]{1,2,0:T(8,128)(2,1)S(1)}, bf16[8,64,8]{1,2,0:T(8,128)(2,1)}, u32[]{:S(2)}) copy-start(bf16[8,64,8]{1,2,0:T(8,128)(2,1)} %param.40) | copy-start | bytes 24580
  56.2 28.1 %copy-start.65 = (bf16[2,64,64]{2,1,0:T(8,128)(2,1)S(1)}, bf16[2,64,64]{2,1,0:T(8,128)(2,1)}, u32[]{:S(2)}) copy-start(bf16[2,64,64]{2,1,0:T(8,128)(2,1)} %param.38) | copy-start | bytes 49156
  84.3 58.6 %copy-start.19 = (bf16[1088,128]{0,1:T(8,128)(2,1)}, bf16[1088,128]{0,1:T(8,128)(2,1)S(1)}, u32[]{:S(2)}) copy-start(bf16[1088,128]{0,1:T(8,128)(2,1)S(1)} %copy.89) | copy-start | bytes 835588
  89.7 17.9 copy-start.22
  90.9 18.0 copy-start.24
  168.3 28.6 %copy-start.26 = (f32[2,128,64]{2,1,0:T(8,128)S(1)}, f32[2,128,64]{2,1,0:T(8,128)}, u32[]{:S(2)}) copy-start(f32[2,128,64]{2,1,0:T(8,128)} %get-tuple-element.194) | copy-start | bytes 196612
  196.9 20.3 %copy-start.56 = (f32[2,4,1024]{2,1,0:T(4,128)}, f32[2,4,1024]{2,1,0:T(4,128)S(1)}, u32[]{:S(2)}) copy-start(f32[2,4,1024]{2,1,0:T(4,128)S(1)} %bitcast_add_fusion.8) | copy-start | bytes 98308
  203.1 14.1 copy-start.15
  203.1 14.1 copy-start.30
  231.7 417.3 %all-reduce.20.cloned.1.call-start = ((), (), s32[]{:S(2)}) async-start(), calls=%async_computation.13 | async-start | bytes 16777216 | tf_op jit(solution)/shard_map/psum | solution.py:235
  419.0 14.8 copy-start.38
  468.9 13.0 copy-start.101
  495.3 36.3 %copy-start.21 = (bf16[1088,128]{0,1:T(8,128)(2,1)S(1)}, bf16[1088,128]{0,1:T(8,128)(2,1)}, u32[]{:S(2)}) copy-start(bf16[1088,128]{0,1:T(8,128)(2,1)} %copy-done.19) | copy-start | bytes 835588
  495.3 36.3 %copy-start.66 = (bf16[2,64,64]{2,1,0:T(8,128)(2,1)S(1)}, bf16[2,64,64]{2,1,0:T(8,128)(2,1)}, u32[]{:S(2)}) copy-start(bf16[2,64,64]{2,1,0:T(8,128)(2,1)} %param.38) | copy-start | bytes 49156
  495.4 520.1 %reduce-scatter.34.cloned.1.call-start = ((), (), s32[]{:S(2)}) async-start(), calls=%async_computation.21 | async-start | bytes 36864 | tf_op jit(solution)/shard_map/reduce_scatter | solution.py:454
  708.7 55.7 %copy-start.69 = (f32[1,8,1024]{2,1,0:T(8,128)}, f32[1,8,1024]{2,1,0:T(8,128)S(1)}, u32[]{:S(2)}) copy-start(f32[1,8,1024]{2,1,0:T(8,128)S(1)} %multiply_divide_fusion) | copy-start | bytes 98308
  790.2 238.5 %reduce-scatter.42.cloned.1.call-start = ((), (), s32[]{:S(2)}) async-start(), calls=%async_computation.25 | async-start | bytes 73728
  792.9 68.6 %copy-start.29 = (f32[1088,2,128]{0,2,1:T(8,128)S(1)}, f32[1088,2,128]{0,2,1:T(8,128)}, u32[]{:S(2)}) copy-start(f32[1088,2,128]{0,2,1:T(8,128)} %convolution_bitcast_fusion) | copy-start | bytes 3342340
  792.9 68.6 %copy-start.32 = (bf16[1088,128]{0,1:T(8,128)(2,1)S(1)}, bf16[1088,128]{0,1:T(8,128)(2,1)}, u32[]{:S(2)}) copy-start(bf16[1088,128]{0,1:T(8,128)(2,1)} %copy.95) | copy-start | bytes 835588
  863.2 14.1 copy-start.14
  876.0 15.5 collective-permute-start.1
  877.3 12.2 copy-start.28
  877.3 13.2 copy-start.72
  891.4 138.0 %reduce-scatter.26.cloned.1.call-start = ((), (), s32[]{:S(2)}) async-start(), calls=%async_computation.17 | async-start | bytes 36864 | tf_op jit(solution)/shard_map/reduce_scatter | solution.py:424
  897.3 17.8 copy-start.51
  915.2 148.6 %reduce-scatter.28.cloned.1.call-start = ((), (), s32[]{:S(2)}) async-start(), calls=%async_computation.18 | async-start | bytes 36864 | tf_op jit(solution)/shard_map/reduce_scatter | solution.py:430
  918.8 201.3 %reduce-scatter.30.cloned.1.call-start = ((), (), s32[]{:S(2)}) async-start(), calls=%async_computation.19 | async-start | bytes 36864 | tf_op jit(solution)/shard_map/reduce_scatter | solution.py:436
  922.3 262.1 %reduce-scatter.24.cloned.1.call-start = ((), (), s32[]{:S(2)}) async-start(), calls=%async_computation.16 | async-start | bytes 589824 | tf_op jit(solution)/shard_map/reduce_scatter | solution.py:421
  926.8 322.4 %reduce-scatter.22.cloned.1.call-start = ((), (), s32[]{:S(2)}) async-start(), calls=%async_computation.15 | async-start | bytes 589824 | tf_op jit(solution)/shard_map/reduce_scatter | solution.py:418
  931.3 389.2 %reduce-scatter.32.cloned.1.call-start = ((), (), s32[]{:S(2)}) async-start(), calls=%async_computation.20 | async-start | bytes 2359296 | tf_op jit(solution)/shard_map/reduce_scatter | solution.py:448
  937.4 454.0 %reduce-scatter.20.cloned.1.call-start = ((), (), s32[]{:S(2)}) async-start(), calls=%async_computation.14 | async-start | bytes 2359296 | tf_op jit(solution)/shard_map/reduce_scatter | solution.py:415
  944.4 602.3 %all-reduce.22.cloned.1.call-start = ((), (), s32[]{:S(2)}) async-start(), calls=%async_computation.26 | async-start | bytes 16777216 | tf_op jit(solution)/shard_map/psum | solution.py:233
  944.5 14.0 copy-start.40
  944.5 14.0 copy-start.100
  965.4 737.1 %reduce-scatter.40.cloned.1.call-start = ((), (), s32[]{:S(2)}) async-start(), calls=%async_computation.24 | async-start | bytes 9437184 | tf_op jit(solution)/shard_map/reduce_scatter | solution.py:460
  979.8 874.7 %reduce-scatter.38.cloned.1.call-start = ((), (), s32[]{:S(2)}) async-start(), calls=%async_computation.23 | async-start | bytes 9437184 | tf_op jit(solution)/shard_map/reduce_scatter | solution.py:466
  993.9 1012.1 %reduce-scatter.36.cloned.1.call-start = ((), (), s32[]{:S(2)}) async-start(), calls=%async_computation.22 | async-start | bytes 9437184 | tf_op jit(solution)/shard_map/reduce_scatter | solution.py:463
  1024.1 522.6 %copy-start.68 = (f32[2048]{0:T(1024)S(1)}, f32[2048]{0:T(1024)}, u32[]{:S(2)}) copy-start(f32[2048]{0:T(1024)} %copy-done.67) | copy-start | bytes 24580
  1024.1 522.6 %copy-start.78 = (bf16[2048,8]{0,1:T(8,128)(2,1)S(1)}, bf16[2048,8]{0,1:T(8,128)(2,1)}, u32[]{:S(2)}) copy-start(bf16[2048,8]{0,1:T(8,128)(2,1)} %param.35) | copy-start | bytes 98308
  1024.1 522.6 %copy-start.84 = (f32[1024]{0:T(1024)S(1)}, f32[1024]{0:T(1024)}, u32[]{:S(2)}) copy-start(f32[1024]{0:T(1024)} %copy-done.83) | copy-start | bytes 12292
  1546.7 13.7 copy-start.96
  1618.3 390.5 %copy-start.1 = (bf16[512,2048]{1,0:T(8,128)(2,1)S(1)}, bf16[512,2048]{1,0:T(8,128)(2,1)}, u32[]{:S(2)}) copy-start(bf16[512,2048]{1,0:T(8,128)(2,1)} %param.39) | copy-start | bytes 6291460
  (71 other events, 378.3 us)
Sparse Core Ops, SparseCore 0:
  231.8 177.9 all-reduce.17
  495.5 153.4 all-reduce.19
  790.3 53.6 reduce-scatter.33
  891.6 59.7 reduce-scatter.41
  954.9 52.5 reduce-scatter.25
  1011.1 52.6 reduce-scatter.27
  1067.5 52.5 reduce-scatter.29
  1123.4 60.9 reduce-scatter.23
  1188.2 60.8 reduce-scatter.21
  1253.1 67.3 reduce-scatter.31
  1324.5 66.8 reduce-scatter.19
  1394.4 152.2 all-reduce.21
  1550.3 152.1 reduce-scatter.39
  1706.5 147.9 reduce-scatter.37
  1858.0 147.9 reduce-scatter.35
where the time goes:
time: 2020 us
  waiting for transfers between devices  1170 us (58%)
  matrix products  402 us (20%)
  blocking collectives  211 us (10%)
  other arithmetic  151 us (7%)
  local copies, waits for them, and re-layouts  49.6 us (2%)
    psum x1, waiting for transfers between devices, local(): lax.psum((attn_part, output_adapter_path), 'kv')  178 us
    psum x1, waiting for transfers between devices, local(): ffn_out = lax.psum(down_part.astype(jnp.bfloat16), 'kv').astype(jnp.float32)  153 us
    reduce_scatter x1, waiting for transfers between devices, local(): lax.psum_scatter(grad_up_part.astype(jnp.bfloat16), 'seq', scatter_dimens...  149 us
    reduce_scatter x1, waiting for transfers between devices, local(): lax.psum_scatter(grad_gate_part.astype(jnp.bfloat16), 'seq', scatter_dime...  149 us
    psum x1, waiting for transfers between devices, local(): g_normed_two = lax.psum(g_part_two, 'kv')  115 us
    unnamed x3, blocking collectives  85.6 us
    reduce_scatter x1, waiting for transfers between devices, local(): lax.psum_scatter(grad_down.astype(jnp.bfloat16), 'seq', scatter_dimension...  74.2 us
    reduce_scatter x1, waiting for transfers between devices, local(): lax.psum_scatter(grad_wo.astype(jnp.bfloat16), 'seq', scatter_dimension=1...  69.8 us
  transfers between devices with their start and end apart: 17, of which 12 were waited for; matrix products, arithmetic and copies ran while one was open for 13% of the time, Pallas kernels for 0%

commit v1 on v0

v1 whole, which is shorter than its diff:
```python
import jax
import jax.numpy as jnp
from jax import lax
from jax.sharding import PartitionSpec as P

WIN = 64
EPSILON = 1e-05
EXACT = lax.Precision.HIGHEST
F32 = jnp.float32
BF16 = jnp.bfloat16


def dot(a, b, out=F32):
    return jnp.dot(a, b, preferred_element_type=F32).astype(out)


def dot_nt(a, b, out=F32):
    return lax.dot_general(a, b, (((1,), (1,)), ((), ())), preferred_element_type=F32).astype(out)


def dot_tn(a, b, out=F32):
    return lax.dot_general(a, b, (((0,), (0,)), ((), ())), preferred_element_type=F32).astype(out)


def take(x, i):
    return lax.dynamic_index_in_dim(x, i, 0, False)


class Grid:
    def __init__(self):
        self.kv = lax.axis_size("kv")
        self.seq = lax.axis_size("seq")
        self.outer = self.kv // 2
        self.line = self.seq // 2
        k = lax.axis_index("kv")
        s = lax.axis_index("seq")
        self.core, self.y = k % 2, k // 2
        self.x, self.z = s % 2, s // 2
        self.s = s
        self.core_swap = [(i, i ^ 1) for i in range(self.kv)]
        self.x_swap = [(i, i ^ 1) for i in range(self.seq)]
        self.z_groups = [[2 * z + x for z in range(self.line)] for x in range(2)]

    def y_shift(self, j):
        m = self.outer
        return [(y * 2 + c, (y + j) % m * 2 + c) for y in range(m) for c in range(2)]

    def first_row(self, rows):
        return self.core * (rows // 2) + self.y * (rows // self.kv)

    def share(self, x):
        rows = x.shape[0]
        return lax.dynamic_slice_in_dim(x, self.first_row(rows), rows // self.kv, 0)

    def reduce_rows(self, part):
        rows, width = part.shape
        halves = part.reshape(2, rows // 2, width)
        got = lax.ppermute(take(halves, 1 - self.core), "kv", self.core_swap)
        half = take(halves, self.core).astype(F32) + got.astype(F32)
        m = self.outer
        blocks = half.reshape(m, rows // self.kv, width)
        total = take(blocks, self.y)
        for j in range(1, m):
            out = take(blocks, (self.y + j) % m).astype(BF16)
            total = total + lax.ppermute(out, "kv", self.y_shift(j)).astype(F32)
        return total

    def gather_rows(self, share):
        rows, width = share.shape
        m = self.outer
        got = [share] + [lax.ppermute(share, "kv", self.y_shift(j)) for j in range(1, m)]
        if m == 2:
            first = self.y == 0
            half = jnp.concatenate(
                [jnp.where(first, got[0], got[1]), jnp.where(first, got[1], got[0])], 0
            )
        else:
            half = jnp.zeros((m, rows, width), share.dtype)
            for j in range(m):
                half = lax.dynamic_update_index_in_dim(half, got[j], (self.y - j) % m, 0)
            half = half.reshape(m * rows, width)
        other = lax.ppermute(half, "kv", self.core_swap)
        first = self.core == 0
        return jnp.concatenate([jnp.where(first, half, other), jnp.where(first, other, half)], 0)

    def sum_kv(self, x):
        x = x + lax.ppermute(x, "kv", self.core_swap).astype(F32)
        total = x
        for j in range(1, self.outer):
            total = total + lax.ppermute(x, "kv", self.y_shift(j))
        return total

    def pair_columns(self, x):
        rows, width = x.shape
        cut = x.reshape(rows, self.line, 2, width // self.seq)
        other = lax.dynamic_index_in_dim(cut, 1 - self.x, 2, False)
        own = lax.dynamic_index_in_dim(cut, self.x, 2, False)
        return other.reshape(rows, width // 2), own.reshape(rows, width // 2)

    def weight_grad(self, left, right):
        got = lax.ppermute(dot_tn(left[0], right, BF16), "seq", self.x_swap)
        part = (dot_tn(left[1], right) + got.astype(F32)).astype(BF16)
        return self.line_scatter(part).astype(F32)

    def line_scatter(self, part):
        return lax.psum_scatter(
            part, "seq", scatter_dimension=0, tiled=True, axis_index_groups=self.z_groups
        )

    def scatter_blocks(self, blocks):
        cut = blocks.reshape(self.line, 2, -1)
        other = lax.dynamic_index_in_dim(cut, 1 - self.x, 1, False).astype(BF16)
        own = lax.dynamic_index_in_dim(cut, self.x, 1, False)
        part = own + lax.ppermute(other, "seq", self.x_swap).astype(F32)
        total = take(part, self.z)
        m = self.line
        for j in range(1, m):
            pairs = [(z * 2 + x, (z + j) % m * 2 + x) for z in range(m) for x in range(2)]
            out = take(part, (self.z + j) % m).astype(BF16)
            total = total + lax.ppermute(out, "seq", pairs).astype(F32)
        return total

    def shift_seq(self, x, by):
        n = self.seq
        return lax.ppermute(x, "seq", [(i, i + by) for i in range(n) if 0 <= i + by < n])

    def sum_before(self, x, sign):
        total = x
        by = 1
        while by < self.seq:
            total = total + self.shift_seq(total, sign * by)
            by *= 2
        return total - x


def feature(inputs, table):
    logits = jnp.einsum("nhd,hde->nhe", inputs, table, preferred_element_type=F32)
    phi = jnp.concatenate([jax.nn.softmax(logits, -1), jax.nn.softmax(-logits, -1)], -1)
    return logits, phi.astype(BF16)


def feature_back(logits, grad_phi):
    half = logits.shape[-1]
    plus = jax.nn.softmax(logits, -1)
    minus = jax.nn.softmax(-logits, -1)
    grad_plus = grad_phi[..., :half]
    grad_minus = grad_phi[..., half:]
    inner = plus * (grad_plus - jnp.sum(plus * grad_plus, -1, keepdims=True))
    outer = minus * (grad_minus - jnp.sum(minus * grad_minus, -1, keepdims=True))
    return (inner - outer).astype(BF16)


def local(
    tokens,
    gain_one,
    query_weight,
    key_weight,
    value_weight,
    query_down,
    query_up,
    key_down,
    key_up,
    value_down,
    value_up,
    query_map,
    key_map,
    output_weight,
    output_down,
    output_up,
    gain_two,
    gate_weight,
    up_weight,
    down_weight,
    start_mask,
    cotangent,
):
    grid = Grid()
    rows = tokens.shape[0]
    rank = query_down.shape[1]
    hd = key_map.shape[-1]
    hk = key_map.shape[0]
    hq = query_map.shape[0]
    group = hq // hk
    scale = hd**-0.5
    offset = grid.s * rows
    positions = offset + jnp.arange(rows, dtype=jnp.int32)
    starts = jnp.where(start_mask == 1, positions, jnp.int32(-1))
    earlier = jnp.arange(rows)[:, None] <= jnp.arange(rows)[None, :]
    opened = jnp.max(jnp.where(earlier, starts[:, None], jnp.int32(-1)), 0)
    last_reset = jnp.max(starts[: rows - WIN])
    ext_pos = offset - WIN + jnp.arange(rows + WIN, dtype=jnp.int32)
    rows_index = jnp.arange(rows, dtype=jnp.int32)[:, None]
    cols_index = jnp.arange(rows + WIN, dtype=jnp.int32)[None, :]
    same_doc = ext_pos[None, :] >= opened[:, None]
    win_mask = ((cols_index > rows_index) & (cols_index <= rows_index + WIN) & same_doc).astype(F32)
    lin_mask = ((cols_index <= rows_index) & same_doc).astype(F32)
    carry_on = (opened < offset - WIN).astype(F32)
    key_keep = ((jnp.arange(rows + WIN) < rows) & (ext_pos >= last_reset)).astype(F32)

    g1 = gain_one.astype(F32)
    g2 = gain_two.astype(F32)
    stream = tokens.astype(F32)
    rms_one = lax.rsqrt(jnp.mean(stream * stream, -1, keepdims=True) + EPSILON)
    normed_one = (stream * rms_one * g1).astype(BF16)
    qup, kup, vup = (u.reshape(rank, -1) for u in (query_up, key_up, value_up))
    weight_qkv = jnp.concatenate(
        [
            (query_weight.astype(F32) + dot(query_down, qup)).astype(BF16),
            (key_weight.astype(F32) + dot(key_down, kup)).astype(BF16),
            (value_weight.astype(F32) + dot(value_down, vup)).astype(BF16),
        ],
        1,
    )
    qw, kw = hq * hd, hk * hd
    low_f32 = dot(normed_one, jnp.concatenate([query_down, key_down, value_down], 1))
    low_all = low_f32.astype(BF16)
    low_rest = (low_f32 - low_all.astype(F32)).astype(BF16)
    up_all = jax.scipy.linalg.block_diag(qup, kup, vup)
    qkv = (
        dot(normed_one, jnp.concatenate([query_weight, key_weight, value_weight], 1))
        + dot(jnp.concatenate([low_all, low_rest], 1), jnp.concatenate([up_all, up_all], 0))
    ).astype(BF16)
    query, key, value = qkv[:, :qw], qkv[:, qw : qw + kw], qkv[:, qw + kw :]
    edge = grid.shift_seq(qkv[rows - WIN :, qw:], 1)
    key_heads = jnp.concatenate([edge[:, :kw], key], 0).reshape(rows + WIN, hk, hd)
    value_heads = jnp.concatenate([edge[:, kw:], value], 0).reshape(rows + WIN, hk, hd)
    query_heads = query.reshape(rows, hq, hd)
    q_logit, q_phi = feature(query_heads, query_map)
    k_logit, k_phi = feature(key_heads, key_map)
    query_grouped = query_heads.reshape(rows, hk, group, hd)
    qphi_grouped = q_phi.reshape(rows, hk, group, 2 * hd)
    weighted = k_phi * key_keep[:, None, None].astype(BF16)
    value_ext = jnp.concatenate([value_heads, jnp.ones((rows + WIN, hk, 1), BF16)], 2)
    state_elem = jnp.einsum("ekf,ekd->kfd", weighted, value_ext, preferred_element_type=F32)
    prior = grid.sum_before(state_elem, 1)
    state_prev, norm_prev = prior[..., :hd], prior[..., hd]
    scores = (
        jnp.einsum("ikgd,ekd->kgie", query_grouped, key_heads, preferred_element_type=F32) * scale
    )
    linear = jnp.einsum("ikgf,ekf->kgie", qphi_grouped, k_phi, preferred_element_type=F32)
    exp_window = jnp.exp(scores) * win_mask
    weight_matrix = exp_window + linear * lin_mask
    qphi_carry = qphi_grouped.astype(F32) * carry_on[:, None, None, None]
    carried = jnp.einsum("ikgf,kfd->kgid", qphi_carry, state_prev, precision=EXACT)
    carried_norm = jnp.einsum("ikgf,kf->kgi", qphi_carry, norm_prev, precision=EXACT)
    totals = jnp.sum(weight_matrix, -1) + carried_norm
    shares = (weight_matrix / totals[..., None]).astype(BF16)
    mixture = (
        jnp.einsum("kgie,ekd->kgid", shares, value_heads, preferred_element_type=F32)
        + carried / totals[..., None]
    )
    heads = jnp.transpose(mixture, (2, 0, 1, 3)).reshape(rows, -1).astype(BF16)

    oup = output_up
    odown = output_down.reshape(-1, rank)
    weight_o = (output_weight.astype(F32) + dot(odown, oup)).astype(BF16)
    attn = grid.reduce_rows(dot(heads, weight_o, BF16))
    resid = grid.share(tokens).astype(F32) + attn
    rms_two = lax.rsqrt(jnp.mean(resid * resid, -1, keepdims=True) + EPSILON)
    normed_two = grid.gather_rows((resid * rms_two * g2).astype(BF16))

    g_hidden = dot_nt(cotangent, down_weight)
    cot_cols = grid.pair_columns(cotangent)
    gate = dot(normed_two, gate_weight)
    up = dot(normed_two, up_weight)
    sig = jax.nn.sigmoid(gate)
    silu = gate * sig
    hidden = (silu * up).astype(BF16)
    grad_down = grid.weight_grad(cot_cols, hidden)
    g_gate = (g_hidden * up * sig * (1.0 + gate * (1.0 - sig))).astype(BF16)
    g_up = (g_hidden * silu).astype(BF16)
    g_two = grid.reduce_rows((dot_nt(g_gate, gate_weight) + dot_nt(g_up, up_weight)).astype(BF16))
    normed_cols = grid.pair_columns(normed_two)
    grad_gate = grid.weight_grad(normed_cols, g_gate)
    grad_up = grid.weight_grad(normed_cols, g_up)
    down = grid.reduce_rows(dot(hidden, down_weight, BF16))
    output = grid.gather_rows((resid + down).astype(BF16))

    norm2_part = jnp.sum(g_two * resid * rms_two, 0)
    s_two = g_two * g2
    g_resid = (
        grid.share(cotangent).astype(F32)
        + rms_two * s_two
        - resid * rms_two**3 * jnp.mean(resid * s_two, -1, keepdims=True)
    )
    g_attn = grid.gather_rows(g_resid.astype(BF16))

    g_heads = dot_nt(g_attn, weight_o, BF16)
    g_attn_cols = grid.pair_columns(g_attn)
    grad_wo = grid.weight_grad(g_attn_cols, heads)
    g_low_o = dot_nt(g_attn, oup, BF16)
    low_o = dot(heads, odown, BF16)
    bo_part = dot_tn(low_o, g_attn)
    ao_part = dot_tn(heads, g_low_o)

    g_mixture = g_heads.reshape(rows, hk, group, hd)
    g_mix_float = jnp.transpose(g_mixture.astype(F32), (1, 2, 0, 3))
    g_share = jnp.einsum("ikgd,ekd->kgie", g_mixture, value_heads, preferred_element_type=F32)
    g_value = jnp.einsum("kgie,ikgd->ekd", shares, g_mixture, preferred_element_type=F32)
    g_total = -(jnp.sum(g_share * weight_matrix, -1) + jnp.sum(g_mix_float * carried, -1)) / (
        totals * totals
    )
    g_weight = g_share / totals[..., None] + g_total[..., None]
    g_carried = g_mix_float / totals[..., None]
    g_scores = (g_weight * exp_window).astype(BF16)
    g_linear = (g_weight * lin_mask).astype(BF16)
    g_query = (
        jnp.einsum("kgie,ekd->ikgd", g_scores, key_heads, preferred_element_type=F32) * scale
    )
    g_key = (
        jnp.einsum("kgie,ikgd->ekd", g_scores, query_grouped, preferred_element_type=F32) * scale
    )
    g_qphi = jnp.einsum("kgie,ekf->ikgf", g_linear, k_phi, preferred_element_type=F32)
    g_carried_ext = jnp.concatenate([g_carried, g_total[..., None]], -1)
    g_qphi = g_qphi + carry_on[:, None, None, None] * (
        jnp.einsum("kgid,kfd->ikgf", g_carried_ext, prior, precision=EXACT)
    )
    g_kphi = jnp.einsum("kgie,ikgf->ekf", g_linear, qphi_grouped, preferred_element_type=F32)
    g_state = jnp.einsum("ikgf,kgid->kfd", qphi_carry, g_carried_ext, precision=EXACT)
    later = grid.sum_before(g_state, -1)
    keep_three = key_keep[:, None, None]
    g_kphi = g_kphi + keep_three * jnp.einsum(
        "kfd,ekd->ekf", later, value_ext.astype(F32), precision=EXACT
    )
    g_value = g_value + keep_three * jnp.einsum(
        "ekf,kfd->ekd", k_phi.astype(F32), later[..., :hd], precision=EXACT
    )
    back_rows = jnp.concatenate(
        [
            g_key[:WIN].reshape(WIN, -1),
            g_value[:WIN].reshape(WIN, -1),
            g_kphi[:WIN].reshape(WIN, -1),
        ],
        1,
    )
    back = grid.shift_seq(back_rows.astype(BF16), -1).astype(F32)
    back = jnp.concatenate([jnp.zeros((rows - WIN, back.shape[1]), F32), back], 0)
    g_kphi_own = g_kphi[WIN:] + back[:, 2 * kw :].reshape(rows, hk, 2 * hd)
    gq_logit = feature_back(q_logit, g_qphi.reshape(rows, hq, 2 * hd))
    g_q = (
        g_query.reshape(rows, -1)
        + jnp.einsum("nhe,hde->nhd", gq_logit, query_map, preferred_element_type=F32).reshape(
            rows, -1
        )
    ).astype(BF16)
    featq_part = jnp.einsum("nhd,nhe->hde", query_heads, gq_logit, preferred_element_type=F32)
    gk_logit = feature_back(k_logit[WIN:], g_kphi_own)
    g_k = (
        g_key[WIN:].reshape(rows, -1)
        + back[:, :kw]
        + jnp.einsum("nhe,hde->nhd", gk_logit, key_map, preferred_element_type=F32).reshape(
            rows, -1
        )
    ).astype(BF16)
    featk_part = jnp.einsum("nhd,nhe->hde", key_heads[WIN:], gk_logit, preferred_element_type=F32)
    g_v = (g_value[WIN:].reshape(rows, -1) + back[:, kw : 2 * kw]).astype(BF16)

    g_qkv = jnp.concatenate([g_q, g_k, g_v], 1)
    g_one = grid.reduce_rows(dot_nt(g_qkv, weight_qkv, BF16))
    grad_qkv = grid.weight_grad(grid.pair_columns(normed_one), g_qkv)
    g_low = jnp.concatenate([dot_nt(g_q, qup, BF16), dot_nt(g_k, kup, BF16), dot_nt(g_v, vup, BF16)], 1)
    a_part = dot_tn(normed_one, g_low)
    bq_part = dot_tn(low_all[:, :rank], g_q)
    bk_part = dot_tn(low_all[:, rank : 2 * rank], g_k)
    bv_part = dot_tn(low_all[:, 2 * rank :], g_v)
    stream_share = grid.share(tokens).astype(F32)
    rms_share = grid.share(rms_one)
    norm1_part = jnp.sum(g_one * stream_share * rms_share, 0)
    s_one = g_one * g1
    grad_tokens = (
        g_resid
        + rms_share * s_one
        - stream_share * rms_share**3 * jnp.mean(stream_share * s_one, -1, keepdims=True)
    )
    grad_tokens = grid.gather_rows(grad_tokens.astype(BF16)).astype(F32)

    n = grid.seq

    def blocks(x, dim):
        shape = x.shape
        x = x.reshape(shape[:dim] + (n, shape[dim] // n) + shape[dim + 1 :])
        return jnp.moveaxis(x, dim, 0).reshape(n, -1)

    both = [(norm1_part, 0), (norm2_part, 0), (a_part, 0), (bo_part, 1)]
    own = [
        (bq_part.reshape(query_up.shape), 2),
        (bk_part.reshape(key_up.shape), 2),
        (bv_part.reshape(value_up.shape), 2),
        (featq_part, 1),
        (featk_part, 1),
        (ao_part.reshape(output_down.shape), 1),
    ]
    cut = [blocks(x, d) for x, d in both + own]
    summed = grid.scatter_blocks(jnp.concatenate(cut, 1))
    n_both = sum(c.shape[1] for c in cut[: len(both)])
    flat = jnp.concatenate([grid.sum_kv(summed[:n_both].astype(BF16)), summed[n_both:]])
    done = []
    at = 0
    for x, d in both + own:
        shape = list(x.shape)
        shape[d] //= n
        size = x.size // n
        done.append(flat[at : at + size].reshape(shape))
        at += size
    norm1, norm2, grad_a, grad_bo, bq, bk, bv, featq, featk, grad_ao = done
    return (
        output,
        grad_tokens,
        norm1,
        grad_qkv[:, :qw],
        grad_qkv[:, qw : qw + kw],
        grad_qkv[:, qw + kw :],
        grad_a[:, :rank],
        bq,
        grad_a[:, rank : 2 * rank],
        bk,
        grad_a[:, 2 * rank :],
        bv,
        featq,
        featk,
        grad_wo.T,
        grad_ao,
        grad_bo,
        norm2,
        grad_gate,
        grad_up,
        grad_down.T,
    )


def solution(mesh):
    placed = (
        P("seq", None),
        P(),
        P(None, "kv"),
        P(None, "kv"),
        P(None, "kv"),
        P(),
        P(None, "kv", None),
        P(),
        P(None, "kv", None),
        P(),
        P(None, "kv", None),
        P("kv", None, None),
        P("kv", None, None),
        P("kv", None),
        P("kv", None, None),
        P(),
        P(),
        P(None, "kv"),
        P(None, "kv"),
        P("kv", None),
        P("seq"),
        P("seq", None),
    )
    return jax.shard_map(
        local,
        mesh=mesh,
        in_specs=placed,
        out_specs=(
            P("seq", None),
            P("seq", None),
            P("seq"),
            P("seq", "kv"),
            P("seq", "kv"),
            P("seq", "kv"),
            P("seq", None),
            P(None, "kv", "seq"),
            P("seq", None),
            P(None, "kv", "seq"),
            P("seq", None),
            P(None, "kv", "seq"),
            P("kv", "seq", None),
            P("kv", "seq", None),
            P("kv", "seq"),
            P("kv", "seq", None),
            P(None, "seq"),
            P("seq"),
            P("seq", "kv"),
            P("seq", "kv"),
            P("kv", "seq"),
        ),
        check_vma=False,
    )
```

time: 2020 us -> 1050 us (0.52)
  waiting for transfers between devices: 1170 us -> 334 us
  blocking collectives: 211 us -> 0 us
  local copies, waits for them, and re-layouts: 49.6 us -> 134 us
  starting transfers between devices: 8.4 us -> 57 us
  matrix products: 402 us -> 356 us
    reduce_scatter x11 -> x5, waiting for transfers between devices: 725 us -> 0.01 us  [line_scatter(): lax.psum_scatter(part, 'seq', scatter_dimension=0, tiled=True, axis_index...]
    psum x3 -> x0, waiting for transfers between devices: 446 us -> none  [the longest x1 178 us: local(): lax.psum((attn_part, output_adapter_path), 'kv')]
    ppermute x2 -> x35, waiting for transfers between devices: 0.01 us -> 334 us  [the longest x5 172 us: weight_grad(): got = lax.ppermute(dot_tn(left[0], right, BF16), 'seq', self.x_swap)]
    all_gather x4 -> x0, blocking collectives: 101 us -> none  [the longest x2 51.5 us: carried_in_2(): lax.all_gather(a.astype(kind), axis)]
    unnamed x3 -> x0, blocking collectives: 85.6 us -> none
    ppermute x2 -> x35, starting transfers between devices: 6.98 us -> 56.6 us  [the longest x8 24.4 us: shift_seq(): lax.ppermute(x, 'seq', [(i, i + by) for i in range(n) if 0 <= i + by < n])]
    dot_general x59 -> x48, matrix products: 285 us -> 238 us  [the longest x16 73 us: dot_tn(): lax.dot_general(a, b, (((0,), (0,)), ((), ())), preferred_element_type=F32)]
    unnamed x214 -> x274, local copies, waits for them, and re-layouts: 19.3 us -> 62 us
  transfers between devices with their start and end apart: 17 -> 40, of which waited for: 12 -> 16; matrix products, arithmetic and copies ran while one was open for 13% -> 44% of each run, Pallas kernels for 0% -> 0%
where the time goes in v1:
time: 1050 us; the launch traced here: 1040 us
  matrix products  356 us (34%)
  waiting for transfers between devices  334 us (32%)
  other arithmetic  147 us (14%)
  local copies, waits for them, and re-layouts  134 us (13%)
  starting transfers between devices  57 us (5%)
  between operations  16.1 us (2%)
    ppermute x5, waiting for transfers between devices, weight_grad(): got = lax.ppermute(dot_tn(left[0], right, BF16), 'seq', self.x_swap)  172 us
    ppermute x4, waiting for transfers between devices, reduce_rows(): total = total + lax.ppermute(out, 'kv', self.y_shift(j)).astype(F32)  84.8 us
    dot_general x16, matrix products, dot_tn(): lax.dot_general(a, b, (((0,), (0,)), ((), ())), preferred_element_type=F32)  73 us
    ppermute x4, waiting for transfers between devices, gather_rows(): lax.ppermute(share, 'kv', self.y_shift(j))  67.8 us
    unnamed x274, local copies, waits for them, and re-layouts  62 us
    dot_general x11, matrix products, dot(): return jnp.dot(a, b, preferred_element_type=F32).astype(out)  61.5 us
    dot_general x8, matrix products, dot_nt(): lax.dot_general(a, b, (((1,), (1,)), ((), ())), preferred_element_type=F32)  52.9 us
    convert_element_type x1, other arithmetic, local(): g_scores = (g_weight * exp_window).astype(BF16)  29.8 us
  transfers between devices with their start and end apart: 40, of which 16 were waited for; matrix products, arithmetic and copies ran while one was open for 44% of the time, Pallas kernels for 0%

profile of v1, /device:TPU:0, one launch (start us, length us, event | category | flops | bytes accessed | tf_op | source)
XLA Modules:
  0.0 1043.5 jit_solution(2214440660085255855)
XLA Ops:
  9.7 6.4 copy.233
  28.4 5.1 collective-permute-start
  40.3 4.7 fusion.23
  64.2 5.6 collective-permute-start.2
  69.8 15.9 %bitcast_multiply_fusion.2 = f32[2,4,1024,1088]{2,3,1,0:T(8,128)} fusion(bf16[1088,2,64,1]{0,2,3,1:T(8,128)(2,1)} %bitcast.436, bf16[1024,2,4,64]{0,3,2,1:T(8,128)(2,1)S(1)} %bitcast.414, f32[1024,1088]{0,1:T(8,128)} %get-tuple-element.229), kind=kOutput, calls=%fused_computation.21 | convolution fusion | flops 1158676480 | bytes 41435136 | tf_op jit(solution)/shard_map/ikgd,ekd->kgie/dot_general | solution.py:238
  90.2 24.9 %fusion.189 = (f32[2,4,1024]{2,1,0:T(4,128)S(1)}, f32[2,4,1024,1088]{2,3,1,0:T(8,128)}) fusion(f32[2,4,1024,1088]{2,3,1,0:T(8,128)} %bitcast_multiply_fusion.2, f32[1024,1088]{0,1:T(8,128)} %get-tuple-element.228, bf16[1024,2,4,128]{3,0,2,1:T(8,128)(2,1)S(1)} %pad_maximum_fusion.4, bf16[1088,2,128]{2,0,1:T(8,128)(2,1)} %copy-done.35), kind=kOutput, calls=%fused_computation.376 | convolution fusion | flops 2308431872 | bytes 78446592 | tf_op jit(solution)/shard_map/ikgf,ekf->kgie/dot_general | solution.py:240
  115.1 5.0 fusion.26
  127.8 14.0 %divide_convert_fusion = bf16[2,4,1024,1088]{2,3,1,0:T(8,128)(2,1)S(1)} fusion(f32[2,4,1024,1088]{2,3,1,0:T(8,128)} %get-tuple-element.241, f32[2,4,1024]{2,1,0:T(4,128)S(1)} %bitcast_add_fusion.8), kind=kLoop, calls=%fused_computation.24 | loop fusion | flops 17825792 | bytes 53510144 | tf_op jit(solution)/shard_map/convert_element_type | solution.py:247
  164.3 23.7 %collective-permute-done.5 = bf16[256,2048]{1,0:T(8,128)(2,1)S(1)} collective-permute-done((bf16[256,2048]{1,0:T(8,128)(2,1)S(1)}, bf16[256,2048]{1,0:T(8,128)(2,1)S(1)}, u32[]{:S(2)}, u32[]{:S(2)}) %collective-permute-start.5) | collective-permute-done | bytes 1048608 | tf_op jit(solution)/shard_map/ppermute | solution.py:65
  192.2 23.0 %collective-permute-done.6 = bf16[256,2048]{1,0:T(8,128)(2,1)} collective-permute-done((bf16[256,2048]{1,0:T(8,128)(2,1)S(1)}, bf16[256,2048]{1,0:T(8,128)(2,1)}, u32[]{:S(2)}, u32[]{:S(2)}) %collective-permute-start.6) | collective-permute-done | bytes 1048608 | tf_op jit(solution)/shard_map/ppermute | solution.py:71
  219.4 14.8 %fusion.194 = f32[1024,2048]{1,0:T(8,128)} fusion(bf16[1024,2048]{1,0:T(8,128)(2,1)} %param.43, bf16[2048,2048]{1,0:T(8,128)(2,1)} %param.41), kind=kOutput, calls=%fused_computation.377 | convolution fusion | flops 8589934592 | bytes 20971520 | tf_op jit(solution)/shard_map/dot_general | solution.py:18
  238.9 13.2 %fusion.175 = f32[1024,2048]{1,0:T(8,128)} fusion(bf16[2048,2048]{1,0:T(8,128)(2,1)} %param.40, bf16[512,2048]{1,0:T(8,128)(2,1)S(1)} %get-tuple-element.201, bf16[512,2048]{1,0:T(8,128)(2,1)S(1)} %get-tuple-element.200), kind=kOutput, calls=%fused_computation.362 | convolution fusion | flops 8598323200 | bytes 20971520 | tf_op jit(solution)/shard_map/dot_general | solution.py:14
  252.1 21.1 %multiply_convert_fusion.2 = (bf16[1024,2048]{1,0:T(8,128)(2,1)}, bf16[1024,2048]{1,0:T(8,128)(2,1)}, bf16[1024,2048]{1,0:T(8,128)(2,1)}) fusion(f32[1024,2048]{1,0:T(8,128)} %fusion.194, f32[1024,2048]{1,0:T(8,128)} %fusion.175, bf16[2048,2048]{1,0:T(8,128)(2,1)} %param.39, bf16[512,2048]{1,0:T(8,128)(2,1)} %copy-done.44, bf16[512,2048]{1,0:T(8,128)(2,1)} %copy-done.42), kind=kOutput, calls=%fused_computation.34 | convolution fusion | flops 8629780480 | bytes 41943040 | tf_op jit(solution)/shard_map/dot_general | solution.py:14
  273.2 15.2 %fusion.195 = f32[1024,2048]{1,0:T(8,128)} fusion(bf16[1024,2048]{1,0:T(8,128)(2,1)} %get-tuple-element.184, bf16[2048,2048]{1,0:T(8,128)(2,1)} %param.39), kind=kOutput, calls=%fused_computation.378 | convolution fusion | flops 8589934592 | bytes 20971520 | tf_op jit(solution)/shard_map/dot_general | solution.py:18
  288.4 12.8 %add_convert_fusion.3 = bf16[1024,2048]{1,0:T(8,128)(2,1)S(1)} fusion(f32[1024,2048]{1,0:T(8,128)} %fusion.195, bf16[1024,2048]{1,0:T(8,128)(2,1)S(1)} %copy-done.119, bf16[2048,2048]{1,0:T(8,128)(2,1)} %param.40), kind=kOutput, calls=%fused_computation.33 | convolution fusion | flops 8594128896 | bytes 25165824 | tf_op jit(solution)/shard_map/dot_general | solution.py:18
  303.4 11.2 %convolution_convert_fusion = bf16[1024,2048]{1,0:T(8,128)(2,1)S(1)} fusion(bf16[1024,2048]{1,0:T(8,128)(2,1)S(1)} %copy-done.121, bf16[2048,2048]{1,0:T(8,128)(2,1)} %param.41), kind=kOutput, calls=%fused_computation.64 | convolution fusion | flops 8592031744 | bytes 16777216 | tf_op jit(solution)/shard_map/dot_general | solution.py:14
  321.7 20.8 %collective-permute-done.13 = bf16[256,2048]{1,0:T(8,128)(2,1)S(1)} collective-permute-done((bf16[256,2048]{1,0:T(8,128)(2,1)S(1)}, bf16[256,2048]{1,0:T(8,128)(2,1)S(1)}, u32[]{:S(2)}, u32[]{:S(2)}) %collective-permute-start.13) | collective-permute-done | bytes 1048608 | tf_op jit(solution)/shard_map/ppermute | solution.py:65
  343.8 20.2 %collective-permute-done.9 = bf16[256,2048]{1,0:T(8,128)(2,1)S(1)} collective-permute-done((bf16[256,2048]{1,0:T(8,128)(2,1)S(1)}, bf16[256,2048]{1,0:T(8,128)(2,1)S(1)}, u32[]{:S(2)}, u32[]{:S(2)}) %collective-permute-start.9) | collective-permute-done | bytes 1048608 | tf_op jit(solution)/shard_map/ppermute | solution.py:65
  369.4 22.8 %collective-permute-done.14 = bf16[256,2048]{1,0:T(8,128)(2,1)} collective-permute-done((bf16[256,2048]{1,0:T(8,128)(2,1)S(1)}, bf16[256,2048]{1,0:T(8,128)(2,1)}, u32[]{:S(2)}, u32[]{:S(2)}) %collective-permute-start.14) | collective-permute-done | bytes 1048608 | tf_op jit(solution)/shard_map/ppermute | solution.py:71
  399.1 6.5 copy.269
  406.3 4.8 constant_dynamic-slice_fusion
  414.7 9.2 convolution_convert_fusion.3
  434.8 22.6 %fusion.15 = (f32[2,4,1024]{2,1,0:T(4,128)S(1)}, f32[2,1088,1024,4]{2,1,3,0:T(8,128)}) fusion(f32[2,4,1024,1088]{2,3,1,0:T(8,128)} %get-tuple-element.241, bf16[1088,2,64,1]{0,2,3,1:T(8,128)(2,1)S(1)} %bitcast.441, bf16[1024,2,4,64]{0,3,2,1:T(8,128)(2,1)S(1)} %bitcast.410), kind=kOutput, calls=%fused_computation.18 | convolution fusion | flops 1158668288 | bytes 72663040 | tf_op jit(solution)/shard_map/ikgd,ekd->kgie/dot_general | solution.py:298
  457.4 6.6 copy.267
  472.6 29.8 %multiply_convert_fusion.1 = (bf16[2,4,1024,1088]{2,3,1,0:T(8,128)(2,1)}, bf16[2,4,1024,1088]{2,3,1,0:T(8,128)(2,1)S(1)}) fusion(f32[2,4,1024,1088]{2,3,1,0:T(8,128)} %bitcast_multiply_fusion.2, f32[2,4,1024]{2,1,0:T(4,128)S(1)} %bitcast.478, f32[2,4,1024]{2,1,0:T(4,128)S(1)} %copy-done.79, f32[2,1088,1024,4]{2,1,3,0:T(8,128)} %get-tuple-element.243, ...), kind=kLoop, calls=%fused_computation.23 | loop fusion | flops 53477376 | bytes 111476736 | tf_op jit(solution)/shard_map/convert_element_type | solution.py:305
  502.4 6.2 fusion.114
  522.0 6.9 fusion.95
  528.9 11.8 %fusion.57 = (bf16[1024,2,4,64]{0,3,2,1:T(8,128)(2,1)}, f32[2,64,4,1024]{3,1,2,0:T(8,128)}) fusion(f32[1024,2,4,64]{0,3,2,1:T(8,128)} %bitcast.423, bf16[1088,2,64,1]{0,2,3,1:T(8,128)(2,1)} %bitcast.437, bf16[2,4,1024,1088]{2,3,1,0:T(8,128)(2,1)} %get-tuple-element.181), kind=kOutput, calls=%fused_computation.123 | convolution fusion | flops 1142423552 | bytes 23347200 | tf_op jit(solution)/shard_map/kgie,ekd->ikgd/dot_general | solution.py:308
  540.7 12.8 %fusion.47 = f32[1088,2,64]{0,2,1:T(8,128)} fusion(bf16[1024,2,4,64]{0,3,2,1:T(8,128)(2,1)} %bitcast.415, bf16[2,4,1024,1088]{2,3,1,0:T(8,128)(2,1)} %get-tuple-element.181), kind=kOutput, calls=%fused_computation.104 | convolution fusion | flops 1140989952 | bytes 19431424 | tf_op jit(solution)/shard_map/kgie,ikgd->ekd/dot_general | solution.py:311
  554.8 11.9 %convolution_bitcast_fusion = f32[1088,2,128]{2,0,1:T(8,128)} fusion(bf16[2,4,1024,1088]{2,3,1,0:T(8,128)(2,1)} %copy-done.5, bf16[1024,2,4,128]{3,0,2,1:T(8,128)(2,1)S(1)} %copy-done.8), kind=kOutput, calls=%fused_computation.94 | convolution fusion | flops 2281701376 | bytes 21037056 | tf_op jit(solution)/shard_map/kgie,ikgf->ekf/dot_general | solution.py:318
  568.2 9.9 convolution_bitcast_fusion.2
  596.9 10.3 fusion.89
  624.5 31.6 %collective-permute-done.30 = bf16[1024,768]{1,0:T(8,128)(2,1)S(1)} collective-permute-done((bf16[1024,768]{1,0:T(8,128)(2,1)S(1)}, bf16[1024,768]{1,0:T(8,128)(2,1)S(1)}, u32[]{:S(2)}, u32[]{:S(2)}) %collective-permute-start.30) | collective-permute-done | bytes 1572896 | tf_op jit(solution)/shard_map/ppermute | solution.py:101
  660.6 8.9 add_convert_fusion
  675.3 6.4 copy.268
  685.2 4.7 convolution_convert_fusion.4
  691.7 87.2 %collective-permute-done.33 = bf16[1024,2048]{1,0:T(8,128)(2,1)S(1)} collective-permute-done((bf16[1024,2048]{1,0:T(8,128)(2,1)S(1)}, bf16[1024,2048]{1,0:T(8,128)(2,1)S(1)}, u32[]{:S(2)}, u32[]{:S(2)}) %collective-permute-start.33) | collective-permute-done | bytes 4194336 | tf_op jit(solution)/shard_map/ppermute | solution.py:101
  778.9 6.1 add_convert_fusion.1
  785.1 8.2 convolution_convert_fusion.5
  812.7 11.2 %collective-permute-done.10 = bf16[256,2048]{1,0:T(8,128)(2,1)} collective-permute-done((bf16[256,2048]{1,0:T(8,128)(2,1)S(1)}, bf16[256,2048]{1,0:T(8,128)(2,1)}, u32[]{:S(2)}, u32[]{:S(2)}) %collective-permute-start.10) | collective-permute-done | bytes 1048608 | tf_op jit(solution)/shard_map/ppermute | solution.py:71
  828.0 53.7 %collective-permute-done.32 = bf16[1024,2048]{1,0:T(8,128)(2,1)} collective-permute-done((bf16[1024,2048]{1,0:T(8,128)(2,1)}, bf16[1024,2048]{1,0:T(8,128)(2,1)}, u32[]{:S(2)}, u32[]{:S(2)}) %collective-permute-start.32) | collective-permute-done | bytes 4194336 | tf_op jit(solution)/shard_map/ppermute | solution.py:101
  881.7 8.1 add_convert_fusion.2
  890.5 5.0 convolution_bitcast_fusion.4
  895.5 6.2 fusion.97
  904.3 5.9 convolution_convert_fusion.2
  943.2 20.1 %collective-permute-done.21 = bf16[256,2048]{1,0:T(8,128)(2,1)S(1)} collective-permute-done((bf16[256,2048]{1,0:T(8,128)(2,1)}, bf16[256,2048]{1,0:T(8,128)(2,1)S(1)}, u32[]{:S(2)}, u32[]{:S(2)}) %collective-permute-start.21) | collective-permute-done | bytes 1048608 | tf_op jit(solution)/shard_map/ppermute | solution.py:65
  983.3 4.9 collective-permute-start.26
  992.3 10.8 %collective-permute-done.22 = bf16[256,2048]{1,0:T(8,128)(2,1)} collective-permute-done((bf16[256,2048]{1,0:T(8,128)(2,1)S(1)}, bf16[256,2048]{1,0:T(8,128)(2,1)}, u32[]{:S(2)}, u32[]{:S(2)}) %collective-permute-start.22) | collective-permute-done | bytes 1048608 | tf_op jit(solution)/shard_map/ppermute | solution.py:71
  (539 shorter events, 318.7 us)
Async XLA Ops:
  7.2 981.6 %reduce-scatter.8.cloned.1.call-start = ((), (), s32[]{:S(2)}) async-start(), calls=%async_computation.6 | async-start | bytes 1310720 | tf_op jit(solution)/shard_map/reduce_scatter | solution.py:106
  28.4 23.8 %collective-permute-start = (bf16[64,256]{1,0:T(8,128)(2,1)S(1)}, bf16[64,256]{1,0:T(8,128)(2,1)S(1)}, u32[]{:S(2)}, u32[]{:S(2)}) collective-permute-start(bf16[64,256]{1,0:T(8,128)(2,1)S(1)} %slice.247), channel_id=1, source_target_pairs={{0,4},{4,8},{8,12},{12,16},{16,20},{20,24},{24,28},{1,5},{5,9},{9,... | collective-permute-start | bytes 98312 | tf_op jit(solution)/shard_map/ppermute | solution.py:125
  34.2 35.6 %copy-start.10 = (bf16[1024,512]{0,1:T(8,128)(2,1)}, bf16[1024,512]{0,1:T(8,128)(2,1)S(1)}, u32[]{:S(2)}) copy-start(bf16[1024,512]{0,1:T(8,128)(2,1)S(1)} %copy.235) | copy-start | bytes 3145732
  40.2 82.8 %copy-start.91 = (f32[1024]{0:T(1024)}, f32[1024]{0:T(1024)S(1)}, u32[]{:S(2)}) copy-start(f32[1024]{0:T(1024)S(1)} %compare_convert_fusion) | copy-start | bytes 12292
  58.7 5.4 collective-permute-start.1
  63.4 59.7 %copy-start.6 = (bf16[1024,2,4,128]{3,0,2,1:T(8,128)(2,1)}, bf16[1024,2,4,128]{3,0,2,1:T(8,128)(2,1)S(1)}, u32[]{:S(2)}) copy-start(bf16[1024,2,4,128]{3,0,2,1:T(8,128)(2,1)S(1)} %pad_maximum_fusion.4) | copy-start | bytes 6291460
  64.2 21.6 %collective-permute-start.2 = (f32[2,128,65]{1,2,0:T(8,128)S(1)}, f32[2,128,65]{1,2,0:T(8,128)S(1)}, u32[]{:S(2)}, u32[]{:S(2)}) collective-permute-start(f32[2,128,65]{1,2,0:T(8,128)S(1)} %add.374), channel_id=1, source_target_pairs={{0,8},{4,12},{8,16},{12,20},{16,24},{20,28},{1,9},{5,13},{9,17},{1... | collective-permute-start | bytes 199688 | tf_op jit(solution)/shard_map/ppermute | solution.py:125
  85.7 29.4 %collective-permute-start.3 = (f32[2,128,65]{1,2,0:T(8,128)S(1)}, f32[2,128,65]{1,2,0:T(8,128)S(1)}, u32[]{:S(2)}, u32[]{:S(2)}) collective-permute-start(f32[2,128,65]{1,2,0:T(8,128)S(1)} %add.375), channel_id=1, source_target_pairs={{0,16},{4,20},{8,24},{12,28},{1,17},{5,21},{9,25},{13,29},{2,18},{... | collective-permute-start | bytes 199688 | tf_op jit(solution)/shard_map/ppermute | solution.py:125
  153.2 4.4 collective-permute-start.4
  162.7 25.3 %collective-permute-start.5 = (bf16[256,2048]{1,0:T(8,128)(2,1)S(1)}, bf16[256,2048]{1,0:T(8,128)(2,1)S(1)}, u32[]{:S(2)}, u32[]{:S(2)}) collective-permute-start(bf16[256,2048]{1,0:T(8,128)(2,1)S(1)} %fusion.103), channel_id=1, source_target_pairs={{0,2},{1,3},{2,0},{3,1},{4,6},{5,7},{6,4},{7,5},{8,10},{9,11},{10,... | collective-permute-start | bytes 3145736 | tf_op jit(solution)/shard_map/ppermute | solution.py:65
  190.6 24.5 %collective-permute-start.6 = (bf16[256,2048]{1,0:T(8,128)(2,1)S(1)}, bf16[256,2048]{1,0:T(8,128)(2,1)}, u32[]{:S(2)}, u32[]{:S(2)}) collective-permute-start(bf16[256,2048]{1,0:T(8,128)(2,1)S(1)} %multiply_convert_fusion.5), channel_id=1, source_target_pairs={{0,2},{1,3},{2,0},{3,1},{4,6},{5,7},{6,4},{7,5},{8,10},{9,11},{10,... | collective-permute-start | bytes 3145736 | tf_op jit(solution)/shard_map/ppermute | solution.py:71
  219.4 14.8 %collective-permute-start.7 = (bf16[512,2048]{1,0:T(8,128)(2,1)}, bf16[512,2048]{1,0:T(8,128)(2,1)}, u32[]{:S(2)}, u32[]{:S(2)}) collective-permute-start(bf16[512,2048]{1,0:T(8,128)(2,1)} %pad_maximum_fusion.5), channel_id=1, source_target_pairs={{0,1},{1,0},{2,3},{3,2},{4,5},{5,4},{6,7},{7,6},{8,9},{9,8},{10,11... | collective-permute-start | bytes 6291464 | tf_op jit(solution)/shard_map/ppermute | solution.py:82
  301.4 14.0 %collective-permute-start.12 = (bf16[512,2048]{1,0:T(8,128)(2,1)S(1)}, bf16[512,2048]{1,0:T(8,128)(2,1)S(1)}, u32[]{:S(2)}, u32[]{:S(2)}) collective-permute-start(bf16[512,2048]{1,0:T(8,128)(2,1)S(1)} %dynamic-slice_bitcast_fusion.1), channel_id=1, source_target_pairs={{0,1},{1,0},{2,3},{3,2},{4,5},{5,4},{6,7},{7,6},{8,9},{9,8},{10,11... | collective-permute-start | bytes 6291464 | tf_op jit(solution)/shard_map/ppermute | solution.py:58
  314.8 4.4 collective-permute-start.8
  316.3 26.1 %collective-permute-start.13 = (bf16[256,2048]{1,0:T(8,128)(2,1)S(1)}, bf16[256,2048]{1,0:T(8,128)(2,1)S(1)}, u32[]{:S(2)}, u32[]{:S(2)}) collective-permute-start(bf16[256,2048]{1,0:T(8,128)(2,1)S(1)} %fusion.105), channel_id=1, source_target_pairs={{0,2},{1,3},{2,0},{3,1},{4,6},{5,7},{6,4},{7,5},{8,10},{9,11},{10,... | collective-permute-start | bytes 3145736 | tf_op jit(solution)/shard_map/ppermute | solution.py:65
  320.1 43.9 %collective-permute-start.9 = (bf16[256,2048]{1,0:T(8,128)(2,1)S(1)}, bf16[256,2048]{1,0:T(8,128)(2,1)S(1)}, u32[]{:S(2)}, u32[]{:S(2)}) collective-permute-start(bf16[256,2048]{1,0:T(8,128)(2,1)S(1)} %fusion.104), channel_id=1, source_target_pairs={{0,2},{1,3},{2,0},{3,1},{4,6},{5,7},{6,4},{7,5},{8,10},{9,11},{10,... | collective-permute-start | bytes 3145736 | tf_op jit(solution)/shard_map/ppermute | solution.py:65
  367.9 24.3 %collective-permute-start.14 = (bf16[256,2048]{1,0:T(8,128)(2,1)S(1)}, bf16[256,2048]{1,0:T(8,128)(2,1)}, u32[]{:S(2)}, u32[]{:S(2)}) collective-permute-start(bf16[256,2048]{1,0:T(8,128)(2,1)S(1)} %get-tuple-element.175), channel_id=1, source_target_pairs={{0,2},{1,3},{2,0},{3,1},{4,6},{5,7},{6,4},{7,5},{8,10},{9,11},{10,... | collective-permute-start | bytes 3145736 | tf_op jit(solution)/shard_map/ppermute | solution.py:71
  395.1 28.8 %collective-permute-start.15 = (bf16[512,2048]{1,0:T(8,128)(2,1)}, bf16[512,2048]{1,0:T(8,128)(2,1)}, u32[]{:S(2)}, u32[]{:S(2)}) collective-permute-start(bf16[512,2048]{1,0:T(8,128)(2,1)} %pad_maximum_fusion.7), channel_id=1, source_target_pairs={{0,1},{1,0},{2,3},{3,2},{4,5},{5,4},{6,7},{7,6},{8,9},{9,8},{10,11... | collective-permute-start | bytes 6291464 | tf_op jit(solution)/shard_map/ppermute | solution.py:82
  424.0 236.7 %collective-permute-start.34 = (bf16[1024,2048]{1,0:T(8,128)(2,1)}, bf16[1024,2048]{1,0:T(8,128)(2,1)}, u32[]{:S(2)}, u32[]{:S(2)}) collective-permute-start(bf16[1024,2048]{1,0:T(8,128)(2,1)} %convolution_convert_fusion.3), channel_id=1, source_target_pairs={{0,4},{4,0},{8,12},{12,8},{16,20},{20,16},{24,28},{28,24},{1,5},{5... | collective-permute-start | bytes 12582920 | tf_op jit(solution)/shard_map/ppermute | solution.py:101
  470.4 142.9 %collective-permute-start.31 = (bf16[1024,512]{1,0:T(8,128)(2,1)}, bf16[1024,512]{1,0:T(8,128)(2,1)}, u32[]{:S(2)}, u32[]{:S(2)}) collective-permute-start(bf16[1024,512]{1,0:T(8,128)(2,1)} %convolution_convert_fusion.7), channel_id=1, source_target_pairs={{0,4},{4,0},{8,12},{12,8},{16,20},{20,16},{24,28},{28,24},{1,5},{5... | collective-permute-start | bytes 3145736 | tf_op jit(solution)/shard_map/ppermute | solution.py:101
  518.7 34.8 %collective-permute-start.16 = (f32[2,128,65]{1,2,0:T(8,128)S(1)}, f32[2,128,65]{1,2,0:T(8,128)S(1)}, u32[]{:S(2)}, u32[]{:S(2)}) collective-permute-start(f32[2,128,65]{1,2,0:T(8,128)S(1)} %fusion.100), channel_id=1, source_target_pairs={{4,0},{8,4},{12,8},{16,12},{20,16},{24,20},{28,24},{5,1},{9,5},{13... | collective-permute-start | bytes 199688 | tf_op jit(solution)/shard_map/ppermute | solution.py:125
  553.5 13.2 %collective-permute-start.17 = (f32[2,128,65]{1,2,0:T(8,128)S(1)}, f32[2,128,65]{1,2,0:T(8,128)S(1)}, u32[]{:S(2)}, u32[]{:S(2)}) collective-permute-start(f32[2,128,65]{1,2,0:T(8,128)S(1)} %add.407), channel_id=1, source_target_pairs={{8,0},{12,4},{16,8},{20,12},{24,16},{28,20},{9,1},{13,5},{17,9},{2... | collective-permute-start | bytes 199688 | tf_op jit(solution)/shard_map/ppermute | solution.py:125
  566.8 12.3 %collective-permute-start.18 = (f32[2,128,65]{1,2,0:T(8,128)S(1)}, f32[2,128,65]{1,2,0:T(8,128)S(1)}, u32[]{:S(2)}, u32[]{:S(2)}) collective-permute-start(f32[2,128,65]{1,2,0:T(8,128)S(1)} %add.408), channel_id=1, source_target_pairs={{16,0},{20,4},{24,8},{28,12},{17,1},{21,5},{25,9},{29,13},{18,2},{... | collective-permute-start | bytes 199688 | tf_op jit(solution)/shard_map/ppermute | solution.py:125
  584.3 6.8 collective-permute-start.19
  586.7 69.4 %copy-start.54 = (bf16[1024,512]{0,1:T(8,128)(2,1)}, bf16[1024,512]{0,1:T(8,128)(2,1)S(1)}, u32[]{:S(2)}) copy-start(bf16[1024,512]{0,1:T(8,128)(2,1)S(1)} %fusion.56) | copy-start | bytes 3145732
  617.9 397.2 %reduce-scatter.6.cloned.1.call-start = ((), (), s32[]{:S(2)}) async-start(), calls=%async_computation.5 | async-start | bytes 1966080 | tf_op jit(solution)/shard_map/reduce_scatter | solution.py:106
  618.0 38.2 %copy-start.69 = (bf16[1024,4,1,256]{0,3,2,1:T(8,128)(2,1)S(1)}, bf16[1024,4,1,256]{0,3,2,1:T(8,128)(2,1)}, u32[]{:S(2)}) copy-start(bf16[1024,4,1,256]{0,3,2,1:T(8,128)(2,1)} %get-tuple-element.192) | copy-start | bytes 6291460
  621.5 34.6 %collective-permute-start.30 = (bf16[1024,768]{1,0:T(8,128)(2,1)S(1)}, bf16[1024,768]{1,0:T(8,128)(2,1)S(1)}, u32[]{:S(2)}, u32[]{:S(2)}) collective-permute-start(bf16[1024,768]{1,0:T(8,128)(2,1)S(1)} %convolution_convert_fusion.6), channel_id=1, source_target_pairs={{0,4},{4,0},{8,12},{12,8},{16,20},{20,16},{24,28},{28,24},{1,5},{5... | collective-permute-start | bytes 4718600 | tf_op jit(solution)/shard_map/ppermute | solution.py:101
  660.4 358.1 %reduce-scatter.14.cloned.1.call-start = ((), (), s32[]{:S(2)}) async-start(), calls=%async_computation.9 | async-start | bytes 5242880 | tf_op jit(solution)/shard_map/reduce_scatter | solution.py:106
  669.5 354.6 %reduce-scatter.12.cloned.1.call-start = ((), (), s32[]{:S(2)}) async-start(), calls=%async_computation.8 | async-start | bytes 5242880 | tf_op jit(solution)/shard_map/reduce_scatter | solution.py:106
  684.5 94.3 %copy-start.70 = (bf16[1024,4,1,256]{0,3,2,1:T(8,128)(2,1)}, bf16[1024,4,1,256]{0,3,2,1:T(8,128)(2,1)S(1)}, u32[]{:S(2)}) copy-start(bf16[1024,4,1,256]{0,3,2,1:T(8,128)(2,1)S(1)} %get-tuple-element.189) | copy-start | bytes 6291460
  689.9 89.0 %collective-permute-start.33 = (bf16[1024,2048]{1,0:T(8,128)(2,1)S(1)}, bf16[1024,2048]{1,0:T(8,128)(2,1)S(1)}, u32[]{:S(2)}, u32[]{:S(2)}) collective-permute-start(bf16[1024,2048]{1,0:T(8,128)(2,1)S(1)} %convolution_convert_fusion.4), channel_id=1, source_target_pairs={{0,4},{4,0},{8,12},{12,8},{16,20},{20,16},{24,28},{28,24},{1,5},{5... | collective-permute-start | bytes 12582920 | tf_op jit(solution)/shard_map/ppermute | solution.py:101
  785.0 241.9 %reduce-scatter.10.cloned.1.call-start = ((), (), s32[]{:S(2)}) async-start(), calls=%async_computation.7 | async-start | bytes 5242880 | tf_op jit(solution)/shard_map/reduce_scatter | solution.py:106
  793.3 88.4 %collective-permute-start.32 = (bf16[1024,2048]{1,0:T(8,128)(2,1)}, bf16[1024,2048]{1,0:T(8,128)(2,1)}, u32[]{:S(2)}, u32[]{:S(2)}) collective-permute-start(bf16[1024,2048]{1,0:T(8,128)(2,1)} %convolution_convert_fusion.5), channel_id=1, source_target_pairs={{0,4},{4,0},{8,12},{12,8},{16,20},{20,16},{24,28},{28,24},{1,5},{5... | collective-permute-start | bytes 12582920 | tf_op jit(solution)/shard_map/ppermute | solution.py:101
  803.5 20.4 %collective-permute-start.10 = (bf16[256,2048]{1,0:T(8,128)(2,1)S(1)}, bf16[256,2048]{1,0:T(8,128)(2,1)}, u32[]{:S(2)}, u32[]{:S(2)}) collective-permute-start(bf16[256,2048]{1,0:T(8,128)(2,1)S(1)} %copy-done.61), channel_id=1, source_target_pairs={{0,2},{1,3},{2,0},{3,1},{4,6},{5,7},{6,4},{7,5},{8,10},{9,11},{10,... | collective-permute-start | bytes 3145736 | tf_op jit(solution)/shard_map/ppermute | solution.py:71
  823.9 57.7 %copy-start.118 = (bf16[1024,2048]{1,0:T(8,128)(2,1)S(1)}, bf16[1024,2048]{1,0:T(8,128)(2,1)}, u32[]{:S(2)}) copy-start(bf16[1024,2048]{1,0:T(8,128)(2,1)} %get-tuple-element.184) | copy-start | bytes 12582916
  825.5 56.2 %copy-start.71 = (bf16[1024,4,1,256]{0,3,2,1:T(8,128)(2,1)S(1)}, bf16[1024,4,1,256]{0,3,2,1:T(8,128)(2,1)}, u32[]{:S(2)}) copy-start(bf16[1024,4,1,256]{0,3,2,1:T(8,128)(2,1)} %copy-done.70) | copy-start | bytes 6291460
  828.0 94.3 %collective-permute-start.11 = (bf16[512,2048]{1,0:T(8,128)(2,1)}, bf16[512,2048]{1,0:T(8,128)(2,1)}, u32[]{:S(2)}, u32[]{:S(2)}) collective-permute-start(bf16[512,2048]{1,0:T(8,128)(2,1)} %pad_maximum_fusion.6), channel_id=1, source_target_pairs={{0,1},{1,0},{2,3},{3,2},{4,5},{5,4},{6,7},{7,6},{8,9},{9,8},{10,11... | collective-permute-start | bytes 6291464 | tf_op jit(solution)/shard_map/ppermute | solution.py:82
  913.9 17.5 %collective-permute-start.20 = (bf16[512,2048]{1,0:T(8,128)(2,1)}, bf16[512,2048]{1,0:T(8,128)(2,1)}, u32[]{:S(2)}, u32[]{:S(2)}) collective-permute-start(bf16[512,2048]{1,0:T(8,128)(2,1)} %dynamic-slice_bitcast_fusion), channel_id=1, source_target_pairs={{0,1},{1,0},{2,3},{3,2},{4,5},{5,4},{6,7},{7,6},{8,9},{9,8},{10,11... | collective-permute-start | bytes 6291464 | tf_op jit(solution)/shard_map/ppermute | solution.py:58
  937.7 25.6 %collective-permute-start.21 = (bf16[256,2048]{1,0:T(8,128)(2,1)}, bf16[256,2048]{1,0:T(8,128)(2,1)S(1)}, u32[]{:S(2)}, u32[]{:S(2)}) collective-permute-start(bf16[256,2048]{1,0:T(8,128)(2,1)} %fusion.106), channel_id=1, source_target_pairs={{0,2},{1,3},{2,0},{3,1},{4,6},{5,7},{6,4},{7,5},{8,10},{9,11},{10,... | collective-permute-start | bytes 3145736 | tf_op jit(solution)/shard_map/ppermute | solution.py:65
  974.2 5.7 collective-permute-start.24
  978.3 24.8 %collective-permute-start.22 = (bf16[256,2048]{1,0:T(8,128)(2,1)S(1)}, bf16[256,2048]{1,0:T(8,128)(2,1)}, u32[]{:S(2)}, u32[]{:S(2)}) collective-permute-start(bf16[256,2048]{1,0:T(8,128)(2,1)S(1)} %fusion.52), channel_id=1, source_target_pairs={{0,2},{1,3},{2,0},{3,1},{4,6},{5,7},{6,4},{7,5},{8,10},{9,11},{10,... | collective-permute-start | bytes 3145736 | tf_op jit(solution)/shard_map/ppermute | solution.py:71
  980.4 10.5 %collective-permute-start.25 = (bf16[15104]{0:T(1024)(128)(2,1)S(1)}, bf16[15104]{0:T(1024)(128)(2,1)S(1)}, u32[]{:S(2)}, u32[]{:S(2)}) collective-permute-start(bf16[15104]{0:T(1024)(128)(2,1)S(1)} %get-tuple-element.172), channel_id=1, source_target_pairs={{0,8},{4,12},{8,16},{12,20},{16,24},{20,28},{24,0},{28,4},{1,9},{5... | collective-permute-start | bytes 90632 | tf_op jit(solution)/shard_map/ppermute | solution.py:120
  983.3 7.7 collective-permute-start.26
  988.3 3.9 collective-permute-start.27
  992.2 13.7 %collective-permute-start.28 = (bf16[8704]{0:T(1024)(128)(2,1)S(1)}, bf16[8704]{0:T(1024)(128)(2,1)S(1)}, u32[]{:S(2)}, u32[]{:S(2)}) collective-permute-start(bf16[8704]{0:T(1024)(128)(2,1)S(1)} %slice.363), channel_id=1, source_target_pairs={{0,1},{1,0},{2,3},{3,2},{4,5},{5,4},{6,7},{7,6},{8,9},{9,8},{10,11... | collective-permute-start | bytes 52232 | tf_op jit(solution)/shard_map/ppermute | solution.py:87
  1005.9 23.9 %collective-permute-start.23 = (bf16[512,2048]{1,0:T(8,128)(2,1)}, bf16[512,2048]{1,0:T(8,128)(2,1)}, u32[]{:S(2)}, u32[]{:S(2)}) collective-permute-start(bf16[512,2048]{1,0:T(8,128)(2,1)} %pad_maximum_fusion.8), channel_id=1, source_target_pairs={{0,1},{1,0},{2,3},{3,2},{4,5},{5,4},{6,7},{7,6},{8,9},{9,8},{10,11... | collective-permute-start | bytes 6291464 | tf_op jit(solution)/shard_map/ppermute | solution.py:82
  1005.9 5.8 collective-permute-start.29
  (116 other events, 701.5 us)
Sparse Core Ops, SparseCore 0:
  618.0 29.9 reduce-scatter.7
  660.5 37.7 reduce-scatter.5
  700.7 75.7 reduce-scatter.13
  785.1 79.9 reduce-scatter.11
  889.9 80.4 reduce-scatter.9

commit v2 on v1

v2 whole, which is shorter than its diff:
```python
import jax
import jax.numpy as jnp
from jax import lax
from jax.experimental import pallas as pl
from jax.experimental.pallas import tpu as pltpu
from jax.sharding import PartitionSpec as P

WIN = 64
CHUNK = 128
ANY = pl.BlockSpec(memory_space=pl.ANY)
COST = pl.CostEstimate(flops=1, bytes_accessed=1, transcendentals=0)
EPSILON = 1e-05
EXACT = lax.Precision.HIGHEST
F32 = jnp.float32
BF16 = jnp.bfloat16


def dot(a, b, out=F32):
    return jnp.dot(a, b, preferred_element_type=F32).astype(out)


def dot_nt(a, b, out=F32):
    return lax.dot_general(a, b, (((1,), (1,)), ((), ())), preferred_element_type=F32).astype(out)


def dot_tn(a, b, out=F32):
    return lax.dot_general(a, b, (((0,), (0,)), ((), ())), preferred_element_type=F32).astype(out)


def dot_tt(a, b, out=F32):
    return lax.dot_general(a, b, (((0,), (1,)), ((), ())), preferred_element_type=F32).astype(out)


def tie(*xs):
    return lax.optimization_barrier(xs)


def add(terms):
    total = terms[0].astype(F32)
    for t in terms[1:]:
        total = total + t.astype(F32)
    return total


def take(x, i):
    return lax.dynamic_index_in_dim(x, i, 0, False)


class Grid:
    def __init__(self):
        self.kv = lax.axis_size("kv")
        self.seq = lax.axis_size("seq")
        self.outer = self.kv // 2
        self.line = self.seq // 2
        k = lax.axis_index("kv")
        s = lax.axis_index("seq")
        self.core, self.y = k % 2, k // 2
        self.x, self.z = s % 2, s // 2
        self.s = s
        self.core_swap = [(i, i ^ 1) for i in range(self.kv)]
        self.x_swap = [(i, i ^ 1) for i in range(self.seq)]
        self.z_groups = [[2 * z + x for z in range(self.line)] for x in range(2)]

    def y_shift(self, j):
        m = self.outer
        return [(y * 2 + c, (y + j) % m * 2 + c) for y in range(m) for c in range(2)]

    def own_rows(self, x, parts):
        rows, width = x.shape
        cut = x.reshape(parts, 2, rows // (2 * parts), width)
        return lax.dynamic_index_in_dim(cut, self.core, 1, False).reshape(rows // 2, width)

    def other_rows(self, x, parts):
        rows, width = x.shape
        cut = x.reshape(parts, 2, rows // (2 * parts), width)
        return lax.dynamic_index_in_dim(cut, 1 - self.core, 1, False).reshape(rows // 2, width)

    def across_cores(self, x):
        return lax.ppermute(x, "kv", self.core_swap)

    def core_sum(self, part, parts):
        got = self.across_cores(self.other_rows(part, parts))
        return (self.own_rows(part, parts).astype(F32) + got.astype(F32)).astype(BF16)

    def outer_terms(self, half):
        terms = [half] + [lax.ppermute(half, "kv", self.y_shift(j)) for j in range(1, self.outer)]
        if self.outer == 2:
            return terms
        stack = jnp.stack(terms)
        return [take(stack, (self.y - i) % self.outer) for i in range(self.outer)]

    def gather_rows(self, own, parts):
        other = self.across_cores(own)
        first = self.core == 0
        shape = (parts, 1, own.shape[0] // parts, own.shape[1])
        low = jnp.where(first, own, other).reshape(shape)
        high = jnp.where(first, other, own).reshape(shape)
        return jnp.concatenate([low, high], 1).reshape(2 * own.shape[0], own.shape[1])

    def sum_kv(self, x):
        x = x + lax.ppermute(x, "kv", self.core_swap).astype(F32)
        total = x
        for j in range(1, self.outer):
            total = total + lax.ppermute(x, "kv", self.y_shift(j))
        return total

    def line_scatter(self, part):
        return lax.psum_scatter(
            part, "seq", scatter_dimension=0, tiled=True, axis_index_groups=self.z_groups
        )

    def scatter_blocks(self, blocks):
        cut = blocks.reshape(self.line, 2, -1)
        other = lax.dynamic_index_in_dim(cut, 1 - self.x, 1, False).astype(BF16)
        own = lax.dynamic_index_in_dim(cut, self.x, 1, False)
        part = own + lax.ppermute(other, "seq", self.x_swap).astype(F32)
        total = take(part, self.z)
        m = self.line
        for j in range(1, m):
            pairs = [(z * 2 + x, (z + j) % m * 2 + x) for z in range(m) for x in range(2)]
            out = take(part, (self.z + j) % m).astype(BF16)
            total = total + lax.ppermute(out, "seq", pairs).astype(F32)
        return total

    def shift_seq(self, x, by):
        n = self.seq
        return lax.ppermute(x, "seq", [(i, i + by) for i in range(n) if 0 <= i + by < n])

    def sum_before(self, x, sign):
        near = self.shift_seq(x, sign)
        total = x + near
        by = 2
        while by < self.seq:
            total = total + self.shift_seq(total, sign * by)
            by *= 2
        return total - x, near


def softmax_pair(logits):
    top = jnp.exp(logits - jnp.max(logits, 0, keepdims=True))
    low = jnp.exp(jnp.min(logits, 0, keepdims=True) - logits)
    return top * (1.0 / jnp.sum(top, 0, keepdims=True)), low * (1.0 / jnp.sum(low, 0, keepdims=True))


def softmax_pair_back(p, n, grad):
    hd = p.shape[0]
    up, un = p * grad[:hd], n * grad[hd:]
    return up - p * jnp.sum(up, 0, keepdims=True) - (un - n * jnp.sum(un, 0, keepdims=True))


def halves(x):
    top = x.astype(BF16)
    return top, (x - top.astype(F32)).astype(BF16)


def dot2(x, b):
    top, rest = halves(x)
    return dot(top, b) + dot(rest, b)


def value_rows(v, keep):
    hd, n = v.shape
    ones = (lax.broadcasted_iota(jnp.int32, (hd, n), 0) == 0).astype(F32)
    return (jnp.concatenate([v.astype(F32), ones], 0) * keep).astype(BF16)


def key_kernel(kv_ref, map_ref, keep_ref, phi_cols_ref, phi_ref, k_ref, v_ref, state_ref):
    hk, hd = map_ref.shape[:2]
    for g in range(hk):
        k = kv_ref[g * hd : (g + 1) * hd, :]
        v = kv_ref[(hk + g) * hd : (hk + g + 1) * hd, :]
        p, n = softmax_pair(dot(map_ref[g], k))
        phi = jnp.concatenate([p, n], 0)
        phi_cols_ref[g] = phi.astype(BF16)
        phi_ref[g] = phi.T.astype(BF16)
        kv = jnp.concatenate([k, v], 0).astype(F32).T
        k_ref[g] = kv[:, :hd].astype(BF16)
        v_ref[g] = kv[:, hd:].astype(BF16)
        state_ref[g] = dot_nt(value_rows(v, keep_ref[...]), phi.astype(BF16))


def masks(open_ref, base):
    shape = (2 * CHUNK, CHUNK)
    a = lax.broadcasted_iota(jnp.int32, shape, 0)
    b = lax.broadcasted_iota(jnp.int32, shape, 1)
    start = open_ref[:, pl.ds(base, CHUNK)] - base
    doc = a >= start
    near = a > b + (CHUNK - WIN)
    return doc & near & (a <= b + CHUNK), doc & ~near, (start < 0).astype(F32)


def lanes(parts):
    return jnp.concatenate(parts, 1)


def attend_kernel(
    q_ref, kv_ref, phi_cols_ref, phi_ref, k_ref, map_ref, prior_ref, open_ref, keep_ref, cont_ref,
    heads_ref, total_ref, states_ref, state,
):
    hk, hd = phi_ref.shape[0], map_ref.shape[1]
    hq = map_ref.shape[0]
    group = hq // hk
    scale = hd**-0.5
    state[...] = prior_ref[...]

    def chunk(i, _):
        base = pl.multiple_of(i * CHUNK, CHUNK)
        here = pl.ds(base, CHUNK)
        keys = pl.ds(base, 2 * CHUNK)
        win, lin, far = masks(open_ref, base)
        for g in range(hk):
            q = [q_ref[h * hd : (h + 1) * hd, here] for h in range(g * group, (g + 1) * group)]
            phi = []
            for j in range(group):
                p, n = softmax_pair(dot(map_ref[g * group + j], q[j]))
                phi.append(jnp.concatenate([p, n], 0).astype(BF16))
            phi4 = lanes(phi)
            past = state[g]
            states_ref[i, g] = past
            scores = dot(k_ref[g, keys, :], lanes(q)) * scale
            linear = dot(phi_ref[g, keys, :], phi4)
            carried = dot2(past[: hd + 8], phi4)
            weights = []
            totals = []
            for j in range(group):
                cut = slice(j * CHUNK, (j + 1) * CHUNK)
                w = jnp.where(win, jnp.exp(scores[:, cut]), 0.0) + jnp.where(lin, linear[:, cut], 0.0)
                weights.append(w.astype(BF16))
                totals.append(jnp.sum(w, 0, keepdims=True) + far * carried[hd : hd + 1, cut])
            v = kv_ref[(hk + g) * hd : (hk + g + 1) * hd, keys]
            mixed = dot(v, lanes(weights))
            for j in range(group):
                cut = slice(j * CHUNK, (j + 1) * CHUNK)
                h = g * group + j
                out = (mixed[:, cut] + far * carried[:hd, cut]) * (1.0 / totals[j])
                heads_ref[h * hd : (h + 1) * hd, here] = out.astype(BF16)
                total_ref[h : h + 1, here] = totals[j]
            own = value_rows(kv_ref[(hk + g) * hd : (hk + g + 1) * hd, here], keep_ref[:, here])
            state[g] = cont_ref[i] * past + dot_nt(own, phi_cols_ref[g, :, here])
        return 0

    lax.fori_loop(0, heads_ref.shape[1] // CHUNK, chunk, 0)


def attend_back_kernel(
    q_ref, kv_ref, phi_cols_ref, phi_ref, k_ref, v_ref, map_ref, map_t_ref, states_ref, heads_ref,
    total_ref, g_ref, open_ref, keep_ref, cont_ref,
    gq_ref, feat_ref, gk_ref, gv_ref, gphi_ref, first_ref, gl_ref, grad_t,
):
    hk, hd = phi_ref.shape[0], map_ref.shape[1]
    hq = map_ref.shape[0]
    group = hq // hk
    scale = hd**-0.5
    count = heads_ref.shape[1] // CHUNK
    first_ref[...] = jnp.zeros_like(first_ref)
    grad_t[...] = jnp.zeros_like(grad_t)
    gk_ref[...] = jnp.zeros_like(gk_ref)
    gv_ref[...] = jnp.zeros_like(gv_ref)
    gphi_ref[...] = jnp.zeros_like(gphi_ref)

    def chunk(step, _):
        i = count - 1 - step
        base = pl.multiple_of(i * CHUNK, CHUNK)
        here = pl.ds(base, CHUNK)
        keys = pl.ds(base, 2 * CHUNK)
        win, lin, far = masks(open_ref, base)
        for g in range(hk):
            rows = [slice(h * hd, (h + 1) * hd) for h in range(g * group, (g + 1) * group)]
            key_rows = slice(g * hd, (g + 1) * hd)
            value_row = slice((hk + g) * hd, (hk + g + 1) * hd)
            q4 = lanes([q_ref[r, here] for r in rows])
            g4 = lanes([g_ref[r, here] for r in rows])
            pairs = [softmax_pair(dot(map_ref[g * group + j], q_ref[rows[j], here])) for j in range(group)]
            phi = [jnp.concatenate([p, n], 0) for p, n in pairs]
            phi4 = lanes([x.astype(BF16) for x in phi])
            scores = dot(k_ref[g, keys, :], q4) * scale
            linear = dot(phi_ref[g, keys, :], phi4)
            g_w = dot(v_ref[g, keys, :], g4)
            shares, g_scores, g_linear, g_ext = [], [], [], []
            for j in range(group):
                cut = slice(j * CHUNK, (j + 1) * CHUNK)
                h = g * group + j
                inv = 1.0 / total_ref[h : h + 1, here]
                g_here = g_ref[rows[j], here].astype(F32)
                g_total = -inv * jnp.sum(g_here * heads_ref[rows[j], here].astype(F32), 0, keepdims=True)
                ex = jnp.where(win, jnp.exp(scores[:, cut]), 0.0)
                w = ex + jnp.where(lin, linear[:, cut], 0.0)
                shares.append((w * inv).astype(BF16))
                g_weight = g_w[:, cut] * inv + g_total
                g_scores.append((g_weight * ex).astype(BF16))
                g_linear.append(jnp.where(lin, g_weight, 0.0).astype(BF16))
                row = lax.broadcasted_iota(jnp.int32, (hd, CHUNK), 0) == 0
                g_ext.append(
                    (jnp.concatenate([g_here * inv, jnp.where(row, g_total, 0.0)], 0) * far).astype(BF16)
                )
            shares, g_scores, g_linear, g_ext = map(lanes, (shares, g_scores, g_linear, g_ext))
            gv_ref[key_rows, keys] += dot_nt(g4, shares)
            gk_ref[key_rows, keys] += dot_nt(q4, g_scores) * scale
            gphi_ref[g, :, keys] += dot_nt(phi4, g_linear)
            g_query = dot(kv_ref[key_rows, keys], g_scores) * scale
            past = states_ref[i, g].T
            g_phi = dot(phi_cols_ref[g, :, keys], g_linear) + dot2(past, g_ext)
            for j in range(group):
                cut = slice(j * CHUNK, (j + 1) * CHUNK)
                gl = softmax_pair_back(*pairs[j], g_phi[:, cut]).astype(BF16)
                gl_ref[rows[j], here] = gl
                gq = g_query[:, cut] + dot(map_t_ref[g * group + j], gl)
                gq_ref[rows[j], here] = gq.astype(BF16)
            keep = keep_ref[:, here]
            own = value_rows(kv_ref[value_row, here], keep)
            gphi_ref[g, :, here] += dot2(grad_t[g], own)
            gv_ref[key_rows, here] += dot2(first_ref[g, :hd, :], phi_cols_ref[g, :, here]) * keep
            cont = cont_ref[i]
            first_ref[g] = cont * first_ref[g] + dot_nt(g_ext, phi4)
            grad_t[g] = cont * grad_t[g] + dot_nt(phi4, g_ext)
        return 0

    lax.fori_loop(0, count, chunk, 0)
    for h in range(hq):
        r = slice(h * hd, (h + 1) * hd)
        feat_ref[h] = dot_nt(q_ref[r, :], gl_ref[r, :])


def key_back_kernel(
    kv_ref, phi_cols_ref, map_ref, map_t_ref, gk_ref, gv_ref, gphi_ref, edge_ref, later_ref, last_ref,
    keep_ref, g_ref, feat_ref,
):
    hk, hd = map_ref.shape[:2]
    n = kv_ref.shape[1]
    cut = n - CHUNK

    def joined(own, edge):
        return jnp.concatenate([own[:, : cut - CHUNK], own[:, cut - CHUNK :] + edge.astype(F32)], 1)

    for g in range(hk):
        key_rows = slice(g * hd, (g + 1) * hd)
        k = kv_ref[key_rows, CHUNK:]
        v = kv_ref[(hk + g) * hd : (hk + g + 1) * hd, CHUNK:]
        keep = keep_ref[:, CHUNK:]
        phi = phi_cols_ref[g, :, CHUNK:]
        own = value_rows(v, keep)
        one = value_rows(v[:, cut - CHUNK :], jnp.ones((1, CHUNK), F32))
        later, last = later_ref[g], last_ref[g]
        g_phi = gphi_ref[g, :, CHUNK:] + lanes(
            [dot2(later.T, own[:, : cut - CHUNK]), dot2(last.T, one)]
        )
        g_phi = joined(g_phi, edge_ref[2 * hk * hd + g * 2 * hd : 2 * hk * hd + (g + 1) * 2 * hd, :])
        g_v = gv_ref[key_rows, CHUNK:] + lanes(
            [
                dot2(later[:hd], phi[:, : cut - CHUNK]) * keep[:, : cut - CHUNK],
                dot2(last[:hd], phi[:, cut - CHUNK :]),
            ]
        )
        g_v = joined(g_v, edge_ref[(hk + g) * hd : (hk + g + 1) * hd, :])
        g_ref[(hk + g) * hd : (hk + g + 1) * hd, :] = g_v.astype(BF16)
        p, q = softmax_pair(dot(map_ref[g], k))
        gl = softmax_pair_back(p, q, g_phi).astype(BF16)
        g_k = joined(gk_ref[key_rows, CHUNK:], edge_ref[key_rows, :]) + dot(map_t_ref[g], gl)
        g_ref[key_rows, :] = g_k.astype(BF16)
        feat_ref[g] = dot_nt(k, gl)


def call(kernel, outs, args, scratch=(), smem=(), after=()):
    count = len(args)
    vmem = pl.BlockSpec(memory_space=pltpu.VMEM)
    specs = [pl.BlockSpec(memory_space=pltpu.SMEM) if i in smem else vmem for i in range(len(args))]
    return pl.pallas_call(
        lambda *refs: kernel(*refs[:count], *refs[count + len(after) :]),
        out_shape=[jax.ShapeDtypeStruct(s, d) for s, d in outs],
        in_specs=specs + [ANY] * len(after),
        out_specs=[vmem] * len(outs),
        scratch_shapes=[pltpu.VMEM(s, d) for s, d in scratch],
        compiler_params=pltpu.CompilerParams(vmem_limit_bytes=48 * 2**20),
        cost_estimate=COST,
    )(*args, *after)


def project_kernel(
    x_ref, gain_ref, wq_ref, wk_ref, wv_ref, down_ref, up_ref, normed_ref, q_ref, kv_ref, low_ref
):
    x = x_ref[...].astype(F32)
    rms = lax.rsqrt(jnp.mean(x * x, -1, keepdims=True) + EPSILON)
    normed = (x * rms * gain_ref[...].astype(F32)).astype(BF16)
    normed_ref[...] = normed
    low, rest = halves(dot(normed, down_ref[...]))
    low_ref[...] = low
    qw, kw = wq_ref.shape[1], wk_ref.shape[1]

    def rows(weight, at, width):
        up = up_ref[:, at : at + width]
        return (dot(normed, weight[...]) + dot(low, up) + dot(rest, up)).T.astype(BF16)

    kv_ref[:kw, :] = rows(wk_ref, qw, kw)
    kv_ref[kw:, :] = rows(wv_ref, qw + kw, kw)
    q_ref[...] = rows(wq_ref, 0, qw)


def project(tokens, gain, wq, wk, wv, down, up, tile=256):
    t, d = tokens.shape
    qw, kw = wq.shape[1], wk.shape[1]
    whole = lambda a: pl.BlockSpec(a.shape, lambda i: (0,) * a.ndim)
    row = lambda w: pl.BlockSpec((tile, w), lambda i: (i, 0))
    col = lambda h: pl.BlockSpec((h, tile), lambda i: (0, i))
    gain = gain[None]
    return pl.pallas_call(
        project_kernel,
        grid=(t // tile,),
        in_specs=[row(d)] + [whole(a) for a in (gain, wq, wk, wv, down, up)],
        out_specs=[row(d), col(qw), col(2 * kw), row(down.shape[1])],
        out_shape=[
            jax.ShapeDtypeStruct((t, d), BF16),
            jax.ShapeDtypeStruct((qw, t), BF16),
            jax.ShapeDtypeStruct((2 * kw, t), BF16),
            jax.ShapeDtypeStruct((t, down.shape[1]), BF16),
        ],
        compiler_params=pltpu.CompilerParams(vmem_limit_bytes=48 * 2**20),
        cost_estimate=COST,
    )(tokens, gain, wq, wk, wv, down, up)


def matmul_kernel(product, pairs, out_ref):
    sub = min(256, out_ref.shape[0])
    for r in range(0, out_ref.shape[0], sub):
        total = None
        for a_ref, b_ref in pairs:
            term = product(a_ref[r : r + sub, :], b_ref[...])
            total = term if total is None else total + term
        out_ref[r : r + sub, :] = total.astype(out_ref.dtype)


def matmul(pairs, transposed, out, tile=512, after=()):
    rows = pairs[0][0].shape[0]
    width = pairs[0][1].shape[0 if transposed else 1]
    product = dot_nt if transposed else dot
    specs, args = [], []
    for a, b in pairs:
        specs.append(pl.BlockSpec(a.shape, lambda i: (0, 0)))
        if transposed:
            specs.append(pl.BlockSpec((tile, b.shape[1]), lambda i: (i, 0)))
        else:
            specs.append(pl.BlockSpec((b.shape[0], tile), lambda i: (0, i)))
        args += [a, b]

    def kernel(*refs):
        used = refs[: 2 * len(pairs)]
        matmul_kernel(product, list(zip(used[::2], used[1::2])), refs[-1])

    return pl.pallas_call(
        kernel,
        grid=(width // tile,),
        in_specs=specs + [ANY] * len(after),
        out_specs=pl.BlockSpec((rows, tile), lambda i: (0, i)),
        out_shape=jax.ShapeDtypeStruct((rows, width), out),
        compiler_params=pltpu.CompilerParams(vmem_limit_bytes=56 * 2**20),
        cost_estimate=COST,
    )(*args, *after)


def grad_block(line, select, a, b, product, piece=(0, 1), got=None, after=()):
    rows, width = a.shape
    block = width // (2 * line)
    if product is dot_tt:
        n = b.shape[0]
        b_spec = pl.BlockSpec(b.shape, lambda j, s: (0, 0))
    else:
        n = b.shape[1] // piece[1]
        b_spec = pl.BlockSpec((rows, n), lambda j, s: (0, piece[0]))

    def kernel(sel_ref, a_ref, b_ref, *refs):
        value = product(a_ref[...], b_ref[...])
        if got is not None:
            value = value + refs[0][...].astype(F32)
        refs[-1][...] = value.astype(BF16)

    spec = pl.BlockSpec((block, n), lambda j, s: (j, 0))
    more = [] if got is None else [got]
    return pl.pallas_call(
        kernel,
        grid_spec=pltpu.PrefetchScalarGridSpec(
            num_scalar_prefetch=1,
            grid=(line,),
            in_specs=[
                pl.BlockSpec((rows, block), lambda j, s: (0, 2 * j + s[0])),
                b_spec,
            ]
            + [spec] * len(more)
            + [ANY] * len(after),
            out_specs=spec,
        ),
        out_shape=jax.ShapeDtypeStruct((line * block, n), BF16),
        compiler_params=pltpu.CompilerParams(vmem_limit_bytes=48 * 2**20),
        cost_estimate=COST,
    )(select, a, b, *more, *after)


def gated_kernel(core_ref, own_ref, other_ref, wg_ref, wu_ref, gh_ref, *refs):
    normed_ref, hidden_ref, gate_ref, up_ref = refs[-4:]
    half = own_ref.shape[0]

    @pl.when(pl.program_id(0) == 0)
    def _():
        first = core_ref[0] == 0

        @pl.when(first)
        def _():
            normed_ref[:half, :] = own_ref[...]
            normed_ref[half:, :] = other_ref[...]

        @pl.when(jnp.logical_not(first))
        def _():
            normed_ref[:half, :] = other_ref[...]
            normed_ref[half:, :] = own_ref[...]

    for r in range(0, 2 * half, half):
        cut = slice(r, r + half)
        x = normed_ref[cut, :]
        gate = dot(x, wg_ref[...])
        up = dot(x, wu_ref[...])
        sig = 1.0 / (1.0 + jnp.exp(-gate))
        silu = gate * sig
        hidden_ref[cut, :] = (silu * up).astype(BF16)
        g = gh_ref[cut, :].astype(F32)
        gate_ref[cut, :] = (g * up * (sig + silu * (1.0 - sig))).astype(BF16)
        up_ref[cut, :] = (g * silu).astype(BF16)


def gated(c, rows, core, own, other, wg, wu, gh, held, tile=512):
    half, d = own.shape
    f = wg.shape[1]
    here = pl.BlockSpec((2 * half, tile), lambda i, s: (c, i))
    part = pl.BlockSpec((2 * half, tile), lambda i, s: (0, i))
    held_specs = [pl.BlockSpec(memory_space=pl.ANY)] * len(held)
    shapes = [jax.ShapeDtypeStruct((rows, d), BF16)] + [jax.ShapeDtypeStruct((rows, f), BF16)] * 3
    return pl.pallas_call(
        gated_kernel,
        grid_spec=pltpu.PrefetchScalarGridSpec(
            num_scalar_prefetch=1,
            grid=(f // tile,),
            in_specs=[
                pl.BlockSpec((half, d), lambda i, s: (0, 0)),
                pl.BlockSpec((half, d), lambda i, s: (0, 0)),
                pl.BlockSpec((d, tile), lambda i, s: (0, i)),
                pl.BlockSpec((d, tile), lambda i, s: (0, i)),
                part,
            ]
            + held_specs,
            out_specs=[pl.BlockSpec((2 * half, d), lambda i, s: (c, 0)), here, here, here],
        ),
        out_shape=shapes,
        input_output_aliases={6 + i: i for i in range(len(held))},
        compiler_params=pltpu.CompilerParams(vmem_limit_bytes=56 * 2**20),
        cost_estimate=COST,
    )(core, own, other, wg, wu, gh, *held)


def local(
    tokens,
    gain_one,
    query_weight,
    key_weight,
    value_weight,
    query_down,
    query_up,
    key_down,
    key_up,
    value_down,
    value_up,
    query_map,
    key_map,
    output_weight,
    output_down,
    output_up,
    gain_two,
    gate_weight,
    up_weight,
    down_weight,
    start_mask,
    cotangent,
):
    grid = Grid()
    rows = tokens.shape[0]
    rank = query_down.shape[1]
    hd = key_map.shape[-1]
    hk = key_map.shape[0]
    hq = query_map.shape[0]
    group = hq // hk
    count = rows // CHUNK
    length = rows + CHUNK
    index = jnp.arange(rows, dtype=jnp.int32)
    starts = jnp.where(start_mask == 1, index + CHUNK, jnp.int32(-1))
    opened = jnp.max(jnp.where(index[:, None] <= index[None, :], starts[:, None], jnp.int32(-1)), 0)
    ends = jnp.concatenate([jnp.full((1,), -1, jnp.int32), opened[CHUNK - 1 : -1 : CHUNK]])
    cont = (ends < jnp.arange(count, dtype=jnp.int32) * CHUNK).astype(F32)
    place = jnp.arange(length, dtype=jnp.int32)
    ends_at = jnp.concatenate([jnp.repeat(ends, CHUNK), jnp.full((CHUNK,), length, jnp.int32)])
    keep = (place >= ends_at).astype(F32)[None]
    keep_all = ((place >= ends[count - 1]) & (place < rows)).astype(F32)[None]
    opened = opened[None]

    g1 = gain_one.astype(F32)
    g2 = gain_two.astype(F32)
    qup, kup, vup = (u.reshape(rank, -1) for u in (query_up, key_up, value_up))
    qw, kw = hq * hd, hk * hd
    wide = 128 - 3 * rank
    up_all = jnp.pad(jax.scipy.linalg.block_diag(qup, kup, vup), ((0, wide), (0, 0)))
    down_all = jnp.pad(jnp.concatenate([query_down, key_down, value_down], 1), ((0, 0), (0, wide)))
    normed_one, query, kv, low_all = project(
        tokens, gain_one, query_weight, key_weight, value_weight, down_all, up_all
    )
    edge = grid.shift_seq(kv[:, rows - CHUNK :], 1)
    kv = jnp.concatenate([edge, kv], 1)

    query_map_t = jnp.swapaxes(query_map, 1, 2)
    key_map_t = jnp.swapaxes(key_map, 1, 2)
    phi_dim = 2 * hd
    phi_cols, phi, key, value, state = call(
        key_kernel,
        [
            ((hk, phi_dim, length), BF16),
            ((hk, length, phi_dim), BF16),
            ((hk, length, hd), BF16),
            ((hk, length, hd), BF16),
            ((hk, phi_dim, phi_dim), F32),
        ],
        (kv, key_map_t, keep_all),
    )
    prior, _ = grid.sum_before(state, 1)
    parts = 2
    chunk = rows // parts
    g_hidden = matmul([(cotangent[:chunk], down_weight)], True, F32)
    oup = output_up
    odown = output_down.reshape(-1, rank)
    weight_o = (output_weight.astype(F32) + dot(odown, oup)).astype(BF16)
    prior, g_hidden, weight_o = tie(prior, g_hidden, weight_o)
    heads, totals, states = call(
        attend_kernel,
        [((qw, rows), BF16), ((hq, rows), F32), ((count, hk, phi_dim, phi_dim), F32)],
        (query, kv, phi_cols, phi, key, query_map_t, prior, opened, keep, cont),
        scratch=[((hk, phi_dim, phi_dim), F32)],
        smem=(9,),
    )

    part = [dot_tn(heads[:, c * chunk : (c + 1) * chunk], weight_o, BF16) for c in range(parts)]
    half = [grid.core_sum(p, 1) for p in part]
    own_tokens = [grid.own_rows(tokens[c * chunk : (c + 1) * chunk], 1) for c in range(parts)]
    own_tokens[0], half[1] = tie(own_tokens[0], half[1])
    terms = [grid.outer_terms(h) for h in half]
    held = ()
    resid, rms_two = [], []
    for c in range(parts):
        if c:
            held = list(held)
            terms[c][-1], held[0] = tie(terms[c][-1], held[0])
        r = own_tokens[c].astype(F32) + add(terms[c])
        rms = lax.rsqrt(jnp.mean(r * r, -1, keepdims=True) + EPSILON)
        own = (r * rms * g2).astype(BF16)
        core = grid.core.astype(jnp.int32)[None]
        if c:
            g_hidden = g_rest
        else:
            g_rest = matmul([(cotangent[chunk:], down_weight)], True, F32, after=[own])
        held = gated(
            c, rows, core, own, grid.across_cores(own), gate_weight, up_weight, g_hidden, held
        )
        resid.append(r)
        rms_two.append(rms)
    normed_two, hidden, g_gate, g_up = held
    resid = jnp.concatenate(resid, 0)
    rms_two = jnp.concatenate(rms_two, 0)

    mine = grid.x.astype(jnp.int32)[None]
    yours = 1 - mine

    early, late = (0, 2), (1, 2)

    def to_pair(a, b, product=dot_tn, piece=(0, 1), after=()):
        return grad_block(grid.line, yours, a, b, product, piece, None, after)

    def from_pair(a, b, got, product=dot_tn, piece=(0, 1), after=()):
        return grad_block(grid.line, mine, a, b, product, piece, got, after)

    def swap(x):
        return lax.ppermute(x, "seq", grid.x_swap)

    s_d0 = to_pair(cotangent, hidden, dot_tn, early)
    s_d1 = to_pair(cotangent, hidden, dot_tn, late, [s_d0])
    r_d0, r_d1 = swap(s_d0), swap(s_d1)
    g_two = matmul([(g_gate, gate_weight), (g_up, up_weight)], True, BF16, after=[s_d1])
    half = grid.core_sum(g_two, parts)
    terms = grid.outer_terms(half)
    s_g0 = to_pair(normed_two, g_gate, dot_tn, early, [g_two])
    s_g1 = to_pair(normed_two, g_gate, dot_tn, late, [s_g0])
    r_g0, r_g1 = swap(s_g0), swap(s_g1)
    k_d0 = from_pair(cotangent, hidden, r_d0, dot_tn, early, [s_g1])
    grad_d0 = grid.line_scatter(k_d0)
    s_u0 = to_pair(normed_two, g_up, dot_tn, early, [k_d0])
    s_u1 = to_pair(normed_two, g_up, dot_tn, late, [s_u0])
    r_u0, r_u1 = swap(s_u0), swap(s_u1)
    down = matmul([(hidden, down_weight)], False, BF16, after=[s_u1])
    terms[-1], down = tie(terms[-1], down)

    g_two = add(terms)
    norm2_part = jnp.sum(g_two * resid * rms_two, 0)
    s_two = g_two * g2
    g_resid = (
        grid.own_rows(cotangent, parts).astype(F32)
        + rms_two * s_two
        - resid * rms_two**3 * jnp.mean(resid * s_two, -1, keepdims=True)
    )
    own_attn = g_resid.astype(BF16)
    g_attn = grid.gather_rows(own_attn, parts)
    k_d1 = from_pair(cotangent, hidden, r_d1, dot_tn, late, [own_attn])
    grad_d1 = grid.line_scatter(k_d1)
    half = grid.core_sum(down, parts)
    down_terms = grid.outer_terms(half)
    weight_qkv = jnp.concatenate([query_weight, key_weight, value_weight], 1)
    weight_qkv = (weight_qkv.astype(F32) + dot(down_all, up_all)).astype(BF16)
    g_attn, weight_qkv = tie(g_attn, weight_qkv)

    g_heads = dot_nt(weight_o, g_attn, BF16)
    g_q, featq_part, gk, gv, gphi, first = call(
        attend_back_kernel,
        [
            ((qw, rows), BF16),
            ((hq, hd, hd), F32),
            ((kw, length), F32),
            ((kw, length), F32),
            ((hk, phi_dim, length), F32),
            ((hk, phi_dim, phi_dim), F32),
        ],
        (
            query, kv, phi_cols, phi, key, value, query_map_t, query_map, states, heads,
            totals, g_heads, opened, keep, cont,
        ),
        scratch=[((qw, rows), BF16), ((hk, phi_dim, phi_dim), F32)],
        smem=(14,),
        after=[half, k_d1],
    )
    later, near = grid.sum_before(first, -1)
    back = [gk[:, :CHUNK], gv[:, :CHUNK], gphi[:, :, :CHUNK].reshape(hk * phi_dim, CHUNK)]
    back = grid.shift_seq(jnp.concatenate(back, 0).astype(BF16), -1)
    s_o = to_pair(g_attn, heads, dot_tt, after=[g_q])
    r_o = swap(s_o)
    k_g0 = from_pair(normed_two, g_gate, r_g0, dot_tn, early, [s_o, grad_d0])
    grad_g0 = grid.line_scatter(k_g0)
    g_kv, featk_part = call(
        key_back_kernel,
        [((2 * kw, rows), BF16), ((hk, hd, hd), F32)],
        (kv, phi_cols, key_map_t, key_map, gk, gv, gphi, back, later, later - near, keep_all),
        after=[k_g0],
    )

    g_qkv = jnp.concatenate([g_q, g_kv], 0)
    g_one = dot_tt(g_qkv, weight_qkv, BF16)
    terms = grid.outer_terms(grid.core_sum(g_one, parts))
    s_qkv = to_pair(normed_one, g_qkv, dot_tt, after=[g_one])
    k_g1 = from_pair(normed_two, g_gate, r_g1, dot_tn, late, [s_qkv, grad_d1])
    grad_g1 = grid.line_scatter(k_g1)
    g_low = dot(up_all, g_qkv, BF16)
    a_part = dot(g_low, normed_one)
    b_part = dot_tt(low_all, g_qkv)
    bq_part = b_part[:rank, :qw]
    bk_part = b_part[rank : 2 * rank, qw : qw + kw]
    bv_part = b_part[2 * rank : 3 * rank, qw + kw :]
    g_low_o = dot_nt(g_attn, oup, BF16)
    low_o = dot_tn(odown, heads, BF16)
    bo_part = dot(low_o, g_attn)
    ao_part = dot(heads, g_low_o)
    down_terms[-1], s_qkv = tie(down_terms[-1], s_qkv)
    r_qkv = swap(s_qkv)
    output = grid.gather_rows((resid + add(down_terms)).astype(BF16), parts)
    terms[-1], k_g1, a_part, b_part, bo_part, ao_part, output = tie(
        terms[-1], k_g1, a_part, b_part, bo_part, ao_part, output
    )

    stream = grid.own_rows(tokens, parts).astype(F32)
    rms_one = lax.rsqrt(jnp.mean(stream * stream, -1, keepdims=True) + EPSILON)
    g_one = add(terms)
    norm1_part = jnp.sum(g_one * stream * rms_one, 0)
    s_one = g_one * g1
    own_grad = (
        g_resid
        + rms_one * s_one
        - stream * rms_one**3 * jnp.mean(stream * s_one, -1, keepdims=True)
    ).astype(BF16)
    grad_tokens = grid.gather_rows(own_grad, parts).astype(F32)
    k_u0 = from_pair(normed_two, g_up, r_u0, dot_tn, early, [own_grad, grad_g0])
    grad_u0 = grid.line_scatter(k_u0)
    k_u1 = from_pair(normed_two, g_up, r_u1, dot_tn, late, [k_u0, grad_g1])
    grad_u1 = grid.line_scatter(k_u1)
    k_o = from_pair(g_attn, heads, r_o, dot_tt, after=[k_u1, grad_u0])
    grad_wo = grid.line_scatter(k_o).astype(F32)
    k_qkv = from_pair(normed_one, g_qkv, r_qkv, dot_tt, after=[k_o])
    grad_qkv = grid.line_scatter(k_qkv).astype(F32)
    grad_gate = jnp.concatenate([grad_g0, grad_g1], 1).astype(F32)
    grad_up = jnp.concatenate([grad_u0, grad_u1], 1).astype(F32)
    grad_down = jnp.concatenate([grad_d0.T, grad_d1.T], 0).astype(F32)

    n = grid.seq

    def blocks(x, dim):
        shape = x.shape
        x = x.reshape(shape[:dim] + (n, shape[dim] // n) + shape[dim + 1 :])
        return jnp.moveaxis(x, dim, 0).reshape(n, -1)

    norm_parts = [p * (1.0 / grid.outer) for p in (norm1_part, norm2_part)]
    both = [(norm_parts[0], 0), (norm_parts[1], 0), (a_part[: 3 * rank], 1), (bo_part, 1)]
    own = [
        (bq_part.reshape(query_up.shape), 2),
        (bk_part.reshape(key_up.shape), 2),
        (bv_part.reshape(value_up.shape), 2),
        (featq_part, 1),
        (featk_part, 1),
        (ao_part.reshape(output_down.shape), 1),
    ]
    cut = [blocks(x, d) for x, d in both + own]
    summed = grid.scatter_blocks(jnp.concatenate(cut, 1))
    n_both = sum(c.shape[1] for c in cut[: len(both)])
    flat = jnp.concatenate([grid.sum_kv(summed[:n_both].astype(BF16)), summed[n_both:]])
    done = []
    at = 0
    for x, d in both + own:
        shape = list(x.shape)
        shape[d] //= n
        size = x.size // n
        done.append(flat[at : at + size].reshape(shape))
        at += size
    norm1, norm2, grad_a, grad_bo, bq, bk, bv, featq, featk, grad_ao = done
    return (
        output,
        grad_tokens,
        norm1,
        grad_qkv[:, :qw],
        grad_qkv[:, qw : qw + kw],
        grad_qkv[:, qw + kw :],
        grad_a[:rank].T,
        bq,
        grad_a[rank : 2 * rank].T,
        bk,
        grad_a[2 * rank :].T,
        bv,
        featq,
        featk,
        grad_wo.T,
        grad_ao,
        grad_bo,
        norm2,
        grad_gate,
        grad_up,
        grad_down,
    )


def solution(mesh):
    placed = (
        P("seq", None),
        P(),
        P(None, "kv"),
        P(None, "kv"),
        P(None, "kv"),
        P(),
        P(None, "kv", None),
        P(),
        P(None, "kv", None),
        P(),
        P(None, "kv", None),
        P("kv", None, None),
        P("kv", None, None),
        P("kv", None),
        P("kv", None, None),
        P(),
        P(),
        P(None, "kv"),
        P(None, "kv"),
        P("kv", None),
        P("seq"),
        P("seq", None),
    )
    return jax.shard_map(
        local,
        mesh=mesh,
        in_specs=placed,
        out_specs=(
            P("seq", None),
            P("seq", None),
            P("seq"),
            P("seq", "kv"),
            P("seq", "kv"),
            P("seq", "kv"),
            P("seq", None),
            P(None, "kv", "seq"),
            P("seq", None),
            P(None, "kv", "seq"),
            P("seq", None),
            P(None, "kv", "seq"),
            P("kv", "seq", None),
            P("kv", "seq", None),
            P("kv", "seq"),
            P("kv", "seq", None),
            P(None, "seq"),
            P("seq"),
            P("seq", "kv"),
            P("seq", "kv"),
            P("kv", "seq"),
        ),
        check_vma=False,
    )
```

time: 1050 us -> 714 us (0.68)
  matrix products: 356 us -> 31.5 us
  Pallas kernels: 0 us -> 218 us
  waiting for transfers between devices: 334 us -> 222 us
  other arithmetic: 147 us -> 61.3 us
  local copies, waits for them, and re-layouts: 134 us -> 101 us
    pallas_call x0 -> x27, Pallas kernels: none -> 218 us  [the longest x16 84.4 us: grad_block(): pl.pallas_call(kernel, grid_spec=pltpu.PrefetchScalarGridSpec(num_scalar_...]
    ppermute x21 -> x23, waiting for transfers between devices: 331 us -> 130 us  [the longest x5 73.9 us: outer_terms(): lax.ppermute(half, 'kv', self.y_shift(j))]
    dot_general x21 -> x2, matrix products: 160 us -> 5.12 us  [dot_tt(): lax.dot_general(a, b, (((0,), (1,)), ((), ())), preferred_element_type=F32)]
    dot_general x16 -> x2, matrix products: 73 us -> 4.3 us  [dot_tn(): lax.dot_general(a, b, (((0,), (0,)), ((), ())), preferred_element_type=F32)]
    dot_general x8 -> x1, matrix products: 52.9 us -> 3.34 us  [dot_nt(): lax.dot_general(a, b, (((1,), (1,)), ((), ())), preferred_element_type=F32)]
    dot_general x11 -> x5, matrix products: 61.5 us -> 18.8 us  [dot(): return jnp.dot(a, b, preferred_element_type=F32).astype(out)]
    ppermute x8, waiting for transfers between devices: 2.47 us -> 41.3 us  [shift_seq(): lax.ppermute(x, 'seq', [(i, i + by) for i in range(n) if 0 <= i + by < n])]
    convert_element_type x15 -> x16, other arithmetic: 69.3 us -> 38.9 us  [the longest x5 16.4 us: core_sum(): (self.own_rows(part, parts).astype(F32) + got.astype(F32)).astype(BF16)]
  transfers between devices with their start and end apart: 40 -> 45, of which waited for: 16 -> 16; matrix products, arithmetic and copies ran while one was open for 44% -> 20% of each run, Pallas kernels for 0% -> 24%
where the time goes in v2:
time: 714 us; the launch traced here: 707 us
  waiting for transfers between devices  222 us (31%)
  Pallas kernels  218 us (31%)
  local copies, waits for them, and re-layouts  101 us (14%)
  other arithmetic  61.3 us (9%)
  starting transfers between devices  57.9 us (8%)
  matrix products  31.5 us (4%)
  between operations  16.1 us (2%)
    pallas_call x16, Pallas kernels, grad_block(): pl.pallas_call(kernel, grid_spec=pltpu.PrefetchScalarGridSpec(num_scalar_...  84.4 us
    ppermute x5, waiting for transfers between devices, outer_terms(): lax.ppermute(half, 'kv', self.y_shift(j))  73.9 us
    pallas_call x4, Pallas kernels, matmul(): pl.pallas_call(kernel, grid=(width // tile,), in_specs=specs + [ANY] * le...  55.4 us
    ppermute x8, waiting for transfers between devices, swap(): return lax.ppermute(x, 'seq', grid.x_swap)  55.1 us
    unnamed x226, local copies, waits for them, and re-layouts  50 us
    ppermute x8, waiting for transfers between devices, shift_seq(): lax.ppermute(x, 'seq', [(i, i + by) for i in range(n) if 0 <= i + by < n])  41.3 us
    pallas_call x4, Pallas kernels, call(): pl.pallas_call(lambda *refs: kernel(*refs[:count], *refs[count + len(afte...  35.8 us
    pallas_call x2, Pallas kernels, gated(): pl.pallas_call(gated_kernel, grid_spec=pltpu.PrefetchScalarGridSpec(num_s...  32.4 us
  transfers between devices with their start and end apart: 45, of which 16 were waited for; matrix products, arithmetic and copies ran while one was open for 20% of the time, Pallas kernels for 24%

profile of v2, /device:TPU:0, one launch (start us, length us, event | category | flops | bytes accessed | tf_op | source)
XLA Modules:
  0.0 707.2 jit_solution(14772153330932902827)
XLA Ops:
  13.2 10.0 %shard_map.373 = (bf16[1024,2048]{1,0:T(8,128)(2,1)}, bf16[512,1024]{1,0:T(8,128)(2,1)S(1)}, bf16[256,1024]{1,0:T(8,128)(2,1)S(1)}, bf16[1024,128]{1,0:T(8,128)(2,1)S(1)}) custom-call(bf16[1024,2048]{1,0:T(8,128)(2,1)} %x_ref.1, bf16[1,2048]{1,0:T(2,128)(2,1)S(1)} %broadcast_in_dim.30.gain_ref, bf16[2048,512]{1,0:T(8,128)(2,1)S(1)} %copy-done.30, ...), custom_call_target="tpu_custom_call" | custom-call | flops 1 | bytes 1 | tf_op jit(solution)/shard_map/pallas_call | solution.py:405
  24.0 4.8 collective-permute-start
  29.9 4.8 fusion.38
  50.6 5.7 collective-permute-start.3
  56.3 9.2 %shard_map.375.gh_ref = f32[512,2048]{1,0:T(8,128)} custom-call(bf16[512,2048]{1,0:T(8,128)(2,1)} %get-tuple-element.225.refs_0_, bf16[2048,2048]{1,0:T(8,128)(2,1)} %refs_1_.7), custom_call_target="tpu_custom_call" | custom-call | flops 1 | bytes 1 | tf_op jit(solution)/shard_map/pallas_call | solution.py:448
  69.0 9.0 %shard_map.376 = (bf16[512,1024]{1,0:T(8,128)(2,1)S(1)}, f32[8,1024]{1,0:T(8,128)S(1)}, f32[8,2,128,128]{3,2,1,0:T(8,128)S(1)}) custom-call(bf16[512,1024]{1,0:T(8,128)(2,1)S(1)} %get-tuple-element.67.refs_0_, bf16[256,1152]{1,0:T(8,128)(2,1)S(1)} %constant_dynamic-update-slice_fusion.refs_0_.refs_1_, bf16[2,128,1152]{2,1,0:T(8,128)(2,1)S(1)} %copy-done.17, ...), custom_call_target="tpu_custom_call" | custom-call | flops 1 | bytes 1 | tf_op jit(solution)/shard_map/pallas_call | solution.py:367
  90.3 21.3 %collective-permute-done.6 = bf16[256,2048]{1,0:T(8,128)(2,1)S(1)} collective-permute-done((bf16[256,2048]{1,0:T(8,128)(2,1)S(1)}, bf16[256,2048]{1,0:T(8,128)(2,1)S(1)}, u32[]{:S(2)}, u32[]{:S(2)}) %collective-permute-start.6) | collective-permute-done | bytes 1048608 | tf_op jit(solution)/shard_map/ppermute | solution.py:86
  116.2 15.9 %shard_map.377 = (bf16[1024,2048]{1,0:T(8,128)(2,1)}, bf16[1024,2048]{1,0:T(8,128)(2,1)}, bf16[1024,2048]{1,0:T(8,128)(2,1)}, bf16[1024,2048]{1,0:T(8,128)(2,1)}) custom-call(s32[1]{0:T(128)} %bitcast.18.core_ref, bf16[256,2048]{1,0:T(8,128)(2,1)} %copy-done.83, bf16[256,2048]{1,0:T(8,128)(2,1)} %copy-done.91, bf16[2048,2048]{1,0:T(8,128)(2,1)} %refs_1_.6, ...), custom_call_target="tpu_custom_call" | custom-call | flops 1 | bytes 1 | tf_op jit(solution)/shard_map/pallas_call | solution.py:534
  132.1 6.4 collective-permute-done.7
  143.1 9.2 %shard_map.378.gh_ref = f32[512,2048]{1,0:T(8,128)} custom-call(bf16[512,2048]{1,0:T(8,128)(2,1)} %get-tuple-element.224.refs_0_, bf16[2048,2048]{1,0:T(8,128)(2,1)} %refs_1_.7, bf16[256,2048]{1,0:T(8,128)(2,1)} %copy-done.83), custom_call_target="tpu_custom_call" | custom-call | flops 1 | bytes 1 | tf_op jit(solution)/shard_map/pallas_call | solution.py:448
  152.3 16.5 %shard_map.379 = (bf16[1024,2048]{1,0:T(8,128)(2,1)}, bf16[1024,2048]{1,0:T(8,128)(2,1)}, bf16[1024,2048]{1,0:T(8,128)(2,1)}, bf16[1024,2048]{1,0:T(8,128)(2,1)}) custom-call(s32[1]{0:T(128)} %bitcast.18.core_ref, bf16[256,2048]{1,0:T(8,128)(2,1)} %multiply_convert_fusion.own_ref, ...), custom_call_target="tpu_custom_call", output_to_operand_aliasing={{0}: (6, {}), {1}: (7, {}), {2}: (8, {}), {3}: (9, {})} | custom-call | flops 1 | bytes 1 | tf_op jit(solution)/shard_map/pallas_call | solution.py:534
  168.7 5.1 shard_map.380.refs_0_
  173.9 5.1 shard_map.381.refs_4_
  181.3 23.8 %shard_map.382.refs_0_ = bf16[1024,2048]{1,0:T(8,128)(2,1)} custom-call(bf16[1024,2048]{1,0:T(8,128)(2,1)} %get-tuple-element.88.refs_0_.b_ref, bf16[2048,2048]{1,0:T(8,128)(2,1)} %refs_1_.6, bf16[1024,2048]{1,0:T(8,128)(2,1)} %get-tuple-element.89.refs_2_.b_ref, bf16[2048,2048]{1,0:T(8,128)(2,1)} %refs_3_.2, bf16[1024,1024]{1,0:T(8,128)(2,1)} %copy-done.11), custom_call_target="tpu_custom_call" | custom-call | flops 1 | bytes 1 | tf_op jit(solution)/shard_map/pallas_call | solution.py:448
  205.1 4.8 constant_dynamic-slice_fusion.6
  210.1 6.1 shard_map.383.refs_0_
  216.2 5.1 shard_map.384.refs_1_
  222.7 5.7 collective-permute-done.12.refs_0_
  228.4 6.1 shard_map.385.refs_0_
  234.6 4.6 fusion.2
  243.2 6.3 shard_map.386.refs_0_
  249.5 5.1 shard_map.387.refs_2_
  256.0 13.2 %shard_map.388 = bf16[1024,2048]{1,0:T(8,128)(2,1)} custom-call(bf16[1024,2048]{1,0:T(8,128)(2,1)} %get-tuple-element.90.b_ref.refs_0_, bf16[2048,2048]{1,0:T(8,128)(2,1)} %refs_1_.7, bf16[1024,1024]{1,0:T(8,128)(2,1)} %copy-done.8), custom_call_target="tpu_custom_call" | custom-call | flops 1 | bytes 1 | tf_op jit(solution)/shard_map/pallas_call | solution.py:448
  269.2 17.6 %collective-permute-done.11 = bf16[512,2048]{1,0:T(8,128)(2,1)} collective-permute-done((bf16[512,2048]{1,0:T(8,128)(2,1)}, bf16[512,2048]{1,0:T(8,128)(2,1)}, u32[]{:S(2)}, u32[]{:S(2)}) %collective-permute-start.11) | collective-permute-done | bytes 2097184 | tf_op jit(solution)/shard_map/ppermute | solution.py:86
  286.8 5.0 multiply_reduce_fusion
  291.8 5.3 fusion.36
  297.0 6.2 shard_map.389.refs_16_
  303.3 5.0 constant_dynamic-slice_fusion.4
  325.8 24.2 %shard_map.390 = (bf16[512,1024]{1,0:T(8,128)(2,1)S(1)}, f32[8,64,64]{2,1,0:T(8,128)S(1)}, f32[128,1152]{1,0:T(8,128)S(1)}, f32[128,1152]{1,0:T(8,128)S(1)}, f32...) custom-call(bf16[512,1024]{1,0:T(8,128)(2,1)} %copy-done.21, ...), custom_call_target="tpu_custom_call" | custom-call | flops 1 | bytes 1 | tf_op jit(solution)/shard_map/pallas_call | solution.py:367
  355.7 4.6 collective-permute-done.20.refs_0_
  365.5 6.1 shard_map.392.refs_11_
  373.3 5.6 collective-permute-done.17
  380.2 7.1 collective-permute-start.23
  397.2 22.0 %collective-permute-done.19 = f32[2,128,128]{2,1,0:T(8,128)S(1)} collective-permute-done((f32[2,128,128]{2,1,0:T(8,128)S(1)}, f32[2,128,128]{2,1,0:T(8,128)S(1)}, u32[]{:S(2)}, u32[]{:S(2)}) %collective-permute-start.19) | collective-permute-done | bytes 131104 | tf_op jit(solution)/shard_map/ppermute | solution.py:127
  419.2 9.8 %collective-permute-done.16.refs_7_ = bf16[512,128]{1,0:T(8,128)(2,1)S(1)} collective-permute-done((bf16[512,128]{1,0:T(8,128)(2,1)S(1)}, bf16[512,128]{1,0:T(8,128)(2,1)S(1)}, u32[]{:S(2)}, u32[]{:S(2)}) %collective-permute-start.16) | collective-permute-done | bytes 131104 | tf_op jit(solution)/shard_map/ppermute | solution.py:127
  440.3 4.5 shard_map.394.refs_1_
  444.8 4.5 add_convert_fusion.1
  452.0 5.5 shard_map.395
  459.4 4.4 fusion
  483.4 28.7 %collective-permute-done.22 = bf16[512,2048]{1,0:T(8,128)(2,1)} collective-permute-done((bf16[512,2048]{1,0:T(8,128)(2,1)}, bf16[512,2048]{1,0:T(8,128)(2,1)}, u32[]{:S(2)}, u32[]{:S(2)}) %collective-permute-start.22) | collective-permute-done | bytes 2097184 | tf_op jit(solution)/shard_map/ppermute | solution.py:86
  516.1 4.2 fusion.7.refs_1_
  521.4 5.5 shard_map.396.refs_1_
  539.0 38.3 %collective-permute-done.35.refs_0_ = bf16[1024,1024]{1,0:T(8,128)(2,1)} collective-permute-done((bf16[1024,1024]{1,0:T(8,128)(2,1)}, bf16[1024,1024]{1,0:T(8,128)(2,1)}, u32[]{:S(2)}, u32[]{:S(2)}) %collective-permute-start.35) | collective-permute-done | bytes 2097184 | tf_op jit(solution)/shard_map/ppermute | solution.py:683
  578.4 5.5 shard_map.397.refs_1_
  593.4 6.4 collective-permute-done.34.refs_0_
  607.5 27.2 %collective-permute-done.27 = bf16[4,15104]{1,0:T(4,128)(2,1)S(1)} collective-permute-done((bf16[4,15104]{1,0:T(4,128)(2,1)S(1)}, bf16[4,15104]{1,0:T(4,128)(2,1)S(1)}, u32[]{:S(2)}, u32[]{:S(2)}) %collective-permute-start.27) | collective-permute-done | bytes 120864 | tf_op jit(solution)/shard_map/ppermute | solution.py:116
  646.9 4.3 shard_map.399
  673.9 22.9 %reduce-scatter.19.cloned.1.call-done = bf16[256,768]{1,0:T(8,128)(2,1)} async-done(((bf16[1024,768]{1,0:T(8,128)(2,1)}), bf16[256,768]{1,0:T(8,128)(2,1)}) %reduce-scatter.19.cloned.1.call-update) | async-done | bytes 393232 | tf_op jit(solution)/shard_map/reduce_scatter | solution.py:108
  (447 shorter events, 206.9 us)
Async XLA Ops:
  7.2 354.4 %reduce-scatter.9.cloned.1.call-start = ((), (), s32[]{:S(2)}) async-start(), calls=%async_computation.8 | async-start | bytes 2621440 | tf_op jit(solution)/shard_map/reduce_scatter | solution.py:108
  10.8 297.9 %copy-start.93 = (bf16[24,768]{1,0:T(8,128)(2,1)}, bf16[24,768]{1,0:T(8,128)(2,1)S(1)}, u32[]{:S(2)}) copy-start(bf16[24,768]{1,0:T(8,128)(2,1)S(1)} %fusion.28) | copy-start | bytes 110596
  24.0 11.6 %collective-permute-start = (bf16[256,128]{1,0:T(8,128)(2,1)S(1)}, bf16[256,128]{1,0:T(8,128)(2,1)S(1)}, u32[]{:S(2)}, u32[]{:S(2)}) collective-permute-start(bf16[256,128]{1,0:T(8,128)(2,1)S(1)} %slice.200), channel_id=1, source_target_pairs={{0,4},{4,8},{8,12},{12,16},{16,20},{20,24},{24,28},{1,5},{5,9},{9,... | collective-permute-start | bytes 196616 | tf_op jit(solution)/shard_map/ppermute | solution.py:127
  36.8 7.3 %collective-permute-start.1 = (f32[2,128,128]{2,1,0:T(8,128)S(1)}, f32[2,128,128]{2,1,0:T(8,128)S(1)}, u32[]{:S(2)}, u32[]{:S(2)}) collective-permute-start(f32[2,128,128]{2,1,0:T(8,128)S(1)} %get-tuple-element.73), channel_id=1, source_target_pairs={{0,4},{4,8},{8,12},{12,16},{16,20},{20,24},{24,28},{1,5},{5,9},{9,... | collective-permute-start | bytes 393224 | tf_op jit(solution)/shard_map/ppermute | solution.py:127
  44.1 6.5 collective-permute-start.2
  50.6 15.2 %collective-permute-start.3 = (f32[2,128,128]{2,1,0:T(8,128)S(1)}, f32[2,128,128]{2,1,0:T(8,128)S(1)}, u32[]{:S(2)}, u32[]{:S(2)}) collective-permute-start(f32[2,128,128]{2,1,0:T(8,128)S(1)} %add.243), channel_id=1, source_target_pairs={{0,16},{4,20},{8,24},{12,28},{1,17},{5,21},{9,25},{13,29},{2,18},{... | collective-permute-start | bytes 393224 | tf_op jit(solution)/shard_map/ppermute | solution.py:127
  80.8 3.8 collective-permute-start.5
  84.0 4.8 collective-permute-start.4
  86.5 25.0 %collective-permute-start.6 = (bf16[256,2048]{1,0:T(8,128)(2,1)S(1)}, bf16[256,2048]{1,0:T(8,128)(2,1)S(1)}, u32[]{:S(2)}, u32[]{:S(2)}) collective-permute-start(bf16[256,2048]{1,0:T(8,128)(2,1)S(1)} %fusion.13), channel_id=1, source_target_pairs={{0,2},{1,3},{2,0},{3,1},{4,6},{5,7},{6,4},{7,5},{8,10},{9,11},{10,... | collective-permute-start | bytes 3145736 | tf_op jit(solution)/shard_map/ppermute | solution.py:86
  112.2 179.6 %copy-start.71 = (f32[256,2048]{1,0:T(8,128)}, f32[256,2048]{1,0:T(8,128)S(1)}, u32[]{:S(2)}) copy-start(f32[256,2048]{1,0:T(8,128)S(1)} %get-tuple-element.211) | copy-start | bytes 6291460
  112.5 2.7 collective-permute-start.8
  112.5 25.9 %collective-permute-start.7 = (bf16[256,2048]{1,0:T(8,128)(2,1)}, bf16[256,2048]{1,0:T(8,128)(2,1)}, u32[]{:S(2)}, u32[]{:S(2)}) collective-permute-start(bf16[256,2048]{1,0:T(8,128)(2,1)} %fusion.14), channel_id=1, source_target_pairs={{0,2},{1,3},{2,0},{3,1},{4,6},{5,7},{6,4},{7,5},{8,10},{9,11},{10,... | collective-permute-start | bytes 3145736 | tf_op jit(solution)/shard_map/ppermute | solution.py:86
  143.1 9.2 %collective-permute-start.9 = (bf16[256,2048]{1,0:T(8,128)(2,1)}, bf16[256,2048]{1,0:T(8,128)(2,1)}, u32[]{:S(2)}, u32[]{:S(2)}) collective-permute-start(bf16[256,2048]{1,0:T(8,128)(2,1)} %multiply_convert_fusion.own_ref), channel_id=1, source_target_pairs={{0,1},{1,0},{2,3},{3,2},{4,5},{5,4},{6,7},{7,6},{8,9},{9,8},{10,11... | collective-permute-start | bytes 3145736 | tf_op jit(solution)/shard_map/ppermute | solution.py:79
  180.3 48.0 %collective-permute-start.12 = (bf16[1024,1024]{1,0:T(8,128)(2,1)S(1)}, bf16[1024,1024]{1,0:T(8,128)(2,1)S(1)}, u32[]{:S(2)}, u32[]{:S(2)}) collective-permute-start(bf16[1024,1024]{1,0:T(8,128)(2,1)S(1)} %shard_map.380.refs_0_), channel_id=1, source_target_pairs={{0,4},{4,0},{8,12},{12,8},{16,20},{20,16},{24,28},{28,24},{1,5},{5... | collective-permute-start | bytes 6291464 | tf_op jit(solution)/shard_map/ppermute | solution.py:683
  209.9 24.7 %collective-permute-start.10 = (bf16[512,2048]{1,0:T(8,128)(2,1)}, bf16[512,2048]{1,0:T(8,128)(2,1)}, u32[]{:S(2)}, u32[]{:S(2)}) collective-permute-start(bf16[512,2048]{1,0:T(8,128)(2,1)} %bitcast.24), channel_id=1, source_target_pairs={{0,1},{1,0},{2,3},{3,2},{4,5},{5,4},{6,7},{7,6},{8,9},{9,8},{10,11... | collective-permute-start | bytes 6291464 | tf_op jit(solution)/shard_map/ppermute | solution.py:79
  234.5 215.0 %reduce-scatter.11.cloned.1.call-start = ((), (), s32[]{:S(2)}) async-start(), calls=%async_computation.9 | async-start | bytes 2621440 | tf_op jit(solution)/shard_map/reduce_scatter | solution.py:108
  239.2 47.6 %collective-permute-start.11 = (bf16[512,2048]{1,0:T(8,128)(2,1)}, bf16[512,2048]{1,0:T(8,128)(2,1)}, u32[]{:S(2)}, u32[]{:S(2)}) collective-permute-start(bf16[512,2048]{1,0:T(8,128)(2,1)} %fusion.2), channel_id=1, source_target_pairs={{0,2},{1,3},{2,0},{3,1},{4,6},{5,7},{6,4},{7,5},{8,10},{9,11},{10,... | collective-permute-start | bytes 6291464 | tf_op jit(solution)/shard_map/ppermute | solution.py:86
  240.7 56.3 %collective-permute-start.15 = (bf16[1024,1024]{1,0:T(8,128)(2,1)S(1)}, bf16[1024,1024]{1,0:T(8,128)(2,1)S(1)}, u32[]{:S(2)}, u32[]{:S(2)}) collective-permute-start(bf16[1024,1024]{1,0:T(8,128)(2,1)S(1)} %copy-done.12), channel_id=1, source_target_pairs={{0,4},{4,0},{8,12},{12,8},{16,20},{20,16},{24,28},{28,24},{1,5},{5... | collective-permute-start | bytes 6291464 | tf_op jit(solution)/shard_map/ppermute | solution.py:683
  297.0 16.5 %collective-permute-start.13 = (bf16[512,2048]{1,0:T(8,128)(2,1)}, bf16[512,2048]{1,0:T(8,128)(2,1)}, u32[]{:S(2)}, u32[]{:S(2)}) collective-permute-start(bf16[512,2048]{1,0:T(8,128)(2,1)} %get-tuple-element.206.refs_1_), channel_id=1, source_target_pairs={{0,1},{1,0},{2,3},{3,2},{4,5},{5,4},{6,7},{7,6},{8,9},{9,8},{10,11... | collective-permute-start | bytes 6291464 | tf_op jit(solution)/shard_map/ppermute | solution.py:79
  303.2 217.1 %reduce-scatter.13.cloned.1.call-start = ((), (), s32[]{:S(2)}) async-start(), calls=%async_computation.10 | async-start | bytes 2621440 | tf_op jit(solution)/shard_map/reduce_scatter | solution.py:108
  308.3 8.3 %collective-permute-start.14 = (bf16[512,2048]{1,0:T(8,128)(2,1)}, bf16[512,2048]{1,0:T(8,128)(2,1)}, u32[]{:S(2)}, u32[]{:S(2)}) collective-permute-start(bf16[512,2048]{1,0:T(8,128)(2,1)} %bitcast.32), channel_id=1, source_target_pairs={{0,1},{1,0},{2,3},{3,2},{4,5},{5,4},{6,7},{7,6},{8,9},{9,8},{10,11... | collective-permute-start | bytes 6291464 | tf_op jit(solution)/shard_map/ppermute | solution.py:79
  312.6 47.8 %collective-permute-start.20 = (bf16[1024,1024]{1,0:T(8,128)(2,1)}, bf16[1024,1024]{1,0:T(8,128)(2,1)S(1)}, u32[]{:S(2)}, u32[]{:S(2)}) collective-permute-start(bf16[1024,1024]{1,0:T(8,128)(2,1)} %shard_map.383.refs_0_), channel_id=1, source_target_pairs={{0,4},{4,0},{8,12},{12,8},{16,20},{20,16},{24,28},{28,24},{1,5},{5... | collective-permute-start | bytes 6291464 | tf_op jit(solution)/shard_map/ppermute | solution.py:683
  371.7 205.7 %reduce-scatter.15.cloned.1.call-start = ((), (), s32[]{:S(2)}) async-start(), calls=%async_computation.11 | async-start | bytes 2621440 | tf_op jit(solution)/shard_map/reduce_scatter | solution.py:108
  371.7 57.3 %copy-start.19 = (bf16[2,128,1152]{2,1,0:T(8,128)(2,1)S(1)}, bf16[2,128,1152]{2,1,0:T(8,128)(2,1)}, u32[]{:S(2)}) copy-start(bf16[2,128,1152]{2,1,0:T(8,128)(2,1)} %copy-done.16) | copy-start | bytes 1769476
  371.8 7.1 %collective-permute-start.17 = (f32[2,128,128]{2,1,0:T(8,128)S(1)}, f32[2,128,128]{2,1,0:T(8,128)S(1)}, u32[]{:S(2)}, u32[]{:S(2)}) collective-permute-start(f32[2,128,128]{2,1,0:T(8,128)S(1)} %get-tuple-element.99), channel_id=1, source_target_pairs={{4,0},{8,4},{12,8},{16,12},{20,16},{24,20},{28,24},{5,1},{9,5},{13... | collective-permute-start | bytes 393224 | tf_op jit(solution)/shard_map/ppermute | solution.py:127
  378.9 15.7 %collective-permute-start.18 = (f32[2,128,128]{2,1,0:T(8,128)S(1)}, f32[2,128,128]{2,1,0:T(8,128)S(1)}, u32[]{:S(2)}, u32[]{:S(2)}) collective-permute-start(f32[2,128,128]{2,1,0:T(8,128)S(1)} %add.263), channel_id=1, source_target_pairs={{8,0},{12,4},{16,8},{20,12},{24,16},{28,20},{9,1},{13,5},{17,9},{2... | collective-permute-start | bytes 393224 | tf_op jit(solution)/shard_map/ppermute | solution.py:127
  380.2 69.3 %collective-permute-start.23 = (bf16[1024,1024]{1,0:T(8,128)(2,1)}, bf16[1024,1024]{1,0:T(8,128)(2,1)}, u32[]{:S(2)}, u32[]{:S(2)}) collective-permute-start(bf16[1024,1024]{1,0:T(8,128)(2,1)} %copy-done.9), channel_id=1, source_target_pairs={{0,4},{4,0},{8,12},{12,8},{16,20},{20,16},{24,28},{28,24},{1,5},{5... | collective-permute-start | bytes 6291464 | tf_op jit(solution)/shard_map/ppermute | solution.py:683
  387.3 57.5 %collective-permute-start.24 = (bf16[512,2048]{1,0:T(8,128)(2,1)}, bf16[512,2048]{1,0:T(8,128)(2,1)}, u32[]{:S(2)}, u32[]{:S(2)}) collective-permute-start(bf16[512,2048]{1,0:T(8,128)(2,1)} %fusion.1.refs_15_), channel_id=1, source_target_pairs={{0,2},{1,3},{2,0},{3,1},{4,6},{5,7},{6,4},{7,5},{8,10},{9,11},{10,... | collective-permute-start | bytes 6291464 | tf_op jit(solution)/shard_map/ppermute | solution.py:86
  391.7 37.3 %collective-permute-start.16 = (bf16[512,128]{1,0:T(8,128)(2,1)S(1)}, bf16[512,128]{1,0:T(8,128)(2,1)S(1)}, u32[]{:S(2)}, u32[]{:S(2)}) collective-permute-start(bf16[512,128]{1,0:T(8,128)(2,1)S(1)} %pad_maximum_fusion.3), channel_id=1, source_target_pairs={{4,0},{8,4},{12,8},{16,12},{20,16},{24,20},{28,24},{5,1},{9,5},{13... | collective-permute-start | bytes 393224 | tf_op jit(solution)/shard_map/ppermute | solution.py:127
  394.6 24.6 %collective-permute-start.19 = (f32[2,128,128]{2,1,0:T(8,128)S(1)}, f32[2,128,128]{2,1,0:T(8,128)S(1)}, u32[]{:S(2)}, u32[]{:S(2)}) collective-permute-start(f32[2,128,128]{2,1,0:T(8,128)S(1)} %add.264), channel_id=1, source_target_pairs={{16,0},{20,4},{24,8},{28,12},{17,1},{21,5},{25,9},{29,13},{18,2},{... | collective-permute-start | bytes 393224 | tf_op jit(solution)/shard_map/ppermute | solution.py:127
  438.8 20.6 %collective-permute-start.21 = (bf16[512,2048]{1,0:T(8,128)(2,1)}, bf16[512,2048]{1,0:T(8,128)(2,1)}, u32[]{:S(2)}, u32[]{:S(2)}) collective-permute-start(bf16[512,2048]{1,0:T(8,128)(2,1)} %bitcast.36), channel_id=1, source_target_pairs={{0,1},{1,0},{2,3},{3,2},{4,5},{5,4},{6,7},{7,6},{8,9},{9,8},{10,11... | collective-permute-start | bytes 6291464 | tf_op jit(solution)/shard_map/ppermute | solution.py:79
  449.4 28.6 %collective-permute-start.25 = (bf16[512,2048]{1,0:T(8,128)(2,1)}, bf16[512,2048]{1,0:T(8,128)(2,1)}, u32[]{:S(2)}, u32[]{:S(2)}) collective-permute-start(bf16[512,2048]{1,0:T(8,128)(2,1)} %add_convert_fusion.1), channel_id=1, source_target_pairs={{0,1},{1,0},{2,3},{3,2},{4,5},{5,4},{6,7},{7,6},{8,9},{9,8},{10,11... | collective-permute-start | bytes 6291464 | tf_op jit(solution)/shard_map/ppermute | solution.py:79
  449.4 70.9 %collective-permute-start.36 = (bf16[1024,1024]{1,0:T(8,128)(2,1)}, bf16[1024,1024]{1,0:T(8,128)(2,1)}, u32[]{:S(2)}, u32[]{:S(2)}) collective-permute-start(bf16[1024,1024]{1,0:T(8,128)(2,1)} %shard_map.386.refs_0_), channel_id=1, source_target_pairs={{0,4},{4,0},{8,12},{12,8},{16,20},{20,16},{24,28},{28,24},{1,5},{5... | collective-permute-start | bytes 6291464 | tf_op jit(solution)/shard_map/ppermute | solution.py:683
  458.9 140.9 %reduce-scatter.17.cloned.1.call-start = ((), (), s32[]{:S(2)}) async-start(), calls=%async_computation.12 | async-start | bytes 2621440 | tf_op jit(solution)/shard_map/reduce_scatter | solution.py:108
  463.8 48.3 %collective-permute-start.22 = (bf16[512,2048]{1,0:T(8,128)(2,1)}, bf16[512,2048]{1,0:T(8,128)(2,1)}, u32[]{:S(2)}, u32[]{:S(2)}) collective-permute-start(bf16[512,2048]{1,0:T(8,128)(2,1)} %fusion), channel_id=1, source_target_pairs={{0,2},{1,3},{2,0},{3,1},{4,6},{5,7},{6,4},{7,5},{8,10},{9,11},{10,... | collective-permute-start | bytes 6291464 | tf_op jit(solution)/shard_map/ppermute | solution.py:86
  528.3 141.0 %reduce-scatter.23.cloned.1.call-start = ((), (), s32[]{:S(2)}) async-start(), calls=%async_computation.15 | async-start | bytes 2621440 | tf_op jit(solution)/shard_map/reduce_scatter | solution.py:108
  528.4 48.9 %collective-permute-start.35 = (bf16[1024,1024]{1,0:T(8,128)(2,1)}, bf16[1024,1024]{1,0:T(8,128)(2,1)}, u32[]{:S(2)}, u32[]{:S(2)}) collective-permute-start(bf16[1024,1024]{1,0:T(8,128)(2,1)} %copy-done.8), channel_id=1, source_target_pairs={{0,4},{4,0},{8,12},{12,8},{16,20},{20,16},{24,28},{28,24},{1,5},{5... | collective-permute-start | bytes 6291464 | tf_op jit(solution)/shard_map/ppermute | solution.py:683
  530.2 69.6 %collective-permute-start.34 = (bf16[1024,512]{1,0:T(8,128)(2,1)}, bf16[1024,512]{1,0:T(8,128)(2,1)}, u32[]{:S(2)}, u32[]{:S(2)}) collective-permute-start(bf16[1024,512]{1,0:T(8,128)(2,1)} %copy-done.22), channel_id=1, source_target_pairs={{0,4},{4,0},{8,12},{12,8},{16,20},{20,16},{24,28},{28,24},{1,5},{5... | collective-permute-start | bytes 3145736 | tf_op jit(solution)/shard_map/ppermute | solution.py:683
  534.0 112.9 %collective-permute-start.33 = (bf16[1024,768]{1,0:T(8,128)(2,1)}, bf16[1024,768]{1,0:T(8,128)(2,1)}, u32[]{:S(2)}, u32[]{:S(2)}) collective-permute-start(bf16[1024,768]{1,0:T(8,128)(2,1)} %copy-done.14), channel_id=1, source_target_pairs={{0,4},{4,0},{8,12},{12,8},{16,20},{20,16},{24,28},{28,24},{1,5},{5... | collective-permute-start | bytes 4718600 | tf_op jit(solution)/shard_map/ppermute | solution.py:683
  585.2 86.7 %reduce-scatter.21.cloned.1.call-start = ((), (), s32[]{:S(2)}) async-start(), calls=%async_computation.14 | async-start | bytes 1310720 | tf_op jit(solution)/shard_map/reduce_scatter | solution.py:108
  590.2 44.5 %collective-permute-start.27 = (bf16[4,15104]{1,0:T(4,128)(2,1)S(1)}, bf16[4,15104]{1,0:T(4,128)(2,1)S(1)}, u32[]{:S(2)}, u32[]{:S(2)}) collective-permute-start(bf16[4,15104]{1,0:T(4,128)(2,1)S(1)} %bitcast.218), channel_id=1, source_target_pairs={{0,4},{4,0},{8,12},{12,8},{16,20},{20,16},{24,28},{28,24},{1,5},{5... | collective-permute-start | bytes 362504 | tf_op jit(solution)/shard_map/ppermute | solution.py:116
  607.3 89.5 %reduce-scatter.19.cloned.1.call-start = ((), (), s32[]{:S(2)}) async-start(), calls=%async_computation.13 | async-start | bytes 1966080 | tf_op jit(solution)/shard_map/reduce_scatter | solution.py:108
  635.3 11.0 %collective-permute-start.28 = (bf16[15104]{0:T(1024)(128)(2,1)S(1)}, bf16[15104]{0:T(1024)(128)(2,1)S(1)}, u32[]{:S(2)}, u32[]{:S(2)}) collective-permute-start(bf16[15104]{0:T(1024)(128)(2,1)S(1)} %get-tuple-element.201), channel_id=1, source_target_pairs={{0,8},{4,12},{8,16},{12,20},{16,24},{20,28},{24,0},{28,4},{1,9},{5... | collective-permute-start | bytes 90632 | tf_op jit(solution)/shard_map/ppermute | solution.py:122
  637.7 8.5 %collective-permute-start.29 = (bf16[15104]{0:T(1024)(128)(2,1)S(1)}, bf16[15104]{0:T(1024)(128)(2,1)S(1)}, u32[]{:S(2)}, u32[]{:S(2)}) collective-permute-start(bf16[15104]{0:T(1024)(128)(2,1)S(1)} %get-tuple-element.203), channel_id=1, source_target_pairs={{0,16},{4,20},{8,24},{12,28},{16,0},{20,4},{24,8},{28,12},{1,17},{... | collective-permute-start | bytes 90632 | tf_op jit(solution)/shard_map/ppermute | solution.py:122
  638.7 7.6 %collective-permute-start.30 = (bf16[15104]{0:T(1024)(128)(2,1)S(1)}, bf16[15104]{0:T(1024)(128)(2,1)S(1)}, u32[]{:S(2)}, u32[]{:S(2)}) collective-permute-start(bf16[15104]{0:T(1024)(128)(2,1)S(1)} %get-tuple-element.202), channel_id=1, source_target_pairs={{0,24},{4,28},{8,0},{12,4},{16,8},{20,12},{24,16},{28,20},{1,25},{... | collective-permute-start | bytes 90632 | tf_op jit(solution)/shard_map/ppermute | solution.py:122
  646.1 16.8 %collective-permute-start.26 = (bf16[512,2048]{1,0:T(8,128)(2,1)}, bf16[512,2048]{1,0:T(8,128)(2,1)}, u32[]{:S(2)}, u32[]{:S(2)}) collective-permute-start(bf16[512,2048]{1,0:T(8,128)(2,1)} %fusion.7.refs_1_), channel_id=1, source_target_pairs={{0,1},{1,0},{2,3},{3,2},{4,5},{5,4},{6,7},{7,6},{8,9},{9,8},{10,11... | collective-permute-start | bytes 6291464 | tf_op jit(solution)/shard_map/ppermute | solution.py:79
  646.3 6.1 collective-permute-start.31
  652.5 5.8 collective-permute-start.32
  (102 other events, 809.6 us)
Sparse Core Ops, SparseCore 0:
  234.6 42.1 reduce-scatter.8
  303.3 42.2 reduce-scatter.10
  371.8 50.7 reduce-scatter.12
  459.0 45.2 reduce-scatter.14
  528.4 44.9 reduce-scatter.16
  585.4 44.9 reduce-scatter.22
  632.7 27.1 reduce-scatter.20
  662.2 34.5 reduce-scatter.18

commit v3 on v2

--- a/solution.py
+++ b/solution.py
@@ -8,11 +8,14 @@
 WIN = 64
 CHUNK = 128
 ANY = pl.BlockSpec(memory_space=pl.ANY)
-COST = pl.CostEstimate(flops=1, bytes_accessed=1, transcendentals=0)
 EPSILON = 1e-05
 EXACT = lax.Precision.HIGHEST
 F32 = jnp.float32
 BF16 = jnp.bfloat16
+
+
+def cost(us):
+    return pl.CostEstimate(flops=int(us * 0.45e9), bytes_accessed=1, transcendentals=0)
 
 
 def dot(a, b, out=F32):
@@ -70,17 +73,20 @@
         cut = x.reshape(parts, 2, rows // (2 * parts), width)
         return lax.dynamic_index_in_dim(cut, self.core, 1, False).reshape(rows // 2, width)
 
-    def other_rows(self, x, parts):
-        rows, width = x.shape
-        cut = x.reshape(parts, 2, rows // (2 * parts), width)
-        return lax.dynamic_index_in_dim(cut, 1 - self.core, 1, False).reshape(rows // 2, width)
-
-    def across_cores(self, x):
-        return lax.ppermute(x, "kv", self.core_swap)
-
-    def core_sum(self, part, parts):
-        got = self.across_cores(self.other_rows(part, parts))
-        return (self.own_rows(part, parts).astype(F32) + got.astype(F32)).astype(BF16)
+    def across_cores(self, x, pieces=1):
+        rows = x.shape[0] // pieces
+        cuts = [x[i * rows : (i + 1) * rows] for i in range(pieces)]
+        got = [lax.ppermute(c, "kv", self.core_swap) for c in cuts]
+        return jnp.concatenate(got, 0) if pieces > 1 else got[0]
+
+    def core_sum(self, keep, send):
+        return (keep.astype(F32) + self.across_cores(send, 4).astype(F32)).astype(BF16)
+
+    def swap(self, x):
+        return lax.ppermute(x, "seq", self.x_swap)
+
+    def pair_sum(self, keep, got):
+        return (keep.astype(F32) + got.astype(F32)).astype(BF16)
 
     def outer_terms(self, half):
         terms = [half] + [lax.ppermute(half, "kv", self.y_shift(j)) for j in range(1, self.outer)]
@@ -90,7 +96,7 @@
         return [take(stack, (self.y - i) % self.outer) for i in range(self.outer)]
 
     def gather_rows(self, own, parts):
-        other = self.across_cores(own)
+        other = self.across_cores(own, 4)
         first = self.core == 0
         shape = (parts, 1, own.shape[0] // parts, own.shape[1])
         low = jnp.where(first, own, other).reshape(shape)
@@ -108,6 +114,13 @@
         return lax.psum_scatter(
             part, "seq", scatter_dimension=0, tiled=True, axis_index_groups=self.z_groups
         )
+
+    def finish(self, x):
+        cut = x.reshape(2, x.shape[0] // 2, x.shape[1])
+        got = self.swap(take(cut, 1 - self.x))
+        own = take(cut, self.x)
+        first = self.x == 0
+        return jnp.where(first, own, got), jnp.where(first, got, own)
 
     def scatter_blocks(self, blocks):
         cut = blocks.reshape(self.line, 2, -1)
@@ -124,14 +137,15 @@
 
     def shift_seq(self, x, by):
         n = self.seq
-        return lax.ppermute(x, "seq", [(i, i + by) for i in range(n) if 0 <= i + by < n])
-
-    def sum_before(self, x, sign):
-        near = self.shift_seq(x, sign)
+        pairs = [(i, i + by) for i in range(n) if 0 <= i + by < n]
+        return lax.ppermute(x, "seq", pairs)
+
+    def sum_before(self, x, sign, kind):
+        near = self.shift_seq(x.astype(kind), sign).astype(F32)
         total = x + near
         by = 2
         while by < self.seq:
-            total = total + self.shift_seq(total, sign * by)
+            total = total + self.shift_seq(total.astype(kind), sign * by).astype(F32)
             by *= 2
         return total - x, near
 
@@ -160,7 +174,7 @@
 
 def value_rows(v, keep):
     hd, n = v.shape
-    ones = (lax.broadcasted_iota(jnp.int32, (hd, n), 0) == 0).astype(F32)
+    ones = (lax.broadcasted_iota(jnp.int32, (16, n), 0) == 0).astype(F32)
     return (jnp.concatenate([v.astype(F32), ones], 0) * keep).astype(BF16)
 
 
@@ -219,7 +233,7 @@
             states_ref[i, g] = past
             scores = dot(k_ref[g, keys, :], lanes(q)) * scale
             linear = dot(phi_ref[g, keys, :], phi4)
-            carried = dot2(past[: hd + 8], phi4)
+            carried = dot2(past, phi4)
             weights = []
             totals = []
             for j in range(group):
@@ -289,7 +303,7 @@
                 g_weight = g_w[:, cut] * inv + g_total
                 g_scores.append((g_weight * ex).astype(BF16))
                 g_linear.append(jnp.where(lin, g_weight, 0.0).astype(BF16))
-                row = lax.broadcasted_iota(jnp.int32, (hd, CHUNK), 0) == 0
+                row = lax.broadcasted_iota(jnp.int32, (16, CHUNK), 0) == 0
                 g_ext.append(
                     (jnp.concatenate([g_here * inv, jnp.where(row, g_total, 0.0)], 0) * far).astype(BF16)
                 )
@@ -360,7 +374,7 @@
         feat_ref[g] = dot_nt(k, gl)
 
 
-def call(kernel, outs, args, scratch=(), smem=(), after=()):
+def call(us, kernel, outs, args, scratch=(), smem=(), after=()):
     count = len(args)
     vmem = pl.BlockSpec(memory_space=pltpu.VMEM)
     specs = [pl.BlockSpec(memory_space=pltpu.SMEM) if i in smem else vmem for i in range(len(args))]
@@ -371,7 +385,7 @@
         out_specs=[vmem] * len(outs),
         scratch_shapes=[pltpu.VMEM(s, d) for s, d in scratch],
         compiler_params=pltpu.CompilerParams(vmem_limit_bytes=48 * 2**20),
-        cost_estimate=COST,
+        cost_estimate=cost(us),
     )(*args, *after)
 
 
@@ -414,66 +428,107 @@
             jax.ShapeDtypeStruct((t, down.shape[1]), BF16),
         ],
         compiler_params=pltpu.CompilerParams(vmem_limit_bytes=48 * 2**20),
-        cost_estimate=COST,
+        cost_estimate=cost(10.0),
     )(tokens, gain, wq, wk, wv, down, up)
 
 
-def matmul_kernel(product, pairs, out_ref):
-    sub = min(256, out_ref.shape[0])
-    for r in range(0, out_ref.shape[0], sub):
-        total = None
-        for a_ref, b_ref in pairs:
-            term = product(a_ref[r : r + sub, :], b_ref[...])
-            total = term if total is None else total + term
-        out_ref[r : r + sub, :] = total.astype(out_ref.dtype)
-
-
-def matmul(pairs, transposed, out, tile=512, after=()):
-    rows = pairs[0][0].shape[0]
-    width = pairs[0][1].shape[0 if transposed else 1]
-    product = dot_nt if transposed else dot
+def matmul(pairs, mode, chosen, out, split=None, tile=512, after=()):
+    a0, b0 = pairs[0]
+    over = 0 if mode in ("left", "both") else 1
+    rows = a0.shape[1 - over]
+    half = a0.shape[over]
+    width = {"rows": b0.shape[0] // 2, "columns": b0.shape[0], "both": b0.shape[0]}.get(mode, b0.shape[1])
+    tile = min(tile, width)
+    product = {"rows": dot_nt, "columns": dot_nt, "inner": dot, "left": dot_tn, "both": dot_tt}[mode]
+    b_spec = {
+        "rows": pl.BlockSpec((tile, half), lambda i, s: (s[0] * (width // tile) + i, 0)),
+        "columns": pl.BlockSpec((tile, half), lambda i, s: (i, s[0])),
+        "inner": pl.BlockSpec((half, tile), lambda i, s: (s[0], i)),
+        "left": pl.BlockSpec((half, tile), lambda i, s: (0, i)),
+        "both": pl.BlockSpec((tile, half), lambda i, s: (i, 0)),
+    }[mode]
     specs, args = [], []
     for a, b in pairs:
-        specs.append(pl.BlockSpec(a.shape, lambda i: (0, 0)))
-        if transposed:
-            specs.append(pl.BlockSpec((tile, b.shape[1]), lambda i: (i, 0)))
-        else:
-            specs.append(pl.BlockSpec((b.shape[0], tile), lambda i: (0, i)))
+        specs += [pl.BlockSpec(a.shape, lambda i, s: (0, 0)), b_spec]
         args += [a, b]
+    sub = rows // 4
+    core = jnp.zeros((), jnp.int32) if split is None else split
+
+    def kernel(sel, *refs):
+        used = refs[: 2 * len(pairs)]
+        outs = refs[2 * len(pairs) + len(after) :]
+
+        def block(start):
+            total = None
+            for a_ref, b_ref in zip(used[::2], used[1::2]):
+                a = a_ref[pl.ds(start, sub), :] if over else a_ref[:, pl.ds(start, sub)]
+                term = product(a, b_ref[...])
+                total = term if total is None else total + term
+            return total.astype(out)
+
+        for c in range(2):
+            for k in range(2):
+                if split is None:
+                    at = (2 * c + k) * sub
+                    outs[0][at : at + sub, :] = block(at)
+                else:
+                    other = sel[1] if k == 0 else 1 - sel[1]
+                    start = pl.multiple_of((2 * c + other) * sub, sub)
+                    outs[k][c * sub : (c + 1) * sub, :] = block(start)
+
+    n_out = 1 if split is None else 2
+    us = 1.0 + sum(a.size for a, _ in pairs) * width * 1.5e-9
+    made = pl.pallas_call(
+        kernel,
+        grid_spec=pltpu.PrefetchScalarGridSpec(
+            num_scalar_prefetch=1,
+            grid=(width // tile,),
+            in_specs=specs + [ANY] * len(after),
+            out_specs=[pl.BlockSpec((rows // n_out, tile), lambda i, s: (0, i))] * n_out,
+        ),
+        out_shape=[jax.ShapeDtypeStruct((rows // n_out, width), out)] * n_out,
+        compiler_params=pltpu.CompilerParams(vmem_limit_bytes=56 * 2**20),
+        cost_estimate=cost(us),
+    )(jnp.stack([chosen, core]).astype(jnp.int32), *args, *after)
+    return made if split is not None else made[0]
+
+
+def grad_pair(count, pairs, after=()):
+    rows, width = pairs[0][0].shape
+    n = pairs[0][1].shape[1]
+    block = width // count
+    specs = [pl.BlockSpec((rows, block), lambda j: (0, j)), pl.BlockSpec((rows, n), lambda j: (0, 0))]
 
     def kernel(*refs):
-        used = refs[: 2 * len(pairs)]
-        matmul_kernel(product, list(zip(used[::2], used[1::2])), refs[-1])
+        value = dot_tn(refs[0][...], refs[1][...])
+        for i in range(1, len(pairs)):
+            value = value + dot_tn(refs[2 * i][...], refs[2 * i + 1][...])
+        refs[-1][...] = value.astype(BF16)
 
     return pl.pallas_call(
         kernel,
-        grid=(width // tile,),
-        in_specs=specs + [ANY] * len(after),
-        out_specs=pl.BlockSpec((rows, tile), lambda i: (0, i)),
-        out_shape=jax.ShapeDtypeStruct((rows, width), out),
-        compiler_params=pltpu.CompilerParams(vmem_limit_bytes=56 * 2**20),
-        cost_estimate=COST,
-    )(*args, *after)
-
-
-def grad_block(line, select, a, b, product, piece=(0, 1), got=None, after=()):
+        grid=(count,),
+        in_specs=specs * len(pairs) + [ANY] * len(after),
+        out_specs=pl.BlockSpec((block, n), lambda j: (j, 0)),
+        out_shape=jax.ShapeDtypeStruct((width, n), BF16),
+        compiler_params=pltpu.CompilerParams(vmem_limit_bytes=48 * 2**20),
+        cost_estimate=cost(13.0),
+    )(*[x for pair in pairs for x in pair], *after)
+
+
+def grad_block(line, select, a, b, product, got=None, after=()):
     rows, width = a.shape
     block = width // (2 * line)
-    if product is dot_tt:
-        n = b.shape[0]
-        b_spec = pl.BlockSpec(b.shape, lambda j, s: (0, 0))
-    else:
-        n = b.shape[1] // piece[1]
-        b_spec = pl.BlockSpec((rows, n), lambda j, s: (0, piece[0]))
-
-    def kernel(sel_ref, a_ref, b_ref, *refs):
+    n = b.shape[0] if product is dot_tt else b.shape[1]
+    more = [] if got is None else [got]
+
+    def kernel(sel, a_ref, b_ref, *rest):
         value = product(a_ref[...], b_ref[...])
         if got is not None:
-            value = value + refs[0][...].astype(F32)
-        refs[-1][...] = value.astype(BF16)
+            value = value + rest[0][...].astype(F32)
+        rest[-1][...] = value.astype(BF16)
 
     spec = pl.BlockSpec((block, n), lambda j, s: (j, 0))
-    more = [] if got is None else [got]
     return pl.pallas_call(
         kernel,
         grid_spec=pltpu.PrefetchScalarGridSpec(
@@ -481,7 +536,7 @@
             grid=(line,),
             in_specs=[
                 pl.BlockSpec((rows, block), lambda j, s: (0, 2 * j + s[0])),
-                b_spec,
+                pl.BlockSpec(b.shape, lambda j, s: (0, 0)),
             ]
             + [spec] * len(more)
             + [ANY] * len(after),
@@ -489,17 +544,17 @@
         ),
         out_shape=jax.ShapeDtypeStruct((line * block, n), BF16),
         compiler_params=pltpu.CompilerParams(vmem_limit_bytes=48 * 2**20),
-        cost_estimate=COST,
-    )(select, a, b, *more, *after)
-
-
-def gated_kernel(core_ref, own_ref, other_ref, wg_ref, wu_ref, gh_ref, *refs):
+        cost_estimate=cost(1.0),
+    )(select.astype(jnp.int32)[None], a, b, *more, *after)
+
+
+def gated_kernel(sel_ref, own_ref, other_ref, wg_ref, wu_ref, gh_ref, *refs):
     normed_ref, hidden_ref, gate_ref, up_ref = refs[-4:]
     half = own_ref.shape[0]
 
     @pl.when(pl.program_id(0) == 0)
     def _():
-        first = core_ref[0] == 0
+        first = sel_ref[0] == 0
 
         @pl.when(first)
         def _():
@@ -524,12 +579,11 @@
         up_ref[cut, :] = (g * silu).astype(BF16)
 
 
-def gated(c, rows, core, own, other, wg, wu, gh, held, tile=512):
+def gated(c, rows, sel, own, other, wg, wu, gh, held, after, tile=256):
     half, d = own.shape
-    f = wg.shape[1]
+    f = wg.shape[1] // 2
     here = pl.BlockSpec((2 * half, tile), lambda i, s: (c, i))
-    part = pl.BlockSpec((2 * half, tile), lambda i, s: (0, i))
-    held_specs = [pl.BlockSpec(memory_space=pl.ANY)] * len(held)
+    weight = pl.BlockSpec((d, tile), lambda i, s: (0, s[1] * (f // tile) + i))
     shapes = [jax.ShapeDtypeStruct((rows, d), BF16)] + [jax.ShapeDtypeStruct((rows, f), BF16)] * 3
     return pl.pallas_call(
         gated_kernel,
@@ -539,18 +593,18 @@
             in_specs=[
                 pl.BlockSpec((half, d), lambda i, s: (0, 0)),
                 pl.BlockSpec((half, d), lambda i, s: (0, 0)),
-                pl.BlockSpec((d, tile), lambda i, s: (0, i)),
-                pl.BlockSpec((d, tile), lambda i, s: (0, i)),
-                part,
+                weight,
+                weight,
+                here,
             ]
-            + held_specs,
+            + [ANY] * (len(held) + len(after)),
             out_specs=[pl.BlockSpec((2 * half, d), lambda i, s: (c, 0)), here, here, here],
         ),
         out_shape=shapes,
         input_output_aliases={6 + i: i for i in range(len(held))},
         compiler_params=pltpu.CompilerParams(vmem_limit_bytes=56 * 2**20),
-        cost_estimate=COST,
-    )(core, own, other, wg, wu, gh, *held)
+        cost_estimate=cost(11.0),
+    )(sel, own, other, wg, wu, gh, *held, *after)
 
 
 def local(
@@ -614,111 +668,131 @@
     key_map_t = jnp.swapaxes(key_map, 1, 2)
     phi_dim = 2 * hd
     phi_cols, phi, key, value, state = call(
+        2.0,
         key_kernel,
         [
             ((hk, phi_dim, length), BF16),
             ((hk, length, phi_dim), BF16),
             ((hk, length, hd), BF16),
             ((hk, length, hd), BF16),
-            ((hk, phi_dim, phi_dim), F32),
+            ((hk, hd + 16, phi_dim), F32),
         ],
         (kv, key_map_t, keep_all),
     )
-    prior, _ = grid.sum_before(state, 1)
+    prior, _ = grid.sum_before(state, 1, F32)
     parts = 2
     chunk = rows // parts
-    g_hidden = matmul([(cotangent[:chunk], down_weight)], True, F32)
+    core, mine = grid.core.astype(jnp.int32), grid.x.astype(jnp.int32)
+    g_hidden = matmul([(cotangent, down_weight)], "rows", mine, F32)
     oup = output_up
     odown = output_down.reshape(-1, rank)
     weight_o = (output_weight.astype(F32) + dot(odown, oup)).astype(BF16)
-    prior, g_hidden, weight_o = tie(prior, g_hidden, weight_o)
+    cot_own = grid.own_rows(cotangent, parts)
+    prior, g_hidden, weight_o, cot_own = tie(prior, g_hidden, weight_o, cot_own)
+    cot_got = grid.swap(cot_own)
     heads, totals, states = call(
+        9.0,
         attend_kernel,
-        [((qw, rows), BF16), ((hq, rows), F32), ((count, hk, phi_dim, phi_dim), F32)],
+        [((qw, rows), BF16), ((hq, rows), F32), ((count, hk, hd + 16, phi_dim), F32)],
         (query, kv, phi_cols, phi, key, query_map_t, prior, opened, keep, cont),
-        scratch=[((hk, phi_dim, phi_dim), F32)],
+        scratch=[((hk, hd + 16, phi_dim), F32)],
         smem=(9,),
     )
 
-    part = [dot_tn(heads[:, c * chunk : (c + 1) * chunk], weight_o, BF16) for c in range(parts)]
-    half = [grid.core_sum(p, 1) for p in part]
+    kept, sent = matmul([(heads, weight_o)], "left", mine, BF16, core)
+    cuts = [slice(c * chunk // 2, (c + 1) * chunk // 2) for c in range(parts)]
+    half = [grid.core_sum(kept[cut], sent[cut]) for cut in cuts]
     own_tokens = [grid.own_rows(tokens[c * chunk : (c + 1) * chunk], 1) for c in range(parts)]
     own_tokens[0], half[1] = tie(own_tokens[0], half[1])
     terms = [grid.outer_terms(h) for h in half]
-    held = ()
-    resid, rms_two = [], []
-    for c in range(parts):
-        if c:
-            held = list(held)
-            terms[c][-1], held[0] = tie(terms[c][-1], held[0])
+    cot_got, terms[0][-1] = tie(cot_got, terms[0][-1])
+    held, held_pair = (), ()
+    resid, rms_two, own, got = [], [], [], []
+    select = jnp.stack([core, mine])
+
+    def normed(c):
         r = own_tokens[c].astype(F32) + add(terms[c])
         rms = lax.rsqrt(jnp.mean(r * r, -1, keepdims=True) + EPSILON)
-        own = (r * rms * g2).astype(BF16)
-        core = grid.core.astype(jnp.int32)[None]
-        if c:
-            g_hidden = g_rest
-        else:
-            g_rest = matmul([(cotangent[chunk:], down_weight)], True, F32, after=[own])
-        held = gated(
-            c, rows, core, own, grid.across_cores(own), gate_weight, up_weight, g_hidden, held
-        )
         resid.append(r)
         rms_two.append(rms)
+        own.append((r * rms * g2).astype(BF16))
+        got.append(None)
+
+    def inner(c, mine_c, gh, held, after):
+        return gated(
+            c, rows, select, mine_c, grid.across_cores(mine_c), gate_weight, up_weight, gh, held, after
+        )
+
+    normed(0)
+    got[0] = grid.swap(own[0])
+    held = list(inner(0, own[0], g_hidden, held, []))
+    terms[1][-1], held[1] = tie(terms[1][-1], held[1])
+    normed(1)
+    got[1] = grid.swap(own[1])
+    cot_got, mark = tie(cot_got, own[1])
+    cot_pair = grid.gather_rows(cot_got, parts)
+    g_pair = matmul([(cot_pair, down_weight)], "rows", mine, F32, after=[mark])
+    held = inner(1, own[1], g_hidden, held, [g_pair])
+    held_pair = list(inner(0, got[0], g_pair, held_pair, [held[1]]))
+    got[1], held_pair[1] = tie(got[1], held_pair[1])
+    held_pair = inner(1, got[1], g_pair, held_pair, [])
     normed_two, hidden, g_gate, g_up = held
+    normed_pair, hidden_pair, gate_pair, up_pair = held_pair
     resid = jnp.concatenate(resid, 0)
     rms_two = jnp.concatenate(rms_two, 0)
 
-    mine = grid.x.astype(jnp.int32)[None]
+    count_d = 2 * grid.line
     yours = 1 - mine
 
-    early, late = (0, 2), (1, 2)
-
-    def to_pair(a, b, product=dot_tn, piece=(0, 1), after=()):
-        return grad_block(grid.line, yours, a, b, product, piece, None, after)
-
-    def from_pair(a, b, got, product=dot_tn, piece=(0, 1), after=()):
-        return grad_block(grid.line, mine, a, b, product, piece, got, after)
-
-    def swap(x):
-        return lax.ppermute(x, "seq", grid.x_swap)
-
-    s_d0 = to_pair(cotangent, hidden, dot_tn, early)
-    s_d1 = to_pair(cotangent, hidden, dot_tn, late, [s_d0])
-    r_d0, r_d1 = swap(s_d0), swap(s_d1)
-    g_two = matmul([(g_gate, gate_weight), (g_up, up_weight)], True, BF16, after=[s_d1])
-    half = grid.core_sum(g_two, parts)
+    def to_pair(a, b, product=dot_tn, after=()):
+        return grad_block(grid.line, yours, a, b, product, None, after)
+
+    def from_pair(a, b, got, product=dot_tn, after=()):
+        return grad_block(grid.line, mine, a, b, product, got, after)
+
+    kept, sent = matmul(
+        [(gate_pair, gate_weight), (up_pair, up_weight)], "columns", mine, BF16, core
+    )
+    theirs = grid.core_sum(kept, sent)
+    kept, sent = matmul(
+        [(g_gate, gate_weight), (g_up, up_weight)], "columns", mine, BF16, core, after=[kept]
+    )
+    ours = grid.core_sum(kept, sent)
+    w_d = grad_pair(count_d, [(cotangent, hidden), (cot_pair, hidden_pair)], after=[kept])
+    w_g = grad_pair(count_d, [(normed_two, g_gate), (normed_pair, gate_pair)], after=[w_d])
+    theirs = grid.swap(theirs)
+    theirs, w_d, w_g = tie(theirs, w_d, w_g)
+    grad_d = grid.line_scatter(w_d)
+    grad_g = grid.line_scatter(w_g)
+    half = grid.pair_sum(ours, theirs)
     terms = grid.outer_terms(half)
-    s_g0 = to_pair(normed_two, g_gate, dot_tn, early, [g_two])
-    s_g1 = to_pair(normed_two, g_gate, dot_tn, late, [s_g0])
-    r_g0, r_g1 = swap(s_g0), swap(s_g1)
-    k_d0 = from_pair(cotangent, hidden, r_d0, dot_tn, early, [s_g1])
-    grad_d0 = grid.line_scatter(k_d0)
-    s_u0 = to_pair(normed_two, g_up, dot_tn, early, [k_d0])
-    s_u1 = to_pair(normed_two, g_up, dot_tn, late, [s_u0])
-    r_u0, r_u1 = swap(s_u0), swap(s_u1)
-    down = matmul([(hidden, down_weight)], False, BF16, after=[s_u1])
-    terms[-1], down = tie(terms[-1], down)
+    down_theirs = matmul([(hidden_pair, down_weight)], "inner", mine, BF16, core, after=[half])
+    down_ours = matmul([(hidden, down_weight)], "inner", mine, BF16, core, after=[down_theirs[0]])
+    w_u = grad_pair(
+        count_d, [(normed_two, g_up), (normed_pair, up_pair)], after=[down_ours[0]]
+    )
+    terms[-1], w_u, *down_ours = tie(terms[-1], w_u, *down_ours)
+    grad_u = grid.line_scatter(w_u)
 
     g_two = add(terms)
     norm2_part = jnp.sum(g_two * resid * rms_two, 0)
     s_two = g_two * g2
     g_resid = (
-        grid.own_rows(cotangent, parts).astype(F32)
+        cot_own.astype(F32)
         + rms_two * s_two
         - resid * rms_two**3 * jnp.mean(resid * s_two, -1, keepdims=True)
     )
     own_attn = g_resid.astype(BF16)
     g_attn = grid.gather_rows(own_attn, parts)
-    k_d1 = from_pair(cotangent, hidden, r_d1, dot_tn, late, [own_attn])
-    grad_d1 = grid.line_scatter(k_d1)
-    half = grid.core_sum(down, parts)
-    down_terms = grid.outer_terms(half)
+    down_got = grid.swap(grid.core_sum(*down_theirs))
+    down_half = grid.core_sum(*down_ours)
     weight_qkv = jnp.concatenate([query_weight, key_weight, value_weight], 1)
     weight_qkv = (weight_qkv.astype(F32) + dot(down_all, up_all)).astype(BF16)
     g_attn, weight_qkv = tie(g_attn, weight_qkv)
 
     g_heads = dot_nt(weight_o, g_attn, BF16)
     g_q, featq_part, gk, gv, gphi, first = call(
+        24.0,
         attend_back_kernel,
         [
             ((qw, rows), BF16),
@@ -726,53 +800,58 @@
             ((kw, length), F32),
             ((kw, length), F32),
             ((hk, phi_dim, length), F32),
-            ((hk, phi_dim, phi_dim), F32),
+            ((hk, hd + 16, phi_dim), F32),
         ],
         (
             query, kv, phi_cols, phi, key, value, query_map_t, query_map, states, heads,
             totals, g_heads, opened, keep, cont,
         ),
-        scratch=[((qw, rows), BF16), ((hk, phi_dim, phi_dim), F32)],
+        scratch=[((qw, rows), BF16), ((hk, phi_dim, hd + 16), F32)],
         smem=(14,),
-        after=[half, k_d1],
-    )
-    later, near = grid.sum_before(first, -1)
+        after=[grad_d],
+    )
+    first, down_got, down_half = tie(first, down_got, down_half)
+    down_half = grid.pair_sum(down_half, down_got)
+    later, near = grid.sum_before(first, -1, BF16)
     back = [gk[:, :CHUNK], gv[:, :CHUNK], gphi[:, :, :CHUNK].reshape(hk * phi_dim, CHUNK)]
     back = grid.shift_seq(jnp.concatenate(back, 0).astype(BF16), -1)
     s_o = to_pair(g_attn, heads, dot_tt, after=[g_q])
-    r_o = swap(s_o)
-    k_g0 = from_pair(normed_two, g_gate, r_g0, dot_tn, early, [s_o, grad_d0])
-    grad_g0 = grid.line_scatter(k_g0)
+    r_o = grid.swap(s_o)
     g_kv, featk_part = call(
+        2.0,
         key_back_kernel,
         [((2 * kw, rows), BF16), ((hk, hd, hd), F32)],
         (kv, phi_cols, key_map_t, key_map, gk, gv, gphi, back, later, later - near, keep_all),
-        after=[k_g0],
+        after=[s_o],
     )
 
     g_qkv = jnp.concatenate([g_q, g_kv], 0)
-    g_one = dot_tt(g_qkv, weight_qkv, BF16)
-    terms = grid.outer_terms(grid.core_sum(g_one, parts))
-    s_qkv = to_pair(normed_one, g_qkv, dot_tt, after=[g_one])
-    k_g1 = from_pair(normed_two, g_gate, r_g1, dot_tn, late, [s_qkv, grad_d1])
-    grad_g1 = grid.line_scatter(k_g1)
+    kept, sent = matmul([(g_qkv, weight_qkv)], "both", mine, BF16, core)
+    half = grid.core_sum(kept, sent)
+    half, down_half = tie(half, down_half)
+    terms = grid.outer_terms(half)
+    down_terms = grid.outer_terms(down_half)
+    s_qkv = to_pair(normed_one, g_qkv, dot_tt, after=[half])
+    r_qkv = grid.swap(s_qkv)
+    g_late, s_qkv = tie(g_attn, s_qkv)
+    g_low_o = dot_nt(g_late, oup, BF16)
+    low_o = dot_tn(odown, heads, BF16)
+    bo_part = dot(low_o, g_late)
+    ao_part = dot(heads, g_low_o)
+    k_o = from_pair(g_attn, heads, r_o, dot_tt, after=[s_qkv])
     g_low = dot(up_all, g_qkv, BF16)
     a_part = dot(g_low, normed_one)
     b_part = dot_tt(low_all, g_qkv)
     bq_part = b_part[:rank, :qw]
     bk_part = b_part[rank : 2 * rank, qw : qw + kw]
     bv_part = b_part[2 * rank : 3 * rank, qw + kw :]
-    g_low_o = dot_nt(g_attn, oup, BF16)
-    low_o = dot_tn(odown, heads, BF16)
-    bo_part = dot(low_o, g_attn)
-    ao_part = dot(heads, g_low_o)
-    down_terms[-1], s_qkv = tie(down_terms[-1], s_qkv)
-    r_qkv = swap(s_qkv)
-    output = grid.gather_rows((resid + add(down_terms)).astype(BF16), parts)
-    terms[-1], k_g1, a_part, b_part, bo_part, ao_part, output = tie(
-        terms[-1], k_g1, a_part, b_part, bo_part, ao_part, output
-    )
-
+    terms[-1], a_part, b_part, bo_part, ao_part, r_qkv, grad_u, grad_g, k_o = tie(
+        terms[-1], a_part, b_part, bo_part, ao_part, r_qkv, grad_u, grad_g, k_o
+    )
+    grad_o = grid.line_scatter(k_o)
+    k_qkv = from_pair(normed_one, g_qkv, r_qkv, dot_tt, after=[k_o])
+
+    terms[-1], k_qkv = tie(terms[-1], k_qkv)
     stream = grid.own_rows(tokens, parts).astype(F32)
     rms_one = lax.rsqrt(jnp.mean(stream * stream, -1, keepdims=True) + EPSILON)
     g_one = add(terms)
@@ -783,18 +862,17 @@
         + rms_one * s_one
         - stream * rms_one**3 * jnp.mean(stream * s_one, -1, keepdims=True)
     ).astype(BF16)
+    grad_qkv = grid.line_scatter(k_qkv).astype(F32)
+    output = grid.gather_rows((resid + add(down_terms)).astype(BF16), parts)
     grad_tokens = grid.gather_rows(own_grad, parts).astype(F32)
-    k_u0 = from_pair(normed_two, g_up, r_u0, dot_tn, early, [own_grad, grad_g0])
-    grad_u0 = grid.line_scatter(k_u0)
-    k_u1 = from_pair(normed_two, g_up, r_u1, dot_tn, late, [k_u0, grad_g1])
-    grad_u1 = grid.line_scatter(k_u1)
-    k_o = from_pair(g_attn, heads, r_o, dot_tt, after=[k_u1, grad_u0])
-    grad_wo = grid.line_scatter(k_o).astype(F32)
-    k_qkv = from_pair(normed_one, g_qkv, r_qkv, dot_tt, after=[k_o])
-    grad_qkv = grid.line_scatter(k_qkv).astype(F32)
-    grad_gate = jnp.concatenate([grad_g0, grad_g1], 1).astype(F32)
-    grad_up = jnp.concatenate([grad_u0, grad_u1], 1).astype(F32)
-    grad_down = jnp.concatenate([grad_d0.T, grad_d1.T], 0).astype(F32)
+    own_grad, grad_d, grad_g, grad_u = tie(own_grad, grad_d, grad_g, grad_u)
+    down_low, down_high = grid.finish(grad_d)
+    gate_low, gate_high = grid.finish(grad_g)
+    up_low, up_high = grid.finish(grad_u)
+    grad_wo = grad_o.astype(F32)
+    grad_gate = jnp.concatenate([gate_low, gate_high], 1).astype(F32)
+    grad_up = jnp.concatenate([up_low, up_high], 1).astype(F32)
+    grad_down = jnp.concatenate([down_low.T, down_high.T], 0).astype(F32)
 
     n = grid.seq
 
@@ -815,6 +893,7 @@
     ]
     cut = [blocks(x, d) for x, d in both + own]
     summed = grid.scatter_blocks(jnp.concatenate(cut, 1))
+    summed, grad_qkv, grad_wo = tie(summed, grad_qkv, grad_wo)
     n_both = sum(c.shape[1] for c in cut[: len(both)])
     flat = jnp.concatenate([grid.sum_kv(summed[:n_both].astype(BF16)), summed[n_both:]])
     done = []

time: 714 us -> 683 us (0.957)
  waiting for transfers between devices: 222 us -> 143 us
  local copies, waits for them, and re-layouts: 101 us -> 127 us
  other arithmetic: 61.3 us -> 75.2 us
  Pallas kernels: 218 us -> 226 us
  matrix products: 31.5 us -> 24 us
    pallas_call x16 -> x4, Pallas kernels: 84.4 us -> 18.6 us  [grad_block(): pl.pallas_call(kernel, grid_spec=pltpu.PrefetchScalarGridSpec(num_scalar_...]
    pallas_call x4 -> x11, Pallas kernels: 55.4 us -> 118 us  [the longest x8 80 us: matmul(): pl.pallas_call(kernel, grid_spec=pltpu.PrefetchScalarGridSpec(num_scalar_...]
    ppermute x26 -> x66, waiting for transfers between devices: 97.5 us -> 55.3 us  [the longest x8 23.7 us: shift_seq(): return lax.ppermute(x, 'seq', pairs)]
    ppermute x5, waiting for transfers between devices: 73.9 us -> 39.5 us  [outer_terms(): lax.ppermute(half, 'kv', self.y_shift(j))]
    ppermute x1, waiting for transfers between devices: 27.2 us -> 2.47 us  [scatter_blocks(): part = own + lax.ppermute(other, 'seq', self.x_swap).astype(F32)]
    reduce_scatter x8 -> x5, waiting for transfers between devices: 22.9 us -> 44.3 us  [line_scatter(): lax.psum_scatter(part, 'seq', scatter_dimension=0, tiled=True, axis_index...]
    pallas_call x2 -> x4, Pallas kernels: 32.4 us -> 44.4 us  [gated(): pl.pallas_call(gated_kernel, grid_spec=pltpu.PrefetchScalarGridSpec(num_s...]
    slice x1 -> x10, local copies, waits for them, and re-layouts: 4.83 us -> 16.4 us  [across_cores(): cuts = [x[i * rows:(i + 1) * rows] for i in range(pieces)]]
  transfers between devices with their start and end apart: 45 -> 82, of which waited for: 16 -> 29; matrix products, arithmetic and copies ran while one was open for 20% -> 28% of each run, Pallas kernels for 24% -> 26%
where the time goes in v3:
time: 683 us; the launch traced here: 673 us
  Pallas kernels  226 us (33%)
  waiting for transfers between devices  143 us (21%)
  local copies, waits for them, and re-layouts  127 us (19%)
  other arithmetic  75.2 us (11%)
  starting transfers between devices  61.5 us (9%)
  matrix products  24 us (4%)
  between operations  15.6 us (2%)
    pallas_call x8, Pallas kernels, matmul(): pl.pallas_call(kernel, grid_spec=pltpu.PrefetchScalarGridSpec(num_scalar_...  80 us
    unnamed x223, local copies, waits for them, and re-layouts  53.4 us
    pallas_call x4, Pallas kernels, gated(): pl.pallas_call(gated_kernel, grid_spec=pltpu.PrefetchScalarGridSpec(num_s...  44.4 us
    reduce_scatter x5, waiting for transfers between devices, line_scatter(): lax.psum_scatter(part, 'seq', scatter_dimension=0, tiled=True, axis_index...  44.3 us
    ppermute x5, waiting for transfers between devices, outer_terms(): lax.ppermute(half, 'kv', self.y_shift(j))  39.5 us
    pallas_call x3, Pallas kernels, grad_pair(): pl.pallas_call(kernel, grid=(count,), in_specs=specs * len(pairs) + [ANY]...  38 us
    pallas_call x4, Pallas kernels, call(): pl.pallas_call(lambda *refs: kernel(*refs[:count], *refs[count + len(afte...  35.1 us
    ppermute x8, starting transfers between devices, shift_seq(): return lax.ppermute(x, 'seq', pairs)  24.5 us
  transfers between devices with their start and end apart: 82, of which 29 were waited for; matrix products, arithmetic and copies ran while one was open for 28% of the time, Pallas kernels for 26%

profile of v3, /device:TPU:0, one launch (start us, length us, event | category | flops | bytes accessed | tf_op | source)
XLA Modules:
  0.0 673.1 jit_solution(12607873899295729571)
XLA Ops:
  13.8 10.2 %shard_map.373 = (bf16[1024,2048]{1,0:T(8,128)(2,1)}, bf16[512,1024]{1,0:T(8,128)(2,1)S(1)}, bf16[256,1024]{1,0:T(8,128)(2,1)S(1)}, bf16[1024,128]{1,0:T(8,128)(2,1)S(1)}) custom-call(bf16[1024,2048]{1,0:T(8,128)(2,1)} %x_ref.1, bf16[1,2048]{1,0:T(2,128)(2,1)S(1)} %broadcast_in_dim.28.gain_ref, bf16[2048,512]{1,0:T(8,128)(2,1)S(1)} %copy-done.27, ...), custom_call_target="tpu_custom_call" | custom-call | flops 4499999744 | bytes 1 | tf_op jit(solution)/shard_map/pallas_call | solution.py:419
  25.0 4.8 collective-permute-start
  35.6 3.7 add_convert_fusion.9.refs_1_
  39.2 9.7 %shard_map.375.gh_ref = f32[1024,1024]{1,0:T(8,128)} custom-call(s32[2]{0:T(128)} %pad_add_fusion.1.sel, bf16[1024,2048]{1,0:T(8,128)(2,1)} %refs_0_.3, bf16[2048,2048]{1,0:T(8,128)(2,1)} %refs_1_.11), custom_call_target="tpu_custom_call" | custom-call | flops 1899551488 | bytes 1 | tf_op jit(solution)/shard_map/pallas_call | solution.py:481
  56.6 5.2 collective-permute-start.2
  63.9 5.5 collective-permute-start.3
  72.5 9.1 %shard_map.376 = (bf16[512,1024]{1,0:T(8,128)(2,1)S(1)}, f32[8,1024]{1,0:T(8,128)S(1)}, f32[8,2,80,128]{3,2,1,0:T(8,128)S(1)}) custom-call(bf16[512,1024]{1,0:T(8,128)(2,1)S(1)} %copy-done.38, bf16[256,1152]{1,0:T(8,128)(2,1)S(1)} %constant_dynamic-update-slice_fusion.refs_0_.refs_1_, bf16[2,128,1152]{2,1,0:T(8,128)(2,1)S(1)} %get-tuple-element.117.refs_2_.refs_1_, ...), custom_call_target="tpu_custom_call" | custom-call | flops 4049999872 | bytes 1 | tf_op jit(solution)/shard_map/pallas_call | solution.py:381
  83.5 6.5 shard_map.377
  101.4 21.8 %collective-permute-done.13 = bf16[256,2048]{1,0:T(8,128)(2,1)S(1)} collective-permute-done((bf16[256,2048]{1,0:T(8,128)(2,1)S(1)}, bf16[256,2048]{1,0:T(8,128)(2,1)S(1)}, u32[]{:S(2)}, u32[]{:S(2)}) %collective-permute-start.13) | collective-permute-done | bytes 1048608 | tf_op jit(solution)/shard_map/ppermute | solution.py:92
  123.2 17.4 %collective-permute-done.12 = bf16[512,2048]{1,0:T(8,128)(2,1)S(1)} collective-permute-done((bf16[512,2048]{1,0:T(8,128)(2,1)S(1)}, bf16[512,2048]{1,0:T(8,128)(2,1)S(1)}, u32[]{:S(2)}, u32[]{:S(2)}) %collective-permute-start.12) | collective-permute-done | bytes 2097184 | tf_op jit(solution)/shard_map/ppermute | solution.py:86
  145.7 10.9 %shard_map.378 = (bf16[1024,2048]{1,0:T(8,128)(2,1)}, bf16[1024,1024]{1,0:T(8,128)(2,1)}, bf16[1024,1024]{1,0:T(8,128)(2,1)}, bf16[1024,1024]{1,0:T(8,128)(2,1)}) custom-call(s32[2]{0:T(128)} %pad_add_fusion.3.sel_ref, bf16[256,2048]{1,0:T(8,128)(2,1)} %multiply_convert_fusion.1.own_ref, bf16[256,2048]{1,0:T(8,128)(2,1)} %collective-permute-done.15.other_ref, ...), custom_call_target="tpu_custom_call" | custom-call | flops 4950000128 | bytes 1 | tf_op jit(solution)/shard_map/pallas_call | solution.py:588
  156.5 12.0 %collective-permute-done.14 = bf16[256,2048]{1,0:T(8,128)(2,1)} collective-permute-done((bf16[256,2048]{1,0:T(8,128)(2,1)}, bf16[256,2048]{1,0:T(8,128)(2,1)}, u32[]{:S(2)}, u32[]{:S(2)}) %collective-permute-start.14) | collective-permute-done | bytes 1048608 | tf_op jit(solution)/shard_map/ppermute | solution.py:92
  184.7 9.6 %shard_map.379.refs_4_.gh_ref = f32[1024,1024]{1,0:T(8,128)} custom-call(s32[2]{0:T(128)} %pad_add_fusion.1.sel, bf16[1024,2048]{1,0:T(8,128)(2,1)} %bitcast.168, bf16[2048,2048]{1,0:T(8,128)(2,1)} %refs_1_.11, bf16[256,2048]{1,0:T(8,128)(2,1)} %multiply_convert_fusion.refs_2_.own_ref), custom_call_target="tpu_custom_call" | custom-call | flops 1899551488 | bytes 1 | tf_op jit(solution)/shard_map/pallas_call | solution.py:481
  195.3 11.2 %shard_map.380 = (bf16[1024,2048]{1,0:T(8,128)(2,1)}, bf16[1024,1024]{1,0:T(8,128)(2,1)}, bf16[1024,1024]{1,0:T(8,128)(2,1)}, bf16[1024,1024]{1,0:T(8,128)(2,1)}) custom-call(s32[2]{0:T(128)} %pad_add_fusion.3.sel_ref, ...), custom_call_target="tpu_custom_call", output_to_operand_aliasing={{0}: (6, {}), {1}: (7, {}), {2}: (8, {}), {3}: (9, {})} | custom-call | flops 4950000128 | bytes 1 | tf_op jit(solution)/shard_map/pallas_call | solution.py:588
  207.4 11.2 %shard_map.381 = (bf16[1024,2048]{1,0:T(8,128)(2,1)}, bf16[1024,1024]{1,0:T(8,128)(2,1)}, bf16[1024,1024]{1,0:T(8,128)(2,1)}, bf16[1024,1024]{1,0:T(8,128)(2,1)}) custom-call(s32[2]{0:T(128)} %pad_add_fusion.3.sel_ref, bf16[256,2048]{1,0:T(8,128)(2,1)} %collective-permute-done.22.own_ref, bf16[256,2048]{1,0:T(8,128)(2,1)} %copy-done.76, ...), custom_call_target="tpu_custom_call" | custom-call | flops 4950000128 | bytes 1 | tf_op jit(solution)/shard_map/pallas_call | solution.py:588
  222.4 11.2 %shard_map.382 = (bf16[1024,2048]{1,0:T(8,128)(2,1)}, bf16[1024,1024]{1,0:T(8,128)(2,1)}, bf16[1024,1024]{1,0:T(8,128)(2,1)}, bf16[1024,1024]{1,0:T(8,128)(2,1)}) custom-call(s32[2]{0:T(128)} %pad_add_fusion.3.sel_ref, bf16[256,2048]{1,0:T(8,128)(2,1)} %copy-done.74, ...), custom_call_target="tpu_custom_call", output_to_operand_aliasing={{0}: (6, {}), {1}: (7, {}), {2}: (8, {}), {3}: (9, {})} | custom-call | flops 4950000128 | bytes 1 | tf_op jit(solution)/shard_map/pallas_call | solution.py:588
  233.5 14.0 %shard_map.383 = (bf16[512,2048]{1,0:T(8,128)(2,1)}, bf16[512,2048]{1,0:T(8,128)(2,1)}) custom-call(s32[2]{0:T(128)} %pad_add_fusion.sel, bf16[1024,1024]{1,0:T(8,128)(2,1)} %get-tuple-element.152.refs_0_.refs_3_, bf16[2048,2048]{1,0:T(8,128)(2,1)} %refs_1_.9, bf16[1024,1024]{1,0:T(8,128)(2,1)} %get-tuple-element.153.refs_2_.refs_3_, bf16[2048,2048]{1,0:T(8,128)(2,1)} %refs_3_.4), custom_call_target="tpu_custom_call" | custom-call | flops 3349102848 | bytes 1 | tf_op jit(solution)/shard_map/pallas_call | solution.py:481
  257.1 14.5 %shard_map.384 = (bf16[512,2048]{1,0:T(8,128)(2,1)}, bf16[512,2048]{1,0:T(8,128)(2,1)}) custom-call(s32[2]{0:T(128)} %pad_add_fusion.sel, bf16[1024,1024]{1,0:T(8,128)(2,1)} %get-tuple-element.143.refs_0_.refs_1_, bf16[2048,2048]{1,0:T(8,128)(2,1)} %refs_1_.9, bf16[1024,1024]{1,0:T(8,128)(2,1)} %get-tuple-element.144.refs_2_.refs_1_, ...), custom_call_target="tpu_custom_call" | custom-call | flops 3349102848 | bytes 1 | tf_op jit(solution)/shard_map/pallas_call | solution.py:481
  271.6 12.7 %shard_map.385.refs_4_ = bf16[2048,1024]{1,0:T(8,128)(2,1)} custom-call(bf16[1024,2048]{1,0:T(8,128)(2,1)} %refs_0_.3, bf16[1024,1024]{1,0:T(8,128)(2,1)S(1)} %copy-done.3, bf16[1024,2048]{1,0:T(8,128)(2,1)} %bitcast.169, bf16[1024,1024]{1,0:T(8,128)(2,1)S(1)} %copy-done.10, bf16[512,2048]{1,0:T(8,128)(2,1)} %get-tuple-element.155.refs_4_), custom_call_target="tpu_custom_call" | custom-call | flops 5849999872 | bytes 1 | tf_op jit(solution)/shard_map/pallas_call | solution.py:508
  287.4 12.7 %shard_map.386 = bf16[2048,1024]{1,0:T(8,128)(2,1)} custom-call(bf16[1024,2048]{1,0:T(8,128)(2,1)} %get-tuple-element.159.refs_0_, bf16[1024,1024]{1,0:T(8,128)(2,1)S(1)} %copy-done.8, bf16[1024,2048]{1,0:T(8,128)(2,1)} %get-tuple-element.160.refs_2_, bf16[1024,1024]{1,0:T(8,128)(2,1)S(1)} %copy-done.11, bf16[2048,1024]{1,0:T(8,128)(2,1)} %shard_map.385.refs_4_), custom_call_target="tpu_custom_call" | custom-call | flops 5849999872 | bytes 1 | tf_op jit(solution)/shard_map/pallas_call | solution.py:508
  300.1 3.8 collective-permute-done.33
  310.0 4.1 add_convert_fusion.refs_1_
  314.1 4.0 add_convert_fusion.6.refs_2_
  319.7 8.7 %shard_map.387 = (bf16[512,2048]{1,0:T(8,128)(2,1)}, bf16[512,2048]{1,0:T(8,128)(2,1)}) custom-call(s32[2]{0:T(128)} %pad_add_fusion.sel, bf16[1024,1024]{1,0:T(8,128)(2,1)} %get-tuple-element.158.refs_3_.refs_0_, bf16[2048,2048]{1,0:T(8,128)(2,1)} %refs_1_.11, bf16[512,2048]{1,0:T(8,128)(2,1)} %add_convert_fusion.6.refs_2_), custom_call_target="tpu_custom_call" | custom-call | flops 1899551488 | bytes 1 | tf_op jit(solution)/shard_map/pallas_call | solution.py:481
  332.3 9.3 %shard_map.388 = (bf16[512,2048]{1,0:T(8,128)(2,1)}, bf16[512,2048]{1,0:T(8,128)(2,1)}) custom-call(s32[2]{0:T(128)} %pad_add_fusion.sel, bf16[1024,1024]{1,0:T(8,128)(2,1)} %get-tuple-element.145.refs_0_.refs_1_, bf16[2048,2048]{1,0:T(8,128)(2,1)} %refs_1_.11, bf16[512,2048]{1,0:T(8,128)(2,1)} %get-tuple-element.162.refs_2_), custom_call_target="tpu_custom_call" | custom-call | flops 1899551488 | bytes 1 | tf_op jit(solution)/shard_map/pallas_call | solution.py:481
  341.6 12.7 %shard_map.389 = bf16[2048,1024]{1,0:T(8,128)(2,1)} custom-call(bf16[1024,2048]{1,0:T(8,128)(2,1)} %get-tuple-element.159.refs_0_, bf16[1024,1024]{1,0:T(8,128)(2,1)S(1)} %copy-done.9, bf16[1024,2048]{1,0:T(8,128)(2,1)} %get-tuple-element.160.refs_2_, bf16[1024,1024]{1,0:T(8,128)(2,1)S(1)} %copy-done.12, bf16[512,2048]{1,0:T(8,128)(2,1)} %get-tuple-element.174.refs_4_), custom_call_target="tpu_custom_call" | custom-call | flops 5849999872 | bytes 1 | tf_op jit(solution)/shard_map/pallas_call | solution.py:508
  354.4 4.7 add_convert_fusion.5
  360.4 5.7 collective-permute-done.34
  366.1 3.8 multiply_reduce_fusion
  370.0 5.0 fusion.31
  388.1 3.9 add_convert_fusion.4
  397.5 23.4 %shard_map.390 = (bf16[512,1024]{1,0:T(8,128)(2,1)}, f32[8,64,64]{2,1,0:T(8,128)S(1)}, f32[128,1152]{1,0:T(8,128)S(1)}, f32[128,1152]{1,0:T(8,128)S(1)}, f32[2,1...) custom-call(bf16[512,1024]{1,0:T(8,128)(2,1)} %copy-done.37, ...), custom_call_target="tpu_custom_call" | custom-call | flops 10800000000 | bytes 1 | tf_op jit(solution)/shard_map/pallas_call | solution.py:381
  429.6 13.8 %collective-permute-done.50 = bf16[2,80,128]{2,1,0:T(8,128)(2,1)S(1)} collective-permute-done((bf16[2,80,128]{2,1,0:T(8,128)(2,1)S(1)}, bf16[2,80,128]{2,1,0:T(8,128)(2,1)S(1)}, u32[]{:S(2)}, u32[]{:S(2)}) %collective-permute-start.50) | collective-permute-done | bytes 40992 | tf_op jit(solution)/shard_map/ppermute | solution.py:141
  445.0 4.6 shard_map.391.refs_11_
  455.6 7.7 %shard_map.393 = (bf16[512,2048]{1,0:T(8,128)(2,1)}, bf16[512,2048]{1,0:T(8,128)(2,1)}) custom-call(s32[2]{0:T(128)} %pad_add_fusion.sel, bf16[768,1024]{1,0:T(8,128)(2,1)} %copy-done.1, bf16[2048,768]{1,0:T(8,128)(2,1)} %add_convert_fusion.refs_1_), custom_call_target="tpu_custom_call" | custom-call | flops 1537163648 | bytes 1 | tf_op jit(solution)/shard_map/pallas_call | solution.py:481
  466.1 4.0 add_convert_fusion.2
  477.1 4.9 shard_map.394.rest_1_
  485.2 4.2 fusion.9
  490.1 3.7 fusion.10
  493.8 4.3 fusion.11
  498.1 3.8 shard_map.395.rest_1_
  502.9 44.3 %reduce-scatter.8.cloned.1.call-done = bf16[512,1024]{1,0:T(8,128)(2,1)} async-done(((bf16[2048,1024]{1,0:T(8,128)(2,1)}), bf16[512,1024]{1,0:T(8,128)(2,1)}) %reduce-scatter.8.cloned.1.call-update) | async-done | bytes 1048592 | tf_op jit(solution)/shard_map/reduce_scatter | solution.py:114
  548.9 5.2 shard_map.396
  554.1 5.4 fusion.6
  559.6 4.5 fusion.3
  628.9 3.8 broadcast_select_fusion.1
  632.7 3.8 maximum_convert_fusion
  638.5 8.1 %copy.138 = f32[2,2,256,2048]{3,2,1,0:T(8,128)} copy(f32[2,2,256,2048]{3,2,0,1:T(8,128)} %maximum_convert_fusion) | data formatting | bytes 16777216 | tf_op jit(solution)/shard_map/convert_element_type | solution.py:867
  (537 shorter events, 228.4 us)
Async XLA Ops:
  7.2 388.1 %reduce-scatter.6.cloned.1.call-start = ((), (), s32[]{:S(2)}) async-start(), calls=%async_computation.5 | async-start | bytes 5242880 | tf_op jit(solution)/shard_map/reduce_scatter | solution.py:114
  25.0 24.1 %collective-permute-start = (bf16[256,128]{1,0:T(8,128)(2,1)S(1)}, bf16[256,128]{1,0:T(8,128)(2,1)S(1)}, u32[]{:S(2)}, u32[]{:S(2)}) collective-permute-start(bf16[256,128]{1,0:T(8,128)(2,1)S(1)} %slice.329), channel_id=1, source_target_pairs={{0,4},{4,8},{8,12},{12,16},{16,20},{20,24},{24,28},{1,5},{5,9},{9,... | collective-permute-start | bytes 196616 | tf_op jit(solution)/shard_map/ppermute | solution.py:141
  51.1 5.5 collective-permute-start.1
  56.6 7.3 %collective-permute-start.2 = (f32[2,80,128]{2,1,0:T(8,128)S(1)}, f32[2,80,128]{2,1,0:T(8,128)S(1)}, u32[]{:S(2)}, u32[]{:S(2)}) collective-permute-start(f32[2,80,128]{2,1,0:T(8,128)S(1)} %add.245), channel_id=1, source_target_pairs={{0,8},{4,12},{8,16},{12,20},{16,24},{20,28},{1,9},{5,13},{9,17},{1... | collective-permute-start | bytes 245768 | tf_op jit(solution)/shard_map/ppermute | solution.py:141
  63.9 7.3 %collective-permute-start.3 = (f32[2,80,128]{2,1,0:T(8,128)S(1)}, f32[2,80,128]{2,1,0:T(8,128)S(1)}, u32[]{:S(2)}, u32[]{:S(2)}) collective-permute-start(f32[2,80,128]{2,1,0:T(8,128)S(1)} %add.246), channel_id=1, source_target_pairs={{0,16},{4,20},{8,24},{12,28},{1,17},{5,21},{9,25},{13,29},{2,18},{... | collective-permute-start | bytes 245768 | tf_op jit(solution)/shard_map/ppermute | solution.py:141
  93.0 47.6 %collective-permute-start.12 = (bf16[512,2048]{1,0:T(8,128)(2,1)S(1)}, bf16[512,2048]{1,0:T(8,128)(2,1)S(1)}, u32[]{:S(2)}, u32[]{:S(2)}) collective-permute-start(bf16[512,2048]{1,0:T(8,128)(2,1)S(1)} %bitcast.171), channel_id=1, source_target_pairs={{0,4},{4,0},{8,12},{12,8},{16,20},{20,16},{24,28},{28,24},{1,5},{5... | collective-permute-start | bytes 6291464 | tf_op jit(solution)/shard_map/ppermute | solution.py:86
  98.0 25.2 %collective-permute-start.13 = (bf16[256,2048]{1,0:T(8,128)(2,1)S(1)}, bf16[256,2048]{1,0:T(8,128)(2,1)S(1)}, u32[]{:S(2)}, u32[]{:S(2)}) collective-permute-start(bf16[256,2048]{1,0:T(8,128)(2,1)S(1)} %get-tuple-element.354), channel_id=1, source_target_pairs={{0,2},{1,3},{2,0},{3,1},{4,6},{5,7},{6,4},{7,5},{8,10},{9,11},{10,... | collective-permute-start | bytes 3145736 | tf_op jit(solution)/shard_map/ppermute | solution.py:92
  142.7 25.9 %collective-permute-start.14 = (bf16[256,2048]{1,0:T(8,128)(2,1)}, bf16[256,2048]{1,0:T(8,128)(2,1)}, u32[]{:S(2)}, u32[]{:S(2)}) collective-permute-start(bf16[256,2048]{1,0:T(8,128)(2,1)} %get-tuple-element.129), channel_id=1, source_target_pairs={{0,2},{1,3},{2,0},{3,1},{4,6},{5,7},{6,4},{7,5},{8,10},{9,11},{10,... | collective-permute-start | bytes 3145736 | tf_op jit(solution)/shard_map/ppermute | solution.py:92
  144.8 33.7 %collective-permute-start.22 = (bf16[256,2048]{1,0:T(8,128)(2,1)}, bf16[256,2048]{1,0:T(8,128)(2,1)}, u32[]{:S(2)}, u32[]{:S(2)}) collective-permute-start(bf16[256,2048]{1,0:T(8,128)(2,1)} %multiply_convert_fusion.1.own_ref), channel_id=1, source_target_pairs={{0,4},{4,0},{8,12},{12,8},{16,20},{20,16},{24,28},{28,24},{1,5},{5... | collective-permute-start | bytes 3145736 | tf_op jit(solution)/shard_map/ppermute | solution.py:86
  173.5 5.7 collective-permute-start.18
  174.1 6.5 collective-permute-start.19
  174.1 20.3 %collective-permute-start.16 = (bf16[256,2048]{1,0:T(8,128)(2,1)}, bf16[256,2048]{1,0:T(8,128)(2,1)S(1)}, u32[]{:S(2)}, u32[]{:S(2)}) collective-permute-start(bf16[256,2048]{1,0:T(8,128)(2,1)} %multiply_convert_fusion.refs_2_.own_ref), channel_id=1, source_target_pairs={{0,1},{1,0},{2,3},{3,2},{4,5},{5,4},{6,7},{7,6},{8,9},{9,8},{10,11... | collective-permute-start | bytes 3145736 | tf_op jit(solution)/shard_map/ppermute | solution.py:79
  178.5 40.1 %collective-permute-start.21 = (bf16[256,2048]{1,0:T(8,128)(2,1)}, bf16[256,2048]{1,0:T(8,128)(2,1)S(1)}, u32[]{:S(2)}, u32[]{:S(2)}) collective-permute-start(bf16[256,2048]{1,0:T(8,128)(2,1)} %multiply_convert_fusion.refs_2_.own_ref), channel_id=1, source_target_pairs={{0,4},{4,0},{8,12},{12,8},{16,20},{20,16},{24,28},{28,24},{1,5},{5... | collective-permute-start | bytes 3145736 | tf_op jit(solution)/shard_map/ppermute | solution.py:86
  179.3 27.2 %collective-permute-start.23 = (bf16[256,2048]{1,0:T(8,128)(2,1)}, bf16[256,2048]{1,0:T(8,128)(2,1)S(1)}, u32[]{:S(2)}, u32[]{:S(2)}) collective-permute-start(bf16[256,2048]{1,0:T(8,128)(2,1)} %collective-permute-done.22.own_ref), channel_id=1, source_target_pairs={{0,1},{1,0},{2,3},{3,2},{4,5},{5,4},{6,7},{7,6},{8,9},{9,8},{10,11... | collective-permute-start | bytes 3145736 | tf_op jit(solution)/shard_map/ppermute | solution.py:79
  255.7 48.2 %collective-permute-start.33 = (bf16[512,2048]{1,0:T(8,128)(2,1)}, bf16[512,2048]{1,0:T(8,128)(2,1)}, u32[]{:S(2)}, u32[]{:S(2)}) collective-permute-start(bf16[512,2048]{1,0:T(8,128)(2,1)} %add_convert_fusion.7), channel_id=1, source_target_pairs={{0,4},{4,0},{8,12},{12,8},{16,20},{20,16},{24,28},{28,24},{1,5},{5... | collective-permute-start | bytes 6291464 | tf_op jit(solution)/shard_map/ppermute | solution.py:86
  303.9 199.0 %reduce-scatter.10.cloned.1.call-start = ((), (), s32[]{:S(2)}) async-start(), calls=%async_computation.7 | async-start | bytes 5242880 | tf_op jit(solution)/shard_map/reduce_scatter | solution.py:114
  304.7 242.5 %reduce-scatter.8.cloned.1.call-start = ((), (), s32[]{:S(2)}) async-start(), calls=%async_computation.6 | async-start | bytes 5242880 | tf_op jit(solution)/shard_map/reduce_scatter | solution.py:114
  308.3 5.8 collective-permute-start.25
  308.3 5.8 collective-permute-start.26
  308.8 5.3 collective-permute-start.28
  318.1 48.0 %collective-permute-start.34 = (bf16[512,2048]{1,0:T(8,128)(2,1)}, bf16[512,2048]{1,0:T(8,128)(2,1)}, u32[]{:S(2)}, u32[]{:S(2)}) collective-permute-start(bf16[512,2048]{1,0:T(8,128)(2,1)} %add_convert_fusion.6.refs_2_), channel_id=1, source_target_pairs={{0,2},{1,3},{2,0},{3,1},{4,6},{5,7},{6,4},{7,5},{8,10},{9,11},{10,... | collective-permute-start | bytes 6291464 | tf_op jit(solution)/shard_map/ppermute | solution.py:92
  331.3 23.1 %collective-permute-start.40 = (bf16[128,2048]{1,0:T(8,128)(2,1)}, bf16[128,2048]{1,0:T(8,128)(2,1)}, u32[]{:S(2)}, u32[]{:S(2)}) collective-permute-start(bf16[128,2048]{1,0:T(8,128)(2,1)} %get-tuple-element.334), channel_id=1, source_target_pairs={{0,1},{1,0},{2,3},{3,2},{4,5},{5,4},{6,7},{7,6},{8,9},{9,8},{10,11... | collective-permute-start | bytes 1572872 | tf_op jit(solution)/shard_map/ppermute | solution.py:79
  331.3 23.1 %collective-permute-start.41 = (bf16[128,2048]{1,0:T(8,128)(2,1)}, bf16[128,2048]{1,0:T(8,128)(2,1)}, u32[]{:S(2)}, u32[]{:S(2)}) collective-permute-start(bf16[128,2048]{1,0:T(8,128)(2,1)} %get-tuple-element.337), channel_id=1, source_target_pairs={{0,1},{1,0},{2,3},{3,2},{4,5},{5,4},{6,7},{7,6},{8,9},{9,8},{10,11... | collective-permute-start | bytes 1572872 | tf_op jit(solution)/shard_map/ppermute | solution.py:79
  331.8 22.6 %collective-permute-start.42 = (bf16[128,2048]{1,0:T(8,128)(2,1)}, bf16[128,2048]{1,0:T(8,128)(2,1)}, u32[]{:S(2)}, u32[]{:S(2)}) collective-permute-start(bf16[128,2048]{1,0:T(8,128)(2,1)} %get-tuple-element.336), channel_id=1, source_target_pairs={{0,1},{1,0},{2,3},{3,2},{4,5},{5,4},{6,7},{7,6},{8,9},{9,8},{10,11... | collective-permute-start | bytes 1572872 | tf_op jit(solution)/shard_map/ppermute | solution.py:79
  331.8 22.6 %collective-permute-start.43 = (bf16[128,2048]{1,0:T(8,128)(2,1)}, bf16[128,2048]{1,0:T(8,128)(2,1)}, u32[]{:S(2)}, u32[]{:S(2)}) collective-permute-start(bf16[128,2048]{1,0:T(8,128)(2,1)} %get-tuple-element.335), channel_id=1, source_target_pairs={{0,1},{1,0},{2,3},{3,2},{4,5},{5,4},{6,7},{7,6},{8,9},{9,8},{10,11... | collective-permute-start | bytes 1572872 | tf_op jit(solution)/shard_map/ppermute | solution.py:79
  359.0 61.9 %collective-permute-start.44 = (bf16[512,2048]{1,0:T(8,128)(2,1)}, bf16[512,2048]{1,0:T(8,128)(2,1)}, u32[]{:S(2)}, u32[]{:S(2)}) collective-permute-start(bf16[512,2048]{1,0:T(8,128)(2,1)} %add_convert_fusion.5), channel_id=1, source_target_pairs={{0,4},{4,0},{8,12},{12,8},{16,20},{20,16},{24,28},{28,24},{1,5},{5... | collective-permute-start | bytes 6291464 | tf_op jit(solution)/shard_map/ppermute | solution.py:86
  379.5 6.9 %collective-permute-start.45 = (bf16[128,2048]{1,0:T(8,128)(2,1)}, bf16[128,2048]{1,0:T(8,128)(2,1)}, u32[]{:S(2)}, u32[]{:S(2)}) collective-permute-start(bf16[128,2048]{1,0:T(8,128)(2,1)} %get-tuple-element.330), channel_id=1, source_target_pairs={{0,1},{1,0},{2,3},{3,2},{4,5},{5,4},{6,7},{7,6},{8,9},{9,8},{10,11... | collective-permute-start | bytes 1572872 | tf_op jit(solution)/shard_map/ppermute | solution.py:79
  380.6 271.3 %reduce-scatter.14.cloned.1.call-start = ((), (), s32[]{:S(2)}) async-start(), calls=%async_computation.9 | async-start | bytes 1310720 | tf_op jit(solution)/shard_map/reduce_scatter | solution.py:114
  420.9 6.0 collective-permute-start.49
  423.3 28.8 %collective-permute-start.39 = (bf16[512,128]{1,0:T(8,128)(2,1)S(1)}, bf16[512,128]{1,0:T(8,128)(2,1)S(1)}, u32[]{:S(2)}, u32[]{:S(2)}) collective-permute-start(bf16[512,128]{1,0:T(8,128)(2,1)S(1)} %pad_maximum_fusion.4), channel_id=1, source_target_pairs={{4,0},{8,4},{12,8},{16,12},{20,16},{24,20},{28,24},{5,1},{9,5},{13... | collective-permute-start | bytes 393224 | tf_op jit(solution)/shard_map/ppermute | solution.py:141
  427.0 16.4 %collective-permute-start.50 = (bf16[2,80,128]{2,1,0:T(8,128)(2,1)S(1)}, bf16[2,80,128]{2,1,0:T(8,128)(2,1)S(1)}, u32[]{:S(2)}, u32[]{:S(2)}) collective-permute-start(bf16[2,80,128]{2,1,0:T(8,128)(2,1)S(1)} %fusion.22), channel_id=1, source_target_pairs={{8,0},{12,4},{16,8},{20,12},{24,16},{28,20},{9,1},{13,5},{17,9},{2... | collective-permute-start | bytes 122888 | tf_op jit(solution)/shard_map/ppermute | solution.py:141
  443.4 8.7 %collective-permute-start.51 = (bf16[2,80,128]{2,1,0:T(8,128)(2,1)S(1)}, bf16[2,80,128]{2,1,0:T(8,128)(2,1)S(1)}, u32[]{:S(2)}, u32[]{:S(2)}) collective-permute-start(bf16[2,80,128]{2,1,0:T(8,128)(2,1)S(1)} %fusion.21), channel_id=1, source_target_pairs={{16,0},{20,4},{24,8},{28,12},{17,1},{21,5},{25,9},{29,13},{18,2},{... | collective-permute-start | bytes 122888 | tf_op jit(solution)/shard_map/ppermute | solution.py:141
  449.6 48.5 %collective-permute-start.63 = (bf16[1024,512]{1,0:T(8,128)(2,1)}, bf16[1024,512]{1,0:T(8,128)(2,1)}, u32[]{:S(2)}, u32[]{:S(2)}) collective-permute-start(bf16[1024,512]{1,0:T(8,128)(2,1)} %shard_map.391.refs_11_), channel_id=1, source_target_pairs={{0,4},{4,0},{8,12},{12,8},{16,20},{20,16},{24,28},{28,24},{1,5},{5... | collective-permute-start | bytes 3145736 | tf_op jit(solution)/shard_map/ppermute | solution.py:86
  472.4 74.8 %collective-permute-start.61 = (bf16[512,2048]{1,0:T(8,128)(2,1)}, bf16[512,2048]{1,0:T(8,128)(2,1)}, u32[]{:S(2)}, u32[]{:S(2)}) collective-permute-start(bf16[512,2048]{1,0:T(8,128)(2,1)} %add_convert_fusion.3.rest_0_), channel_id=1, source_target_pairs={{0,2},{1,3},{2,0},{3,1},{4,6},{5,7},{6,4},{7,5},{8,10},{9,11},{10,... | collective-permute-start | bytes 6291464 | tf_op jit(solution)/shard_map/ppermute | solution.py:92
  482.0 65.1 %collective-permute-start.62 = (bf16[1024,768]{1,0:T(8,128)(2,1)}, bf16[1024,768]{1,0:T(8,128)(2,1)}, u32[]{:S(2)}, u32[]{:S(2)}) collective-permute-start(bf16[1024,768]{1,0:T(8,128)(2,1)} %shard_map.394.rest_1_), channel_id=1, source_target_pairs={{0,4},{4,0},{8,12},{12,8},{16,20},{20,16},{24,28},{28,24},{1,5},{5... | collective-permute-start | bytes 4718600 | tf_op jit(solution)/shard_map/ppermute | solution.py:86
  489.4 99.5 %collective-permute-start.56 = (bf16[512,2048]{1,0:T(8,128)(2,1)}, bf16[512,2048]{1,0:T(8,128)(2,1)}, u32[]{:S(2)}, u32[]{:S(2)}) collective-permute-start(bf16[512,2048]{1,0:T(8,128)(2,1)} %add_convert_fusion.2), channel_id=1, source_target_pairs={{0,2},{1,3},{2,0},{3,1},{4,6},{5,7},{6,4},{7,5},{8,10},{9,11},{10,... | collective-permute-start | bytes 6291464 | tf_op jit(solution)/shard_map/ppermute | solution.py:92
  547.2 105.7 %reduce-scatter.12.cloned.1.call-start = ((), (), s32[]{:S(2)}) async-start(), calls=%async_computation.8 | async-start | bytes 1966080 | tf_op jit(solution)/shard_map/reduce_scatter | solution.py:114
  567.6 81.7 %collective-permute-start.76 = (bf16[256,1024]{0,1:T(8,128)(2,1)}, bf16[256,1024]{0,1:T(8,128)(2,1)}, u32[]{:S(2)}, u32[]{:S(2)}) collective-permute-start(bf16[256,1024]{0,1:T(8,128)(2,1)} %bitcast.193), channel_id=1, source_target_pairs={{0,4},{4,0},{8,12},{12,8},{16,20},{20,16},{24,28},{28,24},{1,5},{5... | collective-permute-start | bytes 1572872 | tf_op jit(solution)/shard_map/ppermute | solution.py:86
  570.1 41.4 %collective-permute-start.75 = (bf16[256,1024]{0,1:T(8,128)(2,1)}, bf16[256,1024]{0,1:T(8,128)(2,1)}, u32[]{:S(2)}, u32[]{:S(2)}) collective-permute-start(bf16[256,1024]{0,1:T(8,128)(2,1)} %bitcast.194), channel_id=1, source_target_pairs={{0,4},{4,0},{8,12},{12,8},{16,20},{20,16},{24,28},{28,24},{1,5},{5... | collective-permute-start | bytes 1572872 | tf_op jit(solution)/shard_map/ppermute | solution.py:86
  584.7 10.6 %collective-permute-start.68 = (bf16[4,15104]{1,0:T(4,128)(2,1)S(1)}, bf16[4,15104]{1,0:T(4,128)(2,1)S(1)}, u32[]{:S(2)}, u32[]{:S(2)}) collective-permute-start(bf16[4,15104]{1,0:T(4,128)(2,1)S(1)} %bitcast.200), channel_id=1, source_target_pairs={{0,4},{4,0},{8,12},{12,8},{16,20},{20,16},{24,28},{28,24},{1,5},{5... | collective-permute-start | bytes 362504 | tf_op jit(solution)/shard_map/ppermute | solution.py:129
  596.5 12.9 %collective-permute-start.69 = (bf16[15104]{0:T(1024)(128)(2,1)}, bf16[15104]{0:T(1024)(128)(2,1)S(1)}, u32[]{:S(2)}, u32[]{:S(2)}) collective-permute-start(bf16[15104]{0:T(1024)(128)(2,1)} %get-tuple-element.297), channel_id=1, source_target_pairs={{0,8},{4,12},{8,16},{12,20},{16,24},{20,28},{24,0},{28,4},{1,9},{5... | collective-permute-start | bytes 90632 | tf_op jit(solution)/shard_map/ppermute | solution.py:135
  598.0 12.9 %collective-permute-start.70 = (bf16[15104]{0:T(1024)(128)(2,1)}, bf16[15104]{0:T(1024)(128)(2,1)S(1)}, u32[]{:S(2)}, u32[]{:S(2)}) collective-permute-start(bf16[15104]{0:T(1024)(128)(2,1)} %get-tuple-element.299), channel_id=1, source_target_pairs={{0,16},{4,20},{8,24},{12,28},{16,0},{20,4},{24,8},{28,12},{1,17},{... | collective-permute-start | bytes 90632 | tf_op jit(solution)/shard_map/ppermute | solution.py:135
  599.7 11.3 %collective-permute-start.71 = (bf16[15104]{0:T(1024)(128)(2,1)S(1)}, bf16[15104]{0:T(1024)(128)(2,1)S(1)}, u32[]{:S(2)}, u32[]{:S(2)}) collective-permute-start(bf16[15104]{0:T(1024)(128)(2,1)S(1)} %get-tuple-element.298), channel_id=1, source_target_pairs={{0,24},{4,28},{8,0},{12,4},{16,8},{20,12},{24,16},{28,20},{1,25},{... | collective-permute-start | bytes 90632 | tf_op jit(solution)/shard_map/ppermute | solution.py:135
  609.4 18.3 %collective-permute-start.74 = (bf16[256,1024]{0,1:T(8,128)(2,1)}, bf16[256,1024]{0,1:T(8,128)(2,1)}, u32[]{:S(2)}, u32[]{:S(2)}) collective-permute-start(bf16[256,1024]{0,1:T(8,128)(2,1)} %bitcast.195), channel_id=1, source_target_pairs={{0,4},{4,0},{8,12},{12,8},{16,20},{20,16},{24,28},{28,24},{1,5},{5... | collective-permute-start | bytes 1572872 | tf_op jit(solution)/shard_map/ppermute | solution.py:86
  610.9 5.7 collective-permute-start.58
  617.9 5.9 collective-permute-start.66
  618.8 7.0 %collective-permute-start.67 = (bf16[128,2048]{1,0:T(8,128)(2,1)}, bf16[128,2048]{1,0:T(8,128)(2,1)}, u32[]{:S(2)}, u32[]{:S(2)}) collective-permute-start(bf16[128,2048]{1,0:T(8,128)(2,1)} %get-tuple-element.318), channel_id=1, source_target_pairs={{0,1},{1,0},{2,3},{3,2},{4,5},{5,4},{6,7},{7,6},{8,9},{9,8},{10,11... | collective-permute-start | bytes 1572872 | tf_op jit(solution)/shard_map/ppermute | solution.py:79
  655.9 7.5 %collective-permute-start.73 = (f32[8704]{0:T(1024)S(1)}, f32[8704]{0:T(1024)S(1)}, u32[]{:S(2)}, u32[]{:S(2)}) collective-permute-start(f32[8704]{0:T(1024)S(1)} %convert_add_fusion.6), channel_id=1, source_target_pairs={{0,2},{1,3},{2,0},{3,1},{4,6},{5,7},{6,4},{7,5},{8,10},{9,11},{10,... | collective-permute-start | bytes 104456 | tf_op jit(solution)/shard_map/ppermute | solution.py:110
  (131 other events, 811.8 us)
Sparse Core Ops, SparseCore 0:
  304.0 79.3 reduce-scatter.5
  385.8 82.7 reduce-scatter.9
  470.9 76.2 reduce-scatter.7
  549.4 27.6 reduce-scatter.13
  609.3 33.4 reduce-scatter.11

commit v4 on v3

--- a/solution.py
+++ b/solution.py
@@ -73,20 +73,21 @@
         cut = x.reshape(parts, 2, rows // (2 * parts), width)
         return lax.dynamic_index_in_dim(cut, self.core, 1, False).reshape(rows // 2, width)
 
-    def across_cores(self, x, pieces=1):
-        rows = x.shape[0] // pieces
-        cuts = [x[i * rows : (i + 1) * rows] for i in range(pieces)]
-        got = [lax.ppermute(c, "kv", self.core_swap) for c in cuts]
-        return jnp.concatenate(got, 0) if pieces > 1 else got[0]
+    def across_cores(self, x):
+        return lax.ppermute(x, "kv", self.core_swap)
+
+    def blocks_across(self, x):
+        rows = x.shape[0] // 4
+        return [self.across_cores(x[i * rows : (i + 1) * rows]) for i in range(4)]
 
     def core_sum(self, keep, send):
-        return (keep.astype(F32) + self.across_cores(send, 4).astype(F32)).astype(BF16)
+        return sum_rows(keep, self.blocks_across(send))
 
     def swap(self, x):
         return lax.ppermute(x, "seq", self.x_swap)
 
     def pair_sum(self, keep, got):
-        return (keep.astype(F32) + got.astype(F32)).astype(BF16)
+        return sum_rows(keep, [got])
 
     def outer_terms(self, half):
         terms = [half] + [lax.ppermute(half, "kv", self.y_shift(j)) for j in range(1, self.outer)]
@@ -95,13 +96,8 @@
         stack = jnp.stack(terms)
         return [take(stack, (self.y - i) % self.outer) for i in range(self.outer)]
 
-    def gather_rows(self, own, parts):
-        other = self.across_cores(own, 4)
-        first = self.core == 0
-        shape = (parts, 1, own.shape[0] // parts, own.shape[1])
-        low = jnp.where(first, own, other).reshape(shape)
-        high = jnp.where(first, other, own).reshape(shape)
-        return jnp.concatenate([low, high], 1).reshape(2 * own.shape[0], own.shape[1])
+    def gather_rows(self, own, out=BF16):
+        return merge_rows(self.core, own, self.blocks_across(own), out)
 
     def sum_kv(self, x):
         x = x + lax.ppermute(x, "kv", self.core_swap).astype(F32)
@@ -115,12 +111,8 @@
             part, "seq", scatter_dimension=0, tiled=True, axis_index_groups=self.z_groups
         )
 
-    def finish(self, x):
-        cut = x.reshape(2, x.shape[0] // 2, x.shape[1])
-        got = self.swap(take(cut, 1 - self.x))
-        own = take(cut, self.x)
-        first = self.x == 0
-        return jnp.where(first, own, got), jnp.where(first, got, own)
+    def pair_half(self, x):
+        return take(x.reshape(2, x.shape[0] // 2, x.shape[1]), 1 - self.x)
 
     def scatter_blocks(self, blocks):
         cut = blocks.reshape(self.line, 2, -1)
@@ -389,6 +381,104 @@
     )(*args, *after)
 
 
+def sum_rows(keep, got):
+    rows, width = keep.shape
+    count = len(got)
+    steps = max(count, 4)
+    tile = rows // steps
+
+    def kernel(keep_ref, *refs):
+        *got_refs, out_ref = refs
+        if count == 1:
+            out_ref[...] = (keep_ref[...].astype(F32) + got_refs[0][...].astype(F32)).astype(BF16)
+        else:
+            for i in range(count):
+
+                @pl.when(pl.program_id(0) == i)
+                def _(i=i):
+                    out_ref[...] = (keep_ref[...].astype(F32) + got_refs[i][...].astype(F32)).astype(BF16)
+
+    block = pl.BlockSpec((tile, width), lambda i: (i, 0))
+    fixed = pl.BlockSpec((tile, width), lambda i: (0, 0))
+    return pl.pallas_call(
+        kernel,
+        grid=(steps,),
+        in_specs=[block] + [block if count == 1 else fixed] * count,
+        out_specs=block,
+        out_shape=jax.ShapeDtypeStruct((rows, width), BF16),
+        compiler_params=pltpu.CompilerParams(vmem_limit_bytes=32 * 2**20),
+        cost_estimate=cost(2.5),
+    )(keep, *got)
+
+
+def merge_rows(core, own, other, out):
+    rows, width = own.shape
+    tile = rows // 4
+
+    def kernel(core_ref, own_ref, *refs):
+        *other_refs, out_ref = refs
+        for b in range(8):
+            c, k, h = b // 4, (b // 2) % 2, b % 2
+
+            @pl.when((pl.program_id(0) == b) & (core_ref[0] == k))
+            def _(at=2 * c + h):
+                out_ref[...] = own_ref[at * tile : (at + 1) * tile, :].astype(out)
+
+            @pl.when((pl.program_id(0) == b) & (core_ref[0] != k))
+            def _(at=2 * c + h):
+                out_ref[...] = other_refs[at][...].astype(out)
+
+    return pl.pallas_call(
+        kernel,
+        grid_spec=pltpu.PrefetchScalarGridSpec(
+            num_scalar_prefetch=1,
+            grid=(8,),
+            in_specs=[pl.BlockSpec((rows, width), lambda i, s: (0, 0))]
+            + [pl.BlockSpec((tile, width), lambda i, s: (0, 0))] * 4,
+            out_specs=pl.BlockSpec((tile, width), lambda i, s: (i, 0)),
+        ),
+        out_shape=jax.ShapeDtypeStruct((2 * rows, width), out),
+        compiler_params=pltpu.CompilerParams(vmem_limit_bytes=32 * 2**20),
+        cost_estimate=cost(3.5),
+    )(core.astype(jnp.int32)[None], own, *other)
+
+
+def finish(select, whole, got, turned):
+    rows, n = got.shape
+
+    def kernel(sel, own_ref, got_ref, out_ref):
+        def put(ref):
+            value = ref[...].astype(F32)
+            out_ref[...] = value.T if turned else value
+
+        here = pl.program_id(0) == sel[0]
+
+        @pl.when(here)
+        def _():
+            put(own_ref)
+
+        @pl.when(jnp.logical_not(here))
+        def _():
+            put(got_ref)
+
+    block = (n, rows) if turned else (rows, n)
+    return pl.pallas_call(
+        kernel,
+        grid_spec=pltpu.PrefetchScalarGridSpec(
+            num_scalar_prefetch=1,
+            grid=(2,),
+            in_specs=[
+                pl.BlockSpec((rows, n), lambda j, s: (s[0], 0)),
+                pl.BlockSpec((rows, n), lambda j, s: (0, 0)),
+            ],
+            out_specs=pl.BlockSpec(block, (lambda j, s: (j, 0)) if turned else (lambda j, s: (0, j))),
+        ),
+        out_shape=jax.ShapeDtypeStruct((2 * n, rows) if turned else (rows, 2 * n), F32),
+        compiler_params=pltpu.CompilerParams(vmem_limit_bytes=32 * 2**20),
+        cost_estimate=cost(1.0),
+    )(select.astype(jnp.int32)[None], whole, got)
+
+
 def project_kernel(
     x_ref, gain_ref, wq_ref, wk_ref, wv_ref, down_ref, up_ref, normed_ref, q_ref, kv_ref, low_ref
 ):
@@ -687,8 +777,12 @@
     oup = output_up
     odown = output_down.reshape(-1, rank)
     weight_o = (output_weight.astype(F32) + dot(odown, oup)).astype(BF16)
+    weight_qkv = jnp.concatenate([query_weight, key_weight, value_weight], 1)
+    weight_qkv = (weight_qkv.astype(F32) + dot(down_all, up_all)).astype(BF16)
     cot_own = grid.own_rows(cotangent, parts)
-    prior, g_hidden, weight_o, cot_own = tie(prior, g_hidden, weight_o, cot_own)
+    prior, g_hidden, weight_o, weight_qkv, cot_own = tie(
+        prior, g_hidden, weight_o, weight_qkv, cot_own
+    )
     cot_got = grid.swap(cot_own)
     heads, totals, states = call(
         9.0,
@@ -705,7 +799,6 @@
     own_tokens = [grid.own_rows(tokens[c * chunk : (c + 1) * chunk], 1) for c in range(parts)]
     own_tokens[0], half[1] = tie(own_tokens[0], half[1])
     terms = [grid.outer_terms(h) for h in half]
-    cot_got, terms[0][-1] = tie(cot_got, terms[0][-1])
     held, held_pair = (), ()
     resid, rms_two, own, got = [], [], [], []
     select = jnp.stack([core, mine])
@@ -726,13 +819,15 @@
     normed(0)
     got[0] = grid.swap(own[0])
     held = list(inner(0, own[0], g_hidden, held, []))
+    cot_got, held[2] = tie(cot_got, held[2])
     terms[1][-1], held[1] = tie(terms[1][-1], held[1])
     normed(1)
     got[1] = grid.swap(own[1])
     cot_got, mark = tie(cot_got, own[1])
-    cot_pair = grid.gather_rows(cot_got, parts)
+    cot_pair = grid.gather_rows(cot_got)
     g_pair = matmul([(cot_pair, down_weight)], "rows", mine, F32, after=[mark])
-    held = inner(1, own[1], g_hidden, held, [g_pair])
+    held = list(inner(1, own[1], g_hidden, held, [g_pair]))
+    got[0], held[1] = tie(got[0], held[1])
     held_pair = list(inner(0, got[0], g_pair, held_pair, [held[1]]))
     got[1], held_pair[1] = tie(got[1], held_pair[1])
     held_pair = inner(1, got[1], g_pair, held_pair, [])
@@ -750,19 +845,19 @@
     def from_pair(a, b, got, product=dot_tn, after=()):
         return grad_block(grid.line, mine, a, b, product, got, after)
 
+    w_d = grad_pair(count_d, [(cotangent, hidden), (cot_pair, hidden_pair)])
+    grad_d = grid.line_scatter(w_d)
     kept, sent = matmul(
-        [(gate_pair, gate_weight), (up_pair, up_weight)], "columns", mine, BF16, core
+        [(gate_pair, gate_weight), (up_pair, up_weight)], "columns", mine, BF16, core, after=[w_d]
     )
     theirs = grid.core_sum(kept, sent)
     kept, sent = matmul(
         [(g_gate, gate_weight), (g_up, up_weight)], "columns", mine, BF16, core, after=[kept]
     )
     ours = grid.core_sum(kept, sent)
-    w_d = grad_pair(count_d, [(cotangent, hidden), (cot_pair, hidden_pair)], after=[kept])
-    w_g = grad_pair(count_d, [(normed_two, g_gate), (normed_pair, gate_pair)], after=[w_d])
+    w_g = grad_pair(count_d, [(normed_two, g_gate), (normed_pair, gate_pair)], after=[kept])
     theirs = grid.swap(theirs)
-    theirs, w_d, w_g = tie(theirs, w_d, w_g)
-    grad_d = grid.line_scatter(w_d)
+    theirs, w_g = tie(theirs, w_g)
     grad_g = grid.line_scatter(w_g)
     half = grid.pair_sum(ours, theirs)
     terms = grid.outer_terms(half)
@@ -783,12 +878,9 @@
         - resid * rms_two**3 * jnp.mean(resid * s_two, -1, keepdims=True)
     )
     own_attn = g_resid.astype(BF16)
-    g_attn = grid.gather_rows(own_attn, parts)
+    g_attn = grid.gather_rows(own_attn)
     down_got = grid.swap(grid.core_sum(*down_theirs))
     down_half = grid.core_sum(*down_ours)
-    weight_qkv = jnp.concatenate([query_weight, key_weight, value_weight], 1)
-    weight_qkv = (weight_qkv.astype(F32) + dot(down_all, up_all)).astype(BF16)
-    g_attn, weight_qkv = tie(g_attn, weight_qkv)
 
     g_heads = dot_nt(weight_o, g_attn, BF16)
     g_q, featq_part, gk, gv, gphi, first = call(
@@ -845,13 +937,30 @@
     bq_part = b_part[:rank, :qw]
     bk_part = b_part[rank : 2 * rank, qw : qw + kw]
     bv_part = b_part[2 * rank : 3 * rank, qw + kw :]
-    terms[-1], a_part, b_part, bo_part, ao_part, r_qkv, grad_u, grad_g, k_o = tie(
-        terms[-1], a_part, b_part, bo_part, ao_part, r_qkv, grad_u, grad_g, k_o
-    )
-    grad_o = grid.line_scatter(k_o)
+    n = grid.seq
+
+    def blocks(x, dim):
+        shape = x.shape
+        x = x.reshape(shape[:dim] + (n, shape[dim] // n) + shape[dim + 1 :])
+        return jnp.moveaxis(x, dim, 0).reshape(n, -1)
+
+    both = [(a_part[: 3 * rank], 1), (bo_part, 1)]
+    alone = [
+        (norm2_part + lax.ppermute(norm2_part, "kv", grid.core_swap), 0),
+        (bq_part.reshape(query_up.shape), 2),
+        (bk_part.reshape(key_up.shape), 2),
+        (bv_part.reshape(value_up.shape), 2),
+        (featq_part, 1),
+        (featk_part, 1),
+        (ao_part.reshape(output_down.shape), 1),
+    ]
+    cut = [blocks(x, d) for x, d in both + alone]
+    bundle = jnp.concatenate(cut, 1)
+    terms[-1], bundle, r_qkv, grad_g, k_o = tie(terms[-1], bundle, r_qkv, grad_g, k_o)
     k_qkv = from_pair(normed_one, g_qkv, r_qkv, dot_tt, after=[k_o])
 
     terms[-1], k_qkv = tie(terms[-1], k_qkv)
+    grad_oq = grid.line_scatter(jnp.concatenate([k_o, k_qkv], 1))
     stream = grid.own_rows(tokens, parts).astype(F32)
     rms_one = lax.rsqrt(jnp.mean(stream * stream, -1, keepdims=True) + EPSILON)
     g_one = add(terms)
@@ -862,49 +971,30 @@
         + rms_one * s_one
         - stream * rms_one**3 * jnp.mean(stream * s_one, -1, keepdims=True)
     ).astype(BF16)
-    grad_qkv = grid.line_scatter(k_qkv).astype(F32)
-    output = grid.gather_rows((resid + add(down_terms)).astype(BF16), parts)
-    grad_tokens = grid.gather_rows(own_grad, parts).astype(F32)
-    own_grad, grad_d, grad_g, grad_u = tie(own_grad, grad_d, grad_g, grad_u)
-    down_low, down_high = grid.finish(grad_d)
-    gate_low, gate_high = grid.finish(grad_g)
-    up_low, up_high = grid.finish(grad_u)
-    grad_wo = grad_o.astype(F32)
-    grad_gate = jnp.concatenate([gate_low, gate_high], 1).astype(F32)
-    grad_up = jnp.concatenate([up_low, up_high], 1).astype(F32)
-    grad_down = jnp.concatenate([down_low.T, down_high.T], 0).astype(F32)
-
-    n = grid.seq
-
-    def blocks(x, dim):
-        shape = x.shape
-        x = x.reshape(shape[:dim] + (n, shape[dim] // n) + shape[dim + 1 :])
-        return jnp.moveaxis(x, dim, 0).reshape(n, -1)
-
-    norm_parts = [p * (1.0 / grid.outer) for p in (norm1_part, norm2_part)]
-    both = [(norm_parts[0], 0), (norm_parts[1], 0), (a_part[: 3 * rank], 1), (bo_part, 1)]
-    own = [
-        (bq_part.reshape(query_up.shape), 2),
-        (bk_part.reshape(key_up.shape), 2),
-        (bv_part.reshape(value_up.shape), 2),
-        (featq_part, 1),
-        (featk_part, 1),
-        (ao_part.reshape(output_down.shape), 1),
-    ]
-    cut = [blocks(x, d) for x, d in both + own]
-    summed = grid.scatter_blocks(jnp.concatenate(cut, 1))
-    summed, grad_qkv, grad_wo = tie(summed, grad_qkv, grad_wo)
+    grad_tokens = grid.gather_rows(own_grad, F32)
+    down_terms[-1], grad_tokens = tie(down_terms[-1], grad_tokens)
+    fins = grid.swap(jnp.concatenate([grid.pair_half(g) for g in (grad_d, grad_g, grad_u)], 0))
+    down_terms[-1], fins = tie(down_terms[-1], fins)
+    fins = jnp.split(fins, 3, 0)
+    grad_down = finish(mine, grad_d, fins[0], True)
+    grad_gate = finish(mine, grad_g, fins[1], False)
+    grad_up = finish(mine, grad_u, fins[2], False)
+    output = grid.gather_rows((resid + add(down_terms)).astype(BF16))
+    grad_wo, grad_qkv = grad_oq[:, :qw].astype(F32), grad_oq[:, qw:].astype(F32)
+    norm1 = norm1_part + lax.ppermute(norm1_part, "kv", grid.core_swap)
+    norm1 = grid.scatter_blocks(norm1.reshape(n, -1))
+    summed = grid.scatter_blocks(bundle)
     n_both = sum(c.shape[1] for c in cut[: len(both)])
     flat = jnp.concatenate([grid.sum_kv(summed[:n_both].astype(BF16)), summed[n_both:]])
     done = []
     at = 0
-    for x, d in both + own:
+    for x, d in both + alone:
         shape = list(x.shape)
         shape[d] //= n
         size = x.size // n
         done.append(flat[at : at + size].reshape(shape))
         at += size
-    norm1, norm2, grad_a, grad_bo, bq, bk, bv, featq, featk, grad_ao = done
+    grad_a, grad_bo, norm2, bq, bk, bv, featq, featk, grad_ao = done
     return (
         output,
         grad_tokens,

time: 683 us -> 667 us (0.977)
  other arithmetic: 75.2 us -> 38.9 us
  Pallas kernels: 226 us -> 262 us
  local copies, waits for them, and re-layouts: 127 us -> 106 us
  waiting for transfers between devices: 143 us -> 152 us
    reduce_scatter x5 -> x4, waiting for transfers between devices: 44.3 us -> 0.03 us  [line_scatter(): lax.psum_scatter(part, 'seq', scatter_dimension=0, tiled=True, axis_index...]
    ppermute x10 -> x8, waiting for transfers between devices: 21.2 us -> 62 us  [swap(): return lax.ppermute(x, 'seq', self.x_swap)]
    pallas_call x0 -> x16, Pallas kernels: none -> 35.9 us  [the longest x4 15.9 us: merge_rows(): pl.pallas_call(kernel, grid_spec=pltpu.PrefetchScalarGridSpec(num_scalar_...]
    convert_element_type x14 -> x2, other arithmetic: 34.1 us -> 4.26 us  [the longest x1 3.22 us: local(): output = grid.gather_rows((resid + add(down_terms)).astype(BF16))]
    concatenate x15 -> x1, local copies, waits for them, and re-layouts: 13.6 us -> 0.6 us  [local(): bundle = jnp.concatenate(cut, 1)]
    dynamic_slice x9 -> x2, local copies, waits for them, and re-layouts: 11.2 us -> 0.18 us  [take(): return lax.dynamic_index_in_dim(x, i, 0, False)]
    convert_element_type x1 -> x0, local copies, waits for them, and re-layouts: 8.08 us -> none  [local(): grad_tokens = grid.gather_rows(own_grad, parts).astype(F32)]
    ppermute x8, waiting for transfers between devices: 23.7 us -> 15.9 us  [shift_seq(): return lax.ppermute(x, 'seq', pairs)]
  transfers between devices with their start and end apart: 82 -> 85, of which waited for: 29 -> 39; matrix products, arithmetic and copies ran while one was open for 28% -> 17% of each run, Pallas kernels for 26% -> 32%
where the time goes in v4:
time: 667 us; the launch traced here: 658 us
  Pallas kernels  262 us (39%)
  waiting for transfers between devices  152 us (23%)
  local copies, waits for them, and re-layouts  106 us (16%)
  starting transfers between devices  65.7 us (10%)
  other arithmetic  38.9 us (6%)
  matrix products  17.7 us (3%)
  between operations  15.7 us (2%)
    pallas_call x8, Pallas kernels, matmul(): pl.pallas_call(kernel, grid_spec=pltpu.PrefetchScalarGridSpec(num_scalar_...  79.8 us
    ppermute x8, waiting for transfers between devices, swap(): return lax.ppermute(x, 'seq', self.x_swap)  62 us
    unnamed x241, local copies, waits for them, and re-layouts  50.6 us
    ppermute x5, waiting for transfers between devices, outer_terms(): lax.ppermute(half, 'kv', self.y_shift(j))  45.8 us
    pallas_call x4, Pallas kernels, gated(): pl.pallas_call(gated_kernel, grid_spec=pltpu.PrefetchScalarGridSpec(num_s...  44.7 us
    pallas_call x3, Pallas kernels, grad_pair(): pl.pallas_call(kernel, grid=(count,), in_specs=specs * len(pairs) + [ANY]...  38.1 us
    pallas_call x4, Pallas kernels, call(): pl.pallas_call(lambda *refs: kernel(*refs[:count], *refs[count + len(afte...  35.1 us
    ppermute x8, starting transfers between devices, shift_seq(): return lax.ppermute(x, 'seq', pairs)  24.2 us
  transfers between devices with their start and end apart: 85, of which 39 were waited for; matrix products, arithmetic and copies ran while one was open for 17% of the time, Pallas kernels for 32%

profile of v4, /device:TPU:0, one launch (start us, length us, event | category | flops | bytes accessed | tf_op | source)
XLA Modules:
  0.0 657.5 jit_solution(1073200708091807302)
XLA Ops:
  13.8 10.1 %shard_map.373 = (bf16[1024,2048]{1,0:T(8,128)(2,1)}, bf16[512,1024]{1,0:T(8,128)(2,1)S(1)}, bf16[256,1024]{1,0:T(8,128)(2,1)S(1)}, bf16[1024,128]{1,0:T(8,128)(2,1)S(1)}) custom-call(bf16[1024,2048]{1,0:T(8,128)(2,1)} %x_ref.1, bf16[1,2048]{1,0:T(2,128)(2,1)S(1)} %broadcast_in_dim.31.gain_ref, bf16[2048,512]{1,0:T(8,128)(2,1)S(1)} %copy-done.56, ...), custom_call_target="tpu_custom_call" | custom-call | flops 4499999744 | bytes 1 | tf_op jit(solution)/shard_map/pallas_call | solution.py:509
  25.6 5.5 collective-permute-start
  31.1 3.9 add_convert_fusion.refs_1_
  42.9 9.7 %shard_map.375.gh_ref = f32[1024,1024]{1,0:T(8,128)} custom-call(s32[2]{0:T(128)} %pad_add_fusion.1.sel, bf16[1024,2048]{1,0:T(8,128)(2,1)} %refs_0_.3, bf16[2048,2048]{1,0:T(8,128)(2,1)} %refs_1_.11), custom_call_target="tpu_custom_call" | custom-call | flops 1899551488 | bytes 1 | tf_op jit(solution)/shard_map/pallas_call | solution.py:571
  59.9 5.2 collective-permute-start.2
  67.2 5.5 collective-permute-start.3
  74.6 9.1 %shard_map.376 = (bf16[512,1024]{1,0:T(8,128)(2,1)S(1)}, f32[8,1024]{1,0:T(8,128)S(1)}, f32[8,2,80,128]{3,2,1,0:T(8,128)S(1)}) custom-call(bf16[512,1024]{1,0:T(8,128)(2,1)S(1)} %copy-done.67, bf16[256,1152]{1,0:T(8,128)(2,1)S(1)} %constant_dynamic-update-slice_fusion.refs_0_.refs_1_, bf16[2,128,1152]{2,1,0:T(8,128)(2,1)S(1)} %get-tuple-element.112.refs_2_.refs_1_, ...), custom_call_target="tpu_custom_call" | custom-call | flops 4049999872 | bytes 1 | tf_op jit(solution)/shard_map/pallas_call | solution.py:373
  86.1 6.5 shard_map.377
  104.8 18.1 %collective-permute-done.12 = bf16[256,2048]{1,0:T(8,128)(2,1)S(1)} collective-permute-done((bf16[256,2048]{1,0:T(8,128)(2,1)S(1)}, bf16[256,2048]{1,0:T(8,128)(2,1)S(1)}, u32[]{:S(2)}, u32[]{:S(2)}) %collective-permute-start.12) | collective-permute-done | bytes 1048608 | tf_op jit(solution)/shard_map/ppermute | solution.py:93
  127.8 10.8 %shard_map.380 = (bf16[1024,2048]{1,0:T(8,128)(2,1)}, bf16[1024,1024]{1,0:T(8,128)(2,1)}, bf16[1024,1024]{1,0:T(8,128)(2,1)}, bf16[1024,1024]{1,0:T(8,128)(2,1)}) custom-call(s32[2]{0:T(128)} %pad_add_fusion.3.sel_ref, bf16[256,2048]{1,0:T(8,128)(2,1)} %copy-done.86, bf16[256,2048]{1,0:T(8,128)(2,1)} %collective-permute-done.14.other_ref, ...), custom_call_target="tpu_custom_call" | custom-call | flops 4950000128 | bytes 1 | tf_op jit(solution)/shard_map/pallas_call | solution.py:678
  138.6 12.1 %collective-permute-done.13 = bf16[256,2048]{1,0:T(8,128)(2,1)} collective-permute-done((bf16[256,2048]{1,0:T(8,128)(2,1)S(1)}, bf16[256,2048]{1,0:T(8,128)(2,1)}, u32[]{:S(2)}, u32[]{:S(2)}) %collective-permute-start.13) | collective-permute-done | bytes 1048608 | tf_op jit(solution)/shard_map/ppermute | solution.py:93
  163.1 9.6 %shard_map.382.refs_4_.gh_ref = f32[1024,1024]{1,0:T(8,128)} custom-call(s32[2]{0:T(128)} %pad_add_fusion.1.sel, bf16[1024,2048]{1,0:T(8,128)(2,1)} %copy-done.7, bf16[2048,2048]{1,0:T(8,128)(2,1)} %refs_1_.11, bf16[256,2048]{1,0:T(8,128)(2,1)} %copy-done.82), custom_call_target="tpu_custom_call" | custom-call | flops 1899551488 | bytes 1 | tf_op jit(solution)/shard_map/pallas_call | solution.py:571
  173.7 11.6 %shard_map.383 = (bf16[1024,2048]{1,0:T(8,128)(2,1)}, bf16[1024,1024]{1,0:T(8,128)(2,1)}, bf16[1024,1024]{1,0:T(8,128)(2,1)}, bf16[1024,1024]{1,0:T(8,128)(2,1)}) custom-call(s32[2]{0:T(128)} %pad_add_fusion.3.sel_ref, bf16[256,2048]{1,0:T(8,128)(2,1)} %copy-done.82, ...), custom_call_target="tpu_custom_call", output_to_operand_aliasing={{0}: (6, {}), {1}: (7, {}), {2}: (8, {}), {3}: (9, {})} | custom-call | flops 4950000128 | bytes 1 | tf_op jit(solution)/shard_map/pallas_call | solution.py:678
  189.1 11.0 %shard_map.384 = (bf16[1024,2048]{1,0:T(8,128)(2,1)}, bf16[1024,1024]{1,0:T(8,128)(2,1)}, bf16[1024,1024]{1,0:T(8,128)(2,1)}, bf16[1024,1024]{1,0:T(8,128)(2,1)}) custom-call(s32[2]{0:T(128)} %pad_add_fusion.3.sel_ref, bf16[256,2048]{1,0:T(8,128)(2,1)} %copy-done.94, bf16[256,2048]{1,0:T(8,128)(2,1)} %copy-done.97, bf16[2048,2048]{1,0:T(8,128)(2,1)} %refs_1_.9, ...), custom_call_target="tpu_custom_call" | custom-call | flops 4950000128 | bytes 1 | tf_op jit(solution)/shard_map/pallas_call | solution.py:678
  200.1 10.9 %collective-permute-done.21.own_ref = bf16[256,2048]{1,0:T(8,128)(2,1)S(1)} collective-permute-done((bf16[256,2048]{1,0:T(8,128)(2,1)S(1)}, bf16[256,2048]{1,0:T(8,128)(2,1)S(1)}, u32[]{:S(2)}, u32[]{:S(2)}) %collective-permute-start.21) | collective-permute-done | bytes 1048608 | tf_op jit(solution)/shard_map/ppermute | solution.py:87
  214.7 11.3 %shard_map.385 = (bf16[1024,2048]{1,0:T(8,128)(2,1)}, bf16[1024,1024]{1,0:T(8,128)(2,1)}, bf16[1024,1024]{1,0:T(8,128)(2,1)}, bf16[1024,1024]{1,0:T(8,128)(2,1)}) custom-call(s32[2]{0:T(128)} %pad_add_fusion.3.sel_ref, bf16[256,2048]{1,0:T(8,128)(2,1)} %copy-done.95, ...), custom_call_target="tpu_custom_call", output_to_operand_aliasing={{0}: (6, {}), {1}: (7, {}), {2}: (8, {}), {3}: (9, {})} | custom-call | flops 4950000128 | bytes 1 | tf_op jit(solution)/shard_map/pallas_call | solution.py:678
  227.6 12.7 %shard_map.386.refs_4_ = bf16[2048,1024]{1,0:T(8,128)(2,1)} custom-call(bf16[1024,2048]{1,0:T(8,128)(2,1)} %refs_0_.3, bf16[1024,1024]{1,0:T(8,128)(2,1)S(1)} %copy-done.6, bf16[1024,2048]{1,0:T(8,128)(2,1)} %copy-done.7, bf16[1024,1024]{1,0:T(8,128)(2,1)S(1)} %copy-done.19), custom_call_target="tpu_custom_call" | custom-call | flops 5849999872 | bytes 1 | tf_op jit(solution)/shard_map/pallas_call | solution.py:598
  240.3 14.0 %shard_map.387 = (bf16[512,2048]{1,0:T(8,128)(2,1)}, bf16[512,2048]{1,0:T(8,128)(2,1)}) custom-call(s32[2]{0:T(128)} %pad_add_fusion.sel, bf16[1024,1024]{1,0:T(8,128)(2,1)} %get-tuple-element.149.refs_0_.refs_3_, bf16[2048,2048]{1,0:T(8,128)(2,1)} %refs_1_.9, bf16[1024,1024]{1,0:T(8,128)(2,1)} %get-tuple-element.150.refs_2_.refs_3_, ...), custom_call_target="tpu_custom_call" | custom-call | flops 3349102848 | bytes 1 | tf_op jit(solution)/shard_map/pallas_call | solution.py:571
  263.2 14.4 %shard_map.388 = (bf16[512,2048]{1,0:T(8,128)(2,1)}, bf16[512,2048]{1,0:T(8,128)(2,1)}) custom-call(s32[2]{0:T(128)} %pad_add_fusion.sel, bf16[1024,1024]{1,0:T(8,128)(2,1)} %get-tuple-element.138.refs_0_.refs_1_, bf16[2048,2048]{1,0:T(8,128)(2,1)} %refs_1_.9, bf16[1024,1024]{1,0:T(8,128)(2,1)} %get-tuple-element.139.refs_2_.refs_1_, ...), custom_call_target="tpu_custom_call" | custom-call | flops 3349102848 | bytes 1 | tf_op jit(solution)/shard_map/pallas_call | solution.py:571
  277.7 12.7 %shard_map.391 = bf16[2048,1024]{1,0:T(8,128)(2,1)} custom-call(bf16[1024,2048]{1,0:T(8,128)(2,1)} %get-tuple-element.156.refs_0_, bf16[1024,1024]{1,0:T(8,128)(2,1)S(1)} %copy-done.16, bf16[1024,2048]{1,0:T(8,128)(2,1)} %get-tuple-element.157.refs_2_, bf16[1024,1024]{1,0:T(8,128)(2,1)S(1)} %copy-done.20, bf16[512,2048]{1,0:T(8,128)(2,1)} %get-tuple-element.153.keep_ref.refs_4_), custom_call_target="tpu_custom_call" | custom-call | flops 5849999872 | bytes 1 | tf_op jit(solution)/shard_map/pallas_call | solution.py:598
  290.4 20.0 %collective-permute-done.33.refs_0_ = bf16[512,2048]{1,0:T(8,128)(2,1)S(1)} collective-permute-done((bf16[512,2048]{1,0:T(8,128)(2,1)}, bf16[512,2048]{1,0:T(8,128)(2,1)S(1)}, u32[]{:S(2)}, u32[]{:S(2)}) %collective-permute-start.33) | collective-permute-done | bytes 2097184 | tf_op jit(solution)/shard_map/ppermute | solution.py:87
  321.0 8.7 %shard_map.393 = (bf16[512,2048]{1,0:T(8,128)(2,1)}, bf16[512,2048]{1,0:T(8,128)(2,1)}) custom-call(s32[2]{0:T(128)} %pad_add_fusion.sel, bf16[1024,1024]{1,0:T(8,128)(2,1)} %get-tuple-element.151.refs_3_.refs_0_, bf16[2048,2048]{1,0:T(8,128)(2,1)} %refs_1_.11, bf16[512,2048]{1,0:T(8,128)(2,1)} %copy-done.4), custom_call_target="tpu_custom_call" | custom-call | flops 1899551488 | bytes 1 | tf_op jit(solution)/shard_map/pallas_call | solution.py:571
  333.6 9.2 %shard_map.394 = (bf16[512,2048]{1,0:T(8,128)(2,1)}, bf16[512,2048]{1,0:T(8,128)(2,1)}) custom-call(s32[2]{0:T(128)} %pad_add_fusion.sel, bf16[1024,1024]{1,0:T(8,128)(2,1)} %get-tuple-element.142.refs_0_.refs_1_, bf16[2048,2048]{1,0:T(8,128)(2,1)} %refs_1_.11, bf16[512,2048]{1,0:T(8,128)(2,1)} %get-tuple-element.159.refs_2_.keep_ref), custom_call_target="tpu_custom_call" | custom-call | flops 1899551488 | bytes 1 | tf_op jit(solution)/shard_map/pallas_call | solution.py:571
  342.8 12.8 %shard_map.395 = bf16[2048,1024]{1,0:T(8,128)(2,1)} custom-call(bf16[1024,2048]{1,0:T(8,128)(2,1)} %get-tuple-element.156.refs_0_, bf16[1024,1024]{1,0:T(8,128)(2,1)S(1)} %copy-done.17, bf16[1024,2048]{1,0:T(8,128)(2,1)} %get-tuple-element.157.refs_2_, bf16[1024,1024]{1,0:T(8,128)(2,1)S(1)} %copy-done.21, bf16[512,2048]{1,0:T(8,128)(2,1)} %get-tuple-element.169.refs_4_.keep_ref), custom_call_target="tpu_custom_call" | custom-call | flops 5849999872 | bytes 1 | tf_op jit(solution)/shard_map/pallas_call | solution.py:598
  355.5 11.7 %collective-permute-done.34 = bf16[512,2048]{1,0:T(8,128)(2,1)} collective-permute-done((bf16[512,2048]{1,0:T(8,128)(2,1)S(1)}, bf16[512,2048]{1,0:T(8,128)(2,1)}, u32[]{:S(2)}, u32[]{:S(2)}) %collective-permute-start.34) | collective-permute-done | bytes 2097184 | tf_op jit(solution)/shard_map/ppermute | solution.py:93
  370.1 3.9 multiply_reduce_fusion
  374.6 4.8 fusion.35
  410.4 23.4 %shard_map.397 = (bf16[512,1024]{1,0:T(8,128)(2,1)}, f32[8,64,64]{2,1,0:T(8,128)S(1)}, f32[128,1152]{1,0:T(8,128)S(1)}, f32[128,1152]{1,0:T(8,128)S(1)}, f32[2,1...) custom-call(bf16[512,1024]{1,0:T(8,128)(2,1)} %copy-done.66, ...), custom_call_target="tpu_custom_call" | custom-call | flops 10800000000 | bytes 1 | tf_op jit(solution)/shard_map/pallas_call | solution.py:373
  438.3 3.5 collective-permute-done.44.refs_0_
  443.8 4.7 shard_map.400.refs_11_
  453.3 6.1 collective-permute-done.50
  461.4 4.2 shard_map.404
  467.3 4.5 collective-permute-done.51
  479.8 7.6 %shard_map.402 = (bf16[512,2048]{1,0:T(8,128)(2,1)}, bf16[512,2048]{1,0:T(8,128)(2,1)}) custom-call(s32[2]{0:T(128)} %pad_add_fusion.sel, bf16[768,1024]{1,0:T(8,128)(2,1)} %copy-done.2, bf16[2048,768]{1,0:T(8,128)(2,1)} %add_convert_fusion.refs_1_), custom_call_target="tpu_custom_call" | custom-call | flops 1537163648 | bytes 1 | tf_op jit(solution)/shard_map/pallas_call | solution.py:571
  502.7 4.9 shard_map.405.rest_1_
  507.6 3.9 collective-permute-start.59
  515.7 3.7 fusion.10
  524.2 3.8 shard_map.406.rest_1_
  529.0 17.1 %collective-permute-done.59.rest_0_ = bf16[1024,768]{1,0:T(8,128)(2,1)} collective-permute-done((bf16[1024,768]{1,0:T(8,128)(2,1)}, bf16[1024,768]{1,0:T(8,128)(2,1)}, u32[]{:S(2)}, u32[]{:S(2)}) %collective-permute-start.59) | collective-permute-done | bytes 1572896 | tf_op jit(solution)/shard_map/ppermute | solution.py:87
  546.1 4.0 collective-permute-done.57
  551.3 4.5 shard_map.407
  555.8 4.5 fusion.6
  560.4 3.5 fusion.3.own_ref
  575.2 3.9 collective-permute-start.75
  579.9 3.5 collective-permute-done.71
  609.8 6.1 shard_map.408
  615.9 10.5 %collective-permute-done.65 = bf16[768,1024]{1,0:T(8,128)(2,1)} collective-permute-done((bf16[768,1024]{1,0:T(8,128)(2,1)}, bf16[768,1024]{1,0:T(8,128)(2,1)}, u32[]{:S(2)}, u32[]{:S(2)}) %collective-permute-start.65) | collective-permute-done | bytes 1572896 | tf_op jit(solution)/shard_map/ppermute | solution.py:87
  640.6 5.3 shard_map.409
  (550 shorter events, 233.0 us)
Async XLA Ops:
  7.2 402.0 %reduce-scatter.5.cloned.1.call-start = ((), (), s32[]{:S(2)}) async-start(), calls=%async_computation.4 | async-start | bytes 5242880 | tf_op jit(solution)/shard_map/reduce_scatter | solution.py:110
  25.6 27.3 %collective-permute-start = (bf16[256,128]{1,0:T(8,128)(2,1)S(1)}, bf16[256,128]{1,0:T(8,128)(2,1)}, u32[]{:S(2)}, u32[]{:S(2)}) collective-permute-start(bf16[256,128]{1,0:T(8,128)(2,1)S(1)} %slice.361), channel_id=1, source_target_pairs={{0,4},{4,8},{8,12},{12,16},{16,20},{20,24},{24,28},{1,5},{5,9},{9,... | collective-permute-start | bytes 196616 | tf_op jit(solution)/shard_map/ppermute | solution.py:133
  59.9 7.3 %collective-permute-start.2 = (f32[2,80,128]{2,1,0:T(8,128)S(1)}, f32[2,80,128]{2,1,0:T(8,128)S(1)}, u32[]{:S(2)}, u32[]{:S(2)}) collective-permute-start(f32[2,80,128]{2,1,0:T(8,128)S(1)} %add.245), channel_id=1, source_target_pairs={{0,8},{4,12},{8,16},{12,20},{16,24},{20,28},{1,9},{5,13},{9,17},{1... | collective-permute-start | bytes 245768 | tf_op jit(solution)/shard_map/ppermute | solution.py:133
  67.2 7.3 %collective-permute-start.3 = (f32[2,80,128]{2,1,0:T(8,128)S(1)}, f32[2,80,128]{2,1,0:T(8,128)S(1)}, u32[]{:S(2)}, u32[]{:S(2)}) collective-permute-start(f32[2,80,128]{2,1,0:T(8,128)S(1)} %add.246), channel_id=1, source_target_pairs={{0,16},{4,20},{8,24},{12,28},{1,17},{5,21},{9,25},{13,29},{2,18},{... | collective-permute-start | bytes 245768 | tf_op jit(solution)/shard_map/ppermute | solution.py:133
  97.7 25.3 %collective-permute-start.12 = (bf16[256,2048]{1,0:T(8,128)(2,1)S(1)}, bf16[256,2048]{1,0:T(8,128)(2,1)S(1)}, u32[]{:S(2)}, u32[]{:S(2)}) collective-permute-start(bf16[256,2048]{1,0:T(8,128)(2,1)S(1)} %shard_map.379), channel_id=1, source_target_pairs={{0,2},{1,3},{2,0},{3,1},{4,6},{5,7},{6,4},{7,5},{8,10},{9,11},{10,... | collective-permute-start | bytes 3145736 | tf_op jit(solution)/shard_map/ppermute | solution.py:93
  103.8 49.0 %collective-permute-start.16 = (bf16[512,2048]{1,0:T(8,128)(2,1)S(1)}, bf16[512,2048]{1,0:T(8,128)(2,1)S(1)}, u32[]{:S(2)}, u32[]{:S(2)}) collective-permute-start(bf16[512,2048]{1,0:T(8,128)(2,1)S(1)} %bitcast.145), channel_id=1, source_target_pairs={{0,4},{4,0},{8,12},{12,8},{16,20},{20,16},{24,28},{28,24},{1,5},{5... | collective-permute-start | bytes 6291464 | tf_op jit(solution)/shard_map/ppermute | solution.py:87
  125.0 25.7 %collective-permute-start.13 = (bf16[256,2048]{1,0:T(8,128)(2,1)S(1)}, bf16[256,2048]{1,0:T(8,128)(2,1)}, u32[]{:S(2)}, u32[]{:S(2)}) collective-permute-start(bf16[256,2048]{1,0:T(8,128)(2,1)S(1)} %shard_map.378), channel_id=1, source_target_pairs={{0,2},{1,3},{2,0},{3,1},{4,6},{5,7},{6,4},{7,5},{8,10},{9,11},{10,... | collective-permute-start | bytes 3145736 | tf_op jit(solution)/shard_map/ppermute | solution.py:93
  154.4 18.3 %collective-permute-start.15 = (bf16[256,2048]{1,0:T(8,128)(2,1)S(1)}, bf16[256,2048]{1,0:T(8,128)(2,1)S(1)}, u32[]{:S(2)}, u32[]{:S(2)}) collective-permute-start(bf16[256,2048]{1,0:T(8,128)(2,1)S(1)} %multiply_convert_fusion.refs_2_.own_ref), channel_id=1, source_target_pairs={{0,1},{1,0},{2,3},{3,2},{4,5},{5,4},{6,7},{7,6},{8,9},{9,8},{10,11... | collective-permute-start | bytes 3145736 | tf_op jit(solution)/shard_map/ppermute | solution.py:77
  156.1 29.3 %collective-permute-start.22 = (bf16[256,2048]{1,0:T(8,128)(2,1)S(1)}, bf16[256,2048]{1,0:T(8,128)(2,1)S(1)}, u32[]{:S(2)}, u32[]{:S(2)}) collective-permute-start(bf16[256,2048]{1,0:T(8,128)(2,1)S(1)} %copy-done.87), channel_id=1, source_target_pairs={{0,4},{4,0},{8,12},{12,8},{16,20},{20,16},{24,28},{28,24},{1,5},{5... | collective-permute-start | bytes 3145736 | tf_op jit(solution)/shard_map/ppermute | solution.py:87
  185.5 25.5 %collective-permute-start.21 = (bf16[256,2048]{1,0:T(8,128)(2,1)S(1)}, bf16[256,2048]{1,0:T(8,128)(2,1)S(1)}, u32[]{:S(2)}, u32[]{:S(2)}) collective-permute-start(bf16[256,2048]{1,0:T(8,128)(2,1)S(1)} %copy-done.83), channel_id=1, source_target_pairs={{0,4},{4,0},{8,12},{12,8},{16,20},{20,16},{24,28},{28,24},{1,5},{5... | collective-permute-start | bytes 3145736 | tf_op jit(solution)/shard_map/ppermute | solution.py:87
  240.3 305.8 %reduce-scatter.7.cloned.1.call-start = ((), (), s32[]{:S(2)}) async-start(), calls=%async_computation.5 | async-start | bytes 5242880 | tf_op jit(solution)/shard_map/reduce_scatter | solution.py:110
  262.5 47.9 %collective-permute-start.33 = (bf16[512,2048]{1,0:T(8,128)(2,1)}, bf16[512,2048]{1,0:T(8,128)(2,1)S(1)}, u32[]{:S(2)}, u32[]{:S(2)}) collective-permute-start(bf16[512,2048]{1,0:T(8,128)(2,1)} %shard_map.390), channel_id=1, source_target_pairs={{0,4},{4,0},{8,12},{12,8},{16,20},{20,16},{24,28},{28,24},{1,5},{5... | collective-permute-start | bytes 6291464 | tf_op jit(solution)/shard_map/ppermute | solution.py:87
  311.7 274.7 %reduce-scatter.9.cloned.1.call-start = ((), (), s32[]{:S(2)}) async-start(), calls=%async_computation.6 | async-start | bytes 5242880 | tf_op jit(solution)/shard_map/reduce_scatter | solution.py:110
  319.4 47.8 %collective-permute-start.34 = (bf16[512,2048]{1,0:T(8,128)(2,1)S(1)}, bf16[512,2048]{1,0:T(8,128)(2,1)}, u32[]{:S(2)}, u32[]{:S(2)}) collective-permute-start(bf16[512,2048]{1,0:T(8,128)(2,1)S(1)} %shard_map.392.refs_2_), channel_id=1, source_target_pairs={{0,2},{1,3},{2,0},{3,1},{4,6},{5,7},{6,4},{7,5},{8,10},{9,11},{10,... | collective-permute-start | bytes 6291464 | tf_op jit(solution)/shard_map/ppermute | solution.py:93
  332.5 41.5 %collective-permute-start.40 = (bf16[128,2048]{1,0:T(8,128)(2,1)}, bf16[128,2048]{1,0:T(8,128)(2,1)S(1)}, u32[]{:S(2)}, u32[]{:S(2)}) collective-permute-start(bf16[128,2048]{1,0:T(8,128)(2,1)} %get-tuple-element.343), channel_id=1, source_target_pairs={{0,1},{1,0},{2,3},{3,2},{4,5},{5,4},{6,7},{7,6},{8,9},{9,8},{10,11... | collective-permute-start | bytes 1572872 | tf_op jit(solution)/shard_map/ppermute | solution.py:77
  332.5 41.9 %collective-permute-start.41 = (bf16[128,2048]{1,0:T(8,128)(2,1)}, bf16[128,2048]{1,0:T(8,128)(2,1)}, u32[]{:S(2)}, u32[]{:S(2)}) collective-permute-start(bf16[128,2048]{1,0:T(8,128)(2,1)} %get-tuple-element.342), channel_id=1, source_target_pairs={{0,1},{1,0},{2,3},{3,2},{4,5},{5,4},{6,7},{7,6},{8,9},{9,8},{10,11... | collective-permute-start | bytes 1572872 | tf_op jit(solution)/shard_map/ppermute | solution.py:77
  333.0 46.4 %collective-permute-start.42 = (bf16[128,2048]{1,0:T(8,128)(2,1)}, bf16[128,2048]{1,0:T(8,128)(2,1)}, u32[]{:S(2)}, u32[]{:S(2)}) collective-permute-start(bf16[128,2048]{1,0:T(8,128)(2,1)} %get-tuple-element.341), channel_id=1, source_target_pairs={{0,1},{1,0},{2,3},{3,2},{4,5},{5,4},{6,7},{7,6},{8,9},{9,8},{10,11... | collective-permute-start | bytes 1572872 | tf_op jit(solution)/shard_map/ppermute | solution.py:77
  333.1 46.7 %collective-permute-start.43 = (bf16[128,2048]{1,0:T(8,128)(2,1)}, bf16[128,2048]{1,0:T(8,128)(2,1)}, u32[]{:S(2)}, u32[]{:S(2)}) collective-permute-start(bf16[128,2048]{1,0:T(8,128)(2,1)} %get-tuple-element.340), channel_id=1, source_target_pairs={{0,1},{1,0},{2,3},{3,2},{4,5},{5,4},{6,7},{7,6},{8,9},{9,8},{10,11... | collective-permute-start | bytes 1572872 | tf_op jit(solution)/shard_map/ppermute | solution.py:77
  370.0 11.7 %collective-permute-start.45 = (bf16[128,2048]{1,0:T(8,128)(2,1)S(1)}, bf16[128,2048]{1,0:T(8,128)(2,1)S(1)}, u32[]{:S(2)}, u32[]{:S(2)}) collective-permute-start(bf16[128,2048]{1,0:T(8,128)(2,1)S(1)} %get-tuple-element.339), channel_id=1, source_target_pairs={{0,1},{1,0},{2,3},{3,2},{4,5},{5,4},{6,7},{7,6},{8,9},{9,8},{10,11... | collective-permute-start | bytes 1572872 | tf_op jit(solution)/shard_map/ppermute | solution.py:77
  374.1 8.6 %collective-permute-start.46 = (bf16[128,2048]{1,0:T(8,128)(2,1)S(1)}, bf16[128,2048]{1,0:T(8,128)(2,1)S(1)}, u32[]{:S(2)}, u32[]{:S(2)}) collective-permute-start(bf16[128,2048]{1,0:T(8,128)(2,1)S(1)} %get-tuple-element.338), channel_id=1, source_target_pairs={{0,1},{1,0},{2,3},{3,2},{4,5},{5,4},{6,7},{7,6},{8,9},{9,8},{10,11... | collective-permute-start | bytes 1572872 | tf_op jit(solution)/shard_map/ppermute | solution.py:77
  374.5 9.3 %collective-permute-start.47 = (bf16[128,2048]{1,0:T(8,128)(2,1)S(1)}, bf16[128,2048]{1,0:T(8,128)(2,1)S(1)}, u32[]{:S(2)}, u32[]{:S(2)}) collective-permute-start(bf16[128,2048]{1,0:T(8,128)(2,1)S(1)} %get-tuple-element.337), channel_id=1, source_target_pairs={{0,1},{1,0},{2,3},{3,2},{4,5},{5,4},{6,7},{7,6},{8,9},{9,8},{10,11... | collective-permute-start | bytes 1572872 | tf_op jit(solution)/shard_map/ppermute | solution.py:77
  379.4 13.6 %collective-permute-start.48 = (bf16[128,2048]{1,0:T(8,128)(2,1)}, bf16[128,2048]{1,0:T(8,128)(2,1)}, u32[]{:S(2)}, u32[]{:S(2)}) collective-permute-start(bf16[128,2048]{1,0:T(8,128)(2,1)} %get-tuple-element.336), channel_id=1, source_target_pairs={{0,1},{1,0},{2,3},{3,2},{4,5},{5,4},{6,7},{7,6},{8,9},{9,8},{10,11... | collective-permute-start | bytes 1572872 | tf_op jit(solution)/shard_map/ppermute | solution.py:77
  381.3 19.3 %collective-permute-start.35 = (bf16[128,2048]{1,0:T(8,128)(2,1)}, bf16[128,2048]{1,0:T(8,128)(2,1)}, u32[]{:S(2)}, u32[]{:S(2)}) collective-permute-start(bf16[128,2048]{1,0:T(8,128)(2,1)} %get-tuple-element.347), channel_id=1, source_target_pairs={{0,1},{1,0},{2,3},{3,2},{4,5},{5,4},{6,7},{7,6},{8,9},{9,8},{10,11... | collective-permute-start | bytes 1572872 | tf_op jit(solution)/shard_map/ppermute | solution.py:77
  382.5 18.2 %collective-permute-start.36 = (bf16[128,2048]{1,0:T(8,128)(2,1)}, bf16[128,2048]{1,0:T(8,128)(2,1)}, u32[]{:S(2)}, u32[]{:S(2)}) collective-permute-start(bf16[128,2048]{1,0:T(8,128)(2,1)} %get-tuple-element.346), channel_id=1, source_target_pairs={{0,1},{1,0},{2,3},{3,2},{4,5},{5,4},{6,7},{7,6},{8,9},{9,8},{10,11... | collective-permute-start | bytes 1572872 | tf_op jit(solution)/shard_map/ppermute | solution.py:77
  383.4 17.2 %collective-permute-start.37 = (bf16[128,2048]{1,0:T(8,128)(2,1)}, bf16[128,2048]{1,0:T(8,128)(2,1)}, u32[]{:S(2)}, u32[]{:S(2)}) collective-permute-start(bf16[128,2048]{1,0:T(8,128)(2,1)} %get-tuple-element.345), channel_id=1, source_target_pairs={{0,1},{1,0},{2,3},{3,2},{4,5},{5,4},{6,7},{7,6},{8,9},{9,8},{10,11... | collective-permute-start | bytes 1572872 | tf_op jit(solution)/shard_map/ppermute | solution.py:77
  384.6 16.1 %collective-permute-start.38 = (bf16[128,2048]{1,0:T(8,128)(2,1)}, bf16[128,2048]{1,0:T(8,128)(2,1)}, u32[]{:S(2)}, u32[]{:S(2)}) collective-permute-start(bf16[128,2048]{1,0:T(8,128)(2,1)} %get-tuple-element.344), channel_id=1, source_target_pairs={{0,1},{1,0},{2,3},{3,2},{4,5},{5,4},{6,7},{7,6},{8,9},{9,8},{10,11... | collective-permute-start | bytes 1572872 | tf_op jit(solution)/shard_map/ppermute | solution.py:77
  392.3 253.6 %reduce-scatter.11.cloned.1.call-start = ((), (), s32[]{:S(2)}) async-start(), calls=%async_computation.7 | async-start | bytes 3276800 | tf_op jit(solution)/shard_map/reduce_scatter | solution.py:110
  393.0 48.8 %collective-permute-start.44 = (bf16[512,2048]{1,0:T(8,128)(2,1)}, bf16[512,2048]{1,0:T(8,128)(2,1)}, u32[]{:S(2)}, u32[]{:S(2)}) collective-permute-start(bf16[512,2048]{1,0:T(8,128)(2,1)} %copy-done.29), channel_id=1, source_target_pairs={{0,4},{4,0},{8,12},{12,8},{16,20},{20,16},{24,28},{28,24},{1,5},{5... | collective-permute-start | bytes 6291464 | tf_op jit(solution)/shard_map/ppermute | solution.py:87
  435.7 36.9 %collective-permute-start.39 = (bf16[512,128]{1,0:T(8,128)(2,1)}, bf16[512,128]{1,0:T(8,128)(2,1)S(1)}, u32[]{:S(2)}, u32[]{:S(2)}) collective-permute-start(bf16[512,128]{1,0:T(8,128)(2,1)} %pad_maximum_fusion.3), channel_id=1, source_target_pairs={{4,0},{8,4},{12,8},{16,12},{20,16},{24,20},{28,24},{5,1},{9,5},{13... | collective-permute-start | bytes 393224 | tf_op jit(solution)/shard_map/ppermute | solution.py:133
  441.8 9.4 %collective-permute-start.49 = (bf16[2,80,128]{2,1,0:T(8,128)(2,1)S(1)}, bf16[2,80,128]{2,1,0:T(8,128)(2,1)S(1)}, u32[]{:S(2)}, u32[]{:S(2)}) collective-permute-start(bf16[2,80,128]{2,1,0:T(8,128)(2,1)S(1)} %convert_element_type.238), channel_id=1, source_target_pairs={{4,0},{8,4},{12,8},{16,12},{20,16},{24,20},{28,24},{5,1},{9,5},{13... | collective-permute-start | bytes 122888 | tf_op jit(solution)/shard_map/ppermute | solution.py:133
  448.5 75.8 %collective-permute-start.60 = (bf16[1024,512]{1,0:T(8,128)(2,1)}, bf16[1024,512]{1,0:T(8,128)(2,1)}, u32[]{:S(2)}, u32[]{:S(2)}) collective-permute-start(bf16[1024,512]{1,0:T(8,128)(2,1)} %shard_map.400.refs_11_), channel_id=1, source_target_pairs={{0,4},{4,0},{8,12},{12,8},{16,20},{20,16},{24,28},{28,24},{1,5},{5... | collective-permute-start | bytes 3145736 | tf_op jit(solution)/shard_map/ppermute | solution.py:87
  451.2 8.2 %collective-permute-start.50 = (bf16[2,80,128]{2,1,0:T(8,128)(2,1)S(1)}, bf16[2,80,128]{2,1,0:T(8,128)(2,1)S(1)}, u32[]{:S(2)}, u32[]{:S(2)}) collective-permute-start(bf16[2,80,128]{2,1,0:T(8,128)(2,1)S(1)} %fusion.19), channel_id=1, source_target_pairs={{8,0},{12,4},{16,8},{20,12},{24,16},{28,20},{9,1},{13,5},{17,9},{2... | collective-permute-start | bytes 122888 | tf_op jit(solution)/shard_map/ppermute | solution.py:133
  460.1 11.7 %collective-permute-start.51 = (bf16[2,80,128]{2,1,0:T(8,128)(2,1)}, bf16[2,80,128]{2,1,0:T(8,128)(2,1)}, u32[]{:S(2)}, u32[]{:S(2)}) collective-permute-start(bf16[2,80,128]{2,1,0:T(8,128)(2,1)} %fusion.18), channel_id=1, source_target_pairs={{16,0},{20,4},{24,8},{28,12},{17,1},{21,5},{25,9},{29,13},{18,2},{... | collective-permute-start | bytes 122888 | tf_op jit(solution)/shard_map/ppermute | solution.py:133
  501.3 48.8 %collective-permute-start.57 = (bf16[512,2048]{1,0:T(8,128)(2,1)}, bf16[512,2048]{1,0:T(8,128)(2,1)}, u32[]{:S(2)}, u32[]{:S(2)}) collective-permute-start(bf16[512,2048]{1,0:T(8,128)(2,1)} %shard_map.403.rest_0_), channel_id=1, source_target_pairs={{0,2},{1,3},{2,0},{3,1},{4,6},{5,7},{6,4},{7,5},{8,10},{9,11},{10,... | collective-permute-start | bytes 6291464 | tf_op jit(solution)/shard_map/ppermute | solution.py:93
  507.6 38.5 %collective-permute-start.59 = (bf16[1024,768]{1,0:T(8,128)(2,1)}, bf16[1024,768]{1,0:T(8,128)(2,1)}, u32[]{:S(2)}, u32[]{:S(2)}) collective-permute-start(bf16[1024,768]{1,0:T(8,128)(2,1)} %shard_map.405.rest_1_), channel_id=1, source_target_pairs={{0,4},{4,0},{8,12},{12,8},{16,20},{20,16},{24,28},{28,24},{1,5},{5... | collective-permute-start | bytes 4718600 | tf_op jit(solution)/shard_map/ppermute | solution.py:87
  511.5 104.4 %collective-permute-start.56 = (bf16[512,2048]{1,0:T(8,128)(2,1)}, bf16[512,2048]{1,0:T(8,128)(2,1)}, u32[]{:S(2)}, u32[]{:S(2)}) collective-permute-start(bf16[512,2048]{1,0:T(8,128)(2,1)} %shard_map.404), channel_id=1, source_target_pairs={{0,2},{1,3},{2,0},{3,1},{4,6},{5,7},{6,4},{7,5},{8,10},{9,11},{10,... | collective-permute-start | bytes 6291464 | tf_op jit(solution)/shard_map/ppermute | solution.py:93
  565.3 39.2 %collective-permute-start.61 = (bf16[128,2048]{1,0:T(8,128)(2,1)}, bf16[128,2048]{1,0:T(8,128)(2,1)}, u32[]{:S(2)}, u32[]{:S(2)}) collective-permute-start(bf16[128,2048]{1,0:T(8,128)(2,1)} %get-tuple-element.331), channel_id=1, source_target_pairs={{0,1},{1,0},{2,3},{3,2},{4,5},{5,4},{6,7},{7,6},{8,9},{9,8},{10,11... | collective-permute-start | bytes 1572872 | tf_op jit(solution)/shard_map/ppermute | solution.py:77
  565.3 13.8 %collective-permute-start.70 = (f32[2048]{0:T(1024)S(1)}, f32[2048]{0:T(1024)}, u32[]{:S(2)}, u32[]{:S(2)}) collective-permute-start(f32[2048]{0:T(1024)S(1)} %get-tuple-element.304), channel_id=1, source_target_pairs={{0,1},{1,0},{2,3},{3,2},{4,5},{5,4},{6,7},{7,6},{8,9},{9,8},{10,11... | collective-permute-start | bytes 24584 | tf_op jit(solution)/shard_map/ppermute | solution.py:984
  575.2 8.3 %collective-permute-start.75 = (bf16[4,14848]{1,0:T(4,128)(2,1)}, bf16[4,14848]{1,0:T(4,128)(2,1)S(1)}, u32[]{:S(2)}, u32[]{:S(2)}) collective-permute-start(bf16[4,14848]{1,0:T(4,128)(2,1)} %bitcast.128), channel_id=1, source_target_pairs={{0,4},{4,0},{8,12},{12,8},{16,20},{20,16},{24,28},{28,24},{1,5},{5... | collective-permute-start | bytes 356360 | tf_op jit(solution)/shard_map/ppermute | solution.py:121
  584.1 6.1 collective-permute-start.78
  584.2 6.9 %collective-permute-start.77 = (bf16[14848]{0:T(1024)(128)(2,1)S(1)}, bf16[14848]{0:T(1024)(128)(2,1)S(1)}, u32[]{:S(2)}, u32[]{:S(2)}) collective-permute-start(bf16[14848]{0:T(1024)(128)(2,1)S(1)} %get-tuple-element.310), channel_id=1, source_target_pairs={{0,16},{4,20},{8,24},{12,28},{16,0},{20,4},{24,8},{28,12},{1,17},{... | collective-permute-start | bytes 89096 | tf_op jit(solution)/shard_map/ppermute | solution.py:127
  584.3 7.8 %collective-permute-start.76 = (bf16[14848]{0:T(1024)(128)(2,1)S(1)}, bf16[14848]{0:T(1024)(128)(2,1)S(1)}, u32[]{:S(2)}, u32[]{:S(2)}) collective-permute-start(bf16[14848]{0:T(1024)(128)(2,1)S(1)} %get-tuple-element.308), channel_id=1, source_target_pairs={{0,8},{4,12},{8,16},{12,20},{16,24},{20,28},{24,0},{28,4},{1,9},{5... | collective-permute-start | bytes 89096 | tf_op jit(solution)/shard_map/ppermute | solution.py:127
  591.1 35.3 %collective-permute-start.65 = (bf16[768,1024]{1,0:T(8,128)(2,1)}, bf16[768,1024]{1,0:T(8,128)(2,1)}, u32[]{:S(2)}, u32[]{:S(2)}) collective-permute-start(bf16[768,1024]{1,0:T(8,128)(2,1)} %pad_maximum_fusion.2), channel_id=1, source_target_pairs={{0,4},{4,0},{8,12},{12,8},{16,20},{20,16},{24,28},{28,24},{1,5},{5... | collective-permute-start | bytes 4718600 | tf_op jit(solution)/shard_map/ppermute | solution.py:87
  598.2 11.6 %collective-permute-start.62 = (bf16[128,2048]{1,0:T(8,128)(2,1)}, bf16[128,2048]{1,0:T(8,128)(2,1)S(1)}, u32[]{:S(2)}, u32[]{:S(2)}) collective-permute-start(bf16[128,2048]{1,0:T(8,128)(2,1)} %get-tuple-element.330), channel_id=1, source_target_pairs={{0,1},{1,0},{2,3},{3,2},{4,5},{5,4},{6,7},{7,6},{8,9},{9,8},{10,11... | collective-permute-start | bytes 1572872 | tf_op jit(solution)/shard_map/ppermute | solution.py:77
  631.1 9.5 %collective-permute-start.66 = (bf16[128,2048]{1,0:T(8,128)(2,1)}, bf16[128,2048]{1,0:T(8,128)(2,1)}, u32[]{:S(2)}, u32[]{:S(2)}) collective-permute-start(bf16[128,2048]{1,0:T(8,128)(2,1)} %get-tuple-element.327), channel_id=1, source_target_pairs={{0,1},{1,0},{2,3},{3,2},{4,5},{5,4},{6,7},{7,6},{8,9},{9,8},{10,11... | collective-permute-start | bytes 1572872 | tf_op jit(solution)/shard_map/ppermute | solution.py:77
  631.1 9.5 %collective-permute-start.67 = (bf16[128,2048]{1,0:T(8,128)(2,1)}, bf16[128,2048]{1,0:T(8,128)(2,1)}, u32[]{:S(2)}, u32[]{:S(2)}) collective-permute-start(bf16[128,2048]{1,0:T(8,128)(2,1)} %get-tuple-element.326), channel_id=1, source_target_pairs={{0,1},{1,0},{2,3},{3,2},{4,5},{5,4},{6,7},{7,6},{8,9},{9,8},{10,11... | collective-permute-start | bytes 1572872 | tf_op jit(solution)/shard_map/ppermute | solution.py:77
  631.6 9.0 %collective-permute-start.68 = (bf16[128,2048]{1,0:T(8,128)(2,1)}, bf16[128,2048]{1,0:T(8,128)(2,1)}, u32[]{:S(2)}, u32[]{:S(2)}) collective-permute-start(bf16[128,2048]{1,0:T(8,128)(2,1)} %get-tuple-element.325), channel_id=1, source_target_pairs={{0,1},{1,0},{2,3},{3,2},{4,5},{5,4},{6,7},{7,6},{8,9},{9,8},{10,11... | collective-permute-start | bytes 1572872 | tf_op jit(solution)/shard_map/ppermute | solution.py:77
  631.6 9.0 %collective-permute-start.69 = (bf16[128,2048]{1,0:T(8,128)(2,1)}, bf16[128,2048]{1,0:T(8,128)(2,1)}, u32[]{:S(2)}, u32[]{:S(2)}) collective-permute-start(bf16[128,2048]{1,0:T(8,128)(2,1)} %get-tuple-element.324), channel_id=1, source_target_pairs={{0,1},{1,0},{2,3},{3,2},{4,5},{5,4},{6,7},{7,6},{8,9},{9,8},{10,11... | collective-permute-start | bytes 1572872 | tf_op jit(solution)/shard_map/ppermute | solution.py:77
  (148 other events, 835.7 us)
Sparse Core Ops, SparseCore 0:
  240.4 78.5 reduce-scatter.4
  321.4 77.2 reduce-scatter.6
  401.0 82.6 reduce-scatter.8
  579.2 50.9 reduce-scatter.10

commit v5 on v4

--- a/solution.py
+++ b/solution.py
@@ -376,7 +376,7 @@
         in_specs=specs + [ANY] * len(after),
         out_specs=[vmem] * len(outs),
         scratch_shapes=[pltpu.VMEM(s, d) for s, d in scratch],
-        compiler_params=pltpu.CompilerParams(vmem_limit_bytes=48 * 2**20),
+        compiler_params=pltpu.CompilerParams(vmem_limit_bytes=38 * 2**20),
         cost_estimate=cost(us),
     )(*args, *after)
 
@@ -517,7 +517,7 @@
             jax.ShapeDtypeStruct((2 * kw, t), BF16),
             jax.ShapeDtypeStruct((t, down.shape[1]), BF16),
         ],
-        compiler_params=pltpu.CompilerParams(vmem_limit_bytes=48 * 2**20),
+        compiler_params=pltpu.CompilerParams(vmem_limit_bytes=38 * 2**20),
         cost_estimate=cost(10.0),
     )(tokens, gain, wq, wk, wv, down, up)
 
@@ -577,7 +577,7 @@
             out_specs=[pl.BlockSpec((rows // n_out, tile), lambda i, s: (0, i))] * n_out,
         ),
         out_shape=[jax.ShapeDtypeStruct((rows // n_out, width), out)] * n_out,
-        compiler_params=pltpu.CompilerParams(vmem_limit_bytes=56 * 2**20),
+        compiler_params=pltpu.CompilerParams(vmem_limit_bytes=38 * 2**20),
         cost_estimate=cost(us),
     )(jnp.stack([chosen, core]).astype(jnp.int32), *args, *after)
     return made if split is not None else made[0]
@@ -601,7 +601,7 @@
         in_specs=specs * len(pairs) + [ANY] * len(after),
         out_specs=pl.BlockSpec((block, n), lambda j: (j, 0)),
         out_shape=jax.ShapeDtypeStruct((width, n), BF16),
-        compiler_params=pltpu.CompilerParams(vmem_limit_bytes=48 * 2**20),
+        compiler_params=pltpu.CompilerParams(vmem_limit_bytes=38 * 2**20),
         cost_estimate=cost(13.0),
     )(*[x for pair in pairs for x in pair], *after)
 
@@ -633,7 +633,7 @@
             out_specs=spec,
         ),
         out_shape=jax.ShapeDtypeStruct((line * block, n), BF16),
-        compiler_params=pltpu.CompilerParams(vmem_limit_bytes=48 * 2**20),
+        compiler_params=pltpu.CompilerParams(vmem_limit_bytes=38 * 2**20),
         cost_estimate=cost(1.0),
     )(select.astype(jnp.int32)[None], a, b, *more, *after)
 
@@ -692,7 +692,7 @@
         ),
         out_shape=shapes,
         input_output_aliases={6 + i: i for i in range(len(held))},
-        compiler_params=pltpu.CompilerParams(vmem_limit_bytes=56 * 2**20),
+        compiler_params=pltpu.CompilerParams(vmem_limit_bytes=38 * 2**20),
         cost_estimate=cost(11.0),
     )(sel, own, other, wg, wu, gh, *held, *after)
 
@@ -971,9 +971,11 @@
         + rms_one * s_one
         - stream * rms_one**3 * jnp.mean(stream * s_one, -1, keepdims=True)
     ).astype(BF16)
-    grad_tokens = grid.gather_rows(own_grad, F32)
+    own_blocks = grid.blocks_across(own_grad)
+    fins = grid.swap(jnp.concatenate([grid.pair_half(g) for g in (grad_d, grad_g, grad_u)], 0))
+    own_grad, fins = tie(own_grad, fins)
+    grad_tokens = merge_rows(grid.core, own_grad, own_blocks, F32)
     down_terms[-1], grad_tokens = tie(down_terms[-1], grad_tokens)
-    fins = grid.swap(jnp.concatenate([grid.pair_half(g) for g in (grad_d, grad_g, grad_u)], 0))
     down_terms[-1], fins = tie(down_terms[-1], fins)
     fins = jnp.split(fins, 3, 0)
     grad_down = finish(mine, grad_d, fins[0], True)

time: 667 us -> 662 us (level)
  Pallas kernels: 262 us -> 229 us
  local copies, waits for them, and re-layouts: 106 us -> 126 us
  waiting for transfers between devices: 152 us -> 159 us
    unnamed x241 -> x291, local copies, waits for them, and re-layouts: 50.6 us -> 82.7 us
    pallas_call x8, Pallas kernels: 79.8 us -> 63.2 us  [matmul(): pl.pallas_call(kernel, grid_spec=pltpu.PrefetchScalarGridSpec(num_scalar_...]
    pallas_call x4, Pallas kernels: 44.7 us -> 35.4 us  [gated(): pl.pallas_call(gated_kernel, grid_spec=pltpu.PrefetchScalarGridSpec(num_s...]
    slice x10, local copies, waits for them, and re-layouts: 18.6 us -> 10.6 us  [blocks_across(): return [self.across_cores(x[i * rows:(i + 1) * rows]) for i in range(4)]]
  transfers between devices with their start and end apart: 85 -> 85, of which waited for: 39 -> 39; matrix products, arithmetic and copies ran while one was open for 17% -> 14% of each run, Pallas kernels for 32% -> 28%
where the time goes in v5:
time: 662 us; the launch traced here: 652 us
  Pallas kernels  229 us (35%)
  waiting for transfers between devices  159 us (24%)
  local copies, waits for them, and re-layouts  126 us (19%)
  starting transfers between devices  70.2 us (11%)
  other arithmetic  36.1 us (5%)
  matrix products  16.6 us (3%)
  between operations  16.1 us (2%)
    unnamed x291, local copies, waits for them, and re-layouts  82.7 us
    pallas_call x8, Pallas kernels, matmul(): pl.pallas_call(kernel, grid_spec=pltpu.PrefetchScalarGridSpec(num_scalar_...  63.2 us
    ppermute x8, waiting for transfers between devices, swap(): return lax.ppermute(x, 'seq', self.x_swap)  60.7 us
    ppermute x5, waiting for transfers between devices, outer_terms(): lax.ppermute(half, 'kv', self.y_shift(j))  50.5 us
    pallas_call x3, Pallas kernels, grad_pair(): pl.pallas_call(kernel, grid=(count,), in_specs=specs * len(pairs) + [ANY]...  35.7 us
    pallas_call x4, Pallas kernels, gated(): pl.pallas_call(gated_kernel, grid_spec=pltpu.PrefetchScalarGridSpec(num_s...  35.4 us
    pallas_call x4, Pallas kernels, call(): pl.pallas_call(lambda *refs: kernel(*refs[:count], *refs[count + len(afte...  32.9 us
    ppermute x8, starting transfers between devices, shift_seq(): return lax.ppermute(x, 'seq', pairs)  24.1 us
  transfers between devices with their start and end apart: 85, of which 39 were waited for; matrix products, arithmetic and copies ran while one was open for 14% of the time, Pallas kernels for 28%

profile of v5, /device:TPU:0, one launch (start us, length us, event | category | flops | bytes accessed | tf_op | source)
XLA Modules:
  0.0 652.3 jit_solution(7776768877773700972)
XLA Ops:
  16.0 8.7 %shard_map.373 = (bf16[1024,2048]{1,0:T(8,128)(2,1)S(1)}, bf16[512,1024]{1,0:T(8,128)(2,1)S(1)}, bf16[256,1024]{1,0:T(8,128)(2,1)S(1)}, bf16[1024,128]{1,0:T(8,128)(2,1)S(1)}) custom-call(bf16[1024,2048]{1,0:T(8,128)(2,1)S(1)} %copy-done.10, bf16[1,2048]{1,0:T(2,128)(2,1)S(1)} %broadcast_in_dim.31.gain_ref, bf16[2048,512]{1,0:T(8,128)(2,1)S(1)} %copy-done.92, ...), custom_call_target="tpu_custom_call" | custom-call | flops 4499999744 | bytes 1 | tf_op jit(solution)/shard_map/pallas_call | solution.py:509
  28.8 5.5 collective-permute-start
  34.3 4.0 add_convert_fusion.refs_1_
  45.9 7.6 %shard_map.375.gh_ref = f32[1024,1024]{1,0:T(8,128)S(1)} custom-call(s32[2]{0:T(128)S(1)} %pad_add_fusion.1.sel, bf16[1024,2048]{1,0:T(8,128)(2,1)S(1)} %copy-done.23, bf16[2048,2048]{1,0:T(8,128)(2,1)} %refs_1_.11), custom_call_target="tpu_custom_call" | custom-call | flops 1899551488 | bytes 1 | tf_op jit(solution)/shard_map/pallas_call | solution.py:571
  63.6 5.2 collective-permute-start.2
  70.9 5.5 collective-permute-start.3
  78.3 9.1 %shard_map.376 = (bf16[512,1024]{1,0:T(8,128)(2,1)S(1)}, f32[8,1024]{1,0:T(8,128)S(1)}, f32[8,2,80,128]{3,2,1,0:T(8,128)S(1)}) custom-call(bf16[512,1024]{1,0:T(8,128)(2,1)S(1)} %copy-done.104, bf16[256,1152]{1,0:T(8,128)(2,1)S(1)} %constant_dynamic-update-slice_fusion.refs_0_.refs_1_, bf16[2,128,1152]{2,1,0:T(8,128)(2,1)S(1)} %get-tuple-element.114.refs_2_.refs_1_, ...), custom_call_target="tpu_custom_call" | custom-call | flops 4049999872 | bytes 1 | tf_op jit(solution)/shard_map/pallas_call | solution.py:373
  88.9 4.1 shard_map.377
  102.1 19.4 %collective-permute-done.12 = bf16[256,2048]{1,0:T(8,128)(2,1)S(1)} collective-permute-done((bf16[256,2048]{1,0:T(8,128)(2,1)S(1)}, bf16[256,2048]{1,0:T(8,128)(2,1)S(1)}, u32[]{:S(2)}, u32[]{:S(2)}) %collective-permute-start.12) | collective-permute-done | bytes 1048608 | tf_op jit(solution)/shard_map/ppermute | solution.py:93
  125.2 8.7 %shard_map.380 = (bf16[1024,2048]{1,0:T(8,128)(2,1)S(1)}, bf16[1024,1024]{1,0:T(8,128)(2,1)S(1)}, bf16[1024,1024]{1,0:T(8,128)(2,1)S(1)}, bf16[1024,1024]{1,0:T(8,128)(2,1)S(1)}) custom-call(s32[2]{0:T(128)S(1)} %pad_add_fusion.3.sel_ref, bf16[256,2048]{1,0:T(8,128)(2,1)S(1)} %multiply_convert_fusion.1.own_ref, ...), custom_call_target="tpu_custom_call" | custom-call | flops 4950000128 | bytes 1 | tf_op jit(solution)/shard_map/pallas_call | solution.py:678
  134.0 14.2 %collective-permute-done.13 = bf16[256,2048]{1,0:T(8,128)(2,1)S(1)} collective-permute-done((bf16[256,2048]{1,0:T(8,128)(2,1)S(1)}, bf16[256,2048]{1,0:T(8,128)(2,1)S(1)}, u32[]{:S(2)}, u32[]{:S(2)}) %collective-permute-start.13) | collective-permute-done | bytes 1048608 | tf_op jit(solution)/shard_map/ppermute | solution.py:93
  157.2 8.1 %shard_map.382.refs_4_.gh_ref = f32[1024,1024]{1,0:T(8,128)S(1)} custom-call(s32[2]{0:T(128)S(1)} %pad_add_fusion.1.sel, bf16[1024,2048]{1,0:T(8,128)(2,1)S(1)} %shard_map.381.refs_0_.refs_2_, bf16[2048,2048]{1,0:T(8,128)(2,1)} %refs_1_.11, bf16[256,2048]{1,0:T(8,128)(2,1)S(1)} %multiply_convert_fusion.refs_2_.own_ref), custom_call_target="tpu_custom_call" | custom-call | flops 1899551488 | bytes 1 | tf_op jit(solution)/shard_map/pallas_call | solution.py:571
  167.3 8.7 %shard_map.383 = (bf16[1024,2048]{1,0:T(8,128)(2,1)S(1)}, bf16[1024,1024]{1,0:T(8,128)(2,1)S(1)}, bf16[1024,1024]{1,0:T(8,128)(2,1)S(1)}, bf16[1024,1024]{1,0:T(8,128)(2,1)S(1)}) custom-call(s32[2]{0:T(128)S(1)} %pad_add_fusion.3.sel_ref, ...), custom_call_target="tpu_custom_call", output_to_operand_aliasing={{0}: (6, {}), {1}: (7, {}), {2}: (8, {}), {3}: (9, {})} | custom-call | flops 4950000128 | bytes 1 | tf_op jit(solution)/shard_map/pallas_call | solution.py:678
  180.1 8.9 %shard_map.384 = (bf16[1024,2048]{1,0:T(8,128)(2,1)S(1)}, bf16[1024,1024]{1,0:T(8,128)(2,1)S(1)}, bf16[1024,1024]{1,0:T(8,128)(2,1)S(1)}, bf16[1024,1024]{1,0:T(8,128)(2,1)S(1)}) custom-call(s32[2]{0:T(128)S(1)} %pad_add_fusion.3.sel_ref, bf16[256,2048]{1,0:T(8,128)(2,1)S(1)} %collective-permute-done.22.own_ref, ...), custom_call_target="tpu_custom_call" | custom-call | flops 4950000128 | bytes 1 | tf_op jit(solution)/shard_map/pallas_call | solution.py:678
  189.0 14.0 %collective-permute-done.21.own_ref = bf16[256,2048]{1,0:T(8,128)(2,1)S(1)} collective-permute-done((bf16[256,2048]{1,0:T(8,128)(2,1)S(1)}, bf16[256,2048]{1,0:T(8,128)(2,1)S(1)}, u32[]{:S(2)}, u32[]{:S(2)}) %collective-permute-start.21) | collective-permute-done | bytes 1048608 | tf_op jit(solution)/shard_map/ppermute | solution.py:87
  205.6 9.0 %shard_map.385 = (bf16[1024,2048]{1,0:T(8,128)(2,1)S(1)}, bf16[1024,1024]{1,0:T(8,128)(2,1)S(1)}, bf16[1024,1024]{1,0:T(8,128)(2,1)S(1)}, bf16[1024,1024]{1,0:T(8,128)(2,1)S(1)}) custom-call(s32[2]{0:T(128)S(1)} %pad_add_fusion.3.sel_ref, ...), custom_call_target="tpu_custom_call", output_to_operand_aliasing={{0}: (6, {}), {1}: (7, {}), {2}: (8, {}), {3}: (9, {})} | custom-call | flops 4950000128 | bytes 1 | tf_op jit(solution)/shard_map/pallas_call | solution.py:678
  219.3 11.8 %shard_map.386.refs_4_ = bf16[2048,1024]{1,0:T(8,128)(2,1)S(1)} custom-call(bf16[1024,2048]{1,0:T(8,128)(2,1)S(1)} %copy-done.24, bf16[1024,1024]{1,0:T(8,128)(2,1)S(1)} %get-tuple-element.144.refs_0_.refs_1_, bf16[1024,2048]{1,0:T(8,128)(2,1)} %copy-done.17, bf16[1024,1024]{1,0:T(8,128)(2,1)S(1)} %get-tuple-element.153.refs_3_.refs_0_), custom_call_target="tpu_custom_call" | custom-call | flops 5849999872 | bytes 1 | tf_op jit(solution)/shard_map/pallas_call | solution.py:598
  239.9 11.9 %shard_map.387 = (bf16[512,2048]{1,0:T(8,128)(2,1)S(1)}, bf16[512,2048]{1,0:T(8,128)(2,1)S(1)}) custom-call(s32[2]{0:T(128)S(1)} %pad_add_fusion.sel, bf16[1024,1024]{1,0:T(8,128)(2,1)S(1)} %copy-done.35, bf16[2048,2048]{1,0:T(8,128)(2,1)} %refs_1_.9, bf16[1024,1024]{1,0:T(8,128)(2,1)S(1)} %copy-done.38, bf16[2048,2048]{1,0:T(8,128)(2,1)} %refs_3_.4, ...), custom_call_target="tpu_custom_call" | custom-call | flops 3349102848 | bytes 1 | tf_op jit(solution)/shard_map/pallas_call | solution.py:571
  259.0 12.2 %shard_map.388 = (bf16[512,2048]{1,0:T(8,128)(2,1)S(1)}, bf16[512,2048]{1,0:T(8,128)(2,1)S(1)}) custom-call(s32[2]{0:T(128)S(1)} %pad_add_fusion.sel, bf16[1024,1024]{1,0:T(8,128)(2,1)S(1)} %get-tuple-element.140.refs_0_.refs_1_, bf16[2048,2048]{1,0:T(8,128)(2,1)} %refs_1_.9, bf16[1024,1024]{1,0:T(8,128)(2,1)S(1)} %copy-done.30, bf16[2048,2048]{1,0:T(8,128)(2,1)} %refs_3_.4, ...), custom_call_target="tpu_custom_call" | custom-call | flops 3349102848 | bytes 1 | tf_op jit(solution)/shard_map/pallas_call | solution.py:571
  272.5 12.0 %shard_map.391 = bf16[2048,1024]{1,0:T(8,128)(2,1)S(1)} custom-call(bf16[1024,2048]{1,0:T(8,128)(2,1)S(1)} %copy-done.42, bf16[1024,1024]{1,0:T(8,128)(2,1)S(1)} %get-tuple-element.140.refs_0_.refs_1_, bf16[1024,2048]{1,0:T(8,128)(2,1)} %copy-done.44, bf16[1024,1024]{1,0:T(8,128)(2,1)S(1)} %copy-done.36, ...), custom_call_target="tpu_custom_call" | custom-call | flops 5849999872 | bytes 1 | tf_op jit(solution)/shard_map/pallas_call | solution.py:598
  287.8 18.6 %collective-permute-done.33.refs_0_ = bf16[512,2048]{1,0:T(8,128)(2,1)} collective-permute-done((bf16[512,2048]{1,0:T(8,128)(2,1)}, bf16[512,2048]{1,0:T(8,128)(2,1)}, u32[]{:S(2)}, u32[]{:S(2)}) %collective-permute-start.33) | collective-permute-done | bytes 2097184 | tf_op jit(solution)/shard_map/ppermute | solution.py:87
  316.1 7.1 %shard_map.393 = (bf16[512,2048]{1,0:T(8,128)(2,1)S(1)}, bf16[512,2048]{1,0:T(8,128)(2,1)S(1)}) custom-call(s32[2]{0:T(128)S(1)} %pad_add_fusion.sel, bf16[1024,1024]{1,0:T(8,128)(2,1)S(1)} %copy-done.33, bf16[2048,2048]{1,0:T(8,128)(2,1)} %refs_1_.11, bf16[512,2048]{1,0:T(8,128)(2,1)S(1)} %shard_map.392.refs_2_), custom_call_target="tpu_custom_call" | custom-call | flops 1899551488 | bytes 1 | tf_op jit(solution)/shard_map/pallas_call | solution.py:571
  326.3 7.4 %shard_map.394 = (bf16[512,2048]{1,0:T(8,128)(2,1)S(1)}, bf16[512,2048]{1,0:T(8,128)(2,1)S(1)}) custom-call(s32[2]{0:T(128)S(1)} %pad_add_fusion.sel, bf16[1024,1024]{1,0:T(8,128)(2,1)S(1)} %copy-done.16, bf16[2048,2048]{1,0:T(8,128)(2,1)} %refs_1_.11, bf16[512,2048]{1,0:T(8,128)(2,1)S(1)} %get-tuple-element.161.refs_2_.keep_ref), custom_call_target="tpu_custom_call" | custom-call | flops 1899551488 | bytes 1 | tf_op jit(solution)/shard_map/pallas_call | solution.py:571
  335.0 11.9 %shard_map.395 = bf16[2048,1024]{1,0:T(8,128)(2,1)S(1)} custom-call(bf16[1024,2048]{1,0:T(8,128)(2,1)S(1)} %copy-done.43, bf16[1024,1024]{1,0:T(8,128)(2,1)S(1)} %copy-done.31, bf16[1024,2048]{1,0:T(8,128)(2,1)} %copy-done.44, bf16[1024,1024]{1,0:T(8,128)(2,1)S(1)} %copy-done.39, bf16[512,2048]{1,0:T(8,128)(2,1)S(1)} %get-tuple-element.171.refs_4_.keep_ref), custom_call_target="tpu_custom_call" | custom-call | flops 5849999872 | bytes 1 | tf_op jit(solution)/shard_map/pallas_call | solution.py:598
  350.3 12.0 %collective-permute-done.34 = bf16[512,2048]{1,0:T(8,128)(2,1)} collective-permute-done((bf16[512,2048]{1,0:T(8,128)(2,1)S(1)}, bf16[512,2048]{1,0:T(8,128)(2,1)}, u32[]{:S(2)}, u32[]{:S(2)}) %collective-permute-start.34) | collective-permute-done | bytes 2097184 | tf_op jit(solution)/shard_map/ppermute | solution.py:93
  369.1 4.8 fusion.35
  396.7 3.4 convolution_convert_fusion.refs_11_
  409.2 21.2 %shard_map.397 = (bf16[512,1024]{1,0:T(8,128)(2,1)S(1)}, f32[8,64,64]{2,1,0:T(8,128)S(1)}, f32[128,1152]{1,0:T(8,128)S(1)}, f32[128,1152]{1,0:T(8,128)S(1)}, f32...) custom-call(bf16[512,1024]{1,0:T(8,128)(2,1)S(1)} %copy-done.105, bf16[256,1152]{1,0:T(8,128)(2,1)S(1)} %copy-done.68, ...), custom_call_target="tpu_custom_call" | custom-call | flops 10800000000 | bytes 1 | tf_op jit(solution)/shard_map/pallas_call | solution.py:373
  444.5 9.1 %collective-permute-done.50 = bf16[2,80,128]{2,1,0:T(8,128)(2,1)S(1)} collective-permute-done((bf16[2,80,128]{2,1,0:T(8,128)(2,1)S(1)}, bf16[2,80,128]{2,1,0:T(8,128)(2,1)S(1)}, u32[]{:S(2)}, u32[]{:S(2)}) %collective-permute-start.50) | collective-permute-done | bytes 40992 | tf_op jit(solution)/shard_map/ppermute | solution.py:133
  455.6 4.2 shard_map.404
  461.5 4.6 collective-permute-done.51
  473.4 5.0 shard_map.402
  488.5 3.5 shard_map.403.rest_0_
  493.5 3.6 shard_map.405.rest_1_
  497.1 4.9 collective-permute-start.59
  505.7 3.7 fusion.10
  516.4 3.6 shard_map.406.rest_1_
  521.0 15.0 %collective-permute-done.59.rest_0_ = bf16[1024,768]{1,0:T(8,128)(2,1)} collective-permute-done((bf16[1024,768]{1,0:T(8,128)(2,1)}, bf16[1024,768]{1,0:T(8,128)(2,1)}, u32[]{:S(2)}, u32[]{:S(2)}) %collective-permute-start.59) | collective-permute-done | bytes 1572896 | tf_op jit(solution)/shard_map/ppermute | solution.py:87
  536.0 4.8 collective-permute-done.57
  544.3 4.6 shard_map.407
  548.9 4.4 fusion.6
  558.6 4.8 fusion.3.own_ref
  567.0 4.3 collective-permute-start.75
  576.2 4.6 collective-permute-start.78
  583.2 3.7 collective-permute-done.77
  599.0 11.2 %collective-permute-done.61 = bf16[768,1024]{1,0:T(8,128)(2,1)} collective-permute-done((bf16[768,1024]{1,0:T(8,128)(2,1)S(1)}, bf16[768,1024]{1,0:T(8,128)(2,1)}, u32[]{:S(2)}, u32[]{:S(2)}) %collective-permute-start.61) | collective-permute-done | bytes 1572896 | tf_op jit(solution)/shard_map/ppermute | solution.py:87
  615.0 6.1 shard_map.408
  635.4 5.3 shard_map.409
  (600 shorter events, 250.4 us)
Async XLA Ops:
  7.2 395.0 %reduce-scatter.5.cloned.1.call-start = ((), (), s32[]{:S(2)}) async-start(), calls=%async_computation.4 | async-start | bytes 5242880 | tf_op jit(solution)/shard_map/reduce_scatter | solution.py:110
  28.8 26.9 %collective-permute-start = (bf16[256,128]{1,0:T(8,128)(2,1)}, bf16[256,128]{1,0:T(8,128)(2,1)}, u32[]{:S(2)}, u32[]{:S(2)}) collective-permute-start(bf16[256,128]{1,0:T(8,128)(2,1)} %slice.361), channel_id=1, source_target_pairs={{0,4},{4,8},{8,12},{12,16},{16,20},{20,24},{24,28},{1,5},{5,9},{9,... | collective-permute-start | bytes 196616 | tf_op jit(solution)/shard_map/ppermute | solution.py:133
  63.6 7.3 %collective-permute-start.2 = (f32[2,80,128]{2,1,0:T(8,128)S(1)}, f32[2,80,128]{2,1,0:T(8,128)S(1)}, u32[]{:S(2)}, u32[]{:S(2)}) collective-permute-start(f32[2,80,128]{2,1,0:T(8,128)S(1)} %add.245), channel_id=1, source_target_pairs={{0,8},{4,12},{8,16},{12,20},{16,24},{20,28},{1,9},{5,13},{9,17},{1... | collective-permute-start | bytes 245768 | tf_op jit(solution)/shard_map/ppermute | solution.py:133
  70.9 7.3 %collective-permute-start.3 = (f32[2,80,128]{2,1,0:T(8,128)S(1)}, f32[2,80,128]{2,1,0:T(8,128)S(1)}, u32[]{:S(2)}, u32[]{:S(2)}) collective-permute-start(f32[2,80,128]{2,1,0:T(8,128)S(1)} %add.246), channel_id=1, source_target_pairs={{0,16},{4,20},{8,24},{12,28},{1,17},{5,21},{9,25},{13,29},{2,18},{... | collective-permute-start | bytes 245768 | tf_op jit(solution)/shard_map/ppermute | solution.py:133
  96.3 25.3 %collective-permute-start.12 = (bf16[256,2048]{1,0:T(8,128)(2,1)S(1)}, bf16[256,2048]{1,0:T(8,128)(2,1)S(1)}, u32[]{:S(2)}, u32[]{:S(2)}) collective-permute-start(bf16[256,2048]{1,0:T(8,128)(2,1)S(1)} %shard_map.379), channel_id=1, source_target_pairs={{0,2},{1,3},{2,0},{3,1},{4,6},{5,7},{6,4},{7,5},{8,10},{9,11},{10,... | collective-permute-start | bytes 3145736 | tf_op jit(solution)/shard_map/ppermute | solution.py:93
  101.1 47.7 %collective-permute-start.16 = (bf16[512,2048]{1,0:T(8,128)(2,1)S(1)}, bf16[512,2048]{1,0:T(8,128)(2,1)S(1)}, u32[]{:S(2)}, u32[]{:S(2)}) collective-permute-start(bf16[512,2048]{1,0:T(8,128)(2,1)S(1)} %bitcast.145), channel_id=1, source_target_pairs={{0,4},{4,0},{8,12},{12,8},{16,20},{20,16},{24,28},{28,24},{1,5},{5... | collective-permute-start | bytes 6291464 | tf_op jit(solution)/shard_map/ppermute | solution.py:87
  122.6 25.6 %collective-permute-start.13 = (bf16[256,2048]{1,0:T(8,128)(2,1)S(1)}, bf16[256,2048]{1,0:T(8,128)(2,1)S(1)}, u32[]{:S(2)}, u32[]{:S(2)}) collective-permute-start(bf16[256,2048]{1,0:T(8,128)(2,1)S(1)} %shard_map.378), channel_id=1, source_target_pairs={{0,2},{1,3},{2,0},{3,1},{4,6},{5,7},{6,4},{7,5},{8,10},{9,11},{10,... | collective-permute-start | bytes 3145736 | tf_op jit(solution)/shard_map/ppermute | solution.py:93
  150.1 17.2 %collective-permute-start.15 = (bf16[256,2048]{1,0:T(8,128)(2,1)S(1)}, bf16[256,2048]{1,0:T(8,128)(2,1)S(1)}, u32[]{:S(2)}, u32[]{:S(2)}) collective-permute-start(bf16[256,2048]{1,0:T(8,128)(2,1)S(1)} %multiply_convert_fusion.refs_2_.own_ref), channel_id=1, source_target_pairs={{0,1},{1,0},{2,3},{3,2},{4,5},{5,4},{6,7},{7,6},{8,9},{9,8},{10,11... | collective-permute-start | bytes 3145736 | tf_op jit(solution)/shard_map/ppermute | solution.py:77
  152.1 25.3 %collective-permute-start.22 = (bf16[256,2048]{1,0:T(8,128)(2,1)S(1)}, bf16[256,2048]{1,0:T(8,128)(2,1)S(1)}, u32[]{:S(2)}, u32[]{:S(2)}) collective-permute-start(bf16[256,2048]{1,0:T(8,128)(2,1)S(1)} %multiply_convert_fusion.1.own_ref), channel_id=1, source_target_pairs={{0,4},{4,0},{8,12},{12,8},{16,20},{20,16},{24,28},{28,24},{1,5},{5... | collective-permute-start | bytes 3145736 | tf_op jit(solution)/shard_map/ppermute | solution.py:87
  177.5 25.4 %collective-permute-start.21 = (bf16[256,2048]{1,0:T(8,128)(2,1)S(1)}, bf16[256,2048]{1,0:T(8,128)(2,1)S(1)}, u32[]{:S(2)}, u32[]{:S(2)}) collective-permute-start(bf16[256,2048]{1,0:T(8,128)(2,1)S(1)} %multiply_convert_fusion.refs_2_.own_ref), channel_id=1, source_target_pairs={{0,4},{4,0},{8,12},{12,8},{16,20},{20,16},{24,28},{28,24},{1,5},{5... | collective-permute-start | bytes 3145736 | tf_op jit(solution)/shard_map/ppermute | solution.py:87
  234.4 301.6 %reduce-scatter.7.cloned.1.call-start = ((), (), s32[]{:S(2)}) async-start(), calls=%async_computation.5 | async-start | bytes 5242880 | tf_op jit(solution)/shard_map/reduce_scatter | solution.py:110
  258.3 48.0 %collective-permute-start.33 = (bf16[512,2048]{1,0:T(8,128)(2,1)}, bf16[512,2048]{1,0:T(8,128)(2,1)}, u32[]{:S(2)}, u32[]{:S(2)}) collective-permute-start(bf16[512,2048]{1,0:T(8,128)(2,1)} %shard_map.390), channel_id=1, source_target_pairs={{0,4},{4,0},{8,12},{12,8},{16,20},{20,16},{24,28},{28,24},{1,5},{5... | collective-permute-start | bytes 6291464 | tf_op jit(solution)/shard_map/ppermute | solution.py:87
  306.3 265.9 %reduce-scatter.9.cloned.1.call-start = ((), (), s32[]{:S(2)}) async-start(), calls=%async_computation.6 | async-start | bytes 5242880 | tf_op jit(solution)/shard_map/reduce_scatter | solution.py:110
  314.5 47.9 %collective-permute-start.34 = (bf16[512,2048]{1,0:T(8,128)(2,1)S(1)}, bf16[512,2048]{1,0:T(8,128)(2,1)}, u32[]{:S(2)}, u32[]{:S(2)}) collective-permute-start(bf16[512,2048]{1,0:T(8,128)(2,1)S(1)} %shard_map.392.refs_2_), channel_id=1, source_target_pairs={{0,2},{1,3},{2,0},{3,1},{4,6},{5,7},{6,4},{7,5},{8,10},{9,11},{10,... | collective-permute-start | bytes 6291464 | tf_op jit(solution)/shard_map/ppermute | solution.py:93
  324.6 43.8 %collective-permute-start.40 = (bf16[128,2048]{1,0:T(8,128)(2,1)}, bf16[128,2048]{1,0:T(8,128)(2,1)}, u32[]{:S(2)}, u32[]{:S(2)}) collective-permute-start(bf16[128,2048]{1,0:T(8,128)(2,1)} %get-tuple-element.347), channel_id=1, source_target_pairs={{0,1},{1,0},{2,3},{3,2},{4,5},{5,4},{6,7},{7,6},{8,9},{9,8},{10,11... | collective-permute-start | bytes 1572872 | tf_op jit(solution)/shard_map/ppermute | solution.py:77
  324.6 44.3 %collective-permute-start.41 = (bf16[128,2048]{1,0:T(8,128)(2,1)}, bf16[128,2048]{1,0:T(8,128)(2,1)}, u32[]{:S(2)}, u32[]{:S(2)}) collective-permute-start(bf16[128,2048]{1,0:T(8,128)(2,1)} %get-tuple-element.346), channel_id=1, source_target_pairs={{0,1},{1,0},{2,3},{3,2},{4,5},{5,4},{6,7},{7,6},{8,9},{9,8},{10,11... | collective-permute-start | bytes 1572872 | tf_op jit(solution)/shard_map/ppermute | solution.py:77
  325.1 48.7 %collective-permute-start.42 = (bf16[128,2048]{1,0:T(8,128)(2,1)}, bf16[128,2048]{1,0:T(8,128)(2,1)}, u32[]{:S(2)}, u32[]{:S(2)}) collective-permute-start(bf16[128,2048]{1,0:T(8,128)(2,1)} %get-tuple-element.345), channel_id=1, source_target_pairs={{0,1},{1,0},{2,3},{3,2},{4,5},{5,4},{6,7},{7,6},{8,9},{9,8},{10,11... | collective-permute-start | bytes 1572872 | tf_op jit(solution)/shard_map/ppermute | solution.py:77
  325.1 49.1 %collective-permute-start.43 = (bf16[128,2048]{1,0:T(8,128)(2,1)}, bf16[128,2048]{1,0:T(8,128)(2,1)}, u32[]{:S(2)}, u32[]{:S(2)}) collective-permute-start(bf16[128,2048]{1,0:T(8,128)(2,1)} %get-tuple-element.344), channel_id=1, source_target_pairs={{0,1},{1,0},{2,3},{3,2},{4,5},{5,4},{6,7},{7,6},{8,9},{9,8},{10,11... | collective-permute-start | bytes 1572872 | tf_op jit(solution)/shard_map/ppermute | solution.py:77
  365.1 11.2 %collective-permute-start.45 = (bf16[128,2048]{1,0:T(8,128)(2,1)S(1)}, bf16[128,2048]{1,0:T(8,128)(2,1)S(1)}, u32[]{:S(2)}, u32[]{:S(2)}) collective-permute-start(bf16[128,2048]{1,0:T(8,128)(2,1)S(1)} %get-tuple-element.343), channel_id=1, source_target_pairs={{0,1},{1,0},{2,3},{3,2},{4,5},{5,4},{6,7},{7,6},{8,9},{9,8},{10,11... | collective-permute-start | bytes 1572872 | tf_op jit(solution)/shard_map/ppermute | solution.py:77
  368.5 8.8 %collective-permute-start.46 = (bf16[128,2048]{1,0:T(8,128)(2,1)S(1)}, bf16[128,2048]{1,0:T(8,128)(2,1)S(1)}, u32[]{:S(2)}, u32[]{:S(2)}) collective-permute-start(bf16[128,2048]{1,0:T(8,128)(2,1)S(1)} %get-tuple-element.342), channel_id=1, source_target_pairs={{0,1},{1,0},{2,3},{3,2},{4,5},{5,4},{6,7},{7,6},{8,9},{9,8},{10,11... | collective-permute-start | bytes 1572872 | tf_op jit(solution)/shard_map/ppermute | solution.py:77
  368.9 9.5 %collective-permute-start.47 = (bf16[128,2048]{1,0:T(8,128)(2,1)S(1)}, bf16[128,2048]{1,0:T(8,128)(2,1)S(1)}, u32[]{:S(2)}, u32[]{:S(2)}) collective-permute-start(bf16[128,2048]{1,0:T(8,128)(2,1)S(1)} %get-tuple-element.341), channel_id=1, source_target_pairs={{0,1},{1,0},{2,3},{3,2},{4,5},{5,4},{6,7},{7,6},{8,9},{9,8},{10,11... | collective-permute-start | bytes 1572872 | tf_op jit(solution)/shard_map/ppermute | solution.py:77
  373.8 12.4 %collective-permute-start.48 = (bf16[128,2048]{1,0:T(8,128)(2,1)}, bf16[128,2048]{1,0:T(8,128)(2,1)}, u32[]{:S(2)}, u32[]{:S(2)}) collective-permute-start(bf16[128,2048]{1,0:T(8,128)(2,1)} %get-tuple-element.340), channel_id=1, source_target_pairs={{0,1},{1,0},{2,3},{3,2},{4,5},{5,4},{6,7},{7,6},{8,9},{9,8},{10,11... | collective-permute-start | bytes 1572872 | tf_op jit(solution)/shard_map/ppermute | solution.py:77
  375.8 17.6 %collective-permute-start.35 = (bf16[128,2048]{1,0:T(8,128)(2,1)}, bf16[128,2048]{1,0:T(8,128)(2,1)}, u32[]{:S(2)}, u32[]{:S(2)}) collective-permute-start(bf16[128,2048]{1,0:T(8,128)(2,1)} %get-tuple-element.351), channel_id=1, source_target_pairs={{0,1},{1,0},{2,3},{3,2},{4,5},{5,4},{6,7},{7,6},{8,9},{9,8},{10,11... | collective-permute-start | bytes 1572872 | tf_op jit(solution)/shard_map/ppermute | solution.py:77
  377.1 16.4 %collective-permute-start.36 = (bf16[128,2048]{1,0:T(8,128)(2,1)}, bf16[128,2048]{1,0:T(8,128)(2,1)}, u32[]{:S(2)}, u32[]{:S(2)}) collective-permute-start(bf16[128,2048]{1,0:T(8,128)(2,1)} %get-tuple-element.350), channel_id=1, source_target_pairs={{0,1},{1,0},{2,3},{3,2},{4,5},{5,4},{6,7},{7,6},{8,9},{9,8},{10,11... | collective-permute-start | bytes 1572872 | tf_op jit(solution)/shard_map/ppermute | solution.py:77
  378.0 15.4 %collective-permute-start.37 = (bf16[128,2048]{1,0:T(8,128)(2,1)}, bf16[128,2048]{1,0:T(8,128)(2,1)}, u32[]{:S(2)}, u32[]{:S(2)}) collective-permute-start(bf16[128,2048]{1,0:T(8,128)(2,1)} %get-tuple-element.349), channel_id=1, source_target_pairs={{0,1},{1,0},{2,3},{3,2},{4,5},{5,4},{6,7},{7,6},{8,9},{9,8},{10,11... | collective-permute-start | bytes 1572872 | tf_op jit(solution)/shard_map/ppermute | solution.py:77
  379.2 14.2 %collective-permute-start.38 = (bf16[128,2048]{1,0:T(8,128)(2,1)}, bf16[128,2048]{1,0:T(8,128)(2,1)}, u32[]{:S(2)}, u32[]{:S(2)}) collective-permute-start(bf16[128,2048]{1,0:T(8,128)(2,1)} %get-tuple-element.348), channel_id=1, source_target_pairs={{0,1},{1,0},{2,3},{3,2},{4,5},{5,4},{6,7},{7,6},{8,9},{9,8},{10,11... | collective-permute-start | bytes 1572872 | tf_op jit(solution)/shard_map/ppermute | solution.py:77
  385.6 255.1 %reduce-scatter.11.cloned.1.call-start = ((), (), s32[]{:S(2)}) async-start(), calls=%async_computation.7 | async-start | bytes 3276800 | tf_op jit(solution)/shard_map/reduce_scatter | solution.py:110
  386.3 48.3 %collective-permute-start.44 = (bf16[512,2048]{1,0:T(8,128)(2,1)}, bf16[512,2048]{1,0:T(8,128)(2,1)}, u32[]{:S(2)}, u32[]{:S(2)}) collective-permute-start(bf16[512,2048]{1,0:T(8,128)(2,1)} %copy-done.55), channel_id=1, source_target_pairs={{0,4},{4,0},{8,12},{12,8},{16,20},{20,16},{24,28},{28,24},{1,5},{5... | collective-permute-start | bytes 6291464 | tf_op jit(solution)/shard_map/ppermute | solution.py:87
  431.2 35.7 %collective-permute-start.39 = (bf16[512,128]{1,0:T(8,128)(2,1)}, bf16[512,128]{1,0:T(8,128)(2,1)S(1)}, u32[]{:S(2)}, u32[]{:S(2)}) collective-permute-start(bf16[512,128]{1,0:T(8,128)(2,1)} %pad_maximum_fusion.3), channel_id=1, source_target_pairs={{4,0},{8,4},{12,8},{16,12},{20,16},{24,20},{28,24},{5,1},{9,5},{13... | collective-permute-start | bytes 393224 | tf_op jit(solution)/shard_map/ppermute | solution.py:133
  434.6 7.8 %collective-permute-start.49 = (bf16[2,80,128]{2,1,0:T(8,128)(2,1)S(1)}, bf16[2,80,128]{2,1,0:T(8,128)(2,1)S(1)}, u32[]{:S(2)}, u32[]{:S(2)}) collective-permute-start(bf16[2,80,128]{2,1,0:T(8,128)(2,1)S(1)} %convert_element_type.238), channel_id=1, source_target_pairs={{4,0},{8,4},{12,8},{16,12},{20,16},{24,20},{28,24},{5,1},{9,5},{13... | collective-permute-start | bytes 122888 | tf_op jit(solution)/shard_map/ppermute | solution.py:133
  439.7 74.5 %collective-permute-start.60 = (bf16[1024,512]{1,0:T(8,128)(2,1)}, bf16[1024,512]{1,0:T(8,128)(2,1)}, u32[]{:S(2)}, u32[]{:S(2)}) collective-permute-start(bf16[1024,512]{1,0:T(8,128)(2,1)} %shard_map.400.refs_11_), channel_id=1, source_target_pairs={{0,4},{4,0},{8,12},{12,8},{16,20},{20,16},{24,28},{28,24},{1,5},{5... | collective-permute-start | bytes 3145736 | tf_op jit(solution)/shard_map/ppermute | solution.py:87
  442.4 11.2 %collective-permute-start.50 = (bf16[2,80,128]{2,1,0:T(8,128)(2,1)S(1)}, bf16[2,80,128]{2,1,0:T(8,128)(2,1)S(1)}, u32[]{:S(2)}, u32[]{:S(2)}) collective-permute-start(bf16[2,80,128]{2,1,0:T(8,128)(2,1)S(1)} %fusion.19), channel_id=1, source_target_pairs={{8,0},{12,4},{16,8},{20,12},{24,16},{28,20},{9,1},{13,5},{17,9},{2... | collective-permute-start | bytes 122888 | tf_op jit(solution)/shard_map/ppermute | solution.py:133
  454.3 11.8 %collective-permute-start.51 = (bf16[2,80,128]{2,1,0:T(8,128)(2,1)}, bf16[2,80,128]{2,1,0:T(8,128)(2,1)}, u32[]{:S(2)}, u32[]{:S(2)}) collective-permute-start(bf16[2,80,128]{2,1,0:T(8,128)(2,1)} %fusion.18), channel_id=1, source_target_pairs={{16,0},{20,4},{24,8},{28,12},{17,1},{21,5},{25,9},{29,13},{18,2},{... | collective-permute-start | bytes 122888 | tf_op jit(solution)/shard_map/ppermute | solution.py:133
  492.0 48.8 %collective-permute-start.57 = (bf16[512,2048]{1,0:T(8,128)(2,1)}, bf16[512,2048]{1,0:T(8,128)(2,1)}, u32[]{:S(2)}, u32[]{:S(2)}) collective-permute-start(bf16[512,2048]{1,0:T(8,128)(2,1)} %shard_map.403.rest_0_), channel_id=1, source_target_pairs={{0,2},{1,3},{2,0},{3,1},{4,6},{5,7},{6,4},{7,5},{8,10},{9,11},{10,... | collective-permute-start | bytes 6291464 | tf_op jit(solution)/shard_map/ppermute | solution.py:93
  497.1 38.9 %collective-permute-start.59 = (bf16[1024,768]{1,0:T(8,128)(2,1)}, bf16[1024,768]{1,0:T(8,128)(2,1)}, u32[]{:S(2)}, u32[]{:S(2)}) collective-permute-start(bf16[1024,768]{1,0:T(8,128)(2,1)} %shard_map.405.rest_1_), channel_id=1, source_target_pairs={{0,4},{4,0},{8,12},{12,8},{16,20},{20,16},{24,28},{28,24},{1,5},{5... | collective-permute-start | bytes 4718600 | tf_op jit(solution)/shard_map/ppermute | solution.py:87
  502.0 119.1 %collective-permute-start.56 = (bf16[512,2048]{1,0:T(8,128)(2,1)}, bf16[512,2048]{1,0:T(8,128)(2,1)}, u32[]{:S(2)}, u32[]{:S(2)}) collective-permute-start(bf16[512,2048]{1,0:T(8,128)(2,1)} %shard_map.404), channel_id=1, source_target_pairs={{0,2},{1,3},{2,0},{3,1},{4,6},{5,7},{6,4},{7,5},{8,10},{9,11},{10,... | collective-permute-start | bytes 6291464 | tf_op jit(solution)/shard_map/ppermute | solution.py:93
  553.3 18.1 %collective-permute-start.70 = (f32[2048]{0:T(1024)S(1)}, f32[2048]{0:T(1024)}, u32[]{:S(2)}, u32[]{:S(2)}) collective-permute-start(f32[2048]{0:T(1024)S(1)} %get-tuple-element.308), channel_id=1, source_target_pairs={{0,1},{1,0},{2,3},{3,2},{4,5},{5,4},{6,7},{7,6},{8,9},{9,8},{10,11... | collective-permute-start | bytes 24584 | tf_op jit(solution)/shard_map/ppermute | solution.py:986
  567.0 8.5 %collective-permute-start.75 = (bf16[4,14848]{1,0:T(4,128)(2,1)}, bf16[4,14848]{1,0:T(4,128)(2,1)S(1)}, u32[]{:S(2)}, u32[]{:S(2)}) collective-permute-start(bf16[4,14848]{1,0:T(4,128)(2,1)} %bitcast.128), channel_id=1, source_target_pairs={{0,4},{4,0},{8,12},{12,8},{16,20},{20,16},{24,28},{28,24},{1,5},{5... | collective-permute-start | bytes 356360 | tf_op jit(solution)/shard_map/ppermute | solution.py:121
  572.2 8.6 %collective-permute-start.71 = (bf16[4,256]{1,0:T(4,128)(2,1)S(1)}, bf16[4,256]{1,0:T(4,128)(2,1)S(1)}, u32[]{:S(2)}, u32[]{:S(2)}) collective-permute-start(bf16[4,256]{1,0:T(4,128)(2,1)S(1)} %bitcast.169), channel_id=1, source_target_pairs={{0,4},{4,0},{8,12},{12,8},{16,20},{20,16},{24,28},{28,24},{1,5},{5... | collective-permute-start | bytes 6152 | tf_op jit(solution)/shard_map/ppermute | solution.py:121
  573.5 36.7 %collective-permute-start.61 = (bf16[768,1024]{1,0:T(8,128)(2,1)S(1)}, bf16[768,1024]{1,0:T(8,128)(2,1)}, u32[]{:S(2)}, u32[]{:S(2)}) collective-permute-start(bf16[768,1024]{1,0:T(8,128)(2,1)S(1)} %pad_maximum_fusion.2), channel_id=1, source_target_pairs={{0,4},{4,0},{8,12},{12,8},{16,20},{20,16},{24,28},{28,24},{1,5},{5... | collective-permute-start | bytes 4718600 | tf_op jit(solution)/shard_map/ppermute | solution.py:87
  576.2 7.0 %collective-permute-start.78 = (bf16[14848]{0:T(1024)(128)(2,1)S(1)}, bf16[14848]{0:T(1024)(128)(2,1)S(1)}, u32[]{:S(2)}, u32[]{:S(2)}) collective-permute-start(bf16[14848]{0:T(1024)(128)(2,1)S(1)} %get-tuple-element.313), channel_id=1, source_target_pairs={{0,24},{4,28},{8,0},{12,4},{16,8},{20,12},{24,16},{28,20},{1,25},{... | collective-permute-start | bytes 89096 | tf_op jit(solution)/shard_map/ppermute | solution.py:127
  591.6 23.4 %collective-permute-start.62 = (bf16[128,2048]{1,0:T(8,128)(2,1)}, bf16[128,2048]{1,0:T(8,128)(2,1)S(1)}, u32[]{:S(2)}, u32[]{:S(2)}) collective-permute-start(bf16[128,2048]{1,0:T(8,128)(2,1)} %get-tuple-element.335), channel_id=1, source_target_pairs={{0,1},{1,0},{2,3},{3,2},{4,5},{5,4},{6,7},{7,6},{8,9},{9,8},{10,11... | collective-permute-start | bytes 1572872 | tf_op jit(solution)/shard_map/ppermute | solution.py:77
  593.8 21.2 %collective-permute-start.63 = (bf16[128,2048]{1,0:T(8,128)(2,1)}, bf16[128,2048]{1,0:T(8,128)(2,1)S(1)}, u32[]{:S(2)}, u32[]{:S(2)}) collective-permute-start(bf16[128,2048]{1,0:T(8,128)(2,1)} %get-tuple-element.334), channel_id=1, source_target_pairs={{0,1},{1,0},{2,3},{3,2},{4,5},{5,4},{6,7},{7,6},{8,9},{9,8},{10,11... | collective-permute-start | bytes 1572872 | tf_op jit(solution)/shard_map/ppermute | solution.py:77
  599.0 16.0 %collective-permute-start.64 = (bf16[128,2048]{1,0:T(8,128)(2,1)}, bf16[128,2048]{1,0:T(8,128)(2,1)}, u32[]{:S(2)}, u32[]{:S(2)}) collective-permute-start(bf16[128,2048]{1,0:T(8,128)(2,1)} %get-tuple-element.333), channel_id=1, source_target_pairs={{0,1},{1,0},{2,3},{3,2},{4,5},{5,4},{6,7},{7,6},{8,9},{9,8},{10,11... | collective-permute-start | bytes 1572872 | tf_op jit(solution)/shard_map/ppermute | solution.py:77
  625.8 9.5 %collective-permute-start.66 = (bf16[128,2048]{1,0:T(8,128)(2,1)}, bf16[128,2048]{1,0:T(8,128)(2,1)}, u32[]{:S(2)}, u32[]{:S(2)}) collective-permute-start(bf16[128,2048]{1,0:T(8,128)(2,1)} %get-tuple-element.331), channel_id=1, source_target_pairs={{0,1},{1,0},{2,3},{3,2},{4,5},{5,4},{6,7},{7,6},{8,9},{9,8},{10,11... | collective-permute-start | bytes 1572872 | tf_op jit(solution)/shard_map/ppermute | solution.py:77
  626.3 9.0 %collective-permute-start.67 = (bf16[128,2048]{1,0:T(8,128)(2,1)}, bf16[128,2048]{1,0:T(8,128)(2,1)}, u32[]{:S(2)}, u32[]{:S(2)}) collective-permute-start(bf16[128,2048]{1,0:T(8,128)(2,1)} %get-tuple-element.330), channel_id=1, source_target_pairs={{0,1},{1,0},{2,3},{3,2},{4,5},{5,4},{6,7},{7,6},{8,9},{9,8},{10,11... | collective-permute-start | bytes 1572872 | tf_op jit(solution)/shard_map/ppermute | solution.py:77
  626.3 9.0 %collective-permute-start.68 = (bf16[128,2048]{1,0:T(8,128)(2,1)}, bf16[128,2048]{1,0:T(8,128)(2,1)}, u32[]{:S(2)}, u32[]{:S(2)}) collective-permute-start(bf16[128,2048]{1,0:T(8,128)(2,1)} %get-tuple-element.329), channel_id=1, source_target_pairs={{0,1},{1,0},{2,3},{3,2},{4,5},{5,4},{6,7},{7,6},{8,9},{9,8},{10,11... | collective-permute-start | bytes 1572872 | tf_op jit(solution)/shard_map/ppermute | solution.py:77
  626.8 8.5 %collective-permute-start.69 = (bf16[128,2048]{1,0:T(8,128)(2,1)}, bf16[128,2048]{1,0:T(8,128)(2,1)}, u32[]{:S(2)}, u32[]{:S(2)}) collective-permute-start(bf16[128,2048]{1,0:T(8,128)(2,1)} %get-tuple-element.328), channel_id=1, source_target_pairs={{0,1},{1,0},{2,3},{3,2},{4,5},{5,4},{6,7},{7,6},{8,9},{9,8},{10,11... | collective-permute-start | bytes 1572872 | tf_op jit(solution)/shard_map/ppermute | solution.py:77
  (173 other events, 981.1 us)
Sparse Core Ops, SparseCore 0:
  234.6 78.5 reduce-scatter.4
  315.5 77.3 reduce-scatter.6
  395.2 82.6 reduce-scatter.8
  571.5 54.1 reduce-scatter.10

commit v6 on v5

--- a/solution.py
+++ b/solution.py
@@ -15,7 +15,7 @@
 
 
 def cost(us):
-    return pl.CostEstimate(flops=int(us * 0.45e9), bytes_accessed=1, transcendentals=0)
+    return pl.CostEstimate(flops=int(us * 0.3e9), bytes_accessed=1, transcendentals=0)
 
 
 def dot(a, b, out=F32):

time: 662 us -> 654 us (0.988)
  waiting for transfers between devices: 159 us -> 147 us
  local copies, waits for them, and re-layouts: 126 us -> 136 us
  starting transfers between devices: 70.2 us -> 61.5 us
    unnamed x291 -> x297, local copies, waits for them, and re-layouts: 82.7 us -> 96.1 us
  transfers between devices with their start and end apart: 85 -> 85, of which waited for: 39 -> 38; matrix products, arithmetic and copies ran while one was open for 14% -> 14% of each run, Pallas kernels for 28% -> 29%
where the time goes in v6:
time: 654 us; the launch traced here: 645 us
  Pallas kernels  232 us (35%)
  waiting for transfers between devices  147 us (22%)
  local copies, waits for them, and re-layouts  136 us (21%)
  starting transfers between devices  61.5 us (9%)
  other arithmetic  36.4 us (6%)
  matrix products  16.5 us (3%)
  between operations  16.3 us (2%)
    unnamed x297, local copies, waits for them, and re-layouts  96.1 us
    pallas_call x8, Pallas kernels, matmul(): pl.pallas_call(kernel, grid_spec=pltpu.PrefetchScalarGridSpec(num_scalar_...  63.4 us
    ppermute x8, waiting for transfers between devices, swap(): return lax.ppermute(x, 'seq', self.x_swap)  56 us
    ppermute x5, waiting for transfers between devices, outer_terms(): lax.ppermute(half, 'kv', self.y_shift(j))  48.9 us
    pallas_call x4, Pallas kernels, gated(): pl.pallas_call(gated_kernel, grid_spec=pltpu.PrefetchScalarGridSpec(num_s...  37.4 us
    pallas_call x3, Pallas kernels, grad_pair(): pl.pallas_call(kernel, grid=(count,), in_specs=specs * len(pairs) + [ANY]...  35.6 us
    pallas_call x4, Pallas kernels, call(): pl.pallas_call(lambda *refs: kernel(*refs[:count], *refs[count + len(afte...  32.9 us
    ppermute x8, starting transfers between devices, shift_seq(): return lax.ppermute(x, 'seq', pairs)  22.9 us
  transfers between devices with their start and end apart: 85, of which 38 were waited for; matrix products, arithmetic and copies ran while one was open for 14% of the time, Pallas kernels for 29%

profile of v6, /device:TPU:0, one launch (start us, length us, event | category | flops | bytes accessed | tf_op | source)
XLA Modules:
  0.0 645.0 jit_solution(14851636093239274291)
XLA Ops:
  16.0 8.7 %shard_map.373 = (bf16[1024,2048]{1,0:T(8,128)(2,1)S(1)}, bf16[512,1024]{1,0:T(8,128)(2,1)S(1)}, bf16[256,1024]{1,0:T(8,128)(2,1)S(1)}, bf16[1024,128]{1,0:T(8,128)(2,1)S(1)}) custom-call(bf16[1024,2048]{1,0:T(8,128)(2,1)S(1)} %copy-done.20, bf16[1,2048]{1,0:T(2,128)(2,1)S(1)} %broadcast_in_dim.31.gain_ref, bf16[2048,512]{1,0:T(8,128)(2,1)S(1)} %copy-done.100, ...), custom_call_target="tpu_custom_call" | custom-call | flops 3000000000 | bytes 1 | tf_op jit(solution)/shard_map/pallas_call | solution.py:509
  27.7 4.8 collective-permute-start
  32.6 4.0 add_convert_fusion.refs_1_
  38.8 3.3 constant_dynamic-slice_fusion.7
  44.3 3.7 collective-permute-start.1
  48.0 7.1 %shard_map.375.gh_ref = f32[1024,1024]{1,0:T(8,128)S(1)} custom-call(s32[2]{0:T(128)S(1)} %pad_add_fusion.1.sel, bf16[1024,2048]{1,0:T(8,128)(2,1)S(1)} %copy-done.19, bf16[2048,2048]{1,0:T(8,128)(2,1)} %refs_1_.11), custom_call_target="tpu_custom_call" | custom-call | flops 1266367616 | bytes 1 | tf_op jit(solution)/shard_map/pallas_call | solution.py:571
  57.2 3.5 collective-permute-start.2
  62.8 5.5 collective-permute-start.3
  70.2 9.1 %shard_map.376 = (bf16[512,1024]{1,0:T(8,128)(2,1)S(1)}, f32[8,1024]{1,0:T(8,128)S(1)}, f32[8,2,80,128]{3,2,1,0:T(8,128)S(1)}) custom-call(bf16[512,1024]{1,0:T(8,128)(2,1)S(1)} %copy-done.110, bf16[256,1152]{1,0:T(8,128)(2,1)S(1)} %constant_dynamic-update-slice_fusion.refs_0_.refs_1_, bf16[2,128,1152]{2,1,0:T(8,128)(2,1)S(1)} %get-tuple-element.114.refs_2_.refs_1_, ...), custom_call_target="tpu_custom_call" | custom-call | flops 2700000000 | bytes 1 | tf_op jit(solution)/shard_map/pallas_call | solution.py:373
  79.3 4.1 shard_map.377
  91.8 20.2 %collective-permute-done.12 = bf16[256,2048]{1,0:T(8,128)(2,1)S(1)} collective-permute-done((bf16[256,2048]{1,0:T(8,128)(2,1)S(1)}, bf16[256,2048]{1,0:T(8,128)(2,1)S(1)}, u32[]{:S(2)}, u32[]{:S(2)}) %collective-permute-start.12) | collective-permute-done | bytes 1048608 | tf_op jit(solution)/shard_map/ppermute | solution.py:93
  115.6 8.7 %shard_map.380 = (bf16[1024,2048]{1,0:T(8,128)(2,1)S(1)}, bf16[1024,1024]{1,0:T(8,128)(2,1)S(1)}, bf16[1024,1024]{1,0:T(8,128)(2,1)S(1)}, bf16[1024,1024]{1,0:T(8,128)(2,1)S(1)}) custom-call(s32[2]{0:T(128)S(1)} %pad_add_fusion.3.sel_ref, bf16[256,2048]{1,0:T(8,128)(2,1)S(1)} %multiply_convert_fusion.1.own_ref, ...), custom_call_target="tpu_custom_call" | custom-call | flops 3300000000 | bytes 1 | tf_op jit(solution)/shard_map/pallas_call | solution.py:678
  124.3 14.2 %collective-permute-done.13 = bf16[256,2048]{1,0:T(8,128)(2,1)S(1)} collective-permute-done((bf16[256,2048]{1,0:T(8,128)(2,1)S(1)}, bf16[256,2048]{1,0:T(8,128)(2,1)S(1)}, u32[]{:S(2)}, u32[]{:S(2)}) %collective-permute-start.13) | collective-permute-done | bytes 1048608 | tf_op jit(solution)/shard_map/ppermute | solution.py:93
  148.0 8.1 %shard_map.382.refs_4_.gh_ref = f32[1024,1024]{1,0:T(8,128)S(1)} custom-call(s32[2]{0:T(128)S(1)} %pad_add_fusion.1.sel, bf16[1024,2048]{1,0:T(8,128)(2,1)S(1)} %shard_map.381.refs_0_.refs_2_, bf16[2048,2048]{1,0:T(8,128)(2,1)} %refs_1_.11, bf16[256,2048]{1,0:T(8,128)(2,1)} %multiply_convert_fusion.refs_2_.own_ref), custom_call_target="tpu_custom_call" | custom-call | flops 1266367616 | bytes 1 | tf_op jit(solution)/shard_map/pallas_call | solution.py:571
  158.1 9.7 %shard_map.383 = (bf16[1024,2048]{1,0:T(8,128)(2,1)S(1)}, bf16[1024,1024]{1,0:T(8,128)(2,1)S(1)}, bf16[1024,1024]{1,0:T(8,128)(2,1)S(1)}, bf16[1024,1024]{1,0:T(8,128)(2,1)S(1)}) custom-call(s32[2]{0:T(128)S(1)} %pad_add_fusion.3.sel_ref, ...), custom_call_target="tpu_custom_call", output_to_operand_aliasing={{0}: (6, {}), {1}: (7, {}), {2}: (8, {}), {3}: (9, {})} | custom-call | flops 3300000000 | bytes 1 | tf_op jit(solution)/shard_map/pallas_call | solution.py:678
  174.2 9.6 %shard_map.384 = (bf16[1024,2048]{1,0:T(8,128)(2,1)S(1)}, bf16[1024,1024]{1,0:T(8,128)(2,1)S(1)}, bf16[1024,1024]{1,0:T(8,128)(2,1)S(1)}, bf16[1024,1024]{1,0:T(8,128)(2,1)S(1)}) custom-call(s32[2]{0:T(128)S(1)} %pad_add_fusion.3.sel_ref, bf16[256,2048]{1,0:T(8,128)(2,1)} %collective-permute-done.22.own_ref, bf16[256,2048]{1,0:T(8,128)(2,1)S(1)} %copy-done.74, ...), custom_call_target="tpu_custom_call" | custom-call | flops 3300000000 | bytes 1 | tf_op jit(solution)/shard_map/pallas_call | solution.py:678
  187.8 7.2 %collective-permute-done.21.own_ref = bf16[256,2048]{1,0:T(8,128)(2,1)} collective-permute-done((bf16[256,2048]{1,0:T(8,128)(2,1)}, bf16[256,2048]{1,0:T(8,128)(2,1)}, u32[]{:S(2)}, u32[]{:S(2)}) %collective-permute-start.21) | collective-permute-done | bytes 1048608 | tf_op jit(solution)/shard_map/ppermute | solution.py:87
  202.7 9.4 %shard_map.385 = (bf16[1024,2048]{1,0:T(8,128)(2,1)S(1)}, bf16[1024,1024]{1,0:T(8,128)(2,1)S(1)}, bf16[1024,1024]{1,0:T(8,128)(2,1)S(1)}, bf16[1024,1024]{1,0:T(8,128)(2,1)S(1)}) custom-call(s32[2]{0:T(128)S(1)} %pad_add_fusion.3.sel_ref, ...), custom_call_target="tpu_custom_call", output_to_operand_aliasing={{0}: (6, {}), {1}: (7, {}), {2}: (8, {}), {3}: (9, {})} | custom-call | flops 3300000000 | bytes 1 | tf_op jit(solution)/shard_map/pallas_call | solution.py:678
  219.7 11.8 %shard_map.386.refs_4_ = bf16[2048,1024]{1,0:T(8,128)(2,1)S(1)} custom-call(bf16[1024,2048]{1,0:T(8,128)(2,1)S(1)} %copy-done.19, bf16[1024,1024]{1,0:T(8,128)(2,1)S(1)} %get-tuple-element.144.refs_0_.refs_1_, bf16[1024,2048]{1,0:T(8,128)(2,1)} %copy-done.10, bf16[1024,1024]{1,0:T(8,128)(2,1)S(1)} %copy-done.31), custom_call_target="tpu_custom_call" | custom-call | flops 3900000000 | bytes 1 | tf_op jit(solution)/shard_map/pallas_call | solution.py:598
  239.0 12.4 %shard_map.387 = (bf16[512,2048]{1,0:T(8,128)(2,1)S(1)}, bf16[512,2048]{1,0:T(8,128)(2,1)S(1)}) custom-call(s32[2]{0:T(128)S(1)} %pad_add_fusion.sel, bf16[1024,1024]{1,0:T(8,128)(2,1)S(1)} %copy-done.36, bf16[2048,2048]{1,0:T(8,128)(2,1)} %refs_1_.9, bf16[1024,1024]{1,0:T(8,128)(2,1)S(1)} %copy-done.41, bf16[2048,2048]{1,0:T(8,128)(2,1)} %refs_3_.4, ...), custom_call_target="tpu_custom_call" | custom-call | flops 2232735232 | bytes 1 | tf_op jit(solution)/shard_map/pallas_call | solution.py:571
  259.2 12.2 %shard_map.388 = (bf16[512,2048]{1,0:T(8,128)(2,1)S(1)}, bf16[512,2048]{1,0:T(8,128)(2,1)S(1)}) custom-call(s32[2]{0:T(128)S(1)} %pad_add_fusion.sel, bf16[1024,1024]{1,0:T(8,128)(2,1)S(1)} %get-tuple-element.140.refs_0_.refs_1_, bf16[2048,2048]{1,0:T(8,128)(2,1)} %refs_1_.9, bf16[1024,1024]{1,0:T(8,128)(2,1)S(1)} %copy-done.24, bf16[2048,2048]{1,0:T(8,128)(2,1)} %refs_3_.4, ...), custom_call_target="tpu_custom_call" | custom-call | flops 2232735232 | bytes 1 | tf_op jit(solution)/shard_map/pallas_call | solution.py:571
  272.7 11.9 %shard_map.391 = bf16[2048,1024]{1,0:T(8,128)(2,1)S(1)} custom-call(bf16[1024,2048]{1,0:T(8,128)(2,1)S(1)} %copy-done.12, bf16[1024,1024]{1,0:T(8,128)(2,1)S(1)} %get-tuple-element.140.refs_0_.refs_1_, bf16[1024,2048]{1,0:T(8,128)(2,1)} %copy-done.14, bf16[1024,1024]{1,0:T(8,128)(2,1)S(1)} %copy-done.37, ...), custom_call_target="tpu_custom_call" | custom-call | flops 3900000000 | bytes 1 | tf_op jit(solution)/shard_map/pallas_call | solution.py:598
  288.0 17.9 %collective-permute-done.33.refs_0_ = bf16[512,2048]{1,0:T(8,128)(2,1)} collective-permute-done((bf16[512,2048]{1,0:T(8,128)(2,1)}, bf16[512,2048]{1,0:T(8,128)(2,1)}, u32[]{:S(2)}, u32[]{:S(2)}) %collective-permute-start.33) | collective-permute-done | bytes 2097184 | tf_op jit(solution)/shard_map/ppermute | solution.py:87
  316.1 7.2 %shard_map.393 = (bf16[512,2048]{1,0:T(8,128)(2,1)S(1)}, bf16[512,2048]{1,0:T(8,128)(2,1)S(1)}) custom-call(s32[2]{0:T(128)S(1)} %pad_add_fusion.sel, bf16[1024,1024]{1,0:T(8,128)(2,1)S(1)} %copy-done.32, bf16[2048,2048]{1,0:T(8,128)(2,1)} %refs_1_.11, bf16[512,2048]{1,0:T(8,128)(2,1)S(1)} %shard_map.392.refs_2_), custom_call_target="tpu_custom_call" | custom-call | flops 1266367616 | bytes 1 | tf_op jit(solution)/shard_map/pallas_call | solution.py:571
  326.4 7.4 %shard_map.394 = (bf16[512,2048]{1,0:T(8,128)(2,1)S(1)}, bf16[512,2048]{1,0:T(8,128)(2,1)S(1)}) custom-call(s32[2]{0:T(128)S(1)} %pad_add_fusion.sel, bf16[1024,1024]{1,0:T(8,128)(2,1)S(1)} %copy-done.18, bf16[2048,2048]{1,0:T(8,128)(2,1)} %refs_1_.11, bf16[512,2048]{1,0:T(8,128)(2,1)S(1)} %get-tuple-element.161.refs_2_.keep_ref), custom_call_target="tpu_custom_call" | custom-call | flops 1266367616 | bytes 1 | tf_op jit(solution)/shard_map/pallas_call | solution.py:571
  335.1 11.8 %shard_map.395 = bf16[2048,1024]{1,0:T(8,128)(2,1)S(1)} custom-call(bf16[1024,2048]{1,0:T(8,128)(2,1)S(1)} %copy-done.13, bf16[1024,1024]{1,0:T(8,128)(2,1)S(1)} %copy-done.25, bf16[1024,2048]{1,0:T(8,128)(2,1)} %copy-done.14, bf16[1024,1024]{1,0:T(8,128)(2,1)S(1)} %copy-done.42, bf16[512,2048]{1,0:T(8,128)(2,1)S(1)} %get-tuple-element.171.refs_4_.keep_ref), custom_call_target="tpu_custom_call" | custom-call | flops 3900000000 | bytes 1 | tf_op jit(solution)/shard_map/pallas_call | solution.py:598
  351.9 3.7 shard_map.398
  355.6 6.5 %collective-permute-done.34 = bf16[512,2048]{1,0:T(8,128)(2,1)} collective-permute-done((bf16[512,2048]{1,0:T(8,128)(2,1)S(1)}, bf16[512,2048]{1,0:T(8,128)(2,1)}, u32[]{:S(2)}, u32[]{:S(2)}) %collective-permute-start.34) | collective-permute-done | bytes 2097184 | tf_op jit(solution)/shard_map/ppermute | solution.py:93
  367.4 5.1 fusion.35
  392.6 3.3 convolution_convert_fusion.refs_11_
  407.2 21.2 %shard_map.397 = (bf16[512,1024]{1,0:T(8,128)(2,1)S(1)}, f32[8,64,64]{2,1,0:T(8,128)S(1)}, f32[128,1152]{1,0:T(8,128)S(1)}, f32[128,1152]{1,0:T(8,128)S(1)}, f32...) custom-call(bf16[512,1024]{1,0:T(8,128)(2,1)S(1)} %copy-done.111, bf16[256,1152]{1,0:T(8,128)(2,1)S(1)} %copy-done.76, ...), custom_call_target="tpu_custom_call" | custom-call | flops 7200000000 | bytes 1 | tf_op jit(solution)/shard_map/pallas_call | solution.py:373
  453.2 4.2 shard_map.404
  457.4 7.1 %collective-permute-done.51 = bf16[2,80,128]{2,1,0:T(8,128)(2,1)S(1)} collective-permute-done((bf16[2,80,128]{2,1,0:T(8,128)(2,1)S(1)}, bf16[2,80,128]{2,1,0:T(8,128)(2,1)S(1)}, u32[]{:S(2)}, u32[]{:S(2)}) %collective-permute-start.51) | collective-permute-done | bytes 40992 | tf_op jit(solution)/shard_map/ppermute | solution.py:133
  468.0 5.0 shard_map.402
  484.1 3.5 shard_map.403.rest_0_
  489.1 3.6 shard_map.405.rest_1_
  496.9 3.7 fusion.10
  507.6 3.6 shard_map.406.rest_1_
  512.2 16.3 %collective-permute-done.59.rest_0_ = bf16[1024,768]{1,0:T(8,128)(2,1)} collective-permute-done((bf16[1024,768]{1,0:T(8,128)(2,1)}, bf16[1024,768]{1,0:T(8,128)(2,1)}, u32[]{:S(2)}, u32[]{:S(2)}) %collective-permute-start.59) | collective-permute-done | bytes 1572896 | tf_op jit(solution)/shard_map/ppermute | solution.py:87
  528.4 8.1 %collective-permute-done.57 = bf16[512,2048]{1,0:T(8,128)(2,1)} collective-permute-done((bf16[512,2048]{1,0:T(8,128)(2,1)}, bf16[512,2048]{1,0:T(8,128)(2,1)}, u32[]{:S(2)}, u32[]{:S(2)}) %collective-permute-start.57) | collective-permute-done | bytes 2097184 | tf_op jit(solution)/shard_map/ppermute | solution.py:93
  539.9 4.6 shard_map.407
  544.5 4.0 fusion.6
  552.4 4.8 fusion.3.own_ref
  569.6 4.2 collective-permute-done.78
  588.0 14.6 %collective-permute-done.61 = bf16[768,1024]{1,0:T(8,128)(2,1)} collective-permute-done((bf16[768,1024]{1,0:T(8,128)(2,1)S(1)}, bf16[768,1024]{1,0:T(8,128)(2,1)}, u32[]{:S(2)}, u32[]{:S(2)}) %collective-permute-start.61) | collective-permute-done | bytes 1572896 | tf_op jit(solution)/shard_map/ppermute | solution.py:87
  607.4 6.4 shard_map.408
  613.9 3.2 add_convert_fusion.1.own_ref
  628.0 5.3 shard_map.409
  (606 shorter events, 253.1 us)
Async XLA Ops:
  7.2 390.7 %reduce-scatter.5.cloned.1.call-start = ((), (), s32[]{:S(2)}) async-start(), calls=%async_computation.4 | async-start | bytes 5242880 | tf_op jit(solution)/shard_map/reduce_scatter | solution.py:110
  27.7 15.4 %collective-permute-start = (bf16[256,128]{1,0:T(8,128)(2,1)S(1)}, bf16[256,128]{1,0:T(8,128)(2,1)S(1)}, u32[]{:S(2)}, u32[]{:S(2)}) collective-permute-start(bf16[256,128]{1,0:T(8,128)(2,1)S(1)} %slice.361), channel_id=1, source_target_pairs={{0,4},{4,8},{8,12},{12,16},{16,20},{20,24},{24,28},{1,5},{5,9},{9,... | collective-permute-start | bytes 196616 | tf_op jit(solution)/shard_map/ppermute | solution.py:133
  44.3 12.9 %collective-permute-start.1 = (f32[2,80,128]{2,1,0:T(8,128)S(1)}, f32[2,80,128]{2,1,0:T(8,128)S(1)}, u32[]{:S(2)}, u32[]{:S(2)}) collective-permute-start(f32[2,80,128]{2,1,0:T(8,128)S(1)} %get-tuple-element.117), channel_id=1, source_target_pairs={{0,4},{4,8},{8,12},{12,16},{16,20},{20,24},{24,28},{1,5},{5,9},{9,... | collective-permute-start | bytes 245768 | tf_op jit(solution)/shard_map/ppermute | solution.py:133
  62.8 7.3 %collective-permute-start.3 = (f32[2,80,128]{2,1,0:T(8,128)S(1)}, f32[2,80,128]{2,1,0:T(8,128)S(1)}, u32[]{:S(2)}, u32[]{:S(2)}) collective-permute-start(f32[2,80,128]{2,1,0:T(8,128)S(1)} %add.246), channel_id=1, source_target_pairs={{0,16},{4,20},{8,24},{12,28},{1,17},{5,21},{9,25},{13,29},{2,18},{... | collective-permute-start | bytes 245768 | tf_op jit(solution)/shard_map/ppermute | solution.py:133
  86.7 25.3 %collective-permute-start.12 = (bf16[256,2048]{1,0:T(8,128)(2,1)S(1)}, bf16[256,2048]{1,0:T(8,128)(2,1)S(1)}, u32[]{:S(2)}, u32[]{:S(2)}) collective-permute-start(bf16[256,2048]{1,0:T(8,128)(2,1)S(1)} %shard_map.379), channel_id=1, source_target_pairs={{0,2},{1,3},{2,0},{3,1},{4,6},{5,7},{6,4},{7,5},{8,10},{9,11},{10,... | collective-permute-start | bytes 3145736 | tf_op jit(solution)/shard_map/ppermute | solution.py:93
  89.8 49.3 %collective-permute-start.16 = (bf16[512,2048]{1,0:T(8,128)(2,1)}, bf16[512,2048]{1,0:T(8,128)(2,1)S(1)}, u32[]{:S(2)}, u32[]{:S(2)}) collective-permute-start(bf16[512,2048]{1,0:T(8,128)(2,1)} %bitcast.8), channel_id=1, source_target_pairs={{0,4},{4,0},{8,12},{12,8},{16,20},{20,16},{24,28},{28,24},{1,5},{5... | collective-permute-start | bytes 6291464 | tf_op jit(solution)/shard_map/ppermute | solution.py:87
  112.9 25.6 %collective-permute-start.13 = (bf16[256,2048]{1,0:T(8,128)(2,1)S(1)}, bf16[256,2048]{1,0:T(8,128)(2,1)S(1)}, u32[]{:S(2)}, u32[]{:S(2)}) collective-permute-start(bf16[256,2048]{1,0:T(8,128)(2,1)S(1)} %shard_map.378), channel_id=1, source_target_pairs={{0,2},{1,3},{2,0},{3,1},{4,6},{5,7},{6,4},{7,5},{8,10},{9,11},{10,... | collective-permute-start | bytes 3145736 | tf_op jit(solution)/shard_map/ppermute | solution.py:93
  141.0 17.1 %collective-permute-start.15 = (bf16[256,2048]{1,0:T(8,128)(2,1)}, bf16[256,2048]{1,0:T(8,128)(2,1)}, u32[]{:S(2)}, u32[]{:S(2)}) collective-permute-start(bf16[256,2048]{1,0:T(8,128)(2,1)} %multiply_convert_fusion.refs_2_.own_ref), channel_id=1, source_target_pairs={{0,1},{1,0},{2,3},{3,2},{4,5},{5,4},{6,7},{7,6},{8,9},{9,8},{10,11... | collective-permute-start | bytes 3145736 | tf_op jit(solution)/shard_map/ppermute | solution.py:77
  142.9 26.3 %collective-permute-start.22 = (bf16[256,2048]{1,0:T(8,128)(2,1)S(1)}, bf16[256,2048]{1,0:T(8,128)(2,1)}, u32[]{:S(2)}, u32[]{:S(2)}) collective-permute-start(bf16[256,2048]{1,0:T(8,128)(2,1)S(1)} %multiply_convert_fusion.1.own_ref), channel_id=1, source_target_pairs={{0,4},{4,0},{8,12},{12,8},{16,20},{20,16},{24,28},{28,24},{1,5},{5... | collective-permute-start | bytes 3145736 | tf_op jit(solution)/shard_map/ppermute | solution.py:87
  169.3 25.8 %collective-permute-start.21 = (bf16[256,2048]{1,0:T(8,128)(2,1)}, bf16[256,2048]{1,0:T(8,128)(2,1)}, u32[]{:S(2)}, u32[]{:S(2)}) collective-permute-start(bf16[256,2048]{1,0:T(8,128)(2,1)} %multiply_convert_fusion.refs_2_.own_ref), channel_id=1, source_target_pairs={{0,4},{4,0},{8,12},{12,8},{16,20},{20,16},{24,28},{28,24},{1,5},{5... | collective-permute-start | bytes 3145736 | tf_op jit(solution)/shard_map/ppermute | solution.py:87
  233.6 294.9 %reduce-scatter.7.cloned.1.call-start = ((), (), s32[]{:S(2)}) async-start(), calls=%async_computation.5 | async-start | bytes 5242880 | tf_op jit(solution)/shard_map/reduce_scatter | solution.py:110
  258.0 48.0 %collective-permute-start.33 = (bf16[512,2048]{1,0:T(8,128)(2,1)}, bf16[512,2048]{1,0:T(8,128)(2,1)}, u32[]{:S(2)}, u32[]{:S(2)}) collective-permute-start(bf16[512,2048]{1,0:T(8,128)(2,1)} %shard_map.390), channel_id=1, source_target_pairs={{0,4},{4,0},{8,12},{12,8},{16,20},{20,16},{24,28},{28,24},{1,5},{5... | collective-permute-start | bytes 6291464 | tf_op jit(solution)/shard_map/ppermute | solution.py:87
  306.0 257.8 %reduce-scatter.9.cloned.1.call-start = ((), (), s32[]{:S(2)}) async-start(), calls=%async_computation.6 | async-start | bytes 5242880 | tf_op jit(solution)/shard_map/reduce_scatter | solution.py:110
  314.2 47.8 %collective-permute-start.34 = (bf16[512,2048]{1,0:T(8,128)(2,1)S(1)}, bf16[512,2048]{1,0:T(8,128)(2,1)}, u32[]{:S(2)}, u32[]{:S(2)}) collective-permute-start(bf16[512,2048]{1,0:T(8,128)(2,1)S(1)} %shard_map.392.refs_2_), channel_id=1, source_target_pairs={{0,2},{1,3},{2,0},{3,1},{4,6},{5,7},{6,4},{7,5},{8,10},{9,11},{10,... | collective-permute-start | bytes 6291464 | tf_op jit(solution)/shard_map/ppermute | solution.py:93
  324.7 25.6 %collective-permute-start.40 = (bf16[128,2048]{1,0:T(8,128)(2,1)}, bf16[128,2048]{1,0:T(8,128)(2,1)}, u32[]{:S(2)}, u32[]{:S(2)}) collective-permute-start(bf16[128,2048]{1,0:T(8,128)(2,1)} %get-tuple-element.347), channel_id=1, source_target_pairs={{0,1},{1,0},{2,3},{3,2},{4,5},{5,4},{6,7},{7,6},{8,9},{9,8},{10,11... | collective-permute-start | bytes 1572872 | tf_op jit(solution)/shard_map/ppermute | solution.py:77
  324.7 25.6 %collective-permute-start.41 = (bf16[128,2048]{1,0:T(8,128)(2,1)}, bf16[128,2048]{1,0:T(8,128)(2,1)}, u32[]{:S(2)}, u32[]{:S(2)}) collective-permute-start(bf16[128,2048]{1,0:T(8,128)(2,1)} %get-tuple-element.346), channel_id=1, source_target_pairs={{0,1},{1,0},{2,3},{3,2},{4,5},{5,4},{6,7},{7,6},{8,9},{9,8},{10,11... | collective-permute-start | bytes 1572872 | tf_op jit(solution)/shard_map/ppermute | solution.py:77
  325.2 25.1 %collective-permute-start.42 = (bf16[128,2048]{1,0:T(8,128)(2,1)}, bf16[128,2048]{1,0:T(8,128)(2,1)}, u32[]{:S(2)}, u32[]{:S(2)}) collective-permute-start(bf16[128,2048]{1,0:T(8,128)(2,1)} %get-tuple-element.345), channel_id=1, source_target_pairs={{0,1},{1,0},{2,3},{3,2},{4,5},{5,4},{6,7},{7,6},{8,9},{9,8},{10,11... | collective-permute-start | bytes 1572872 | tf_op jit(solution)/shard_map/ppermute | solution.py:77
  325.2 25.1 %collective-permute-start.43 = (bf16[128,2048]{1,0:T(8,128)(2,1)}, bf16[128,2048]{1,0:T(8,128)(2,1)}, u32[]{:S(2)}, u32[]{:S(2)}) collective-permute-start(bf16[128,2048]{1,0:T(8,128)(2,1)} %get-tuple-element.344), channel_id=1, source_target_pairs={{0,1},{1,0},{2,3},{3,2},{4,5},{5,4},{6,7},{7,6},{8,9},{9,8},{10,11... | collective-permute-start | bytes 1572872 | tf_op jit(solution)/shard_map/ppermute | solution.py:77
  362.3 12.8 %collective-permute-start.45 = (bf16[128,2048]{1,0:T(8,128)(2,1)S(1)}, bf16[128,2048]{1,0:T(8,128)(2,1)S(1)}, u32[]{:S(2)}, u32[]{:S(2)}) collective-permute-start(bf16[128,2048]{1,0:T(8,128)(2,1)S(1)} %get-tuple-element.343), channel_id=1, source_target_pairs={{0,1},{1,0},{2,3},{3,2},{4,5},{5,4},{6,7},{7,6},{8,9},{9,8},{10,11... | collective-permute-start | bytes 1572872 | tf_op jit(solution)/shard_map/ppermute | solution.py:77
  362.4 13.7 %collective-permute-start.46 = (bf16[128,2048]{1,0:T(8,128)(2,1)S(1)}, bf16[128,2048]{1,0:T(8,128)(2,1)S(1)}, u32[]{:S(2)}, u32[]{:S(2)}) collective-permute-start(bf16[128,2048]{1,0:T(8,128)(2,1)S(1)} %get-tuple-element.342), channel_id=1, source_target_pairs={{0,1},{1,0},{2,3},{3,2},{4,5},{5,4},{6,7},{7,6},{8,9},{9,8},{10,11... | collective-permute-start | bytes 1572872 | tf_op jit(solution)/shard_map/ppermute | solution.py:77
  362.9 14.4 %collective-permute-start.47 = (bf16[128,2048]{1,0:T(8,128)(2,1)S(1)}, bf16[128,2048]{1,0:T(8,128)(2,1)S(1)}, u32[]{:S(2)}, u32[]{:S(2)}) collective-permute-start(bf16[128,2048]{1,0:T(8,128)(2,1)S(1)} %get-tuple-element.341), channel_id=1, source_target_pairs={{0,1},{1,0},{2,3},{3,2},{4,5},{5,4},{6,7},{7,6},{8,9},{9,8},{10,11... | collective-permute-start | bytes 1572872 | tf_op jit(solution)/shard_map/ppermute | solution.py:77
  363.0 15.3 %collective-permute-start.48 = (bf16[128,2048]{1,0:T(8,128)(2,1)S(1)}, bf16[128,2048]{1,0:T(8,128)(2,1)S(1)}, u32[]{:S(2)}, u32[]{:S(2)}) collective-permute-start(bf16[128,2048]{1,0:T(8,128)(2,1)S(1)} %get-tuple-element.340), channel_id=1, source_target_pairs={{0,1},{1,0},{2,3},{3,2},{4,5},{5,4},{6,7},{7,6},{8,9},{9,8},{10,11... | collective-permute-start | bytes 1572872 | tf_op jit(solution)/shard_map/ppermute | solution.py:77
  372.5 58.1 %collective-permute-start.44 = (bf16[512,2048]{1,0:T(8,128)(2,1)}, bf16[512,2048]{1,0:T(8,128)(2,1)}, u32[]{:S(2)}, u32[]{:S(2)}) collective-permute-start(bf16[512,2048]{1,0:T(8,128)(2,1)} %shard_map.398), channel_id=1, source_target_pairs={{0,4},{4,0},{8,12},{12,8},{16,20},{20,16},{24,28},{28,24},{1,5},{5... | collective-permute-start | bytes 6291464 | tf_op jit(solution)/shard_map/ppermute | solution.py:87
  375.9 13.5 %collective-permute-start.35 = (bf16[128,2048]{1,0:T(8,128)(2,1)}, bf16[128,2048]{1,0:T(8,128)(2,1)}, u32[]{:S(2)}, u32[]{:S(2)}) collective-permute-start(bf16[128,2048]{1,0:T(8,128)(2,1)} %get-tuple-element.351), channel_id=1, source_target_pairs={{0,1},{1,0},{2,3},{3,2},{4,5},{5,4},{6,7},{7,6},{8,9},{9,8},{10,11... | collective-permute-start | bytes 1572872 | tf_op jit(solution)/shard_map/ppermute | solution.py:77
  376.9 12.5 %collective-permute-start.36 = (bf16[128,2048]{1,0:T(8,128)(2,1)}, bf16[128,2048]{1,0:T(8,128)(2,1)}, u32[]{:S(2)}, u32[]{:S(2)}) collective-permute-start(bf16[128,2048]{1,0:T(8,128)(2,1)} %get-tuple-element.350), channel_id=1, source_target_pairs={{0,1},{1,0},{2,3},{3,2},{4,5},{5,4},{6,7},{7,6},{8,9},{9,8},{10,11... | collective-permute-start | bytes 1572872 | tf_op jit(solution)/shard_map/ppermute | solution.py:77
  378.0 11.4 %collective-permute-start.37 = (bf16[128,2048]{1,0:T(8,128)(2,1)}, bf16[128,2048]{1,0:T(8,128)(2,1)}, u32[]{:S(2)}, u32[]{:S(2)}) collective-permute-start(bf16[128,2048]{1,0:T(8,128)(2,1)} %get-tuple-element.349), channel_id=1, source_target_pairs={{0,1},{1,0},{2,3},{3,2},{4,5},{5,4},{6,7},{7,6},{8,9},{9,8},{10,11... | collective-permute-start | bytes 1572872 | tf_op jit(solution)/shard_map/ppermute | solution.py:77
  379.0 10.4 %collective-permute-start.38 = (bf16[128,2048]{1,0:T(8,128)(2,1)}, bf16[128,2048]{1,0:T(8,128)(2,1)}, u32[]{:S(2)}, u32[]{:S(2)}) collective-permute-start(bf16[128,2048]{1,0:T(8,128)(2,1)} %get-tuple-element.348), channel_id=1, source_target_pairs={{0,1},{1,0},{2,3},{3,2},{4,5},{5,4},{6,7},{7,6},{8,9},{9,8},{10,11... | collective-permute-start | bytes 1572872 | tf_op jit(solution)/shard_map/ppermute | solution.py:77
  381.6 251.8 %reduce-scatter.11.cloned.1.call-start = ((), (), s32[]{:S(2)}) async-start(), calls=%async_computation.7 | async-start | bytes 3276800 | tf_op jit(solution)/shard_map/reduce_scatter | solution.py:110
  433.3 31.2 %collective-permute-start.39 = (bf16[512,128]{1,0:T(8,128)(2,1)}, bf16[512,128]{1,0:T(8,128)(2,1)S(1)}, u32[]{:S(2)}, u32[]{:S(2)}) collective-permute-start(bf16[512,128]{1,0:T(8,128)(2,1)} %pad_maximum_fusion.3), channel_id=1, source_target_pairs={{4,0},{8,4},{12,8},{16,12},{20,16},{24,20},{28,24},{5,1},{9,5},{13... | collective-permute-start | bytes 393224 | tf_op jit(solution)/shard_map/ppermute | solution.py:133
  436.5 15.1 %collective-permute-start.50 = (bf16[2,80,128]{2,1,0:T(8,128)(2,1)S(1)}, bf16[2,80,128]{2,1,0:T(8,128)(2,1)S(1)}, u32[]{:S(2)}, u32[]{:S(2)}) collective-permute-start(bf16[2,80,128]{2,1,0:T(8,128)(2,1)S(1)} %fusion.19), channel_id=1, source_target_pairs={{8,0},{12,4},{16,8},{20,12},{24,16},{28,20},{9,1},{13,5},{17,9},{2... | collective-permute-start | bytes 122888 | tf_op jit(solution)/shard_map/ppermute | solution.py:133
  446.9 58.5 %collective-permute-start.60 = (bf16[1024,512]{1,0:T(8,128)(2,1)}, bf16[1024,512]{1,0:T(8,128)(2,1)}, u32[]{:S(2)}, u32[]{:S(2)}) collective-permute-start(bf16[1024,512]{1,0:T(8,128)(2,1)} %shard_map.400.refs_11_), channel_id=1, source_target_pairs={{0,4},{4,0},{8,12},{12,8},{16,20},{20,16},{24,28},{28,24},{1,5},{5... | collective-permute-start | bytes 3145736 | tf_op jit(solution)/shard_map/ppermute | solution.py:87
  451.6 12.8 %collective-permute-start.51 = (bf16[2,80,128]{2,1,0:T(8,128)(2,1)S(1)}, bf16[2,80,128]{2,1,0:T(8,128)(2,1)S(1)}, u32[]{:S(2)}, u32[]{:S(2)}) collective-permute-start(bf16[2,80,128]{2,1,0:T(8,128)(2,1)S(1)} %fusion.18), channel_id=1, source_target_pairs={{16,0},{20,4},{24,8},{28,12},{17,1},{21,5},{25,9},{29,13},{18,2},{... | collective-permute-start | bytes 122888 | tf_op jit(solution)/shard_map/ppermute | solution.py:133
  475.1 7.3 %collective-permute-start.52 = (bf16[128,2048]{1,0:T(8,128)(2,1)}, bf16[128,2048]{1,0:T(8,128)(2,1)S(1)}, u32[]{:S(2)}, u32[]{:S(2)}) collective-permute-start(bf16[128,2048]{1,0:T(8,128)(2,1)} %get-tuple-element.339), channel_id=1, source_target_pairs={{0,1},{1,0},{2,3},{3,2},{4,5},{5,4},{6,7},{7,6},{8,9},{9,8},{10,11... | collective-permute-start | bytes 1572872 | tf_op jit(solution)/shard_map/ppermute | solution.py:77
  475.1 7.3 %collective-permute-start.53 = (bf16[128,2048]{1,0:T(8,128)(2,1)}, bf16[128,2048]{1,0:T(8,128)(2,1)}, u32[]{:S(2)}, u32[]{:S(2)}) collective-permute-start(bf16[128,2048]{1,0:T(8,128)(2,1)} %get-tuple-element.338), channel_id=1, source_target_pairs={{0,1},{1,0},{2,3},{3,2},{4,5},{5,4},{6,7},{7,6},{8,9},{9,8},{10,11... | collective-permute-start | bytes 1572872 | tf_op jit(solution)/shard_map/ppermute | solution.py:77
  475.6 6.8 %collective-permute-start.55 = (bf16[128,2048]{1,0:T(8,128)(2,1)}, bf16[128,2048]{1,0:T(8,128)(2,1)}, u32[]{:S(2)}, u32[]{:S(2)}) collective-permute-start(bf16[128,2048]{1,0:T(8,128)(2,1)} %get-tuple-element.336), channel_id=1, source_target_pairs={{0,1},{1,0},{2,3},{3,2},{4,5},{5,4},{6,7},{7,6},{8,9},{9,8},{10,11... | collective-permute-start | bytes 1572872 | tf_op jit(solution)/shard_map/ppermute | solution.py:77
  487.6 48.9 %collective-permute-start.57 = (bf16[512,2048]{1,0:T(8,128)(2,1)}, bf16[512,2048]{1,0:T(8,128)(2,1)}, u32[]{:S(2)}, u32[]{:S(2)}) collective-permute-start(bf16[512,2048]{1,0:T(8,128)(2,1)} %shard_map.403.rest_0_), channel_id=1, source_target_pairs={{0,2},{1,3},{2,0},{3,1},{4,6},{5,7},{6,4},{7,5},{8,10},{9,11},{10,... | collective-permute-start | bytes 6291464 | tf_op jit(solution)/shard_map/ppermute | solution.py:93
  492.7 35.7 %collective-permute-start.59 = (bf16[1024,768]{1,0:T(8,128)(2,1)}, bf16[1024,768]{1,0:T(8,128)(2,1)}, u32[]{:S(2)}, u32[]{:S(2)}) collective-permute-start(bf16[1024,768]{1,0:T(8,128)(2,1)} %shard_map.405.rest_1_), channel_id=1, source_target_pairs={{0,4},{4,0},{8,12},{12,8},{16,20},{20,16},{24,28},{28,24},{1,5},{5... | collective-permute-start | bytes 4718600 | tf_op jit(solution)/shard_map/ppermute | solution.py:87
  492.7 121.1 %collective-permute-start.56 = (bf16[512,2048]{1,0:T(8,128)(2,1)}, bf16[512,2048]{1,0:T(8,128)(2,1)}, u32[]{:S(2)}, u32[]{:S(2)}) collective-permute-start(bf16[512,2048]{1,0:T(8,128)(2,1)} %shard_map.404), channel_id=1, source_target_pairs={{0,2},{1,3},{2,0},{3,1},{4,6},{5,7},{6,4},{7,5},{8,10},{9,11},{10,... | collective-permute-start | bytes 6291464 | tf_op jit(solution)/shard_map/ppermute | solution.py:93
  548.5 12.4 %collective-permute-start.70 = (f32[2048]{0:T(1024)S(1)}, f32[2048]{0:T(1024)}, u32[]{:S(2)}, u32[]{:S(2)}) collective-permute-start(f32[2048]{0:T(1024)S(1)} %get-tuple-element.308), channel_id=1, source_target_pairs={{0,1},{1,0},{2,3},{3,2},{4,5},{5,4},{6,7},{7,6},{8,9},{9,8},{10,11... | collective-permute-start | bytes 24584 | tf_op jit(solution)/shard_map/ppermute | solution.py:986
  566.4 36.2 %collective-permute-start.61 = (bf16[768,1024]{1,0:T(8,128)(2,1)S(1)}, bf16[768,1024]{1,0:T(8,128)(2,1)}, u32[]{:S(2)}, u32[]{:S(2)}) collective-permute-start(bf16[768,1024]{1,0:T(8,128)(2,1)S(1)} %pad_maximum_fusion.2), channel_id=1, source_target_pairs={{0,4},{4,0},{8,12},{12,8},{16,20},{20,16},{24,28},{28,24},{1,5},{5... | collective-permute-start | bytes 4718600 | tf_op jit(solution)/shard_map/ppermute | solution.py:87
  567.7 7.8 %collective-permute-start.76 = (bf16[14848]{0:T(1024)(128)(2,1)S(1)}, bf16[14848]{0:T(1024)(128)(2,1)S(1)}, u32[]{:S(2)}, u32[]{:S(2)}) collective-permute-start(bf16[14848]{0:T(1024)(128)(2,1)S(1)} %get-tuple-element.312), channel_id=1, source_target_pairs={{0,8},{4,12},{8,16},{12,20},{16,24},{20,28},{24,0},{28,4},{1,9},{5... | collective-permute-start | bytes 89096 | tf_op jit(solution)/shard_map/ppermute | solution.py:127
  580.7 26.7 %collective-permute-start.62 = (bf16[128,2048]{1,0:T(8,128)(2,1)}, bf16[128,2048]{1,0:T(8,128)(2,1)}, u32[]{:S(2)}, u32[]{:S(2)}) collective-permute-start(bf16[128,2048]{1,0:T(8,128)(2,1)} %get-tuple-element.335), channel_id=1, source_target_pairs={{0,1},{1,0},{2,3},{3,2},{4,5},{5,4},{6,7},{7,6},{8,9},{9,8},{10,11... | collective-permute-start | bytes 1572872 | tf_op jit(solution)/shard_map/ppermute | solution.py:77
  581.4 26.0 %collective-permute-start.63 = (bf16[128,2048]{1,0:T(8,128)(2,1)}, bf16[128,2048]{1,0:T(8,128)(2,1)}, u32[]{:S(2)}, u32[]{:S(2)}) collective-permute-start(bf16[128,2048]{1,0:T(8,128)(2,1)} %get-tuple-element.334), channel_id=1, source_target_pairs={{0,1},{1,0},{2,3},{3,2},{4,5},{5,4},{6,7},{7,6},{8,9},{9,8},{10,11... | collective-permute-start | bytes 1572872 | tf_op jit(solution)/shard_map/ppermute | solution.py:77
  588.0 19.4 %collective-permute-start.64 = (bf16[128,2048]{1,0:T(8,128)(2,1)}, bf16[128,2048]{1,0:T(8,128)(2,1)}, u32[]{:S(2)}, u32[]{:S(2)}) collective-permute-start(bf16[128,2048]{1,0:T(8,128)(2,1)} %get-tuple-element.333), channel_id=1, source_target_pairs={{0,1},{1,0},{2,3},{3,2},{4,5},{5,4},{6,7},{7,6},{8,9},{9,8},{10,11... | collective-permute-start | bytes 1572872 | tf_op jit(solution)/shard_map/ppermute | solution.py:77
  618.5 9.5 %collective-permute-start.66 = (bf16[128,2048]{1,0:T(8,128)(2,1)}, bf16[128,2048]{1,0:T(8,128)(2,1)}, u32[]{:S(2)}, u32[]{:S(2)}) collective-permute-start(bf16[128,2048]{1,0:T(8,128)(2,1)} %get-tuple-element.331), channel_id=1, source_target_pairs={{0,1},{1,0},{2,3},{3,2},{4,5},{5,4},{6,7},{7,6},{8,9},{9,8},{10,11... | collective-permute-start | bytes 1572872 | tf_op jit(solution)/shard_map/ppermute | solution.py:77
  619.0 9.0 %collective-permute-start.67 = (bf16[128,2048]{1,0:T(8,128)(2,1)}, bf16[128,2048]{1,0:T(8,128)(2,1)}, u32[]{:S(2)}, u32[]{:S(2)}) collective-permute-start(bf16[128,2048]{1,0:T(8,128)(2,1)} %get-tuple-element.330), channel_id=1, source_target_pairs={{0,1},{1,0},{2,3},{3,2},{4,5},{5,4},{6,7},{7,6},{8,9},{9,8},{10,11... | collective-permute-start | bytes 1572872 | tf_op jit(solution)/shard_map/ppermute | solution.py:77
  619.0 9.0 %collective-permute-start.68 = (bf16[128,2048]{1,0:T(8,128)(2,1)}, bf16[128,2048]{1,0:T(8,128)(2,1)}, u32[]{:S(2)}, u32[]{:S(2)}) collective-permute-start(bf16[128,2048]{1,0:T(8,128)(2,1)} %get-tuple-element.329), channel_id=1, source_target_pairs={{0,1},{1,0},{2,3},{3,2},{4,5},{5,4},{6,7},{7,6},{8,9},{9,8},{10,11... | collective-permute-start | bytes 1572872 | tf_op jit(solution)/shard_map/ppermute | solution.py:77
  619.5 8.5 %collective-permute-start.69 = (bf16[128,2048]{1,0:T(8,128)(2,1)}, bf16[128,2048]{1,0:T(8,128)(2,1)}, u32[]{:S(2)}, u32[]{:S(2)}) collective-permute-start(bf16[128,2048]{1,0:T(8,128)(2,1)} %get-tuple-element.328), channel_id=1, source_target_pairs={{0,1},{1,0},{2,3},{3,2},{4,5},{5,4},{6,7},{7,6},{8,9},{9,8},{10,11... | collective-permute-start | bytes 1572872 | tf_op jit(solution)/shard_map/ppermute | solution.py:77
  (176 other events, 908.1 us)
Sparse Core Ops, SparseCore 0:
  233.7 77.6 reduce-scatter.4
  313.8 77.3 reduce-scatter.6
  393.5 82.6 reduce-scatter.8
  561.0 52.3 reduce-scatter.10
